TPU v7x, 32 devices: a whole 2x2x4 slice. The times are simulated.
32 devices in a mesh: gz: 4 (over y, core), xy: 8 (over z, x).
Axes of the slice: x: 2, y: 2, z: 4, core: 2. Of those that a mesh axis runs over, the one named last changes fastest.
Arguments:
- fine: bfloat16 [1024, 64, 512], P(('gz', 'xy')), may hold values from -6 to 6
- fine_mask: int32 [1024, 512], P(('gz', 'xy')), may hold values 0 or 1
- slot_source: int32 [1024], P(('gz', 'xy')), may hold values from -1 to 31, as said below
- w_down: bfloat16 [512, 128], replicated, may hold values from -0.25 to 0.25
- w_first: bfloat16 [27, 128, 128], replicated, may hold values from -0.109375 to 0.109375
- w_second: bfloat16 [27, 128, 128], replicated, may hold values from -0.109375 to 0.109375
- w_up: bfloat16 [128, 512], replicated, may hold values from -0.5 to 0.5
Outputs:
- fine_out: bfloat16 [1024, 64, 512], P(('gz', 'xy'))
- coarse: bfloat16 [64, 128, 8, 128], P('gz', 'xy')
Inputs may be any that keep to these rules, and one draw needn't show every extreme that they name: `slot_source`: slot entries of device (g, o): a value m names row m of device (g, (o - m // 4) mod 8); on each device every value appears at most once, and between 4 // 2 (at least 1) and 4 of the rows m // 4 = j are named for each j below 8. Rows that no slot names are inactive.
All inputs are finite; a program needn't handle non-finite values. No bound on the sum of `fine_mask` on one device may be relied on, other than what follows from the above.
Results may differ from a plain program's by a relative error of at most 0.0052.
Values may be sent and summed in bfloat16 or wider, within the bound.
No kernel may reach another device: no remote copies, remote signals or barrier semaphores. Data moves between devices by JAX's collectives and lax.ppermute only.
A program may use at most 64 MiB of HBM per device.

v0:
```python
import functools

import jax
import jax.numpy as jnp
from jax import lax
from jax.experimental import pallas as pl
from jax.experimental.pallas import tpu as pltpu
from jax.sharding import PartitionSpec as P

CAP = 4
K = 8
CELLS = 64
SIDE = 16
COLS = 8
WIDE = SIDE + 4
HID = SIDE + 2
VMEM_LIMIT = 56 * 1024 * 1024


def place_of(base, j, sign, rotated):
    if not rotated:
        return j
    return lax.rem(base + sign * j + K, K)


def expand_mask(mask):
    bricks = mask.shape[0]
    values = mask.astype(jnp.float32)
    cell = lax.broadcasted_iota(jnp.int32, (16, 128), 0)
    lane = lax.broadcasted_iota(jnp.int32, (16, 128), 1)
    chosen = (cell == lane // 8).astype(jnp.float32)
    parts = [
        values[:, t * 128 : (t + 1) * 128].reshape(bricks, 1, 128) * chosen[None] for t in range(4)
    ]
    spread = jnp.concatenate(parts, axis=1).reshape(bricks * CELLS, 128).astype(jnp.bfloat16)
    source = lax.broadcasted_iota(jnp.int32, (128, 512), 0)
    target = lax.broadcasted_iota(jnp.int32, (128, 512), 1)
    widen = ((source & 7) == (target >> 6)).astype(jnp.bfloat16)
    return jnp.dot(spread, widen, preferred_element_type=jnp.float32)


def down_kernel(rotated, base_ref, fine_ref, mask_ref, w_ref, out_ref):
    step = pl.program_id(0)
    bricks = fine_ref.shape[0]
    mask = expand_mask(mask_ref[...]).astype(jnp.bfloat16)
    x = fine_ref[...].reshape(bricks * CELLS, -1) * mask
    y = jnp.dot(x, w_ref[...], preferred_element_type=jnp.float32).astype(jnp.bfloat16)
    rows = CAP * CELLS
    for part in range(bricks // CAP):
        j = step * (bricks // CAP) + part
        out_ref[place_of(base_ref[0], j, 1, rotated)] = y[part * rows : (part + 1) * rows]


def down_call(base, fine, mask, w, rotated):
    bricks, cells, width = fine.shape
    mid = w.shape[1]
    step = 8
    return pl.pallas_call(
        functools.partial(down_kernel, rotated),
        grid=(bricks // step,),
        in_specs=[
            pl.BlockSpec(memory_space=pltpu.SMEM),
            pl.BlockSpec((step, cells, width), lambda i: (i, 0, 0)),
            pl.BlockSpec((step, width), lambda i: (i, 0)),
            pl.BlockSpec((width, mid), lambda i: (0, 0)),
        ],
        out_specs=pl.BlockSpec((K, CAP * cells, mid), lambda i: (0, 0, 0)),
        out_shape=jax.ShapeDtypeStruct((K, CAP * cells, mid), jnp.bfloat16),
        compiler_params=pltpu.CompilerParams(vmem_limit_bytes=VMEM_LIMIT),
        name="down",
    )(base, fine, mask, w)


def up_kernel(rotated, base_ref, fine_ref, mask_ref, w_ref, octant_ref, out_ref):
    step = pl.program_id(0)
    bricks, cells, width = fine_ref.shape
    mask = expand_mask(mask_ref[...])
    count = bricks // CAP
    parts = [
        octant_ref[place_of(base_ref[0], step * count + part, 1, rotated)] for part in range(count)
    ]
    octant = jnp.concatenate(parts, axis=0)
    up = jnp.dot(octant, w_ref[...], preferred_element_type=jnp.float32)
    fine = fine_ref[...].reshape(bricks * cells, width).astype(jnp.float32)
    out = jnp.where(mask > 0.5, fine + up, 0.0).astype(jnp.bfloat16)
    out_ref[...] = out.reshape(bricks, cells, width)


def up_call(base, fine, mask, w, octant, rotated):
    bricks, cells, width = fine.shape
    mid = w.shape[0]
    step = 8
    return pl.pallas_call(
        functools.partial(up_kernel, rotated),
        grid=(bricks // step,),
        in_specs=[
            pl.BlockSpec(memory_space=pltpu.SMEM),
            pl.BlockSpec((step, cells, width), lambda i: (i, 0, 0)),
            pl.BlockSpec((step, width), lambda i: (i, 0)),
            pl.BlockSpec((mid, width), lambda i: (0, 0)),
            pl.BlockSpec((K, CAP * cells, mid), lambda i: (0, 0, 0)),
        ],
        out_specs=pl.BlockSpec((step, cells, width), lambda i: (i, 0, 0)),
        out_shape=jax.ShapeDtypeStruct(fine.shape, jnp.bfloat16),
        compiler_params=pltpu.CompilerParams(vmem_limit_bytes=VMEM_LIMIT),
        name="up",
    )(base, fine, mask, w, octant)


def low_half(shape):
    return lax.broadcasted_iota(jnp.int32, shape, len(shape) - 2) < 4


def slot_flags(source_ref, first):
    pair = [jnp.where(source_ref[first + k] >= 0, 1.0, 0.0).astype(jnp.float32) for k in range(2)]
    return jnp.where(low_half((8, 128)), pair[0], pair[1])


def slot_index(depth_brick, row_brick):
    pd, qd = divmod(depth_brick, 2)
    pr, qr = divmod(row_brick, 2)
    return (pd * 2 + pr) * 8 + qd * 4 + qr * 2


def brick_place(rotated, base_ref, value):
    j = value // CAP
    return place_of(base_ref[0], j, -1, rotated), pl.multiple_of((value % CAP) * CELLS, CELLS)


def take_brick(rotated, base_ref, source_ref, arrived_ref, slot):
    value = source_ref[slot]
    place, first = brick_place(rotated, base_ref, jnp.maximum(value, 0))
    brick = arrived_ref[place, pl.ds(first, CELLS), :].astype(jnp.float32)
    return jnp.where(value >= 0, brick, 0.0).reshape(8, 8, 128)


def place_kernel(rotated, base_ref, source_ref, arrived_ref, block_ref, low_ref, high_ref):
    half = low_half((8, 8, 128))
    for depth_brick in range(4):
        for row_brick in range(4):
            slot = slot_index(depth_brick, row_brick)
            b0 = take_brick(rotated, base_ref, source_ref, arrived_ref, slot)
            b1 = take_brick(rotated, base_ref, source_ref, arrived_ref, slot + 1)
            even = jnp.where(half, b0, pltpu.roll(b1, 4, 1))
            odd = jnp.where(half, pltpu.roll(b0, 4, 1), b1)
            both = jnp.stack([even, odd], axis=1).reshape(4, 32, 128).astype(jnp.bfloat16)
            for vd in range(4):
                row = ((depth_brick * 4 + vd) * SIDE + row_brick * 4) * COLS
                block_ref[row : row + 32] = both[vd]
                place = (depth_brick * 4 + vd) * 16
                if row_brick == 0:
                    low_ref[place : place + 16] = both[vd, :16]
                if row_brick == 3:
                    high_ref[place : place + 16] = both[vd, 16:]
    for row_brick, ref in ((0, low_ref), (3, high_ref)):
        flags = [slot_flags(source_ref, slot_index(d, row_brick)) for d in range(4)]
        ref[256:288] = jnp.concatenate(flags, axis=0).astype(jnp.bfloat16)


def place_call(base, source, arrived, rotated):
    mid = arrived.shape[2]
    smem = pl.BlockSpec(memory_space=pltpu.SMEM)
    vmem = pl.BlockSpec(memory_space=pltpu.VMEM)
    return pl.pallas_call(
        functools.partial(place_kernel, rotated),
        in_specs=[smem, smem, vmem],
        out_specs=[vmem] * 3,
        out_shape=[
            jax.ShapeDtypeStruct((rows, mid), jnp.bfloat16)
            for rows in (SIDE * SIDE * COLS, 288, 288)
        ],
        compiler_params=pltpu.CompilerParams(vmem_limit_bytes=VMEM_LIMIT),
        name="place",
    )(base, source, arrived)


def edge_kernel(source_ref, block_ref, before_ref, after_ref, low_ref, high_ref):
    for ref, planes, brick in ((low_ref, (0, 1), 0), (high_ref, (SIDE - 2, SIDE - 1), 3)):
        for k, plane in enumerate(planes):
            start = k * WIDE * COLS
            ref[start : start + 16] = before_ref[plane * 16 : plane * 16 + 16]
            ref[start + 16 : start + 144] = block_ref[plane * 128 : plane * 128 + 128]
            ref[start + 144 : start + 160] = after_ref[plane * 16 : plane * 16 + 16]
        first = 256 + brick * 8
        flags = [before_ref[256:288].astype(jnp.float32)[brick * 8 : brick * 8 + 8]]
        flags += [slot_flags(source_ref, slot_index(brick, r)) for r in range(4)]
        flags += [after_ref[256:288].astype(jnp.float32)[brick * 8 : brick * 8 + 8]]
        ref[320:368] = jnp.concatenate(flags, axis=0).astype(jnp.bfloat16)


def edge_call(source, block, before, after):
    smem = pl.BlockSpec(memory_space=pltpu.SMEM)
    vmem = pl.BlockSpec(memory_space=pltpu.VMEM)
    return pl.pallas_call(
        edge_kernel,
        in_specs=[smem, vmem, vmem, vmem],
        out_specs=[vmem] * 2,
        out_shape=[jax.ShapeDtypeStruct((368, block.shape[1]), jnp.bfloat16)] * 2,
        compiler_params=pltpu.CompilerParams(vmem_limit_bytes=VMEM_LIMIT),
        name="edge",
    )(source, block, before, after)


def column_taps(plane):
    column = lax.broadcasted_iota(jnp.int32, plane.shape, 1)
    left = jnp.where(column == 0, 0.0, pltpu.roll(plane, 1, 1))
    right = jnp.where(column == COLS - 1, 0.0, pltpu.roll(plane, COLS - 1, 1))
    return left, plane, right


def store_taps(here_ref, next_ref, index, plane):
    rows = plane.shape[0]
    width = plane.shape[2]
    empty = jnp.zeros((1, COLS, width), jnp.float32)
    for k, tap in enumerate(column_taps(plane)):
        lanes = slice(k * width, (k + 1) * width)
        here_ref[index, :, lanes] = tap.reshape(rows * COLS, width).astype(jnp.bfloat16)
        moved = jnp.concatenate([tap[1:], empty], axis=0)
        next_ref[index, :, lanes] = moved.reshape(rows * COLS, width).astype(jnp.bfloat16)


def conv_planes(here_ref, next_ref, w_ref, first, planes, rows):
    total = None
    for dd in range(3):
        span = pl.ds(first + dd, planes)
        taps = [
            here_ref[span, 0:rows, :],
            next_ref[span, 0:rows, :],
            here_ref[span, 16 : rows + 16, :],
        ]
        lhs = jnp.concatenate(taps, axis=2)
        lhs = lhs.reshape(planes * rows, lhs.shape[2])
        part = jnp.dot(lhs, w_ref[dd], preferred_element_type=jnp.float32)
        total = part if total is None else total + part
    return total


def as_planes(value):
    value = value.astype(jnp.float32)
    return value.reshape(value.shape[0] // COLS, COLS, value.shape[1])


def conv_kernel(
    rotated,
    base_ref,
    source_ref,
    block_ref,
    before_ref,
    after_ref,
    under_ref,
    over_ref,
    w1_ref,
    w2_ref,
    coarse_ref,
    back_ref,
    x_here,
    x_next,
    h_here,
    h_next,
    flag_ref,
):
    width = block_ref.shape[1]
    for ref, brick in ((under_ref, 0), (over_ref, 5)):
        flags = as_planes(ref[320:368])
        flag_ref[brick] = flags
        for k in range(2):
            plane = as_planes(ref[k * 160 : (k + 1) * 160])
            store_taps(x_here, x_next, (0 if brick == 0 else WIDE - 2) + k, plane)
    flags_before = as_planes(before_ref[256:288])
    flags_after = as_planes(after_ref[256:288])
    for d in range(4):
        flag_ref[d + 1, 0] = flags_before[d]
        for r in range(4):
            flag_ref[d + 1, r + 1] = slot_flags(source_ref, slot_index(d, r))
        flag_ref[d + 1, 5] = flags_after[d]

    @pl.loop(0, SIDE)
    def _(d):
        edge = pl.ds(pl.multiple_of(d * 16, 16), 16)
        own = pl.ds(pl.multiple_of(d * 128, 128), 128)
        plane = jnp.concatenate(
            [as_planes(before_ref[edge]), as_planes(block_ref[own]), as_planes(after_ref[edge])],
            axis=0,
        )
        store_taps(x_here, x_next, d + 2, plane)

    @pl.loop(0, HID // 3)
    def _(group):
        value = conv_planes(x_here, x_next, w1_ref, group * 3, 3, HID * COLS)
        value = (value / (1.0 + jnp.exp(-value))).reshape(3, HID, COLS, width)
        for k in range(3):
            index = group * 3 + k
            flags = flag_ref[(index + 3) // 4]
            spread = jnp.concatenate(
                [flags[0:1]]
                + [jnp.broadcast_to(flags[r : r + 1], (4, COLS, width)) for r in range(1, 5)]
                + [flags[5:6]],
                axis=0,
            )
            store_taps(h_here, h_next, index, value[k] * spread)

    back_ref[...] = jnp.zeros(back_ref.shape, jnp.bfloat16)

    @pl.loop(0, 4)
    def _(depth_brick):
        value = conv_planes(h_here, h_next, w2_ref, depth_brick * 4, 4, SIDE * COLS)
        value = value.reshape(4, SIDE, COLS, width)
        rows = pl.ds(pl.multiple_of(depth_brick * 512, 512), 512)
        own = block_ref[rows].astype(jnp.float32).reshape(4, SIDE, COLS, width)
        flags = flag_ref[depth_brick + 1]
        spread = jnp.concatenate(
            [jnp.broadcast_to(flags[r : r + 1], (4, COLS, width)) for r in range(1, 5)], axis=0
        )
        value = (value + own) * spread[None]
        coarse_ref[rows] = value.reshape(4 * SIDE * COLS, width).astype(jnp.bfloat16)
        half = low_half((4, 2, COLS, width))
        for r in range(4):
            part = value[:, r * 4 : (r + 1) * 4].reshape(4, 2, 2, COLS, width)
            even, odd = part[:, :, 0], part[:, :, 1]
            b0 = jnp.where(half, even, pltpu.roll(odd, 4, 2))
            b1 = jnp.where(half, pltpu.roll(even, 4, 2), odd)
            slot = ((depth_brick // 2) * 2 + r // 2) * 8 + (depth_brick % 2) * 4 + (r % 2) * 2
            for k, brick in enumerate((b0, b1)):
                source = source_ref[slot + k]

                @pl.when(source >= 0)
                def _():
                    place, first = brick_place(rotated, base_ref, source)
                    back_ref[place, pl.ds(first, CELLS), :] = brick.reshape(CELLS, width).astype(
                        jnp.bfloat16
                    )


def conv_call(base, source, block, before, after, under, over, w_first, w_second, rotated):
    mid = block.shape[1]
    smem = pl.BlockSpec(memory_space=pltpu.SMEM)
    vmem = pl.BlockSpec(memory_space=pltpu.VMEM)
    return pl.pallas_call(
        functools.partial(conv_kernel, rotated),
        in_specs=[smem, smem] + [vmem] * 7,
        out_specs=[vmem] * 2,
        out_shape=[
            jax.ShapeDtypeStruct(block.shape, jnp.bfloat16),
            jax.ShapeDtypeStruct((K, CAP * CELLS, mid), jnp.bfloat16),
        ],
        scratch_shapes=[
            pltpu.VMEM((WIDE, WIDE * COLS, 3 * mid), jnp.bfloat16),
            pltpu.VMEM((WIDE, WIDE * COLS, 3 * mid), jnp.bfloat16),
            pltpu.VMEM((HID, HID * COLS, 3 * mid), jnp.bfloat16),
            pltpu.VMEM((HID, HID * COLS, 3 * mid), jnp.bfloat16),
            pltpu.VMEM((6, 6, COLS, mid), jnp.float32),
        ],
        compiler_params=pltpu.CompilerParams(vmem_limit_bytes=VMEM_LIMIT),
        name="conv",
    )(base, source, block, before, after, under, over, w_first, w_second)


def from_behind(value, axis, steps):
    count = lax.axis_size(axis)
    pairs = [(source, (source + steps) % count) for source in range(count)]
    return lax.ppermute(value, axis, pairs)


def exchange(value, rotated, sign):
    if rotated:
        return lax.all_to_all(value, "xy", 0, 0, tiled=True)
    return jnp.stack([from_behind(value[j], "xy", sign * j) for j in range(K)])


def neighbours(low, high, axis):
    count = lax.axis_size(axis)
    forward = [(i, i + 1) for i in range(count - 1)]
    backward = [(target, source) for source, target in forward]
    return lax.ppermute(high, axis, forward), lax.ppermute(low, axis, backward)


def shards(fine, fine_mask, slot_source, w_down, w_first, w_second, w_up):
    rotated = lax.axis_size("xy") == K
    mid = w_down.shape[1]
    base = lax.axis_index("xy").astype(jnp.int32).reshape(1)
    sent = down_call(base, fine, fine_mask, w_down, rotated)
    arrived = exchange(sent, rotated, 1)
    block, low, high = place_call(base, slot_source, arrived, rotated)
    before, after = neighbours(low, high, "xy")
    under_send, over_send = edge_call(slot_source, block, before, after)
    under, over = neighbours(under_send, over_send, "gz")
    coarse, back = conv_call(
        base,
        slot_source,
        block,
        before,
        after,
        under,
        over,
        w_first.reshape(3, 9 * mid, mid),
        w_second.reshape(3, 9 * mid, mid),
        rotated,
    )
    octant = exchange(back, rotated, -1)
    fine_out = up_call(base, fine, fine_mask, w_up, octant, rotated)
    return fine_out, coarse.reshape(SIDE, SIDE, COLS, mid)


def solution(mesh):
    placed = (
        P(("gz", "xy"), None, None),
        P(("gz", "xy"), None),
        P(("gz", "xy")),
        P(),
        P(),
        P(),
        P(),
    )
    return jax.shard_map(
        shards,
        mesh=mesh,
        in_specs=placed,
        out_specs=(P(("gz", "xy"), None, None), P("gz", "xy", None, None)),
        check_vma=False,
    )
```

profile of v0, /device:TPU:0, one launch (start us, length us, event | category | flops | bytes accessed | tf_op | source)
XLA Modules:
  0.0 86.2 jit_solution(79232466385397894)
XLA Ops:
  0.6 4.3 %down.1 = bf16[8,256,128]{2,1,0:T(8,128)(2,1)} custom-call(s32[1]{0:T(128)} %bitcast.base_ref, bf16[32,64,512]{2,1,0:T(8,128)(2,1)} %fine_ref.3, s32[32,512]{1,0:T(8,128)} %mask_ref.3, bf16[512,128]{1,0:T(8,128)(2,1)} %w_ref.2), custom_call_target="tpu_custom_call" | custom-call | tf_op jit(solution)/shard_map/down/pallas_call | solution.py:58
  4.9 21.9 %all_to_all.10.arrived_ref = bf16[8,256,128]{2,1,0:T(8,128)(2,1)} all-to-all(bf16[8,256,128]{2,1,0:T(8,128)(2,1)} %down.1), channel_id=1, replica_groups=mesh['gz'=4,'xy'=8] {'xy'}, dimensions={0} | all-to-all | bytes 1048576 | tf_op jit(solution)/shard_map/all_to_all | solution.py:366
  26.8 2.1 %place.1 = (bf16[2048,128]{1,0:T(8,128)(2,1)}, bf16[288,128]{1,0:T(8,128)(2,1)}, bf16[288,128]{1,0:T(8,128)(2,1)}) custom-call(s32[1]{0:T(128)} %bitcast.base_ref, s32[32]{0:T(128)} %source_ref.5, bf16[8,256,128]{2,1,0:T(8,128)(2,1)} %all_to_all.10.arrived_ref), custom_call_target="tpu_custom_call" | custom-call | tf_op jit(solution)/shard_map/place/pallas_call | solution.py:164
  28.9 3.4 %collective-permute-start = (bf16[288,128]{1,0:T(8,128)(2,1)}, bf16[288,128]{1,0:T(8,128)(2,1)S(1)}, u32[]{:S(2)}, u32[]{:S(2)}) collective-permute-start(bf16[288,128]{1,0:T(8,128)(2,1)} %get-tuple-element.10), channel_id=1, source_target_pairs={{0,1},{1,2},{2,3},{3,4},{4,5},{5,6},{6,7},{8,9},{9,10},{10,11},{11... | collective-permute-start | bytes 221192 | tf_op jit(solution)/shard_map/ppermute | solution.py:374
  32.3 1.3 %collective-permute-start.1 = (bf16[288,128]{1,0:T(8,128)(2,1)}, bf16[288,128]{1,0:T(8,128)(2,1)S(1)}, u32[]{:S(2)}, u32[]{:S(2)}) collective-permute-start(bf16[288,128]{1,0:T(8,128)(2,1)} %get-tuple-element.11), channel_id=1, source_target_pairs={{1,0},{2,1},{3,2},{4,3},{5,4},{6,5},{7,6},{9,8},{10,9},{11,10},{12... | collective-permute-start | bytes 221192 | tf_op jit(solution)/shard_map/ppermute | solution.py:374
  33.6 1.0 %collective-permute-done.before_ref = bf16[288,128]{1,0:T(8,128)(2,1)S(1)} collective-permute-done((bf16[288,128]{1,0:T(8,128)(2,1)}, bf16[288,128]{1,0:T(8,128)(2,1)S(1)}, u32[]{:S(2)}, u32[]{:S(2)}) %collective-permute-start) | collective-permute-done | bytes 73760 | tf_op jit(solution)/shard_map/ppermute | solution.py:374
  34.6 0.0 copy-start
  34.6 4.2 %collective-permute-done.1.after_ref = bf16[288,128]{1,0:T(8,128)(2,1)S(1)} collective-permute-done((bf16[288,128]{1,0:T(8,128)(2,1)}, bf16[288,128]{1,0:T(8,128)(2,1)S(1)}, u32[]{:S(2)}, u32[]{:S(2)}) %collective-permute-start.1) | collective-permute-done | bytes 73760 | tf_op jit(solution)/shard_map/ppermute | solution.py:374
  38.8 0.0 copy-start.1
  38.8 0.0 copy-done
  38.8 0.6 copy-done.1
  39.4 1.8 %edge.1 = (bf16[368,128]{1,0:T(8,128)(2,1)}, bf16[368,128]{1,0:T(8,128)(2,1)}) custom-call(s32[32]{0:T(128)} %source_ref.5, bf16[2048,128]{1,0:T(8,128)(2,1)} %get-tuple-element.9.block_ref, bf16[288,128]{1,0:T(8,128)(2,1)} %copy-done, bf16[288,128]{1,0:T(8,128)(2,1)} %copy-done.1), custom_call_target="tpu_custom_call" | custom-call | tf_op jit(solution)/shard_map/edge/pallas_call | solution.py:194
  41.2 1.3 %collective-permute-start.2 = (bf16[368,128]{1,0:T(8,128)(2,1)}, bf16[368,128]{1,0:T(8,128)(2,1)S(1)}, u32[]{:S(2)}, u32[]{:S(2)}) collective-permute-start(bf16[368,128]{1,0:T(8,128)(2,1)} %get-tuple-element.12), channel_id=1, source_target_pairs={{0,8},{8,16},{16,24},{1,9},{9,17},{17,25},{2,10},{10,18},{18,26},{... | collective-permute-start | bytes 282632 | tf_op jit(solution)/shard_map/ppermute | solution.py:374
  42.5 1.3 %collective-permute-start.3 = (bf16[368,128]{1,0:T(8,128)(2,1)}, bf16[368,128]{1,0:T(8,128)(2,1)S(1)}, u32[]{:S(2)}, u32[]{:S(2)}) collective-permute-start(bf16[368,128]{1,0:T(8,128)(2,1)} %get-tuple-element.13), channel_id=1, source_target_pairs={{8,0},{16,8},{24,16},{9,1},{17,9},{25,17},{10,2},{18,10},{26,18},{... | collective-permute-start | bytes 282632 | tf_op jit(solution)/shard_map/ppermute | solution.py:374
  43.8 0.0 collective-permute-done.2.under_ref
  43.8 0.0 copy-start.2
  43.8 3.8 %collective-permute-done.3.over_ref = bf16[368,128]{1,0:T(8,128)(2,1)S(1)} collective-permute-done((bf16[368,128]{1,0:T(8,128)(2,1)}, bf16[368,128]{1,0:T(8,128)(2,1)S(1)}, u32[]{:S(2)}, u32[]{:S(2)}) %collective-permute-start.3) | collective-permute-done | bytes 94240 | tf_op jit(solution)/shard_map/ppermute | solution.py:374
  47.6 0.0 copy-start.3
  47.6 0.0 copy-done.2
  47.6 0.6 copy-done.3
  48.3 14.8 %conv.1 = (bf16[2048,128]{1,0:T(8,128)(2,1)}, bf16[8,256,128]{2,1,0:T(8,128)(2,1)}) custom-call(s32[1]{0:T(128)} %bitcast.base_ref, s32[32]{0:T(128)} %source_ref.5, bf16[2048,128]{1,0:T(8,128)(2,1)} %get-tuple-element.9.block_ref, bf16[288,128]{1,0:T(8,128)(2,1)} %copy-done, bf16[288,128]{1,0:T(8,128)(2,1)} %copy-done.1, bf16[368,128]{1,0:T(8,128)(2,1)} %copy-done.2, ...), custom_call_target="tpu_custom_call" | custom-call | tf_op jit(solution)/shard_map/conv/pallas_call | solution.py:338
  63.0 18.3 %all_to_all.11.octant_ref = bf16[8,256,128]{2,1,0:T(8,128)(2,1)} all-to-all(bf16[8,256,128]{2,1,0:T(8,128)(2,1)} %get-tuple-element.14), channel_id=1, replica_groups=mesh['gz'=4,'xy'=8] {'xy'}, dimensions={0} | all-to-all | bytes 1048576 | tf_op jit(solution)/shard_map/all_to_all | solution.py:366
  81.4 4.8 %up.1 = bf16[32,64,512]{2,1,0:T(8,128)(2,1)} custom-call(s32[1]{0:T(128)} %bitcast.base_ref, bf16[32,64,512]{2,1,0:T(8,128)(2,1)} %fine_ref.3, s32[32,512]{1,0:T(8,128)} %mask_ref.3, bf16[128,512]{1,0:T(8,128)(2,1)} %w_ref.3, bf16[8,256,128]{2,1,0:T(8,128)(2,1)} %all_to_all.11.octant_ref), custom_call_target="tpu_custom_call" | custom-call | tf_op jit(solution)/shard_map/up/pallas_call | solution.py:93
Async XLA Ops:
  28.9 5.6 %collective-permute-start = (bf16[288,128]{1,0:T(8,128)(2,1)}, bf16[288,128]{1,0:T(8,128)(2,1)S(1)}, u32[]{:S(2)}, u32[]{:S(2)}) collective-permute-start(bf16[288,128]{1,0:T(8,128)(2,1)} %get-tuple-element.10), channel_id=1, source_target_pairs={{0,1},{1,2},{2,3},{3,4},{4,5},{5,6},{6,7},{8,9},{9,10},{10,11},{11... | collective-permute-start | bytes 221192 | tf_op jit(solution)/shard_map/ppermute | solution.py:374
  32.3 6.5 %collective-permute-start.1 = (bf16[288,128]{1,0:T(8,128)(2,1)}, bf16[288,128]{1,0:T(8,128)(2,1)S(1)}, u32[]{:S(2)}, u32[]{:S(2)}) collective-permute-start(bf16[288,128]{1,0:T(8,128)(2,1)} %get-tuple-element.11), channel_id=1, source_target_pairs={{1,0},{2,1},{3,2},{4,3},{5,4},{6,5},{7,6},{9,8},{10,9},{11,10},{12... | collective-permute-start | bytes 221192 | tf_op jit(solution)/shard_map/ppermute | solution.py:374
  34.6 4.2 %copy-start = (bf16[288,128]{1,0:T(8,128)(2,1)}, bf16[288,128]{1,0:T(8,128)(2,1)S(1)}, u32[]{:S(2)}) copy-start(bf16[288,128]{1,0:T(8,128)(2,1)S(1)} %collective-permute-done.before_ref) | copy-start | bytes 221188
  38.8 0.6 copy-start.1
  41.2 2.6 %collective-permute-start.2 = (bf16[368,128]{1,0:T(8,128)(2,1)}, bf16[368,128]{1,0:T(8,128)(2,1)S(1)}, u32[]{:S(2)}, u32[]{:S(2)}) collective-permute-start(bf16[368,128]{1,0:T(8,128)(2,1)} %get-tuple-element.12), channel_id=1, source_target_pairs={{0,8},{8,16},{16,24},{1,9},{9,17},{17,25},{2,10},{10,18},{18,26},{... | collective-permute-start | bytes 282632 | tf_op jit(solution)/shard_map/ppermute | solution.py:374
  42.5 5.1 %collective-permute-start.3 = (bf16[368,128]{1,0:T(8,128)(2,1)}, bf16[368,128]{1,0:T(8,128)(2,1)S(1)}, u32[]{:S(2)}, u32[]{:S(2)}) collective-permute-start(bf16[368,128]{1,0:T(8,128)(2,1)} %get-tuple-element.13), channel_id=1, source_target_pairs={{8,0},{16,8},{24,16},{9,1},{17,9},{25,17},{10,2},{18,10},{26,18},{... | collective-permute-start | bytes 282632 | tf_op jit(solution)/shard_map/ppermute | solution.py:374
  43.8 3.8 %copy-start.2 = (bf16[368,128]{1,0:T(8,128)(2,1)}, bf16[368,128]{1,0:T(8,128)(2,1)S(1)}, u32[]{:S(2)}) copy-start(bf16[368,128]{1,0:T(8,128)(2,1)S(1)} %collective-permute-done.2.under_ref) | copy-start | bytes 282628
  47.6 0.6 copy-start.3
where the time goes:
time: 87.8 us; the launch traced here: 86.2 us
  blocking collectives  40.2 us (46%)
  Pallas kernels  27.8 us (32%)
  waiting for transfers between devices  8.98 us (10%)
  starting transfers between devices  7.22 us (8%)
  local copies, waits for them, and re-layouts  1.28 us (1%)
    all_to_all x2, blocking collectives, exchange(): return lax.all_to_all(value, 'xy', 0, 0, tiled=True)  40.2 us
    pallas_call x1, Pallas kernels, conv_call(): pl.pallas_call(functools.partial(conv_kernel, rotated), in_specs=[smem, s...  14.8 us
    ppermute x2, waiting for transfers between devices, neighbours(): lax.ppermute(low, axis, backward)  8 us
    pallas_call x1, Pallas kernels, up_call(): pl.pallas_call(functools.partial(up_kernel, rotated), grid=(bricks // ste...  4.79 us
    ppermute x2, starting transfers between devices, neighbours(): lax.ppermute(high, axis, forward)  4.64 us
    pallas_call x1, Pallas kernels, down_call(): pl.pallas_call(functools.partial(down_kernel, rotated), grid=(bricks // s...  4.29 us
    ppermute x2, starting transfers between devices, neighbours(): lax.ppermute(low, axis, backward)  2.58 us
    pallas_call x1, Pallas kernels, place_call(): pl.pallas_call(functools.partial(place_kernel, rotated), in_specs=[smem,...  2.14 us
  transfers between devices with their start and end apart: 4, of which 3 were waited for; matrix products, arithmetic and copies ran while one was open for 0% of the time, Pallas kernels for 0%

commit v1 on v0

--- a/solution.py
+++ b/solution.py
@@ -14,7 +14,7 @@
 COLS = 8
 WIDE = SIDE + 4
 HID = SIDE + 2
-VMEM_LIMIT = 56 * 1024 * 1024
+VMEM_LIMIT = 24 * 1024 * 1024
 
 
 def place_of(base, j, sign, rotated):
@@ -201,38 +201,41 @@
     )(source, block, before, after)
 
 
-def column_taps(plane):
-    column = lax.broadcasted_iota(jnp.int32, plane.shape, 1)
-    left = jnp.where(column == 0, 0.0, pltpu.roll(plane, 1, 1))
-    right = jnp.where(column == COLS - 1, 0.0, pltpu.roll(plane, COLS - 1, 1))
-    return left, plane, right
-
-
-def store_taps(here_ref, next_ref, index, plane):
+def store_rows(here_ref, next_ref, index, plane):
     rows = plane.shape[0]
     width = plane.shape[2]
+    here_ref[index] = plane.reshape(rows * COLS, width).astype(jnp.bfloat16)
     empty = jnp.zeros((1, COLS, width), jnp.float32)
-    for k, tap in enumerate(column_taps(plane)):
-        lanes = slice(k * width, (k + 1) * width)
-        here_ref[index, :, lanes] = tap.reshape(rows * COLS, width).astype(jnp.bfloat16)
-        moved = jnp.concatenate([tap[1:], empty], axis=0)
-        next_ref[index, :, lanes] = moved.reshape(rows * COLS, width).astype(jnp.bfloat16)
-
-
-def conv_planes(here_ref, next_ref, w_ref, first, planes, rows):
-    total = None
+    moved = jnp.concatenate([plane[1:], empty], axis=0)
+    next_ref[index] = moved.reshape(rows * COLS, width).astype(jnp.bfloat16)
+
+
+def gather_weights(w_ref, wide_ref):
+    width = w_ref.shape[2]
+    for tap in range(9):
+        for column in range(3):
+            wide_ref[tap * width : (tap + 1) * width, column * width : (column + 1) * width] = (
+                w_ref[tap * 3 + column]
+            )
+
+
+def conv_planes(here_ref, next_ref, wide_ref, first, planes, rows):
+    width = here_ref.shape[2]
+    taps = []
     for dd in range(3):
         span = pl.ds(first + dd, planes)
-        taps = [
+        taps += [
             here_ref[span, 0:rows, :],
             next_ref[span, 0:rows, :],
             here_ref[span, 16 : rows + 16, :],
         ]
-        lhs = jnp.concatenate(taps, axis=2)
-        lhs = lhs.reshape(planes * rows, lhs.shape[2])
-        part = jnp.dot(lhs, w_ref[dd], preferred_element_type=jnp.float32)
-        total = part if total is None else total + part
-    return total
+    lhs = jnp.concatenate(taps, axis=2).reshape(planes * rows, 9 * width)
+    wide = jnp.dot(lhs, wide_ref[...], preferred_element_type=jnp.float32)
+    wide = wide.reshape(planes * rows // COLS, COLS, 3 * width)
+    column = lax.broadcasted_iota(jnp.int32, (planes * rows // COLS, COLS, width), 1)
+    left = jnp.where(column == 0, 0.0, pltpu.roll(wide[:, :, :width], 1, 1))
+    right = jnp.where(column == COLS - 1, 0.0, pltpu.roll(wide[:, :, 2 * width :], COLS - 1, 1))
+    return left + wide[:, :, width : 2 * width] + right
 
 
 def as_planes(value):
@@ -258,14 +261,18 @@
     h_here,
     h_next,
     flag_ref,
+    wide1_ref,
+    wide2_ref,
 ):
     width = block_ref.shape[1]
+    gather_weights(w1_ref, wide1_ref)
+    gather_weights(w2_ref, wide2_ref)
     for ref, brick in ((under_ref, 0), (over_ref, 5)):
         flags = as_planes(ref[320:368])
         flag_ref[brick] = flags
         for k in range(2):
             plane = as_planes(ref[k * 160 : (k + 1) * 160])
-            store_taps(x_here, x_next, (0 if brick == 0 else WIDE - 2) + k, plane)
+            store_rows(x_here, x_next, (0 if brick == 0 else WIDE - 2) + k, plane)
     flags_before = as_planes(before_ref[256:288])
     flags_after = as_planes(after_ref[256:288])
     for d in range(4):
@@ -282,11 +289,11 @@
             [as_planes(before_ref[edge]), as_planes(block_ref[own]), as_planes(after_ref[edge])],
             axis=0,
         )
-        store_taps(x_here, x_next, d + 2, plane)
+        store_rows(x_here, x_next, d + 2, plane)
 
     @pl.loop(0, HID // 3)
     def _(group):
-        value = conv_planes(x_here, x_next, w1_ref, group * 3, 3, HID * COLS)
+        value = conv_planes(x_here, x_next, wide1_ref, group * 3, 3, HID * COLS)
         value = (value / (1.0 + jnp.exp(-value))).reshape(3, HID, COLS, width)
         for k in range(3):
             index = group * 3 + k
@@ -297,13 +304,13 @@
                 + [flags[5:6]],
                 axis=0,
             )
-            store_taps(h_here, h_next, index, value[k] * spread)
+            store_rows(h_here, h_next, index, value[k] * spread)
 
     back_ref[...] = jnp.zeros(back_ref.shape, jnp.bfloat16)
 
     @pl.loop(0, 4)
     def _(depth_brick):
-        value = conv_planes(h_here, h_next, w2_ref, depth_brick * 4, 4, SIDE * COLS)
+        value = conv_planes(h_here, h_next, wide2_ref, depth_brick * 4, 4, SIDE * COLS)
         value = value.reshape(4, SIDE, COLS, width)
         rows = pl.ds(pl.multiple_of(depth_brick * 512, 512), 512)
         own = block_ref[rows].astype(jnp.float32).reshape(4, SIDE, COLS, width)
@@ -344,11 +351,13 @@
             jax.ShapeDtypeStruct((K, CAP * CELLS, mid), jnp.bfloat16),
         ],
         scratch_shapes=[
-            pltpu.VMEM((WIDE, WIDE * COLS, 3 * mid), jnp.bfloat16),
-            pltpu.VMEM((WIDE, WIDE * COLS, 3 * mid), jnp.bfloat16),
-            pltpu.VMEM((HID, HID * COLS, 3 * mid), jnp.bfloat16),
-            pltpu.VMEM((HID, HID * COLS, 3 * mid), jnp.bfloat16),
+            pltpu.VMEM((WIDE, WIDE * COLS, mid), jnp.bfloat16),
+            pltpu.VMEM((WIDE, WIDE * COLS, mid), jnp.bfloat16),
+            pltpu.VMEM((HID, HID * COLS, mid), jnp.bfloat16),
+            pltpu.VMEM((HID, HID * COLS, mid), jnp.bfloat16),
             pltpu.VMEM((6, 6, COLS, mid), jnp.float32),
+            pltpu.VMEM((9 * mid, 3 * mid), jnp.bfloat16),
+            pltpu.VMEM((9 * mid, 3 * mid), jnp.bfloat16),
         ],
         compiler_params=pltpu.CompilerParams(vmem_limit_bytes=VMEM_LIMIT),
         name="conv",
@@ -392,8 +401,8 @@
         after,
         under,
         over,
-        w_first.reshape(3, 9 * mid, mid),
-        w_second.reshape(3, 9 * mid, mid),
+        w_first,
+        w_second,
         rotated,
     )
     octant = exchange(back, rotated, -1)

time: 87.8 us -> 76.7 us (0.87)
  Pallas kernels: 27.8 us -> 16.4 us
  local copies, waits for them, and re-layouts: 1.28 us -> 3.35 us
  blocking collectives: 40.2 us -> 38.9 us
    pallas_call x1, Pallas kernels: 14.8 us -> 10.4 us  [conv_call(): pl.pallas_call(functools.partial(conv_kernel, rotated), in_specs=[smem, s...]
    pallas_call x1, Pallas kernels: 4.29 us -> 1.73 us  [down_call(): pl.pallas_call(functools.partial(down_kernel, rotated), grid=(bricks // s...]
    unnamed x8 -> x16, local copies, waits for them, and re-layouts: 1.28 us -> 3.35 us
    pallas_call x1, Pallas kernels: 4.79 us -> 2.92 us  [up_call(): pl.pallas_call(functools.partial(up_kernel, rotated), grid=(bricks // ste...]
    all_to_all x2, blocking collectives: 40.2 us -> 38.9 us  [exchange(): return lax.all_to_all(value, 'xy', 0, 0, tiled=True)]
    pallas_call x1, Pallas kernels: 2.14 us -> 0.81 us  [place_call(): pl.pallas_call(functools.partial(place_kernel, rotated), in_specs=[smem,...]
    pallas_call x1, Pallas kernels: 1.78 us -> 0.56 us  [edge_call(): pl.pallas_call(edge_kernel, in_specs=[smem, vmem, vmem, vmem], out_specs=...]
where the time goes in v1:
time: 76.7 us; the launch traced here: 75.3 us
  blocking collectives  38.9 us (51%)
  Pallas kernels  16.4 us (21%)
  waiting for transfers between devices  8.58 us (11%)
  starting transfers between devices  7.38 us (10%)
  local copies, waits for them, and re-layouts  3.35 us (4%)
    all_to_all x2, blocking collectives, exchange(): return lax.all_to_all(value, 'xy', 0, 0, tiled=True)  38.9 us
    pallas_call x1, Pallas kernels, conv_call(): pl.pallas_call(functools.partial(conv_kernel, rotated), in_specs=[smem, s...  10.4 us
    ppermute x2, waiting for transfers between devices, neighbours(): lax.ppermute(low, axis, backward)  7.91 us
    ppermute x2, starting transfers between devices, neighbours(): lax.ppermute(high, axis, forward)  4.79 us
    unnamed x16, local copies, waits for them, and re-layouts  3.35 us
    pallas_call x1, Pallas kernels, up_call(): pl.pallas_call(functools.partial(up_kernel, rotated), grid=(bricks // ste...  2.92 us
    ppermute x2, starting transfers between devices, neighbours(): lax.ppermute(low, axis, backward)  2.58 us
    pallas_call x1, Pallas kernels, down_call(): pl.pallas_call(functools.partial(down_kernel, rotated), grid=(bricks // s...  1.73 us
  transfers between devices with their start and end apart: 4, of which 3 were waited for; matrix products, arithmetic and copies ran while one was open for 0% of the time, Pallas kernels for 0%

profile of v1, /device:TPU:0, one launch (start us, length us, event | category | flops | bytes accessed | tf_op | source)
XLA Modules:
  0.0 75.3 jit_solution(8111624851744520174)
XLA Ops:
  0.6 0.0 copy-start.7
  0.6 0.0 copy-start
  0.7 1.6 %copy-done = bf16[32,64,512]{2,1,0:T(8,128)(2,1)S(1)} copy-done((bf16[32,64,512]{2,1,0:T(8,128)(2,1)S(1)}, bf16[32,64,512]{2,1,0:T(8,128)(2,1)}, u32[]{:S(2)}) %copy-start) | copy-done | bytes 2097176
  2.2 0.0 copy-start.4
  2.2 0.8 %copy-done.4 = s32[32,512]{1,0:T(8,128)S(1)} copy-done((s32[32,512]{1,0:T(8,128)S(1)}, s32[32,512]{1,0:T(8,128)}, u32[]{:S(2)}) %copy-start.4) | copy-done | bytes 65560
  3.1 0.0 copy-start.5
  3.1 0.9 %copy-done.5 = bf16[512,128]{1,0:T(8,128)(2,1)S(1)} copy-done((bf16[512,128]{1,0:T(8,128)(2,1)S(1)}, bf16[512,128]{1,0:T(8,128)(2,1)}, u32[]{:S(2)}) %copy-start.5) | copy-done | bytes 131096
  4.0 0.0 copy-start.2
  4.0 0.0 copy-start.3
  4.0 1.7 %down.1 = bf16[8,256,128]{2,1,0:T(8,128)(2,1)S(1)} custom-call(s32[1]{0:T(128)} %bitcast.base_ref, bf16[32,64,512]{2,1,0:T(8,128)(2,1)S(1)} %copy-done, s32[32,512]{1,0:T(8,128)S(1)} %copy-done.4, bf16[512,128]{1,0:T(8,128)(2,1)S(1)} %copy-done.5), custom_call_target="tpu_custom_call" | custom-call | tf_op jit(solution)/shard_map/down/pallas_call | solution.py:58
  5.7 21.6 %all_to_all.10.arrived_ref = bf16[8,256,128]{2,1,0:T(8,128)(2,1)S(1)} all-to-all(bf16[8,256,128]{2,1,0:T(8,128)(2,1)S(1)} %down.1), channel_id=1, replica_groups=mesh['gz'=4,'xy'=8] {'xy'}, dimensions={0} | all-to-all | bytes 1048576 | tf_op jit(solution)/shard_map/all_to_all | solution.py:375
  27.3 0.0 copy-done.7
  27.3 0.8 %place.1 = (bf16[2048,128]{1,0:T(8,128)(2,1)S(1)}, bf16[288,128]{1,0:T(8,128)(2,1)S(1)}, bf16[288,128]{1,0:T(8,128)(2,1)S(1)}) custom-call(s32[1]{0:T(128)} %bitcast.base_ref, s32[32]{0:T(128)S(1)} %copy-done.7, bf16[8,256,128]{2,1,0:T(8,128)(2,1)S(1)} %all_to_all.10.arrived_ref), custom_call_target="tpu_custom_call" | custom-call | tf_op jit(solution)/shard_map/place/pallas_call | solution.py:164
  28.1 3.4 %collective-permute-start = (bf16[288,128]{1,0:T(8,128)(2,1)S(1)}, bf16[288,128]{1,0:T(8,128)(2,1)S(1)}, u32[]{:S(2)}, u32[]{:S(2)}) collective-permute-start(bf16[288,128]{1,0:T(8,128)(2,1)S(1)} %get-tuple-element.10), channel_id=1, source_target_pairs={{0,1},{1,2},{2,3},{3,4},{4,5},{5,6},{6,7},{8,9},{9,10},{10,11},{11... | collective-permute-start | bytes 221192 | tf_op jit(solution)/shard_map/ppermute | solution.py:383
  31.5 1.3 %collective-permute-start.1 = (bf16[288,128]{1,0:T(8,128)(2,1)S(1)}, bf16[288,128]{1,0:T(8,128)(2,1)S(1)}, u32[]{:S(2)}, u32[]{:S(2)}) collective-permute-start(bf16[288,128]{1,0:T(8,128)(2,1)S(1)} %get-tuple-element.11), channel_id=1, source_target_pairs={{1,0},{2,1},{3,2},{4,3},{5,4},{6,5},{7,6},{9,8},{10,9},{11,10},{12... | collective-permute-start | bytes 221192 | tf_op jit(solution)/shard_map/ppermute | solution.py:383
  32.8 0.7 collective-permute-done.before_ref
  33.5 4.3 %collective-permute-done.1.after_ref = bf16[288,128]{1,0:T(8,128)(2,1)S(1)} collective-permute-done((bf16[288,128]{1,0:T(8,128)(2,1)S(1)}, bf16[288,128]{1,0:T(8,128)(2,1)S(1)}, u32[]{:S(2)}, u32[]{:S(2)}) %collective-permute-start.1) | collective-permute-done | bytes 73760 | tf_op jit(solution)/shard_map/ppermute | solution.py:383
  37.8 0.0 copy-start.1
  37.8 0.0 copy-start.6
  37.8 0.6 edge.1
  38.3 1.4 %collective-permute-start.2 = (bf16[368,128]{1,0:T(8,128)(2,1)S(1)}, bf16[368,128]{1,0:T(8,128)(2,1)S(1)}, u32[]{:S(2)}, u32[]{:S(2)}) collective-permute-start(bf16[368,128]{1,0:T(8,128)(2,1)S(1)} %get-tuple-element.12), channel_id=1, source_target_pairs={{0,8},{8,16},{16,24},{1,9},{9,17},{17,25},{2,10},{10,18},{18,26},{... | collective-permute-start | bytes 282632 | tf_op jit(solution)/shard_map/ppermute | solution.py:383
  39.8 1.3 %collective-permute-start.3 = (bf16[368,128]{1,0:T(8,128)(2,1)S(1)}, bf16[368,128]{1,0:T(8,128)(2,1)S(1)}, u32[]{:S(2)}, u32[]{:S(2)}) collective-permute-start(bf16[368,128]{1,0:T(8,128)(2,1)S(1)} %get-tuple-element.13), channel_id=1, source_target_pairs={{8,0},{16,8},{24,16},{9,1},{17,9},{25,17},{10,2},{18,10},{26,18},{... | collective-permute-start | bytes 282632 | tf_op jit(solution)/shard_map/ppermute | solution.py:383
  41.1 0.0 collective-permute-done.2.under_ref
  41.1 3.6 %collective-permute-done.3.over_ref = bf16[368,128]{1,0:T(8,128)(2,1)S(1)} collective-permute-done((bf16[368,128]{1,0:T(8,128)(2,1)S(1)}, bf16[368,128]{1,0:T(8,128)(2,1)S(1)}, u32[]{:S(2)}, u32[]{:S(2)}) %collective-permute-start.3) | collective-permute-done | bytes 94240 | tf_op jit(solution)/shard_map/ppermute | solution.py:383
  44.7 0.0 copy-done.2
  44.7 0.0 copy-done.3
  44.7 10.4 %conv.1 = (bf16[2048,128]{1,0:T(8,128)(2,1)}, bf16[8,256,128]{2,1,0:T(8,128)(2,1)S(1)}) custom-call(s32[1]{0:T(128)} %bitcast.base_ref, s32[32]{0:T(128)S(1)} %copy-done.7, bf16[2048,128]{1,0:T(8,128)(2,1)S(1)} %get-tuple-element.9.block_ref, bf16[288,128]{1,0:T(8,128)(2,1)S(1)} %collective-permute-done.before_ref, ...), custom_call_target="tpu_custom_call" | custom-call | tf_op jit(solution)/shard_map/conv/pallas_call | solution.py:345
  55.1 17.3 %all_to_all.11.octant_ref = bf16[8,256,128]{2,1,0:T(8,128)(2,1)S(1)} all-to-all(bf16[8,256,128]{2,1,0:T(8,128)(2,1)S(1)} %get-tuple-element.14), channel_id=1, replica_groups=mesh['gz'=4,'xy'=8] {'xy'}, dimensions={0} | all-to-all | bytes 1048576 | tf_op jit(solution)/shard_map/all_to_all | solution.py:375
  72.4 0.0 copy-done.1
  72.4 0.0 copy-done.6
  72.4 2.9 %up.1 = bf16[32,64,512]{2,1,0:T(8,128)(2,1)} custom-call(s32[1]{0:T(128)} %bitcast.base_ref, bf16[32,64,512]{2,1,0:T(8,128)(2,1)S(1)} %copy-done.1, s32[32,512]{1,0:T(8,128)S(1)} %copy-done.4, bf16[128,512]{1,0:T(8,128)(2,1)S(1)} %copy-done.6, bf16[8,256,128]{2,1,0:T(8,128)(2,1)S(1)} %all_to_all.11.octant_ref), custom_call_target="tpu_custom_call" | custom-call | tf_op jit(solution)/shard_map/up/pallas_call | solution.py:93
Async XLA Ops:
  0.6 26.7 %copy-start.7 = (s32[32]{0:T(128)S(1)}, s32[32]{0:T(128)}, u32[]{:S(2)}) copy-start(s32[32]{0:T(128)} %source_ref.5) | copy-start | bytes 388
  0.6 1.6 %copy-start = (bf16[32,64,512]{2,1,0:T(8,128)(2,1)S(1)}, bf16[32,64,512]{2,1,0:T(8,128)(2,1)}, u32[]{:S(2)}) copy-start(bf16[32,64,512]{2,1,0:T(8,128)(2,1)} %fine_ref.3) | copy-start | bytes 6291460
  2.2 0.8 %copy-start.4 = (s32[32,512]{1,0:T(8,128)S(1)}, s32[32,512]{1,0:T(8,128)}, u32[]{:S(2)}) copy-start(s32[32,512]{1,0:T(8,128)} %mask_ref.3) | copy-start | bytes 196612
  3.1 0.9 %copy-start.5 = (bf16[512,128]{1,0:T(8,128)(2,1)S(1)}, bf16[512,128]{1,0:T(8,128)(2,1)}, u32[]{:S(2)}) copy-start(bf16[512,128]{1,0:T(8,128)(2,1)} %w_ref.2) | copy-start | bytes 393220
  4.0 40.7 %copy-start.2 = (bf16[27,128,128]{2,1,0:T(8,128)(2,1)S(1)}, bf16[27,128,128]{2,1,0:T(8,128)(2,1)}, u32[]{:S(2)}) copy-start(bf16[27,128,128]{2,1,0:T(8,128)(2,1)} %w1_ref.1) | copy-start | bytes 2654212
  4.0 40.7 %copy-start.3 = (bf16[27,128,128]{2,1,0:T(8,128)(2,1)S(1)}, bf16[27,128,128]{2,1,0:T(8,128)(2,1)}, u32[]{:S(2)}) copy-start(bf16[27,128,128]{2,1,0:T(8,128)(2,1)} %w2_ref.1) | copy-start | bytes 2654212
  28.1 5.3 %collective-permute-start = (bf16[288,128]{1,0:T(8,128)(2,1)S(1)}, bf16[288,128]{1,0:T(8,128)(2,1)S(1)}, u32[]{:S(2)}, u32[]{:S(2)}) collective-permute-start(bf16[288,128]{1,0:T(8,128)(2,1)S(1)} %get-tuple-element.10), channel_id=1, source_target_pairs={{0,1},{1,2},{2,3},{3,4},{4,5},{5,6},{6,7},{8,9},{9,10},{10,11},{11... | collective-permute-start | bytes 221192 | tf_op jit(solution)/shard_map/ppermute | solution.py:383
  31.5 6.2 %collective-permute-start.1 = (bf16[288,128]{1,0:T(8,128)(2,1)S(1)}, bf16[288,128]{1,0:T(8,128)(2,1)S(1)}, u32[]{:S(2)}, u32[]{:S(2)}) collective-permute-start(bf16[288,128]{1,0:T(8,128)(2,1)S(1)} %get-tuple-element.11), channel_id=1, source_target_pairs={{1,0},{2,1},{3,2},{4,3},{5,4},{6,5},{7,6},{9,8},{10,9},{11,10},{12... | collective-permute-start | bytes 221192 | tf_op jit(solution)/shard_map/ppermute | solution.py:383
  37.8 34.6 %copy-start.1 = (bf16[32,64,512]{2,1,0:T(8,128)(2,1)S(1)}, bf16[32,64,512]{2,1,0:T(8,128)(2,1)}, u32[]{:S(2)}) copy-start(bf16[32,64,512]{2,1,0:T(8,128)(2,1)} %fine_ref.3) | copy-start | bytes 6291460
  37.8 34.6 %copy-start.6 = (bf16[128,512]{1,0:T(8,128)(2,1)S(1)}, bf16[128,512]{1,0:T(8,128)(2,1)}, u32[]{:S(2)}) copy-start(bf16[128,512]{1,0:T(8,128)(2,1)} %w_ref.3) | copy-start | bytes 393220
  38.3 2.7 %collective-permute-start.2 = (bf16[368,128]{1,0:T(8,128)(2,1)S(1)}, bf16[368,128]{1,0:T(8,128)(2,1)S(1)}, u32[]{:S(2)}, u32[]{:S(2)}) collective-permute-start(bf16[368,128]{1,0:T(8,128)(2,1)S(1)} %get-tuple-element.12), channel_id=1, source_target_pairs={{0,8},{8,16},{16,24},{1,9},{9,17},{17,25},{2,10},{10,18},{18,26},{... | collective-permute-start | bytes 282632 | tf_op jit(solution)/shard_map/ppermute | solution.py:383
  39.8 4.9 %collective-permute-start.3 = (bf16[368,128]{1,0:T(8,128)(2,1)S(1)}, bf16[368,128]{1,0:T(8,128)(2,1)S(1)}, u32[]{:S(2)}, u32[]{:S(2)}) collective-permute-start(bf16[368,128]{1,0:T(8,128)(2,1)S(1)} %get-tuple-element.13), channel_id=1, source_target_pairs={{8,0},{16,8},{24,16},{9,1},{17,9},{25,17},{10,2},{18,10},{26,18},{... | collective-permute-start | bytes 282632 | tf_op jit(solution)/shard_map/ppermute | solution.py:383

commit v2 on v1

--- a/solution.py
+++ b/solution.py
@@ -14,6 +14,11 @@
 COLS = 8
 WIDE = SIDE + 4
 HID = SIDE + 2
+EARLY = ((1, 3), (4, 4), (8, 4))
+LATE = ((12, 3),)
+EARLY_PLANES = 11
+LATE_PLANES = 3
+DOWN_LIMIT = 62 * 1024 * 1024
 VMEM_LIMIT = 24 * 1024 * 1024
 
 
@@ -39,34 +44,52 @@
     return jnp.dot(spread, widen, preferred_element_type=jnp.float32)
 
 
-def down_kernel(rotated, base_ref, fine_ref, mask_ref, w_ref, out_ref):
-    step = pl.program_id(0)
-    bricks = fine_ref.shape[0]
-    mask = expand_mask(mask_ref[...]).astype(jnp.bfloat16)
-    x = fine_ref[...].reshape(bricks * CELLS, -1) * mask
-    y = jnp.dot(x, w_ref[...], preferred_element_type=jnp.float32).astype(jnp.bfloat16)
+def down_kernel(rotated, base_ref, fine_hbm, mask_hbm, w_hbm, out_ref, fine_ref, mask_ref, w_ref, sems):
+    parts = sems.shape[0] - 2
+    step = fine_hbm.shape[0] // parts
     rows = CAP * CELLS
-    for part in range(bricks // CAP):
-        j = step * (bricks // CAP) + part
-        out_ref[place_of(base_ref[0], j, 1, rotated)] = y[part * rows : (part + 1) * rows]
+    first = [
+        pltpu.make_async_copy(mask_hbm, mask_ref, sems.at[parts]),
+        pltpu.make_async_copy(w_hbm, w_ref, sems.at[parts + 1]),
+    ]
+    chunks = [
+        pltpu.make_async_copy(
+            fine_hbm.at[pl.ds(part * step, step)], fine_ref.at[pl.ds(part * step, step)], sems.at[part]
+        )
+        for part in range(parts)
+    ]
+    for copy in first + chunks:
+        copy.start()
+    for copy in first:
+        copy.wait()
+    for part in range(parts):
+        bricks = slice(part * step, (part + 1) * step)
+        mask = expand_mask(mask_ref[bricks]).astype(jnp.bfloat16)
+        chunks[part].wait()
+        x = fine_ref[bricks].reshape(step * CELLS, -1) * mask
+        y = jnp.dot(x, w_ref[...], preferred_element_type=jnp.float32).astype(jnp.bfloat16)
+        for inner in range(step // CAP):
+            j = part * (step // CAP) + inner
+            out_ref[place_of(base_ref[0], j, 1, rotated)] = y[inner * rows : (inner + 1) * rows]
 
 
 def down_call(base, fine, mask, w, rotated):
     bricks, cells, width = fine.shape
     mid = w.shape[1]
-    step = 8
+    parts = 4
+    hbm = pl.BlockSpec(memory_space=pltpu.HBM)
     return pl.pallas_call(
         functools.partial(down_kernel, rotated),
-        grid=(bricks // step,),
-        in_specs=[
-            pl.BlockSpec(memory_space=pltpu.SMEM),
-            pl.BlockSpec((step, cells, width), lambda i: (i, 0, 0)),
-            pl.BlockSpec((step, width), lambda i: (i, 0)),
-            pl.BlockSpec((width, mid), lambda i: (0, 0)),
-        ],
-        out_specs=pl.BlockSpec((K, CAP * cells, mid), lambda i: (0, 0, 0)),
+        in_specs=[pl.BlockSpec(memory_space=pltpu.SMEM), hbm, hbm, hbm],
+        out_specs=pl.BlockSpec(memory_space=pltpu.VMEM),
         out_shape=jax.ShapeDtypeStruct((K, CAP * cells, mid), jnp.bfloat16),
-        compiler_params=pltpu.CompilerParams(vmem_limit_bytes=VMEM_LIMIT),
+        scratch_shapes=[
+            pltpu.VMEM(fine.shape, fine.dtype),
+            pltpu.VMEM(mask.shape, mask.dtype),
+            pltpu.VMEM(w.shape, w.dtype),
+            pltpu.SemaphoreType.DMA((parts + 2,)),
+        ],
+        compiler_params=pltpu.CompilerParams(vmem_limit_bytes=DOWN_LIMIT),
         name="down",
     )(base, fine, mask, w)
 
@@ -201,15 +224,6 @@
     )(source, block, before, after)
 
 
-def store_rows(here_ref, next_ref, index, plane):
-    rows = plane.shape[0]
-    width = plane.shape[2]
-    here_ref[index] = plane.reshape(rows * COLS, width).astype(jnp.bfloat16)
-    empty = jnp.zeros((1, COLS, width), jnp.float32)
-    moved = jnp.concatenate([plane[1:], empty], axis=0)
-    next_ref[index] = moved.reshape(rows * COLS, width).astype(jnp.bfloat16)
-
-
 def gather_weights(w_ref, wide_ref):
     width = w_ref.shape[2]
     for tap in range(9):
@@ -219,31 +233,177 @@
             )
 
 
+def as_rows(value):
+    value = value.astype(jnp.float32)
+    return value.reshape(value.shape[0] // COLS, COLS, value.shape[1])
+
+
+def moved_rows(rows):
+    empty = jnp.zeros((1,) + rows.shape[1:], jnp.float32)
+    return jnp.concatenate([rows[1:], empty], axis=0)
+
+
+def as_tiles(rows):
+    return rows.reshape(rows.shape[0] * COLS, rows.shape[2]).astype(jnp.bfloat16)
+
+
+def multiply_taps(lhs, wide_ref):
+    width = wide_ref.shape[1] // 3
+    wide = jnp.dot(lhs, wide_ref[...], preferred_element_type=jnp.float32)
+    wide = wide.reshape(lhs.shape[0] // COLS, COLS, 3 * width)
+    column = lax.broadcasted_iota(jnp.int32, (lhs.shape[0] // COLS, COLS, width), 1)
+    left = jnp.where(column == 0, 0.0, pltpu.roll(wide[:, :, :width], 1, 1))
+    right = jnp.where(column == COLS - 1, 0.0, pltpu.roll(wide[:, :, 2 * width :], COLS - 1, 1))
+    return left + wide[:, :, width : 2 * width] + right
+
+
 def conv_planes(here_ref, next_ref, wide_ref, first, planes, rows):
-    width = here_ref.shape[2]
     taps = []
     for dd in range(3):
-        span = pl.ds(first + dd, planes)
+        span = slice(first + dd, first + dd + planes)
         taps += [
             here_ref[span, 0:rows, :],
             next_ref[span, 0:rows, :],
             here_ref[span, 16 : rows + 16, :],
         ]
-    lhs = jnp.concatenate(taps, axis=2).reshape(planes * rows, 9 * width)
-    wide = jnp.dot(lhs, wide_ref[...], preferred_element_type=jnp.float32)
-    wide = wide.reshape(planes * rows // COLS, COLS, 3 * width)
-    column = lax.broadcasted_iota(jnp.int32, (planes * rows // COLS, COLS, width), 1)
-    left = jnp.where(column == 0, 0.0, pltpu.roll(wide[:, :, :width], 1, 1))
-    right = jnp.where(column == COLS - 1, 0.0, pltpu.roll(wide[:, :, 2 * width :], COLS - 1, 1))
-    return left + wide[:, :, width : 2 * width] + right
-
-
-def as_planes(value):
-    value = value.astype(jnp.float32)
-    return value.reshape(value.shape[0] // COLS, COLS, value.shape[1])
-
-
-def conv_kernel(
+    lhs = jnp.concatenate(taps, axis=2)
+    return multiply_taps(lhs.reshape(planes * rows, lhs.shape[2]), wide_ref)
+
+
+def activate(value, flags):
+    return value / (1.0 + jnp.exp(-value)) * flags
+
+
+def spread_flags(flags, repeats):
+    return jnp.concatenate(
+        [jnp.broadcast_to(flag[None], (count,) + flag.shape) for flag, count in zip(flags, repeats)],
+        axis=0,
+    )
+
+
+def inner_planes(source_ref, block_ref, wide1_ref, hidden_ref, here, moved, groups):
+    width = block_ref.shape[1]
+    base = groups[0][0] - 1
+    for d in range(base, groups[-1][0] + groups[-1][1] + 1):
+        plane = block_ref[d * 128 : (d + 1) * 128]
+        here[d - base] = plane
+        moved[d - base] = as_tiles(moved_rows(as_rows(plane)))
+    inner = SIDE - 2
+    rows = inner * COLS
+    for first, planes in groups:
+        value = conv_planes(here, moved, wide1_ref, first - 1 - base, planes, rows)
+        value = value.reshape(planes, inner, COLS, width)
+        flags = [slot_flags(source_ref, slot_index(first // 4, r)) for r in range(4)]
+        value = activate(value, spread_flags(flags, (3, 4, 4, 3))[None])
+        hidden_ref[first - 1 - base : first - 1 - base + planes] = value.reshape(
+            planes, rows, width
+        ).astype(jnp.bfloat16)
+
+
+def inner_kernel(source_ref, block_ref, w1_ref, hidden_ref, wide1_ref, here, moved):
+    gather_weights(w1_ref, wide1_ref)
+    inner_planes(source_ref, block_ref, wide1_ref, hidden_ref, here, moved, EARLY)
+
+
+def conv_cost(rows, width):
+    return pl.CostEstimate(
+        flops=2 * rows * 27 * width * width, bytes_accessed=27 * width * width * 4, transcendentals=0
+    )
+
+
+def inner_call(source, block, w_first):
+    mid = block.shape[1]
+    smem = pl.BlockSpec(memory_space=pltpu.SMEM)
+    vmem = pl.BlockSpec(memory_space=pltpu.VMEM)
+    rows = (SIDE - 2) * COLS
+    return pl.pallas_call(
+        inner_kernel,
+        in_specs=[smem, vmem, vmem],
+        out_specs=[vmem] * 2,
+        out_shape=[
+            jax.ShapeDtypeStruct((EARLY_PLANES, rows, mid), jnp.bfloat16),
+            jax.ShapeDtypeStruct((9 * mid, 3 * mid), jnp.bfloat16),
+        ],
+        scratch_shapes=[pltpu.VMEM((EARLY_PLANES + 2, SIDE * COLS, mid), jnp.bfloat16)] * 2,
+        compiler_params=pltpu.CompilerParams(vmem_limit_bytes=VMEM_LIMIT),
+        cost_estimate=conv_cost(EARLY_PLANES * rows, mid),
+        name="inner",
+    )(source, block, w_first)
+
+
+def side_kernel(
+    source_ref,
+    block_ref,
+    before_ref,
+    after_ref,
+    wide1_ref,
+    w2_ref,
+    hidden_ref,
+    late_ref,
+    wide2_ref,
+    mixed,
+    here,
+    moved,
+):
+    gather_weights(w2_ref, wide2_ref)
+    inner_planes(source_ref, block_ref, wide1_ref, late_ref, here, moved, LATE)
+    width = block_ref.shape[1]
+    for d in range(SIDE):
+        edge = slice(d * 16, (d + 1) * 16)
+        low = as_rows(block_ref[d * 128 : d * 128 + 16])
+        high = as_rows(block_ref[d * 128 + 112 : d * 128 + 128])
+        before = as_rows(before_ref[edge])
+        after = as_rows(after_ref[edge])
+        mixed[0, edge] = as_tiles(jnp.concatenate([before[1:], low[:1]], axis=0))
+        mixed[1, edge] = as_tiles(jnp.concatenate([high[1:], after[:1]], axis=0))
+    inner = SIDE - 2
+    taps = []
+    for dd in range(3):
+        span = slice(dd * 16, (dd + inner) * 16)
+        low = [block_ref[(d + dd) * 128 : (d + dd) * 128 + 16] for d in range(inner)]
+        high = [block_ref[(d + dd) * 128 + 112 : (d + dd) * 128 + 128] for d in range(inner)]
+        taps.append(jnp.concatenate([before_ref[span]] + high, axis=0))
+        taps.append(jnp.concatenate([mixed[0, span], mixed[1, span]], axis=0))
+        taps.append(jnp.concatenate(low + [after_ref[span]], axis=0))
+    value = multiply_taps(jnp.concatenate(taps, axis=1), wide1_ref)
+    depths = (3, 4, 4, 3)
+    edge_flags = (as_rows(before_ref[256:288]), as_rows(after_ref[256:288]))
+    flags = []
+    for side, row_brick in ((0, 0), (1, 3)):
+        own = [slot_flags(source_ref, slot_index(d, row_brick)) for d in range(4)]
+        pairs = [jnp.stack([edge_flags[side][d], own[d]][:: 1 - 2 * side], axis=0) for d in range(4)]
+        flags.append(spread_flags(pairs, depths))
+    flags = jnp.stack(flags, axis=0)
+    value = activate(value.reshape(2, inner, 2, COLS, width), flags)
+    hidden_ref[...] = value.reshape(2, inner, 16, width).astype(jnp.bfloat16)
+
+
+def side_call(source, block, before, after, wide1, w_second):
+    mid = block.shape[1]
+    smem = pl.BlockSpec(memory_space=pltpu.SMEM)
+    vmem = pl.BlockSpec(memory_space=pltpu.VMEM)
+    inner = SIDE - 2
+    return pl.pallas_call(
+        side_kernel,
+        in_specs=[smem] + [vmem] * 5,
+        out_specs=[vmem] * 3,
+        out_shape=[
+            jax.ShapeDtypeStruct((2, inner, 16, mid), jnp.bfloat16),
+            jax.ShapeDtypeStruct((LATE_PLANES, inner * COLS, mid), jnp.bfloat16),
+            jax.ShapeDtypeStruct((9 * mid, 3 * mid), jnp.bfloat16),
+        ],
+        scratch_shapes=[
+            pltpu.VMEM((2, SIDE * 16, mid), jnp.bfloat16),
+            pltpu.VMEM((LATE_PLANES + 2, SIDE * COLS, mid), jnp.bfloat16),
+            pltpu.VMEM((LATE_PLANES + 2, SIDE * COLS, mid), jnp.bfloat16),
+        ],
+        compiler_params=pltpu.CompilerParams(vmem_limit_bytes=VMEM_LIMIT),
+        cost_estimate=conv_cost(inner * (4 + LATE_PLANES) * COLS, mid),
+        name="side",
+    )(source, block, before, after, wide1, w_second)
+
+
+def final_kernel(
     rotated,
     base_ref,
     source_ref,
@@ -252,73 +412,67 @@
     after_ref,
     under_ref,
     over_ref,
-    w1_ref,
-    w2_ref,
+    early_ref,
+    late_ref,
+    side_ref,
+    wide1_ref,
+    wide2_ref,
     coarse_ref,
     back_ref,
     x_here,
     x_next,
     h_here,
     h_next,
-    flag_ref,
-    wide1_ref,
-    wide2_ref,
+    stage,
 ):
     width = block_ref.shape[1]
-    gather_weights(w1_ref, wide1_ref)
-    gather_weights(w2_ref, wide2_ref)
-    for ref, brick in ((under_ref, 0), (over_ref, 5)):
-        flags = as_planes(ref[320:368])
-        flag_ref[brick] = flags
+    flags_before = as_rows(before_ref[256:288])
+    flags_after = as_rows(after_ref[256:288])
+    for end, ref in ((0, under_ref), (1, over_ref)):
+        planes = []
+        own = [0, 1] if end == 0 else [SIDE - 2, SIDE - 1]
+        for d in own:
+            edge = slice(d * 16, (d + 1) * 16)
+            planes.append(
+                jnp.concatenate(
+                    [before_ref[edge], block_ref[d * 128 : (d + 1) * 128], after_ref[edge]], axis=0
+                )
+            )
+        far = [ref[k * 160 : (k + 1) * 160] for k in range(2)]
+        for index, plane in enumerate(far + planes if end == 0 else planes + far):
+            x_here[index] = plane
+            x_next[index] = as_tiles(moved_rows(as_rows(plane)))
+        value = conv_planes(x_here, x_next, wide1_ref, 0, 2, HID * COLS)
+        value = value.reshape(2, HID, COLS, width)
+        far_flags = as_rows(ref[320:368])
+        brick = 0 if end == 0 else 3
+        own_flags = [flags_before[brick]]
+        own_flags += [slot_flags(source_ref, slot_index(brick, r)) for r in range(4)]
+        own_flags += [flags_after[brick]]
+        spread = [
+            spread_flags([far_flags[r] for r in range(6)], (1, 4, 4, 4, 4, 1)),
+            spread_flags(own_flags, (1, 4, 4, 4, 4, 1)),
+        ]
         for k in range(2):
-            plane = as_planes(ref[k * 160 : (k + 1) * 160])
-            store_rows(x_here, x_next, (0 if brick == 0 else WIDE - 2) + k, plane)
-    flags_before = as_planes(before_ref[256:288])
-    flags_after = as_planes(after_ref[256:288])
-    for d in range(4):
-        flag_ref[d + 1, 0] = flags_before[d]
-        for r in range(4):
-            flag_ref[d + 1, r + 1] = slot_flags(source_ref, slot_index(d, r))
-        flag_ref[d + 1, 5] = flags_after[d]
-
-    @pl.loop(0, SIDE)
-    def _(d):
-        edge = pl.ds(pl.multiple_of(d * 16, 16), 16)
-        own = pl.ds(pl.multiple_of(d * 128, 128), 128)
-        plane = jnp.concatenate(
-            [as_planes(before_ref[edge]), as_planes(block_ref[own]), as_planes(after_ref[edge])],
-            axis=0,
-        )
-        store_rows(x_here, x_next, d + 2, plane)
-
-    @pl.loop(0, HID // 3)
-    def _(group):
-        value = conv_planes(x_here, x_next, wide1_ref, group * 3, 3, HID * COLS)
-        value = (value / (1.0 + jnp.exp(-value))).reshape(3, HID, COLS, width)
-        for k in range(3):
-            index = group * 3 + k
-            flags = flag_ref[(index + 3) // 4]
-            spread = jnp.concatenate(
-                [flags[0:1]]
-                + [jnp.broadcast_to(flags[r : r + 1], (4, COLS, width)) for r in range(1, 5)]
-                + [flags[5:6]],
-                axis=0,
-            )
-            store_rows(h_here, h_next, index, value[k] * spread)
-
-    back_ref[...] = jnp.zeros(back_ref.shape, jnp.bfloat16)
-
-    @pl.loop(0, 4)
-    def _(depth_brick):
+            flags = spread[k if end == 0 else 1 - k]
+            rows = activate(value[k], flags)
+            index = k if end == 0 else HID - 2 + k
+            h_here[index] = as_tiles(rows)
+            h_next[index] = as_tiles(moved_rows(rows))
+    for d in range(SIDE - 2):
+        middle = early_ref[d] if d < EARLY_PLANES else late_ref[d - EARLY_PLANES]
+        plane = jnp.concatenate([side_ref[0, d], middle, side_ref[1, d]], axis=0)
+        h_here[d + 2] = plane
+        h_next[d + 2] = as_tiles(moved_rows(as_rows(plane)))
+
+    stage[...] = jnp.zeros(stage.shape, jnp.bfloat16)
+    for depth_brick in range(4):
         value = conv_planes(h_here, h_next, wide2_ref, depth_brick * 4, 4, SIDE * COLS)
         value = value.reshape(4, SIDE, COLS, width)
-        rows = pl.ds(pl.multiple_of(depth_brick * 512, 512), 512)
+        rows = slice(depth_brick * 512, (depth_brick + 1) * 512)
         own = block_ref[rows].astype(jnp.float32).reshape(4, SIDE, COLS, width)
-        flags = flag_ref[depth_brick + 1]
-        spread = jnp.concatenate(
-            [jnp.broadcast_to(flags[r : r + 1], (4, COLS, width)) for r in range(1, 5)], axis=0
-        )
-        value = (value + own) * spread[None]
+        flags = [slot_flags(source_ref, slot_index(depth_brick, r)) for r in range(4)]
+        value = (value + own) * spread_flags(flags, (4, 4, 4, 4))[None]
         coarse_ref[rows] = value.reshape(4 * SIDE * COLS, width).astype(jnp.bfloat16)
         half = low_half((4, 2, COLS, width))
         for r in range(4):
@@ -326,42 +480,40 @@
             even, odd = part[:, :, 0], part[:, :, 1]
             b0 = jnp.where(half, even, pltpu.roll(odd, 4, 2))
             b1 = jnp.where(half, pltpu.roll(even, 4, 2), odd)
-            slot = ((depth_brick // 2) * 2 + r // 2) * 8 + (depth_brick % 2) * 4 + (r % 2) * 2
+            slot = slot_index(depth_brick, r)
             for k, brick in enumerate((b0, b1)):
                 source = source_ref[slot + k]
-
-                @pl.when(source >= 0)
-                def _():
-                    place, first = brick_place(rotated, base_ref, source)
-                    back_ref[place, pl.ds(first, CELLS), :] = brick.reshape(CELLS, width).astype(
-                        jnp.bfloat16
-                    )
-
-
-def conv_call(base, source, block, before, after, under, over, w_first, w_second, rotated):
+                place, first = brick_place(rotated, base_ref, jnp.maximum(source, 0))
+                row = jnp.where(source >= 0, place * CAP * CELLS + first, K * CAP * CELLS)
+                row = pl.multiple_of(row, CELLS)
+                stage[pl.ds(row, CELLS), :] = brick.reshape(CELLS, width).astype(jnp.bfloat16)
+    for place in range(K):
+        back_ref[place] = stage[place * CAP * CELLS : (place + 1) * CAP * CELLS]
+
+
+def final_call(base, source, block, halo, hidden, wide1, wide2, rotated):
     mid = block.shape[1]
     smem = pl.BlockSpec(memory_space=pltpu.SMEM)
     vmem = pl.BlockSpec(memory_space=pltpu.VMEM)
     return pl.pallas_call(
-        functools.partial(conv_kernel, rotated),
-        in_specs=[smem, smem] + [vmem] * 7,
+        functools.partial(final_kernel, rotated),
+        in_specs=[smem, smem] + [vmem] * 10,
         out_specs=[vmem] * 2,
         out_shape=[
             jax.ShapeDtypeStruct(block.shape, jnp.bfloat16),
             jax.ShapeDtypeStruct((K, CAP * CELLS, mid), jnp.bfloat16),
         ],
         scratch_shapes=[
-            pltpu.VMEM((WIDE, WIDE * COLS, mid), jnp.bfloat16),
-            pltpu.VMEM((WIDE, WIDE * COLS, mid), jnp.bfloat16),
+            pltpu.VMEM((4, WIDE * COLS, mid), jnp.bfloat16),
+            pltpu.VMEM((4, WIDE * COLS, mid), jnp.bfloat16),
             pltpu.VMEM((HID, HID * COLS, mid), jnp.bfloat16),
             pltpu.VMEM((HID, HID * COLS, mid), jnp.bfloat16),
-            pltpu.VMEM((6, 6, COLS, mid), jnp.float32),
-            pltpu.VMEM((9 * mid, 3 * mid), jnp.bfloat16),
-            pltpu.VMEM((9 * mid, 3 * mid), jnp.bfloat16),
+            pltpu.VMEM(((K * CAP + 1) * CELLS, mid), jnp.bfloat16),
         ],
         compiler_params=pltpu.CompilerParams(vmem_limit_bytes=VMEM_LIMIT),
-        name="conv",
-    )(base, source, block, before, after, under, over, w_first, w_second)
+        cost_estimate=conv_cost(SIDE * SIDE * COLS, mid),
+        name="final",
+    )(base, source, block, *halo, *hidden, wide1, wide2)
 
 
 def from_behind(value, axis, steps):
@@ -391,18 +543,19 @@
     arrived = exchange(sent, rotated, 1)
     block, low, high = place_call(base, slot_source, arrived, rotated)
     before, after = neighbours(low, high, "xy")
+    early, wide1 = inner_call(slot_source, block, w_first)
+    before, after, early, wide1 = lax.optimization_barrier((before, after, early, wide1))
     under_send, over_send = edge_call(slot_source, block, before, after)
     under, over = neighbours(under_send, over_send, "gz")
-    coarse, back = conv_call(
+    side, late, wide2 = side_call(slot_source, block, before, after, wide1, w_second)
+    coarse, back = final_call(
         base,
         slot_source,
         block,
-        before,
-        after,
-        under,
-        over,
-        w_first,
-        w_second,
+        (before, after, under, over),
+        (early, late, side),
+        wide1,
+        wide2,
         rotated,
     )
     octant = exchange(back, rotated, -1)

time: 76.7 us -> 70.5 us (0.919)
  waiting for transfers between devices: 8.58 us -> 4.18 us
  local copies, waits for them, and re-layouts: 3.35 us -> 0.03 us
  Pallas kernels: 16.4 us -> 17.8 us
    ppermute x2, waiting for transfers between devices: 7.91 us -> 4.18 us  [neighbours(): lax.ppermute(low, axis, backward)]
    unnamed x16 -> x12, local copies, waits for them, and re-layouts: 3.35 us -> 0.03 us
    pallas_call x2 -> x4, Pallas kernels: 12.1 us -> 13.4 us  [the longest x1 5.07 us: final_call(): pl.pallas_call(functools.partial(final_kernel, rotated), in_specs=[smem,...]
  transfers between devices with their start and end apart: 4 -> 4, of which waited for: 3 -> 2; matrix products, arithmetic and copies ran while one was open for 0% -> 0% of each run, Pallas kernels for 0% -> 6%
where the time goes in v2:
time: 70.5 us; the launch traced here: 69.1 us
  blocking collectives  39.1 us (55%)
  Pallas kernels  17.8 us (25%)
  starting transfers between devices  7.25 us (10%)
  waiting for transfers between devices  4.18 us (6%)
  between operations  0.77 us (1%)
    all_to_all x2, blocking collectives, exchange(): return lax.all_to_all(value, 'xy', 0, 0, tiled=True)  39.1 us
    pallas_call x1, Pallas kernels, final_call(): pl.pallas_call(functools.partial(final_kernel, rotated), in_specs=[smem,...  5.07 us
    ppermute x2, starting transfers between devices, neighbours(): lax.ppermute(high, axis, forward)  4.67 us
    ppermute x2, waiting for transfers between devices, neighbours(): lax.ppermute(low, axis, backward)  4.18 us
    pallas_call x1, Pallas kernels, down_call(): pl.pallas_call(functools.partial(down_kernel, rotated), in_specs=[pl.Bloc...  4.03 us
    pallas_call x1, Pallas kernels, up_call(): pl.pallas_call(functools.partial(up_kernel, rotated), grid=(bricks // ste...  2.98 us
    ppermute x2, starting transfers between devices, neighbours(): lax.ppermute(low, axis, backward)  2.58 us
    pallas_call x1, Pallas kernels, inner_call(): pl.pallas_call(inner_kernel, in_specs=[smem, vmem, vmem], out_specs=[vmem...  2.42 us
  transfers between devices with their start and end apart: 4, of which 2 were waited for; matrix products, arithmetic and copies ran while one was open for 0% of the time, Pallas kernels for 6%

profile of v2, /device:TPU:0, one launch (start us, length us, event | category | flops | bytes accessed | tf_op | source)
XLA Modules:
  0.0 69.1 jit_solution(7626312818053509496)
XLA Ops:
  0.6 0.0 copy-start.3
  0.6 0.0 copy-start.4
  0.7 4.0 %down.1 = bf16[8,256,128]{2,1,0:T(8,128)(2,1)} custom-call(s32[1]{0:T(128)} %bitcast.base_ref, bf16[32,64,512]{2,1,0:T(8,128)(2,1)} %fine_ref.1, s32[32,512]{1,0:T(8,128)} %mask_ref.1, bf16[512,128]{1,0:T(8,128)(2,1)} %w_hbm.1), custom_call_target="tpu_custom_call" | custom-call | tf_op jit(solution)/shard_map/down/pallas_call | solution.py:81
  4.7 21.8 %all_to_all.10.arrived_ref = bf16[8,256,128]{2,1,0:T(8,128)(2,1)S(1)} all-to-all(bf16[8,256,128]{2,1,0:T(8,128)(2,1)} %down.1), channel_id=1, replica_groups=mesh['gz'=4,'xy'=8] {'xy'}, dimensions={0} | all-to-all | bytes 1048576 | tf_op jit(solution)/shard_map/all_to_all | solution.py:527
  26.5 0.0 copy-done.3
  26.5 0.8 %place.1 = (bf16[2048,128]{1,0:T(8,128)(2,1)S(1)}, bf16[288,128]{1,0:T(8,128)(2,1)S(1)}, bf16[288,128]{1,0:T(8,128)(2,1)S(1)}) custom-call(s32[1]{0:T(128)} %bitcast.base_ref, s32[32]{0:T(128)S(1)} %copy-done.3, bf16[8,256,128]{2,1,0:T(8,128)(2,1)S(1)} %all_to_all.10.arrived_ref), custom_call_target="tpu_custom_call" | custom-call | tf_op jit(solution)/shard_map/place/pallas_call | solution.py:187
  27.3 3.4 %collective-permute-start = (bf16[288,128]{1,0:T(8,128)(2,1)S(1)}, bf16[288,128]{1,0:T(8,128)(2,1)S(1)}, u32[]{:S(2)}, u32[]{:S(2)}) collective-permute-start(bf16[288,128]{1,0:T(8,128)(2,1)S(1)} %get-tuple-element.19), channel_id=1, source_target_pairs={{0,1},{1,2},{2,3},{3,4},{4,5},{5,6},{6,7},{8,9},{9,10},{10,11},{11... | collective-permute-start | bytes 221192 | tf_op jit(solution)/shard_map/ppermute | solution.py:535
  30.7 1.3 %collective-permute-start.1 = (bf16[288,128]{1,0:T(8,128)(2,1)S(1)}, bf16[288,128]{1,0:T(8,128)(2,1)S(1)}, u32[]{:S(2)}, u32[]{:S(2)}) collective-permute-start(bf16[288,128]{1,0:T(8,128)(2,1)S(1)} %get-tuple-element.20), channel_id=1, source_target_pairs={{1,0},{2,1},{3,2},{4,3},{5,4},{6,5},{7,6},{9,8},{10,9},{11,10},{12... | collective-permute-start | bytes 221192 | tf_op jit(solution)/shard_map/ppermute | solution.py:535
  32.0 0.0 copy-done.4
  32.0 0.0 copy-start.5
  32.0 2.4 %inner.1 = (bf16[11,112,128]{2,1,0:T(8,128)(2,1)S(1)}, bf16[1152,384]{1,0:T(8,128)(2,1)S(1)}) custom-call(s32[32]{0:T(128)S(1)} %copy-done.3, bf16[2048,128]{1,0:T(8,128)(2,1)S(1)} %get-tuple-element.18.block_ref, bf16[27,128,128]{2,1,0:T(8,128)(2,1)S(1)} %copy-done.4), custom_call_target="tpu_custom_call" | custom-call | flops 1089994752 | bytes 1769472 | tf_op jit(solution)/shard_map/inner/pallas_call | solution.py:319
  34.4 0.0 collective-permute-done.before_ref
  34.5 2.5 %collective-permute-done.1.after_ref = bf16[288,128]{1,0:T(8,128)(2,1)S(1)} collective-permute-done((bf16[288,128]{1,0:T(8,128)(2,1)S(1)}, bf16[288,128]{1,0:T(8,128)(2,1)S(1)}, u32[]{:S(2)}, u32[]{:S(2)}) %collective-permute-start.1) | collective-permute-done | bytes 73760 | tf_op jit(solution)/shard_map/ppermute | solution.py:535
  36.9 0.6 edge.1
  37.5 1.3 %collective-permute-start.2 = (bf16[368,128]{1,0:T(8,128)(2,1)S(1)}, bf16[368,128]{1,0:T(8,128)(2,1)S(1)}, u32[]{:S(2)}, u32[]{:S(2)}) collective-permute-start(bf16[368,128]{1,0:T(8,128)(2,1)S(1)} %get-tuple-element.25), channel_id=1, source_target_pairs={{0,8},{8,16},{16,24},{1,9},{9,17},{17,25},{2,10},{10,18},{18,26},{... | collective-permute-start | bytes 282632 | tf_op jit(solution)/shard_map/ppermute | solution.py:535
  38.8 1.3 %collective-permute-start.3 = (bf16[368,128]{1,0:T(8,128)(2,1)S(1)}, bf16[368,128]{1,0:T(8,128)(2,1)S(1)}, u32[]{:S(2)}, u32[]{:S(2)}) collective-permute-start(bf16[368,128]{1,0:T(8,128)(2,1)S(1)} %get-tuple-element.26), channel_id=1, source_target_pairs={{8,0},{16,8},{24,16},{9,1},{17,9},{25,17},{10,2},{18,10},{26,18},{... | collective-permute-start | bytes 282632 | tf_op jit(solution)/shard_map/ppermute | solution.py:535
  40.1 0.0 copy-done.5
  40.1 1.9 %side.1 = (bf16[2,14,16,128]{3,2,1,0:T(8,128)(2,1)S(1)}, bf16[3,112,128]{2,1,0:T(8,128)(2,1)S(1)}, bf16[1152,384]{1,0:T(8,128)(2,1)S(1)}) custom-call(s32[32]{0:T(128)S(1)} %copy-done.3, bf16[2048,128]{1,0:T(8,128)(2,1)S(1)} %get-tuple-element.18.block_ref, bf16[288,128]{1,0:T(8,128)(2,1)S(1)} %collective-permute-done.before_ref, ...), custom_call_target="tpu_custom_call" | custom-call | flops 693633024 | bytes 1769472 | tf_op jit(solution)/shard_map/side/pallas_call | solution.py:386
  42.0 0.0 collective-permute-done.2.under_ref
  42.0 1.7 %collective-permute-done.3.over_ref = bf16[368,128]{1,0:T(8,128)(2,1)S(1)} collective-permute-done((bf16[368,128]{1,0:T(8,128)(2,1)S(1)}, bf16[368,128]{1,0:T(8,128)(2,1)S(1)}, u32[]{:S(2)}, u32[]{:S(2)}) %collective-permute-start.3) | collective-permute-done | bytes 94240 | tf_op jit(solution)/shard_map/ppermute | solution.py:535
  43.7 0.0 copy-start
  43.7 0.0 copy-start.1
  43.7 0.0 copy-start.2
  43.7 5.1 %final.1 = (bf16[2048,128]{1,0:T(8,128)(2,1)}, bf16[8,256,128]{2,1,0:T(8,128)(2,1)S(1)}) custom-call(s32[1]{0:T(128)} %bitcast.base_ref, s32[32]{0:T(128)S(1)} %copy-done.3, bf16[2048,128]{1,0:T(8,128)(2,1)S(1)} %get-tuple-element.18.block_ref, bf16[288,128]{1,0:T(8,128)(2,1)S(1)} %collective-permute-done.before_ref, ...), custom_call_target="tpu_custom_call" | custom-call | flops 1811939328 | bytes 1769472 | tf_op jit(solution)/shard_map/final/pallas_call | solution.py:498
  48.8 17.3 %all_to_all.11.octant_ref = bf16[8,256,128]{2,1,0:T(8,128)(2,1)S(1)} all-to-all(bf16[8,256,128]{2,1,0:T(8,128)(2,1)S(1)} %get-tuple-element.32), channel_id=1, replica_groups=mesh['gz'=4,'xy'=8] {'xy'}, dimensions={0} | all-to-all | bytes 1048576 | tf_op jit(solution)/shard_map/all_to_all | solution.py:527
  66.1 0.0 copy-done
  66.1 0.0 copy-done.1
  66.1 0.0 copy-done.2
  66.2 3.0 %up.1 = bf16[32,64,512]{2,1,0:T(8,128)(2,1)} custom-call(s32[1]{0:T(128)} %bitcast.base_ref, bf16[32,64,512]{2,1,0:T(8,128)(2,1)S(1)} %copy-done, s32[32,512]{1,0:T(8,128)S(1)} %copy-done.1, bf16[128,512]{1,0:T(8,128)(2,1)S(1)} %copy-done.2, bf16[8,256,128]{2,1,0:T(8,128)(2,1)S(1)} %all_to_all.11.octant_ref), custom_call_target="tpu_custom_call" | custom-call | tf_op jit(solution)/shard_map/up/pallas_call | solution.py:116
Async XLA Ops:
  0.6 25.9 %copy-start.3 = (s32[32]{0:T(128)S(1)}, s32[32]{0:T(128)}, u32[]{:S(2)}) copy-start(s32[32]{0:T(128)} %source_ref.9) | copy-start | bytes 388
  0.6 31.3 %copy-start.4 = (bf16[27,128,128]{2,1,0:T(8,128)(2,1)S(1)}, bf16[27,128,128]{2,1,0:T(8,128)(2,1)}, u32[]{:S(2)}) copy-start(bf16[27,128,128]{2,1,0:T(8,128)(2,1)} %w1_ref.1) | copy-start | bytes 2654212
  27.3 7.1 %collective-permute-start = (bf16[288,128]{1,0:T(8,128)(2,1)S(1)}, bf16[288,128]{1,0:T(8,128)(2,1)S(1)}, u32[]{:S(2)}, u32[]{:S(2)}) collective-permute-start(bf16[288,128]{1,0:T(8,128)(2,1)S(1)} %get-tuple-element.19), channel_id=1, source_target_pairs={{0,1},{1,2},{2,3},{3,4},{4,5},{5,6},{6,7},{8,9},{9,10},{10,11},{11... | collective-permute-start | bytes 221192 | tf_op jit(solution)/shard_map/ppermute | solution.py:535
  30.7 6.2 %collective-permute-start.1 = (bf16[288,128]{1,0:T(8,128)(2,1)S(1)}, bf16[288,128]{1,0:T(8,128)(2,1)S(1)}, u32[]{:S(2)}, u32[]{:S(2)}) collective-permute-start(bf16[288,128]{1,0:T(8,128)(2,1)S(1)} %get-tuple-element.20), channel_id=1, source_target_pairs={{1,0},{2,1},{3,2},{4,3},{5,4},{6,5},{7,6},{9,8},{10,9},{11,10},{12... | collective-permute-start | bytes 221192 | tf_op jit(solution)/shard_map/ppermute | solution.py:535
  32.0 8.1 %copy-start.5 = (bf16[27,128,128]{2,1,0:T(8,128)(2,1)S(1)}, bf16[27,128,128]{2,1,0:T(8,128)(2,1)}, u32[]{:S(2)}) copy-start(bf16[27,128,128]{2,1,0:T(8,128)(2,1)} %w2_ref.1) | copy-start | bytes 2654212
  37.5 4.5 %collective-permute-start.2 = (bf16[368,128]{1,0:T(8,128)(2,1)S(1)}, bf16[368,128]{1,0:T(8,128)(2,1)S(1)}, u32[]{:S(2)}, u32[]{:S(2)}) collective-permute-start(bf16[368,128]{1,0:T(8,128)(2,1)S(1)} %get-tuple-element.25), channel_id=1, source_target_pairs={{0,8},{8,16},{16,24},{1,9},{9,17},{17,25},{2,10},{10,18},{18,26},{... | collective-permute-start | bytes 282632 | tf_op jit(solution)/shard_map/ppermute | solution.py:535
  38.8 4.9 %collective-permute-start.3 = (bf16[368,128]{1,0:T(8,128)(2,1)S(1)}, bf16[368,128]{1,0:T(8,128)(2,1)S(1)}, u32[]{:S(2)}, u32[]{:S(2)}) collective-permute-start(bf16[368,128]{1,0:T(8,128)(2,1)S(1)} %get-tuple-element.26), channel_id=1, source_target_pairs={{8,0},{16,8},{24,16},{9,1},{17,9},{25,17},{10,2},{18,10},{26,18},{... | collective-permute-start | bytes 282632 | tf_op jit(solution)/shard_map/ppermute | solution.py:535
  43.7 22.4 %copy-start = (bf16[32,64,512]{2,1,0:T(8,128)(2,1)S(1)}, bf16[32,64,512]{2,1,0:T(8,128)(2,1)}, u32[]{:S(2)}) copy-start(bf16[32,64,512]{2,1,0:T(8,128)(2,1)} %fine_ref.1) | copy-start | bytes 6291460
  43.7 22.4 %copy-start.1 = (s32[32,512]{1,0:T(8,128)S(1)}, s32[32,512]{1,0:T(8,128)}, u32[]{:S(2)}) copy-start(s32[32,512]{1,0:T(8,128)} %mask_ref.1) | copy-start | bytes 196612
  43.7 22.4 %copy-start.2 = (bf16[128,512]{1,0:T(8,128)(2,1)S(1)}, bf16[128,512]{1,0:T(8,128)(2,1)}, u32[]{:S(2)}) copy-start(bf16[128,512]{1,0:T(8,128)(2,1)} %w_ref.1) | copy-start | bytes 393220

commit v3 on v2

--- a/solution.py
+++ b/solution.py
@@ -157,7 +157,9 @@
     return jnp.where(value >= 0, brick, 0.0).reshape(8, 8, 128)
 
 
-def place_kernel(rotated, base_ref, source_ref, arrived_ref, block_ref, low_ref, high_ref):
+def place_kernel(
+    rotated, base_ref, source_ref, arrived_ref, block_ref, even_ref, odd_ref, low_ref, high_ref
+):
     half = low_half((8, 8, 128))
     for depth_brick in range(4):
         for row_brick in range(4):
@@ -178,6 +180,43 @@
     for row_brick, ref in ((0, low_ref), (3, high_ref)):
         flags = [slot_flags(source_ref, slot_index(d, row_brick)) for d in range(4)]
         ref[256:288] = jnp.concatenate(flags, axis=0).astype(jnp.bfloat16)
+    face_out(base_ref[0], low_ref, high_ref, even_ref, odd_ref)
+
+
+def face_out(index, low_ref, high_ref, even_ref, odd_ref):
+    is_even = index % 2 == 0
+
+    @pl.when(is_even)
+    def _():
+        even_ref[...] = high_ref[...]
+        odd_ref[...] = low_ref[...]
+
+    @pl.when(jnp.logical_not(is_even))
+    def _():
+        even_ref[...] = low_ref[...]
+        odd_ref[...] = high_ref[...]
+
+
+def face_in(index, count, even_ref, odd_ref, low_ref, high_ref):
+    is_even = index % 2 == 0
+
+    @pl.when(is_even)
+    def _():
+        low_ref[...] = odd_ref[0]
+        high_ref[...] = even_ref[1]
+
+    @pl.when(jnp.logical_not(is_even))
+    def _():
+        low_ref[...] = even_ref[0]
+        high_ref[...] = odd_ref[1]
+
+    @pl.when(index == 0)
+    def _():
+        low_ref[...] = jnp.zeros(low_ref.shape, low_ref.dtype)
+
+    @pl.when(index == count - 1)
+    def _():
+        high_ref[...] = jnp.zeros(high_ref.shape, high_ref.dtype)
 
 
 def place_call(base, source, arrived, rotated):
@@ -192,36 +231,55 @@
             jax.ShapeDtypeStruct((rows, mid), jnp.bfloat16)
             for rows in (SIDE * SIDE * COLS, 288, 288)
         ],
+        scratch_shapes=[pltpu.VMEM((288, mid), jnp.bfloat16)] * 2,
         compiler_params=pltpu.CompilerParams(vmem_limit_bytes=VMEM_LIMIT),
         name="place",
     )(base, source, arrived)
 
 
-def edge_kernel(source_ref, block_ref, before_ref, after_ref, low_ref, high_ref):
+def edge_kernel(
+    counts,
+    base_ref,
+    source_ref,
+    block_ref,
+    even_ref,
+    odd_ref,
+    before_ref,
+    after_ref,
+    even_out,
+    odd_out,
+    low_ref,
+    high_ref,
+):
+    face_in(base_ref[0], counts[1], even_ref, odd_ref, before_ref, after_ref)
     for ref, planes, brick in ((low_ref, (0, 1), 0), (high_ref, (SIDE - 2, SIDE - 1), 3)):
         for k, plane in enumerate(planes):
             start = k * WIDE * COLS
             ref[start : start + 16] = before_ref[plane * 16 : plane * 16 + 16]
             ref[start + 16 : start + 144] = block_ref[plane * 128 : plane * 128 + 128]
             ref[start + 144 : start + 160] = after_ref[plane * 16 : plane * 16 + 16]
-        first = 256 + brick * 8
         flags = [before_ref[256:288].astype(jnp.float32)[brick * 8 : brick * 8 + 8]]
         flags += [slot_flags(source_ref, slot_index(brick, r)) for r in range(4)]
         flags += [after_ref[256:288].astype(jnp.float32)[brick * 8 : brick * 8 + 8]]
         ref[320:368] = jnp.concatenate(flags, axis=0).astype(jnp.bfloat16)
-
-
-def edge_call(source, block, before, after):
+    face_out(base_ref[1], low_ref, high_ref, even_out, odd_out)
+
+
+def edge_call(counts, base, source, block, even, odd):
     smem = pl.BlockSpec(memory_space=pltpu.SMEM)
     vmem = pl.BlockSpec(memory_space=pltpu.VMEM)
+    mid = block.shape[1]
     return pl.pallas_call(
-        edge_kernel,
-        in_specs=[smem, vmem, vmem, vmem],
-        out_specs=[vmem] * 2,
-        out_shape=[jax.ShapeDtypeStruct((368, block.shape[1]), jnp.bfloat16)] * 2,
+        functools.partial(edge_kernel, counts),
+        in_specs=[smem, smem, vmem, vmem, vmem],
+        out_specs=[vmem] * 4,
+        out_shape=[
+            jax.ShapeDtypeStruct((rows, mid), jnp.bfloat16) for rows in (288, 288, 368, 368)
+        ],
+        scratch_shapes=[pltpu.VMEM((368, mid), jnp.bfloat16)] * 2,
         compiler_params=pltpu.CompilerParams(vmem_limit_bytes=VMEM_LIMIT),
         name="edge",
-    )(source, block, before, after)
+    )(base, source, block, even, odd)
 
 
 def gather_weights(w_ref, wide_ref):
@@ -405,13 +463,14 @@
 
 def final_kernel(
     rotated,
+    counts,
     base_ref,
     source_ref,
     block_ref,
     before_ref,
     after_ref,
-    under_ref,
-    over_ref,
+    even_ref,
+    odd_ref,
     early_ref,
     late_ref,
     side_ref,
@@ -424,8 +483,11 @@
     h_here,
     h_next,
     stage,
+    under_ref,
+    over_ref,
 ):
     width = block_ref.shape[1]
+    face_in(base_ref[1], counts[0], even_ref, odd_ref, under_ref, over_ref)
     flags_before = as_rows(before_ref[256:288])
     flags_after = as_rows(after_ref[256:288])
     for end, ref in ((0, under_ref), (1, over_ref)):
@@ -491,12 +553,12 @@
         back_ref[place] = stage[place * CAP * CELLS : (place + 1) * CAP * CELLS]
 
 
-def final_call(base, source, block, halo, hidden, wide1, wide2, rotated):
+def final_call(counts, base, source, block, halo, hidden, wide1, wide2, rotated):
     mid = block.shape[1]
     smem = pl.BlockSpec(memory_space=pltpu.SMEM)
     vmem = pl.BlockSpec(memory_space=pltpu.VMEM)
     return pl.pallas_call(
-        functools.partial(final_kernel, rotated),
+        functools.partial(final_kernel, rotated, counts),
         in_specs=[smem, smem] + [vmem] * 10,
         out_specs=[vmem] * 2,
         out_shape=[
@@ -509,6 +571,8 @@
             pltpu.VMEM((HID, HID * COLS, mid), jnp.bfloat16),
             pltpu.VMEM((HID, HID * COLS, mid), jnp.bfloat16),
             pltpu.VMEM(((K * CAP + 1) * CELLS, mid), jnp.bfloat16),
+            pltpu.VMEM((368, mid), jnp.bfloat16),
+            pltpu.VMEM((368, mid), jnp.bfloat16),
         ],
         compiler_params=pltpu.CompilerParams(vmem_limit_bytes=VMEM_LIMIT),
         cost_estimate=conv_cost(SIDE * SIDE * COLS, mid),
@@ -528,31 +592,36 @@
     return jnp.stack([from_behind(value[j], "xy", sign * j) for j in range(K)])
 
 
-def neighbours(low, high, axis):
+def pair_faces(even, odd, axis):
     count = lax.axis_size(axis)
-    forward = [(i, i + 1) for i in range(count - 1)]
-    backward = [(target, source) for source, target in forward]
-    return lax.ppermute(high, axis, forward), lax.ppermute(low, axis, backward)
+    firsts = [[i, i + 1] for i in range(0, count, 2)]
+    seconds = [[i, (i + 1) % count] for i in range(1, count, 2)]
+    return (
+        lax.all_gather(even, axis, axis_index_groups=firsts),
+        lax.all_gather(odd, axis, axis_index_groups=seconds),
+    )
 
 
 def shards(fine, fine_mask, slot_source, w_down, w_first, w_second, w_up):
     rotated = lax.axis_size("xy") == K
     mid = w_down.shape[1]
-    base = lax.axis_index("xy").astype(jnp.int32).reshape(1)
+    base = jnp.stack([lax.axis_index("xy"), lax.axis_index("gz")]).astype(jnp.int32)
+    counts = (lax.axis_size("gz"), lax.axis_size("xy"))
     sent = down_call(base, fine, fine_mask, w_down, rotated)
     arrived = exchange(sent, rotated, 1)
-    block, low, high = place_call(base, slot_source, arrived, rotated)
-    before, after = neighbours(low, high, "xy")
+    block, even, odd = place_call(base, slot_source, arrived, rotated)
+    even, odd = pair_faces(even, odd, "xy")
     early, wide1 = inner_call(slot_source, block, w_first)
-    before, after, early, wide1 = lax.optimization_barrier((before, after, early, wide1))
-    under_send, over_send = edge_call(slot_source, block, before, after)
-    under, over = neighbours(under_send, over_send, "gz")
+    even, odd, early, wide1 = lax.optimization_barrier((even, odd, early, wide1))
+    before, after, even, odd = edge_call(counts, base, slot_source, block, even, odd)
+    even, odd = pair_faces(even, odd, "gz")
     side, late, wide2 = side_call(slot_source, block, before, after, wide1, w_second)
     coarse, back = final_call(
+        counts,
         base,
         slot_source,
         block,
-        (before, after, under, over),
+        (before, after, even, odd),
         (early, late, side),
         wide1,
         wide2,

time: 70.5 us -> 80.8 us (1.15); the launches traced: 69.1 us -> 80.5 us
  blocking collectives: 39.1 us -> 60 us
  starting transfers between devices: 7.25 us -> 0 us
  waiting for transfers between devices: 4.18 us -> 0 us
  Pallas kernels: 17.8 us -> 19.1 us
    all_gather x0 -> x4, blocking collectives: none -> 20 us  [the longest x2 13.1 us: pair_faces(): lax.all_gather(odd, axis, axis_index_groups=seconds)]
    ppermute x4 -> x0, starting transfers between devices: 7.25 us -> none  [the longest x2 4.67 us: neighbours(): lax.ppermute(high, axis, forward)]
    ppermute x4 -> x0, waiting for transfers between devices: 4.18 us -> none  [the longest x2 4.18 us: neighbours(): lax.ppermute(low, axis, backward)]
    all_to_all x2, blocking collectives: 39.1 us -> 40 us  [exchange(): return lax.all_to_all(value, 'xy', 0, 0, tiled=True)]
  transfers between devices with their start and end apart: 4 -> 0, of which waited for: 2 -> 0; matrix products, arithmetic and copies ran while one was open for 0% -> 0% of each run, Pallas kernels for 6% -> 0%
where the time goes in v3:
time: 80.8 us; the launch traced here: 80.5 us
  blocking collectives  60 us (74%)
  Pallas kernels  19.1 us (24%)
    all_to_all x2, blocking collectives, exchange(): return lax.all_to_all(value, 'xy', 0, 0, tiled=True)  40 us
    all_gather x2, blocking collectives, pair_faces(): lax.all_gather(odd, axis, axis_index_groups=seconds)  13.1 us
    all_gather x2, blocking collectives, pair_faces(): lax.all_gather(even, axis, axis_index_groups=firsts)  6.97 us
    pallas_call x1, Pallas kernels, final_call(): pl.pallas_call(functools.partial(final_kernel, rotated, counts), in_specs...  5.1 us
    pallas_call x1, Pallas kernels, down_call(): pl.pallas_call(functools.partial(down_kernel, rotated), in_specs=[pl.Bloc...  4.75 us
    pallas_call x1, Pallas kernels, up_call(): pl.pallas_call(functools.partial(up_kernel, rotated), grid=(bricks // ste...  3.5 us
    pallas_call x1, Pallas kernels, inner_call(): pl.pallas_call(inner_kernel, in_specs=[smem, vmem, vmem], out_specs=[vmem...  2.41 us
    pallas_call x1, Pallas kernels, side_call(): pl.pallas_call(side_kernel, in_specs=[smem] + [vmem] * 5, out_specs=[vmem...  1.91 us

profile of v3, /device:TPU:0, one launch (start us, length us, event | category | flops | bytes accessed | tf_op | source)
XLA Modules:
  0.0 80.5 jit_solution(2914945490839980616)
XLA Ops:
  0.6 0.0 copy-start.4
  0.6 0.6 pad_add_fusion.base_ref
  1.3 0.0 copy-start.3
  1.3 0.0 copy-start.5
  1.3 4.7 %down.1 = bf16[8,256,128]{2,1,0:T(8,128)(2,1)} custom-call(s32[2]{0:T(128)} %pad_add_fusion.base_ref, bf16[32,64,512]{2,1,0:T(8,128)(2,1)} %fine_ref.1, s32[32,512]{1,0:T(8,128)} %mask_ref.1, bf16[512,128]{1,0:T(8,128)(2,1)} %w_hbm.1), custom_call_target="tpu_custom_call" | custom-call | tf_op jit(solution)/shard_map/down/pallas_call | solution.py:81
  6.1 21.8 %all_to_all.10.arrived_ref = bf16[8,256,128]{2,1,0:T(8,128)(2,1)S(1)} all-to-all(bf16[8,256,128]{2,1,0:T(8,128)(2,1)} %down.1), channel_id=1, replica_groups=mesh['gz'=4,'xy'=8] {'xy'}, dimensions={0} | all-to-all | bytes 1048576 | tf_op jit(solution)/shard_map/all_to_all | solution.py:591
  27.8 0.0 copy-done.4
  27.8 0.0 copy-done.3
  27.9 0.8 %place.1 = (bf16[2048,128]{1,0:T(8,128)(2,1)S(1)}, bf16[288,128]{1,0:T(8,128)(2,1)S(1)}, bf16[288,128]{1,0:T(8,128)(2,1)S(1)}) custom-call(s32[2]{0:T(128)S(1)} %copy-done.3, s32[32]{0:T(128)S(1)} %copy-done.4, bf16[8,256,128]{2,1,0:T(8,128)(2,1)S(1)} %all_to_all.10.arrived_ref), custom_call_target="tpu_custom_call" | custom-call | tf_op jit(solution)/shard_map/place/pallas_call | solution.py:226
  28.7 5.0 %all-gather = bf16[576,128]{1,0:T(8,128)(2,1)S(1)} all-gather(bf16[288,128]{1,0:T(8,128)(2,1)S(1)} %get-tuple-element.21), channel_id=2, replica_groups={{0,1},{2,3},{4,5},{6,7},{8,9},{10,11},{12,13},{14,15},{16,17},{18,19},{..., dimensions={0}, use_global_device_ids=true | all-gather | bytes 221184 | tf_op jit(solution)/shard_map/all_gather | solution.py:600
  33.7 7.7 %all-gather.1 = bf16[576,128]{1,0:T(8,128)(2,1)S(1)} all-gather(bf16[288,128]{1,0:T(8,128)(2,1)S(1)} %get-tuple-element.22), channel_id=3, replica_groups={{1,2},{3,4},{5,6},{7,0},{9,10},{11,12},{13,14},{15,8},{17,18},{19,20},{..., dimensions={0}, use_global_device_ids=true | all-gather | bytes 221184 | tf_op jit(solution)/shard_map/all_gather | solution.py:601
  41.4 0.0 copy-done.5
  41.4 0.0 copy-start.6
  41.5 2.4 %inner.1 = (bf16[11,112,128]{2,1,0:T(8,128)(2,1)S(1)}, bf16[1152,384]{1,0:T(8,128)(2,1)S(1)}) custom-call(s32[32]{0:T(128)S(1)} %copy-done.4, bf16[2048,128]{1,0:T(8,128)(2,1)S(1)} %get-tuple-element.20.block_ref, bf16[27,128,128]{2,1,0:T(8,128)(2,1)S(1)} %copy-done.5), custom_call_target="tpu_custom_call" | custom-call | flops 1089994752 | bytes 1769472 | tf_op jit(solution)/shard_map/inner/pallas_call | solution.py:377
  43.9 0.6 edge.1
  44.5 1.9 %all-gather.2 = bf16[736,128]{1,0:T(8,128)(2,1)S(1)} all-gather(bf16[368,128]{1,0:T(8,128)(2,1)S(1)} %get-tuple-element.29), channel_id=4, replica_groups={{0,8},{16,24},{1,9},{17,25},{2,10},{18,26},{3,11},{19,27},{4,12},{20,28..., dimensions={0}, use_global_device_ids=true | all-gather | bytes 282624 | tf_op jit(solution)/shard_map/all_gather | solution.py:600
  46.4 5.3 %all-gather.3 = bf16[736,128]{1,0:T(8,128)(2,1)S(1)} all-gather(bf16[368,128]{1,0:T(8,128)(2,1)S(1)} %get-tuple-element.30), channel_id=5, replica_groups={{8,16},{24,0},{9,17},{25,1},{10,18},{26,2},{11,19},{27,3},{12,20},{28,4..., dimensions={0}, use_global_device_ids=true | all-gather | bytes 282624 | tf_op jit(solution)/shard_map/all_gather | solution.py:601
  51.8 0.0 copy-done.6
  51.8 1.9 %side.1 = (bf16[2,14,16,128]{3,2,1,0:T(8,128)(2,1)S(1)}, bf16[3,112,128]{2,1,0:T(8,128)(2,1)S(1)}, bf16[1152,384]{1,0:T(8,128)(2,1)S(1)}) custom-call(s32[32]{0:T(128)S(1)} %copy-done.4, bf16[2048,128]{1,0:T(8,128)(2,1)S(1)} %get-tuple-element.20.block_ref, bf16[288,128]{1,0:T(8,128)(2,1)S(1)} %get-tuple-element.27.before_ref, ...), custom_call_target="tpu_custom_call" | custom-call | flops 693633024 | bytes 1769472 | tf_op jit(solution)/shard_map/side/pallas_call | solution.py:444
  53.7 0.0 copy-start
  53.7 0.0 copy-start.1
  53.7 0.0 copy-start.2
  53.7 5.1 %final.1 = (bf16[2048,128]{1,0:T(8,128)(2,1)}, bf16[8,256,128]{2,1,0:T(8,128)(2,1)S(1)}) custom-call(s32[2]{0:T(128)S(1)} %copy-done.3, s32[32]{0:T(128)S(1)} %copy-done.4, bf16[2048,128]{1,0:T(8,128)(2,1)S(1)} %get-tuple-element.20.block_ref, bf16[288,128]{1,0:T(8,128)(2,1)S(1)} %get-tuple-element.27.before_ref, ...), custom_call_target="tpu_custom_call" | custom-call | flops 1811939328 | bytes 1769472 | tf_op jit(solution)/shard_map/final/pallas_call | solution.py:560
  58.8 18.2 %all_to_all.11.octant_ref = bf16[8,256,128]{2,1,0:T(8,128)(2,1)S(1)} all-to-all(bf16[8,256,128]{2,1,0:T(8,128)(2,1)S(1)} %get-tuple-element.36), channel_id=1, replica_groups=mesh['gz'=4,'xy'=8] {'xy'}, dimensions={0} | all-to-all | bytes 1048576 | tf_op jit(solution)/shard_map/all_to_all | solution.py:591
  77.0 0.0 copy-done
  77.0 0.0 copy-done.1
  77.0 0.0 copy-done.2
  77.0 3.5 %up.1 = bf16[32,64,512]{2,1,0:T(8,128)(2,1)} custom-call(s32[2]{0:T(128)S(1)} %copy-done.3, bf16[32,64,512]{2,1,0:T(8,128)(2,1)S(1)} %copy-done, s32[32,512]{1,0:T(8,128)S(1)} %copy-done.1, bf16[128,512]{1,0:T(8,128)(2,1)S(1)} %copy-done.2, bf16[8,256,128]{2,1,0:T(8,128)(2,1)S(1)} %all_to_all.11.octant_ref), custom_call_target="tpu_custom_call" | custom-call | tf_op jit(solution)/shard_map/up/pallas_call | solution.py:116
Async XLA Ops:
  0.6 27.2 %copy-start.4 = (s32[32]{0:T(128)S(1)}, s32[32]{0:T(128)}, u32[]{:S(2)}) copy-start(s32[32]{0:T(128)} %source_ref.9) | copy-start | bytes 388
  1.3 26.6 %copy-start.3 = (s32[2]{0:T(128)S(1)}, s32[2]{0:T(128)}, u32[]{:S(2)}) copy-start(s32[2]{0:T(128)} %pad_add_fusion.base_ref) | copy-start | bytes 28
  1.3 40.2 %copy-start.5 = (bf16[27,128,128]{2,1,0:T(8,128)(2,1)S(1)}, bf16[27,128,128]{2,1,0:T(8,128)(2,1)}, u32[]{:S(2)}) copy-start(bf16[27,128,128]{2,1,0:T(8,128)(2,1)} %w1_ref.1) | copy-start | bytes 2654212
  41.4 10.3 %copy-start.6 = (bf16[27,128,128]{2,1,0:T(8,128)(2,1)S(1)}, bf16[27,128,128]{2,1,0:T(8,128)(2,1)}, u32[]{:S(2)}) copy-start(bf16[27,128,128]{2,1,0:T(8,128)(2,1)} %w2_ref.1) | copy-start | bytes 2654212
  53.7 23.3 %copy-start = (bf16[32,64,512]{2,1,0:T(8,128)(2,1)S(1)}, bf16[32,64,512]{2,1,0:T(8,128)(2,1)}, u32[]{:S(2)}) copy-start(bf16[32,64,512]{2,1,0:T(8,128)(2,1)} %fine_ref.1) | copy-start | bytes 6291460
  53.7 23.3 %copy-start.1 = (s32[32,512]{1,0:T(8,128)S(1)}, s32[32,512]{1,0:T(8,128)}, u32[]{:S(2)}) copy-start(s32[32,512]{1,0:T(8,128)} %mask_ref.1) | copy-start | bytes 196612
  53.7 23.3 %copy-start.2 = (bf16[128,512]{1,0:T(8,128)(2,1)S(1)}, bf16[128,512]{1,0:T(8,128)(2,1)}, u32[]{:S(2)}) copy-start(bf16[128,512]{1,0:T(8,128)(2,1)} %w_ref.1) | copy-start | bytes 393220

commit v4 on v2

--- a/solution.py
+++ b/solution.py
@@ -18,14 +18,11 @@
 LATE = ((12, 3),)
 EARLY_PLANES = 11
 LATE_PLANES = 3
+FIRST_SENT = (4, 3, 5)
+LAST_SENT = (2, 6, 1, 7, 0)
+UP_OFFSETS = 4
 DOWN_LIMIT = 62 * 1024 * 1024
 VMEM_LIMIT = 24 * 1024 * 1024
-
-
-def place_of(base, j, sign, rotated):
-    if not rotated:
-        return j
-    return lax.rem(base + sign * j + K, K)
 
 
 def expand_mask(mask):
@@ -44,90 +41,103 @@
     return jnp.dot(spread, widen, preferred_element_type=jnp.float32)
 
 
-def down_kernel(rotated, base_ref, fine_hbm, mask_hbm, w_hbm, out_ref, fine_ref, mask_ref, w_ref, sems):
-    parts = sems.shape[0] - 2
-    step = fine_hbm.shape[0] // parts
-    rows = CAP * CELLS
+def down_kernel(offsets, fine_hbm, mask_hbm, w_hbm, *refs):
+    outs = refs[: len(offsets)]
+    fine_ref, mask_ref, w_ref, sems = refs[len(offsets) :]
+    count = len(offsets)
     first = [
-        pltpu.make_async_copy(mask_hbm, mask_ref, sems.at[parts]),
-        pltpu.make_async_copy(w_hbm, w_ref, sems.at[parts + 1]),
+        pltpu.make_async_copy(mask_hbm, mask_ref, sems.at[count]),
+        pltpu.make_async_copy(w_hbm, w_ref, sems.at[count + 1]),
     ]
     chunks = [
-        pltpu.make_async_copy(
-            fine_hbm.at[pl.ds(part * step, step)], fine_ref.at[pl.ds(part * step, step)], sems.at[part]
-        )
-        for part in range(parts)
+        pltpu.make_async_copy(fine_hbm.at[pl.ds(j * CAP, CAP)], fine_ref.at[k], sems.at[k])
+        for k, j in enumerate(offsets)
     ]
     for copy in first + chunks:
         copy.start()
     for copy in first:
         copy.wait()
-    for part in range(parts):
-        bricks = slice(part * step, (part + 1) * step)
-        mask = expand_mask(mask_ref[bricks]).astype(jnp.bfloat16)
-        chunks[part].wait()
-        x = fine_ref[bricks].reshape(step * CELLS, -1) * mask
-        y = jnp.dot(x, w_ref[...], preferred_element_type=jnp.float32).astype(jnp.bfloat16)
-        for inner in range(step // CAP):
-            j = part * (step // CAP) + inner
-            out_ref[place_of(base_ref[0], j, 1, rotated)] = y[inner * rows : (inner + 1) * rows]
-
-
-def down_call(base, fine, mask, w, rotated):
-    bricks, cells, width = fine.shape
+    for k, j in enumerate(offsets):
+        mask = expand_mask(mask_ref[j * CAP : (j + 1) * CAP]).astype(jnp.bfloat16)
+        chunks[k].wait()
+        x = fine_ref[k].reshape(CAP * CELLS, -1) * mask
+        y = jnp.dot(x, w_ref[...], preferred_element_type=jnp.float32)
+        outs[k][...] = y.astype(jnp.bfloat16)
+
+
+def down_call(fine, mask, w, offsets):
+    cells, width = fine.shape[1:]
     mid = w.shape[1]
-    parts = 4
+    count = len(offsets)
     hbm = pl.BlockSpec(memory_space=pltpu.HBM)
-    return pl.pallas_call(
-        functools.partial(down_kernel, rotated),
-        in_specs=[pl.BlockSpec(memory_space=pltpu.SMEM), hbm, hbm, hbm],
-        out_specs=pl.BlockSpec(memory_space=pltpu.VMEM),
-        out_shape=jax.ShapeDtypeStruct((K, CAP * cells, mid), jnp.bfloat16),
+    rows = count * CAP * cells
+    outs = pl.pallas_call(
+        functools.partial(down_kernel, offsets),
+        in_specs=[hbm, hbm, hbm],
+        out_specs=[pl.BlockSpec(memory_space=pltpu.VMEM)] * count,
+        out_shape=[jax.ShapeDtypeStruct((CAP * cells, mid), jnp.bfloat16)] * count,
         scratch_shapes=[
-            pltpu.VMEM(fine.shape, fine.dtype),
+            pltpu.VMEM((count, CAP, cells, width), fine.dtype),
             pltpu.VMEM(mask.shape, mask.dtype),
             pltpu.VMEM(w.shape, w.dtype),
-            pltpu.SemaphoreType.DMA((parts + 2,)),
+            pltpu.SemaphoreType.DMA((count + 2,)),
         ],
         compiler_params=pltpu.CompilerParams(vmem_limit_bytes=DOWN_LIMIT),
+        cost_estimate=pl.CostEstimate(
+            flops=2 * rows * width * mid, bytes_accessed=rows * width * 2, transcendentals=0
+        ),
         name="down",
-    )(base, fine, mask, w)
-
-
-def up_kernel(rotated, base_ref, fine_ref, mask_ref, w_ref, octant_ref, out_ref):
+    )(fine, mask, w)
+    return dict(zip(offsets, outs))
+
+
+def up_kernel(fine_ref, mask_ref, w_ref, *refs):
+    out_ref = refs[-1]
     step = pl.program_id(0)
     bricks, cells, width = fine_ref.shape
     mask = expand_mask(mask_ref[...])
     count = bricks // CAP
-    parts = [
-        octant_ref[place_of(base_ref[0], step * count + part, 1, rotated)] for part in range(count)
-    ]
-    octant = jnp.concatenate(parts, axis=0)
-    up = jnp.dot(octant, w_ref[...], preferred_element_type=jnp.float32)
-    fine = fine_ref[...].reshape(bricks * cells, width).astype(jnp.float32)
-    out = jnp.where(mask > 0.5, fine + up, 0.0).astype(jnp.bfloat16)
-    out_ref[...] = out.reshape(bricks, cells, width)
-
-
-def up_call(base, fine, mask, w, octant, rotated):
+    steps = UP_OFFSETS // count
+    for part in range(count):
+        octant = refs[part][...]
+        for other in range(1, steps):
+            octant = jnp.where(step == other, refs[other * count + part][...], octant)
+        rows = slice(part * CAP * cells, (part + 1) * CAP * cells)
+        up = jnp.dot(octant, w_ref[...], preferred_element_type=jnp.float32)
+        fine = fine_ref[part * CAP : (part + 1) * CAP].reshape(CAP * cells, width)
+        out = jnp.where(mask[rows] > 0.5, fine.astype(jnp.float32) + up, 0.0)
+        out_ref[part * CAP : (part + 1) * CAP] = out.astype(jnp.bfloat16).reshape(CAP, cells, width)
+
+
+def up_call(fine, mask, w, octants, first, partial):
     bricks, cells, width = fine.shape
     mid = w.shape[0]
     step = 8
+    blocks = bricks // step
+
+    def place(i):
+        return (first + i) % blocks
+
+    partials = [] if partial is None else [partial]
     return pl.pallas_call(
-        functools.partial(up_kernel, rotated),
-        grid=(bricks // step,),
+        up_kernel,
+        grid=(UP_OFFSETS * CAP // step,),
         in_specs=[
-            pl.BlockSpec(memory_space=pltpu.SMEM),
-            pl.BlockSpec((step, cells, width), lambda i: (i, 0, 0)),
-            pl.BlockSpec((step, width), lambda i: (i, 0)),
+            pl.BlockSpec((step, cells, width), lambda i: (place(i), 0, 0)),
+            pl.BlockSpec((step, width), lambda i: (place(i), 0)),
             pl.BlockSpec((mid, width), lambda i: (0, 0)),
-            pl.BlockSpec((K, CAP * cells, mid), lambda i: (0, 0, 0)),
-        ],
-        out_specs=pl.BlockSpec((step, cells, width), lambda i: (i, 0, 0)),
+        ]
+        + [pl.BlockSpec((CAP * cells, mid), lambda i: (0, 0))] * UP_OFFSETS
+        + [pl.BlockSpec(memory_space=pl.ANY)] * len(partials),
+        out_specs=pl.BlockSpec((step, cells, width), lambda i: (place(i), 0, 0)),
         out_shape=jax.ShapeDtypeStruct(fine.shape, jnp.bfloat16),
+        input_output_aliases={3 + UP_OFFSETS: 0} if partials else {},
         compiler_params=pltpu.CompilerParams(vmem_limit_bytes=VMEM_LIMIT),
+        cost_estimate=pl.CostEstimate(
+            flops=bricks * cells * width * mid, bytes_accessed=bricks * cells * width * 2, transcendentals=0
+        ),
         name="up",
-    )(base, fine, mask, w, octant)
+    )(fine, mask, w, *octants, *partials)
 
 
 def low_half(shape):
@@ -145,25 +155,23 @@
     return (pd * 2 + pr) * 8 + qd * 4 + qr * 2
 
 
-def brick_place(rotated, base_ref, value):
-    j = value // CAP
-    return place_of(base_ref[0], j, -1, rotated), pl.multiple_of((value % CAP) * CELLS, CELLS)
-
-
-def take_brick(rotated, base_ref, source_ref, arrived_ref, slot):
+def take_brick(source_ref, arrived, slot):
     value = source_ref[slot]
-    place, first = brick_place(rotated, base_ref, jnp.maximum(value, 0))
-    brick = arrived_ref[place, pl.ds(first, CELLS), :].astype(jnp.float32)
+    first = pl.multiple_of(jnp.maximum(value, 0) * CELLS, CELLS)
+    brick = arrived[pl.ds(first, CELLS), :].astype(jnp.float32)
     return jnp.where(value >= 0, brick, 0.0).reshape(8, 8, 128)
 
 
-def place_kernel(rotated, base_ref, source_ref, arrived_ref, block_ref, low_ref, high_ref):
+def place_kernel(source_ref, *refs):
+    block_ref, low_ref, high_ref, arrived = refs[K:]
+    for j in range(K):
+        arrived[j * CAP * CELLS : (j + 1) * CAP * CELLS] = refs[j][...]
     half = low_half((8, 8, 128))
     for depth_brick in range(4):
         for row_brick in range(4):
             slot = slot_index(depth_brick, row_brick)
-            b0 = take_brick(rotated, base_ref, source_ref, arrived_ref, slot)
-            b1 = take_brick(rotated, base_ref, source_ref, arrived_ref, slot + 1)
+            b0 = take_brick(source_ref, arrived, slot)
+            b1 = take_brick(source_ref, arrived, slot + 1)
             even = jnp.where(half, b0, pltpu.roll(b1, 4, 1))
             odd = jnp.where(half, pltpu.roll(b0, 4, 1), b1)
             both = jnp.stack([even, odd], axis=1).reshape(4, 32, 128).astype(jnp.bfloat16)
@@ -180,21 +188,22 @@
         ref[256:288] = jnp.concatenate(flags, axis=0).astype(jnp.bfloat16)
 
 
-def place_call(base, source, arrived, rotated):
-    mid = arrived.shape[2]
+def place_call(source, arrived):
+    mid = arrived[0].shape[1]
     smem = pl.BlockSpec(memory_space=pltpu.SMEM)
     vmem = pl.BlockSpec(memory_space=pltpu.VMEM)
     return pl.pallas_call(
-        functools.partial(place_kernel, rotated),
-        in_specs=[smem, smem, vmem],
+        place_kernel,
+        in_specs=[smem] + [vmem] * K,
         out_specs=[vmem] * 3,
         out_shape=[
             jax.ShapeDtypeStruct((rows, mid), jnp.bfloat16)
             for rows in (SIDE * SIDE * COLS, 288, 288)
         ],
+        scratch_shapes=[pltpu.VMEM((K * CAP * CELLS, mid), jnp.bfloat16)],
         compiler_params=pltpu.CompilerParams(vmem_limit_bytes=VMEM_LIMIT),
         name="place",
-    )(base, source, arrived)
+    )(source, *arrived)
 
 
 def edge_kernel(source_ref, block_ref, before_ref, after_ref, low_ref, high_ref):
@@ -403,28 +412,11 @@
     )(source, block, before, after, wide1, w_second)
 
 
-def final_kernel(
-    rotated,
-    base_ref,
-    source_ref,
-    block_ref,
-    before_ref,
-    after_ref,
-    under_ref,
-    over_ref,
-    early_ref,
-    late_ref,
-    side_ref,
-    wide1_ref,
-    wide2_ref,
-    coarse_ref,
-    back_ref,
-    x_here,
-    x_next,
-    h_here,
-    h_next,
-    stage,
-):
+def final_kernel(source_ref, *refs):
+    block_ref, before_ref, after_ref, under_ref, over_ref = refs[:5]
+    early_ref, late_ref, side_ref, wide1_ref, wide2_ref, coarse_ref = refs[5:11]
+    backs = refs[11 : 11 + K]
+    x_here, x_next, h_here, h_next, stage = refs[11 + K :]
     width = block_ref.shape[1]
     flags_before = as_rows(before_ref[256:288])
     flags_after = as_rows(after_ref[256:288])
@@ -483,26 +475,24 @@
             slot = slot_index(depth_brick, r)
             for k, brick in enumerate((b0, b1)):
                 source = source_ref[slot + k]
-                place, first = brick_place(rotated, base_ref, jnp.maximum(source, 0))
-                row = jnp.where(source >= 0, place * CAP * CELLS + first, K * CAP * CELLS)
-                row = pl.multiple_of(row, CELLS)
+                row = pl.multiple_of(jnp.where(source >= 0, source, K * CAP) * CELLS, CELLS)
                 stage[pl.ds(row, CELLS), :] = brick.reshape(CELLS, width).astype(jnp.bfloat16)
-    for place in range(K):
-        back_ref[place] = stage[place * CAP * CELLS : (place + 1) * CAP * CELLS]
-
-
-def final_call(base, source, block, halo, hidden, wide1, wide2, rotated):
+    for j in range(K):
+        backs[j][...] = stage[j * CAP * CELLS : (j + 1) * CAP * CELLS]
+
+
+def final_call(source, block, halo, hidden, wide1, wide2):
     mid = block.shape[1]
     smem = pl.BlockSpec(memory_space=pltpu.SMEM)
     vmem = pl.BlockSpec(memory_space=pltpu.VMEM)
     return pl.pallas_call(
-        functools.partial(final_kernel, rotated),
-        in_specs=[smem, smem] + [vmem] * 10,
-        out_specs=[vmem] * 2,
+        final_kernel,
+        in_specs=[smem] + [vmem] * 10,
+        out_specs=[vmem] * (1 + K),
         out_shape=[
             jax.ShapeDtypeStruct(block.shape, jnp.bfloat16),
-            jax.ShapeDtypeStruct((K, CAP * CELLS, mid), jnp.bfloat16),
-        ],
+        ]
+        + [jax.ShapeDtypeStruct((CAP * CELLS, mid), jnp.bfloat16)] * K,
         scratch_shapes=[
             pltpu.VMEM((4, WIDE * COLS, mid), jnp.bfloat16),
             pltpu.VMEM((4, WIDE * COLS, mid), jnp.bfloat16),
@@ -513,19 +503,13 @@
         compiler_params=pltpu.CompilerParams(vmem_limit_bytes=VMEM_LIMIT),
         cost_estimate=conv_cost(SIDE * SIDE * COLS, mid),
         name="final",
-    )(base, source, block, *halo, *hidden, wide1, wide2)
+    )(source, block, *halo, *hidden, wide1, wide2)
 
 
 def from_behind(value, axis, steps):
     count = lax.axis_size(axis)
     pairs = [(source, (source + steps) % count) for source in range(count)]
     return lax.ppermute(value, axis, pairs)
-
-
-def exchange(value, rotated, sign):
-    if rotated:
-        return lax.all_to_all(value, "xy", 0, 0, tiled=True)
-    return jnp.stack([from_behind(value[j], "xy", sign * j) for j in range(K)])
 
 
 def neighbours(low, high, axis):
@@ -536,30 +520,26 @@
 
 
 def shards(fine, fine_mask, slot_source, w_down, w_first, w_second, w_up):
-    rotated = lax.axis_size("xy") == K
     mid = w_down.shape[1]
-    base = lax.axis_index("xy").astype(jnp.int32).reshape(1)
-    sent = down_call(base, fine, fine_mask, w_down, rotated)
-    arrived = exchange(sent, rotated, 1)
-    block, low, high = place_call(base, slot_source, arrived, rotated)
+    sent = down_call(fine, fine_mask, w_down, FIRST_SENT)
+    arrived = {j: from_behind(sent[j], "xy", j) for j in FIRST_SENT}
+    sent = down_call(fine, fine_mask, w_down, LAST_SENT)
+    arrived.update({j: from_behind(sent[j], "xy", j) for j in LAST_SENT if j})
+    arrived[0] = sent[0]
+    block, low, high = place_call(slot_source, [arrived[j] for j in range(K)])
     before, after = neighbours(low, high, "xy")
     early, wide1 = inner_call(slot_source, block, w_first)
     before, after, early, wide1 = lax.optimization_barrier((before, after, early, wide1))
     under_send, over_send = edge_call(slot_source, block, before, after)
     under, over = neighbours(under_send, over_send, "gz")
     side, late, wide2 = side_call(slot_source, block, before, after, wide1, w_second)
-    coarse, back = final_call(
-        base,
-        slot_source,
-        block,
-        (before, after, under, over),
-        (early, late, side),
-        wide1,
-        wide2,
-        rotated,
+    coarse, *back = final_call(
+        slot_source, block, (before, after, under, over), (early, late, side), wide1, wide2
     )
-    octant = exchange(back, rotated, -1)
-    fine_out = up_call(base, fine, fine_mask, w_up, octant, rotated)
+    octant = {j: from_behind(back[j], "xy", -j) for j in FIRST_SENT + LAST_SENT if j}
+    octant[0] = back[0]
+    fine_out = up_call(fine, fine_mask, w_up, [octant[j] for j in (2, 3, 4, 5)], 1, None)
+    fine_out = up_call(fine, fine_mask, w_up, [octant[j] for j in (6, 7, 0, 1)], 3, fine_out)
     return fine_out, coarse.reshape(SIDE, SIDE, COLS, mid)
 
 

time: 70.5 us -> 68.7 us (0.974); the launches traced: 69.1 us -> 68.4 us
  blocking collectives: 39.1 us -> 0 us
  starting transfers between devices: 7.25 us -> 34.3 us
  waiting for transfers between devices: 4.18 us -> 12.3 us
  Pallas kernels: 17.8 us -> 20.1 us
  local copies, waits for them, and re-layouts: 0.03 us -> 0.87 us
    all_to_all x2 -> x0, blocking collectives: 39.1 us -> none  [exchange(): return lax.all_to_all(value, 'xy', 0, 0, tiled=True)]
    ppermute x0 -> x14, starting transfers between devices: none -> 26.1 us  [from_behind(): return lax.ppermute(value, axis, pairs)]
    ppermute x0 -> x14, waiting for transfers between devices: none -> 8.11 us  [from_behind(): return lax.ppermute(value, axis, pairs)]
    pallas_call x4 -> x6, Pallas kernels: 12.9 us -> 15.2 us  [the longest x2 5.93 us: down_call(): pl.pallas_call(functools.partial(down_kernel, offsets), in_specs=[hbm, hb...]
    ppermute x2, starting transfers between devices: 4.67 us -> 5.64 us  [neighbours(): lax.ppermute(high, axis, forward)]
    unnamed x12 -> x14, local copies, waits for them, and re-layouts: 0.03 us -> 0.87 us
  transfers between devices with their start and end apart: 4 -> 18, of which waited for: 2 -> 6; matrix products, arithmetic and copies ran while one was open for 0% -> 0% of each run, Pallas kernels for 6% -> 14%
where the time goes in v4:
time: 68.7 us; the launch traced here: 68.4 us
  starting transfers between devices  34.3 us (50%)
  Pallas kernels  20.1 us (29%)
  waiting for transfers between devices  12.3 us (18%)
  local copies, waits for them, and re-layouts  0.87 us (1%)
  between operations  0.79 us (1%)
    ppermute x14, starting transfers between devices, from_behind(): return lax.ppermute(value, axis, pairs)  26.1 us
    ppermute x14, waiting for transfers between devices, from_behind(): return lax.ppermute(value, axis, pairs)  8.11 us
    pallas_call x2, Pallas kernels, down_call(): pl.pallas_call(functools.partial(down_kernel, offsets), in_specs=[hbm, hb...  5.93 us
    ppermute x2, starting transfers between devices, neighbours(): lax.ppermute(high, axis, forward)  5.64 us
    pallas_call x1, Pallas kernels, final_call(): pl.pallas_call(final_kernel, in_specs=[smem] + [vmem] * 10, out_specs=[vm...  5.06 us
    ppermute x2, waiting for transfers between devices, neighbours(): lax.ppermute(low, axis, backward)  4.18 us
    pallas_call x2, Pallas kernels, up_call(): pl.pallas_call(up_kernel, grid=(UP_OFFSETS * CAP // step,), in_specs=[pl....  3.51 us
    ppermute x2, starting transfers between devices, neighbours(): lax.ppermute(low, axis, backward)  2.58 us
  transfers between devices with their start and end apart: 18, of which 6 were waited for; matrix products, arithmetic and copies ran while one was open for 0% of the time, Pallas kernels for 14%

profile of v4, /device:TPU:0, one launch (start us, length us, event | category | flops | bytes accessed | tf_op | source)
XLA Modules:
  0.0 68.4 jit_solution(8482317692043280606)
XLA Ops:
  0.6 2.7 %down.3 = (bf16[256,128]{1,0:T(8,128)(2,1)}, bf16[256,128]{1,0:T(8,128)(2,1)}, bf16[256,128]{1,0:T(8,128)(2,1)}) custom-call(bf16[32,64,512]{2,1,0:T(8,128)(2,1)} %fine_ref.3, s32[32,512]{1,0:T(8,128)} %mask_ref.3, bf16[512,128]{1,0:T(8,128)(2,1)} %w_hbm.3), custom_call_target="tpu_custom_call" | custom-call | flops 100663296 | bytes 786432 | tf_op jit(solution)/shard_map/down/pallas_call | solution.py:74
  3.4 4.0 %collective-permute-start.2 = (bf16[256,128]{1,0:T(8,128)(2,1)}, bf16[256,128]{1,0:T(8,128)(2,1)S(1)}, u32[]{:S(2)}, u32[]{:S(2)}) collective-permute-start(bf16[256,128]{1,0:T(8,128)(2,1)} %get-tuple-element.36), channel_id=1, source_target_pairs={{0,3},{1,4},{2,5},{3,6},{4,7},{5,0},{6,1},{7,2},{8,11},{9,12},{10,... | collective-permute-start | bytes 196616 | tf_op jit(solution)/shard_map/ppermute | solution.py:512
  7.4 2.6 %collective-permute-start.3 = (bf16[256,128]{1,0:T(8,128)(2,1)}, bf16[256,128]{1,0:T(8,128)(2,1)S(1)}, u32[]{:S(2)}, u32[]{:S(2)}) collective-permute-start(bf16[256,128]{1,0:T(8,128)(2,1)} %get-tuple-element.37), channel_id=1, source_target_pairs={{0,4},{1,5},{2,6},{3,7},{4,0},{5,1},{6,2},{7,3},{8,12},{9,13},{10,... | collective-permute-start | bytes 196616 | tf_op jit(solution)/shard_map/ppermute | solution.py:512
  9.9 1.3 %collective-permute-start.4 = (bf16[256,128]{1,0:T(8,128)(2,1)}, bf16[256,128]{1,0:T(8,128)(2,1)S(1)}, u32[]{:S(2)}, u32[]{:S(2)}) collective-permute-start(bf16[256,128]{1,0:T(8,128)(2,1)} %get-tuple-element.38), channel_id=1, source_target_pairs={{0,5},{1,6},{2,7},{3,0},{4,1},{5,2},{6,3},{7,4},{8,13},{9,14},{10,... | collective-permute-start | bytes 196616 | tf_op jit(solution)/shard_map/ppermute | solution.py:512
  11.3 3.2 %down.2 = (bf16[256,128]{1,0:T(8,128)(2,1)}, bf16[256,128]{1,0:T(8,128)(2,1)}, bf16[256,128]{1,0:T(8,128)(2,1)}, bf16[256,128]{1,0:T(8,128)(2,1)}, bf16[256,128]{1,0:T(8,128)(2,1)}) custom-call(bf16[32,64,512]{2,1,0:T(8,128)(2,1)} %fine_ref.3, s32[32,512]{1,0:T(8,128)} %mask_ref.3, bf16[512,128]{1,0:T(8,128)(2,1)} %w_hbm.3), custom_call_target="tpu_custom_call" | custom-call | flops 167772160 | bytes 1310720 | tf_op jit(solution)/shard_map/down/pallas_call | solution.py:74
  14.5 1.6 %collective-permute-start = (bf16[256,128]{1,0:T(8,128)(2,1)}, bf16[256,128]{1,0:T(8,128)(2,1)S(1)}, u32[]{:S(2)}, u32[]{:S(2)}) collective-permute-start(bf16[256,128]{1,0:T(8,128)(2,1)} %get-tuple-element.34), channel_id=1, source_target_pairs={{0,1},{1,2},{2,3},{3,4},{4,5},{5,6},{6,7},{7,0},{8,9},{9,10},{10,1... | collective-permute-start | bytes 196616 | tf_op jit(solution)/shard_map/ppermute | solution.py:512
  16.1 0.7 collective-permute-start.1
  16.7 3.2 %collective-permute-start.5 = (bf16[256,128]{1,0:T(8,128)(2,1)}, bf16[256,128]{1,0:T(8,128)(2,1)S(1)}, u32[]{:S(2)}, u32[]{:S(2)}) collective-permute-start(bf16[256,128]{1,0:T(8,128)(2,1)} %get-tuple-element.39), channel_id=1, source_target_pairs={{0,6},{1,7},{2,0},{3,1},{4,2},{5,3},{6,4},{7,5},{8,14},{9,15},{10,... | collective-permute-start | bytes 196616 | tf_op jit(solution)/shard_map/ppermute | solution.py:512
  19.9 1.4 %collective-permute-start.6 = (bf16[256,128]{1,0:T(8,128)(2,1)}, bf16[256,128]{1,0:T(8,128)(2,1)S(1)}, u32[]{:S(2)}, u32[]{:S(2)}) collective-permute-start(bf16[256,128]{1,0:T(8,128)(2,1)} %get-tuple-element.40), channel_id=1, source_target_pairs={{0,7},{1,0},{2,1},{3,2},{4,3},{5,4},{6,5},{7,6},{8,15},{9,8},{10,9... | collective-permute-start | bytes 196616 | tf_op jit(solution)/shard_map/ppermute | solution.py:512
  21.3 1.1 %collective-permute-done.refs_1_ = bf16[256,128]{1,0:T(8,128)(2,1)S(1)} collective-permute-done((bf16[256,128]{1,0:T(8,128)(2,1)}, bf16[256,128]{1,0:T(8,128)(2,1)S(1)}, u32[]{:S(2)}, u32[]{:S(2)}) %collective-permute-start) | collective-permute-done | bytes 65568 | tf_op jit(solution)/shard_map/ppermute | solution.py:512
  22.4 2.0 %collective-permute-done.6.refs_7_ = bf16[256,128]{1,0:T(8,128)(2,1)S(1)} collective-permute-done((bf16[256,128]{1,0:T(8,128)(2,1)}, bf16[256,128]{1,0:T(8,128)(2,1)S(1)}, u32[]{:S(2)}, u32[]{:S(2)}) %collective-permute-start.6) | collective-permute-done | bytes 65568 | tf_op jit(solution)/shard_map/ppermute | solution.py:512
  24.4 0.8 %copy-done.3 = bf16[256,128]{1,0:T(8,128)(2,1)S(1)} copy-done((bf16[256,128]{1,0:T(8,128)(2,1)S(1)}, bf16[256,128]{1,0:T(8,128)(2,1)}, u32[]{:S(2)}) %copy-start.3) | copy-done | bytes 65560
  25.2 0.7 %place.1 = (bf16[2048,128]{1,0:T(8,128)(2,1)S(1)}, bf16[288,128]{1,0:T(8,128)(2,1)S(1)}, bf16[288,128]{1,0:T(8,128)(2,1)S(1)}) custom-call(s32[32]{0:T(128)S(1)} %copy-done.4, bf16[256,128]{1,0:T(8,128)(2,1)S(1)} %copy-done.3, bf16[256,128]{1,0:T(8,128)(2,1)S(1)} %collective-permute-done.refs_1_, bf16[256,128]{1,0:T(8,128)(2,1)S(1)} %collective-permute-done.1.refs_2_, ...), custom_call_target="tpu_custom_call" | custom-call | tf_op jit(solution)/shard_map/place/pallas_call | solution.py:195
  26.0 4.3 %collective-permute-start.7 = (bf16[288,128]{1,0:T(8,128)(2,1)S(1)}, bf16[288,128]{1,0:T(8,128)(2,1)S(1)}, u32[]{:S(2)}, u32[]{:S(2)}) collective-permute-start(bf16[288,128]{1,0:T(8,128)(2,1)S(1)} %get-tuple-element.42), channel_id=1, source_target_pairs={{0,1},{1,2},{2,3},{3,4},{4,5},{5,6},{6,7},{8,9},{9,10},{10,11},{11... | collective-permute-start | bytes 221192 | tf_op jit(solution)/shard_map/ppermute | solution.py:519
  30.3 1.3 %collective-permute-start.8 = (bf16[288,128]{1,0:T(8,128)(2,1)S(1)}, bf16[288,128]{1,0:T(8,128)(2,1)S(1)}, u32[]{:S(2)}, u32[]{:S(2)}) collective-permute-start(bf16[288,128]{1,0:T(8,128)(2,1)S(1)} %get-tuple-element.43), channel_id=1, source_target_pairs={{1,0},{2,1},{3,2},{4,3},{5,4},{6,5},{7,6},{9,8},{10,9},{11,10},{12... | collective-permute-start | bytes 221192 | tf_op jit(solution)/shard_map/ppermute | solution.py:519
  31.6 2.4 %inner.1 = (bf16[11,112,128]{2,1,0:T(8,128)(2,1)S(1)}, bf16[1152,384]{1,0:T(8,128)(2,1)S(1)}) custom-call(s32[32]{0:T(128)S(1)} %copy-done.4, bf16[2048,128]{1,0:T(8,128)(2,1)S(1)} %get-tuple-element.41.block_ref.refs_0_, bf16[27,128,128]{2,1,0:T(8,128)(2,1)S(1)} %copy-done.5), custom_call_target="tpu_custom_call" | custom-call | flops 1089994752 | bytes 1769472 | tf_op jit(solution)/shard_map/inner/pallas_call | solution.py:328
  34.1 2.5 %collective-permute-done.8.after_ref.refs_2_ = bf16[288,128]{1,0:T(8,128)(2,1)S(1)} collective-permute-done((bf16[288,128]{1,0:T(8,128)(2,1)S(1)}, bf16[288,128]{1,0:T(8,128)(2,1)S(1)}, u32[]{:S(2)}, u32[]{:S(2)}) %collective-permute-start.8) | collective-permute-done | bytes 73760 | tf_op jit(solution)/shard_map/ppermute | solution.py:519
  36.6 0.6 edge.1
  37.1 1.3 %collective-permute-start.9 = (bf16[368,128]{1,0:T(8,128)(2,1)S(1)}, bf16[368,128]{1,0:T(8,128)(2,1)S(1)}, u32[]{:S(2)}, u32[]{:S(2)}) collective-permute-start(bf16[368,128]{1,0:T(8,128)(2,1)S(1)} %get-tuple-element.48), channel_id=1, source_target_pairs={{0,8},{8,16},{16,24},{1,9},{9,17},{17,25},{2,10},{10,18},{18,26},{... | collective-permute-start | bytes 282632 | tf_op jit(solution)/shard_map/ppermute | solution.py:519
  38.4 1.3 %collective-permute-start.10 = (bf16[368,128]{1,0:T(8,128)(2,1)S(1)}, bf16[368,128]{1,0:T(8,128)(2,1)S(1)}, u32[]{:S(2)}, u32[]{:S(2)}) collective-permute-start(bf16[368,128]{1,0:T(8,128)(2,1)S(1)} %get-tuple-element.49), channel_id=1, source_target_pairs={{8,0},{16,8},{24,16},{9,1},{17,9},{25,17},{10,2},{18,10},{26,18},{... | collective-permute-start | bytes 282632 | tf_op jit(solution)/shard_map/ppermute | solution.py:519
  39.7 1.9 %side.1 = (bf16[2,14,16,128]{3,2,1,0:T(8,128)(2,1)S(1)}, bf16[3,112,128]{2,1,0:T(8,128)(2,1)S(1)}, bf16[1152,384]{1,0:T(8,128)(2,1)S(1)}) custom-call(s32[32]{0:T(128)S(1)} %copy-done.4, bf16[2048,128]{1,0:T(8,128)(2,1)S(1)} %get-tuple-element.41.block_ref.refs_0_, bf16[288,128]{1,0:T(8,128)(2,1)S(1)} %collective-permute-done.7.before_ref.refs_1_, ...), custom_call_target="tpu_custom_call" | custom-call | flops 693633024 | bytes 1769472 | tf_op jit(solution)/shard_map/side/pallas_call | solution.py:395
  41.7 1.7 %collective-permute-done.10.refs_4_ = bf16[368,128]{1,0:T(8,128)(2,1)S(1)} collective-permute-done((bf16[368,128]{1,0:T(8,128)(2,1)S(1)}, bf16[368,128]{1,0:T(8,128)(2,1)S(1)}, u32[]{:S(2)}, u32[]{:S(2)}) %collective-permute-start.10) | collective-permute-done | bytes 94240 | tf_op jit(solution)/shard_map/ppermute | solution.py:519
  43.4 5.1 %final.1 = (bf16[2048,128]{1,0:T(8,128)(2,1)}, bf16[256,128]{1,0:T(8,128)(2,1)S(1)}, bf16[256,128]{1,0:T(8,128)(2,1)S(1)}, bf16[256,128]{1,0:T(8,128)(2,1)S(1)},...) custom-call(s32[32]{0:T(128)S(1)} %copy-done.4, ...), custom_call_target="tpu_custom_call" | custom-call | flops 1811939328 | bytes 1769472 | tf_op jit(solution)/shard_map/final/pallas_call | solution.py:488
  48.4 2.3 %collective-permute-start.14 = (bf16[256,128]{1,0:T(8,128)(2,1)S(1)}, bf16[256,128]{1,0:T(8,128)(2,1)S(1)}, u32[]{:S(2)}, u32[]{:S(2)}) collective-permute-start(bf16[256,128]{1,0:T(8,128)(2,1)S(1)} %get-tuple-element.59), channel_id=1, source_target_pairs={{0,6},{1,7},{2,0},{3,1},{4,2},{5,3},{6,4},{7,5},{8,14},{9,15},{10,... | collective-permute-start | bytes 196616 | tf_op jit(solution)/shard_map/ppermute | solution.py:512
  50.7 2.5 %collective-permute-start.16 = (bf16[256,128]{1,0:T(8,128)(2,1)S(1)}, bf16[256,128]{1,0:T(8,128)(2,1)S(1)}, u32[]{:S(2)}, u32[]{:S(2)}) collective-permute-start(bf16[256,128]{1,0:T(8,128)(2,1)S(1)} %get-tuple-element.61), channel_id=1, source_target_pairs={{0,4},{1,5},{2,6},{3,7},{4,0},{5,1},{6,2},{7,3},{8,12},{9,13},{10,... | collective-permute-start | bytes 196616 | tf_op jit(solution)/shard_map/ppermute | solution.py:512
  53.6 1.5 %collective-permute-start.11 = (bf16[256,128]{1,0:T(8,128)(2,1)S(1)}, bf16[256,128]{1,0:T(8,128)(2,1)S(1)}, u32[]{:S(2)}, u32[]{:S(2)}) collective-permute-start(bf16[256,128]{1,0:T(8,128)(2,1)S(1)} %get-tuple-element.55), channel_id=1, source_target_pairs={{0,2},{1,3},{2,4},{3,5},{4,6},{5,7},{6,0},{7,1},{8,10},{9,11},{10,... | collective-permute-start | bytes 196616 | tf_op jit(solution)/shard_map/ppermute | solution.py:512
  55.1 1.5 %collective-permute-start.12 = (bf16[256,128]{1,0:T(8,128)(2,1)S(1)}, bf16[256,128]{1,0:T(8,128)(2,1)S(1)}, u32[]{:S(2)}, u32[]{:S(2)}) collective-permute-start(bf16[256,128]{1,0:T(8,128)(2,1)S(1)} %get-tuple-element.56), channel_id=1, source_target_pairs={{0,1},{1,2},{2,3},{3,4},{4,5},{5,6},{6,7},{7,0},{8,9},{9,10},{10,1... | collective-permute-start | bytes 196616 | tf_op jit(solution)/shard_map/ppermute | solution.py:512
  56.6 3.2 %collective-permute-start.13 = (bf16[256,128]{1,0:T(8,128)(2,1)S(1)}, bf16[256,128]{1,0:T(8,128)(2,1)S(1)}, u32[]{:S(2)}, u32[]{:S(2)}) collective-permute-start(bf16[256,128]{1,0:T(8,128)(2,1)S(1)} %get-tuple-element.58), channel_id=1, source_target_pairs={{0,7},{1,0},{2,1},{3,2},{4,3},{5,4},{6,5},{7,6},{8,15},{9,8},{10,9... | collective-permute-start | bytes 196616 | tf_op jit(solution)/shard_map/ppermute | solution.py:512
  59.8 2.5 %collective-permute-done.16.refs_2_ = bf16[256,128]{1,0:T(8,128)(2,1)S(1)} collective-permute-done((bf16[256,128]{1,0:T(8,128)(2,1)S(1)}, bf16[256,128]{1,0:T(8,128)(2,1)S(1)}, u32[]{:S(2)}, u32[]{:S(2)}) %collective-permute-start.16) | collective-permute-done | bytes 65568 | tf_op jit(solution)/shard_map/ppermute | solution.py:512
  62.3 2.5 %collective-permute-done.17.refs_3_ = bf16[256,128]{1,0:T(8,128)(2,1)S(1)} collective-permute-done((bf16[256,128]{1,0:T(8,128)(2,1)S(1)}, bf16[256,128]{1,0:T(8,128)(2,1)S(1)}, u32[]{:S(2)}, u32[]{:S(2)}) %collective-permute-start.17) | collective-permute-done | bytes 65568 | tf_op jit(solution)/shard_map/ppermute | solution.py:512
  64.9 1.8 %up.2.refs_4_ = bf16[32,64,512]{2,1,0:T(8,128)(2,1)} custom-call(bf16[32,64,512]{2,1,0:T(8,128)(2,1)S(1)} %copy-done, s32[32,512]{1,0:T(8,128)S(1)} %copy-done.1, bf16[128,512]{1,0:T(8,128)(2,1)S(1)} %copy-done.2, bf16[256,128]{1,0:T(8,128)(2,1)S(1)} %collective-permute-done.14.refs_0_, bf16[256,128]{1,0:T(8,128)(2,1)S(1)} %collective-permute-done.15.refs_1_, ...), custom_call_target="tpu_custom_call" | custom-call | flops 134217728 | bytes 2097152 | tf_op jit(solution)/shard_map/up/pallas_call | solution.py:122
  66.6 1.8 %up.3 = bf16[32,64,512]{2,1,0:T(8,128)(2,1)} custom-call(bf16[32,64,512]{2,1,0:T(8,128)(2,1)S(1)} %copy-done, s32[32,512]{1,0:T(8,128)S(1)} %copy-done.1, bf16[128,512]{1,0:T(8,128)(2,1)S(1)} %copy-done.2, bf16[256,128]{1,0:T(8,128)(2,1)S(1)} %collective-permute-done.11.refs_0_, ...), custom_call_target="tpu_custom_call", output_to_operand_aliasing={{}: (7, {})} | custom-call | flops 134217728 | bytes 2097152 | tf_op jit(solution)/shard_map/up/pallas_call | solution.py:122
  (27 shorter events, 0.5 us)
Async XLA Ops:
  0.6 23.7 %copy-start.4 = (s32[32]{0:T(128)S(1)}, s32[32]{0:T(128)}, u32[]{:S(2)}) copy-start(s32[32]{0:T(128)} %source_ref.9) | copy-start | bytes 388
  0.6 31.0 %copy-start.5 = (bf16[27,128,128]{2,1,0:T(8,128)(2,1)S(1)}, bf16[27,128,128]{2,1,0:T(8,128)(2,1)}, u32[]{:S(2)}) copy-start(bf16[27,128,128]{2,1,0:T(8,128)(2,1)} %w1_ref.1) | copy-start | bytes 2654212
  3.4 13.4 %collective-permute-start.2 = (bf16[256,128]{1,0:T(8,128)(2,1)}, bf16[256,128]{1,0:T(8,128)(2,1)S(1)}, u32[]{:S(2)}, u32[]{:S(2)}) collective-permute-start(bf16[256,128]{1,0:T(8,128)(2,1)} %get-tuple-element.36), channel_id=1, source_target_pairs={{0,3},{1,4},{2,5},{3,6},{4,7},{5,0},{6,1},{7,2},{8,11},{9,12},{10,... | collective-permute-start | bytes 196616 | tf_op jit(solution)/shard_map/ppermute | solution.py:512
  7.4 12.5 %collective-permute-start.3 = (bf16[256,128]{1,0:T(8,128)(2,1)}, bf16[256,128]{1,0:T(8,128)(2,1)S(1)}, u32[]{:S(2)}, u32[]{:S(2)}) collective-permute-start(bf16[256,128]{1,0:T(8,128)(2,1)} %get-tuple-element.37), channel_id=1, source_target_pairs={{0,4},{1,5},{2,6},{3,7},{4,0},{5,1},{6,2},{7,3},{8,12},{9,13},{10,... | collective-permute-start | bytes 196616 | tf_op jit(solution)/shard_map/ppermute | solution.py:512
  9.9 11.4 %collective-permute-start.4 = (bf16[256,128]{1,0:T(8,128)(2,1)}, bf16[256,128]{1,0:T(8,128)(2,1)S(1)}, u32[]{:S(2)}, u32[]{:S(2)}) collective-permute-start(bf16[256,128]{1,0:T(8,128)(2,1)} %get-tuple-element.38), channel_id=1, source_target_pairs={{0,5},{1,6},{2,7},{3,0},{4,1},{5,2},{6,3},{7,4},{8,13},{9,14},{10,... | collective-permute-start | bytes 196616 | tf_op jit(solution)/shard_map/ppermute | solution.py:512
  14.5 7.9 %collective-permute-start = (bf16[256,128]{1,0:T(8,128)(2,1)}, bf16[256,128]{1,0:T(8,128)(2,1)S(1)}, u32[]{:S(2)}, u32[]{:S(2)}) collective-permute-start(bf16[256,128]{1,0:T(8,128)(2,1)} %get-tuple-element.34), channel_id=1, source_target_pairs={{0,1},{1,2},{2,3},{3,4},{4,5},{5,6},{6,7},{7,0},{8,9},{9,10},{10,1... | collective-permute-start | bytes 196616 | tf_op jit(solution)/shard_map/ppermute | solution.py:512
  16.1 6.3 %collective-permute-start.1 = (bf16[256,128]{1,0:T(8,128)(2,1)}, bf16[256,128]{1,0:T(8,128)(2,1)S(1)}, u32[]{:S(2)}, u32[]{:S(2)}) collective-permute-start(bf16[256,128]{1,0:T(8,128)(2,1)} %get-tuple-element.35), channel_id=1, source_target_pairs={{0,2},{1,3},{2,4},{3,5},{4,6},{5,7},{6,0},{7,1},{8,10},{9,11},{10,... | collective-permute-start | bytes 196616 | tf_op jit(solution)/shard_map/ppermute | solution.py:512
  16.7 5.7 %collective-permute-start.5 = (bf16[256,128]{1,0:T(8,128)(2,1)}, bf16[256,128]{1,0:T(8,128)(2,1)S(1)}, u32[]{:S(2)}, u32[]{:S(2)}) collective-permute-start(bf16[256,128]{1,0:T(8,128)(2,1)} %get-tuple-element.39), channel_id=1, source_target_pairs={{0,6},{1,7},{2,0},{3,1},{4,2},{5,3},{6,4},{7,5},{8,14},{9,15},{10,... | collective-permute-start | bytes 196616 | tf_op jit(solution)/shard_map/ppermute | solution.py:512
  19.9 4.5 %collective-permute-start.6 = (bf16[256,128]{1,0:T(8,128)(2,1)}, bf16[256,128]{1,0:T(8,128)(2,1)S(1)}, u32[]{:S(2)}, u32[]{:S(2)}) collective-permute-start(bf16[256,128]{1,0:T(8,128)(2,1)} %get-tuple-element.40), channel_id=1, source_target_pairs={{0,7},{1,0},{2,1},{3,2},{4,3},{5,4},{6,5},{7,6},{8,15},{9,8},{10,9... | collective-permute-start | bytes 196616 | tf_op jit(solution)/shard_map/ppermute | solution.py:512
  24.4 0.8 %copy-start.3 = (bf16[256,128]{1,0:T(8,128)(2,1)S(1)}, bf16[256,128]{1,0:T(8,128)(2,1)}, u32[]{:S(2)}) copy-start(bf16[256,128]{1,0:T(8,128)(2,1)} %get-tuple-element.33.refs_0_) | copy-start | bytes 196612
  26.0 8.1 %collective-permute-start.7 = (bf16[288,128]{1,0:T(8,128)(2,1)S(1)}, bf16[288,128]{1,0:T(8,128)(2,1)S(1)}, u32[]{:S(2)}, u32[]{:S(2)}) collective-permute-start(bf16[288,128]{1,0:T(8,128)(2,1)S(1)} %get-tuple-element.42), channel_id=1, source_target_pairs={{0,1},{1,2},{2,3},{3,4},{4,5},{5,6},{6,7},{8,9},{9,10},{10,11},{11... | collective-permute-start | bytes 221192 | tf_op jit(solution)/shard_map/ppermute | solution.py:519
  30.3 6.2 %collective-permute-start.8 = (bf16[288,128]{1,0:T(8,128)(2,1)S(1)}, bf16[288,128]{1,0:T(8,128)(2,1)S(1)}, u32[]{:S(2)}, u32[]{:S(2)}) collective-permute-start(bf16[288,128]{1,0:T(8,128)(2,1)S(1)} %get-tuple-element.43), channel_id=1, source_target_pairs={{1,0},{2,1},{3,2},{4,3},{5,4},{6,5},{7,6},{9,8},{10,9},{11,10},{12... | collective-permute-start | bytes 221192 | tf_op jit(solution)/shard_map/ppermute | solution.py:519
  31.6 8.1 %copy-start.6 = (bf16[27,128,128]{2,1,0:T(8,128)(2,1)S(1)}, bf16[27,128,128]{2,1,0:T(8,128)(2,1)}, u32[]{:S(2)}) copy-start(bf16[27,128,128]{2,1,0:T(8,128)(2,1)} %w2_ref.1) | copy-start | bytes 2654212
  37.1 4.5 %collective-permute-start.9 = (bf16[368,128]{1,0:T(8,128)(2,1)S(1)}, bf16[368,128]{1,0:T(8,128)(2,1)S(1)}, u32[]{:S(2)}, u32[]{:S(2)}) collective-permute-start(bf16[368,128]{1,0:T(8,128)(2,1)S(1)} %get-tuple-element.48), channel_id=1, source_target_pairs={{0,8},{8,16},{16,24},{1,9},{9,17},{17,25},{2,10},{10,18},{18,26},{... | collective-permute-start | bytes 282632 | tf_op jit(solution)/shard_map/ppermute | solution.py:519
  38.4 4.9 %collective-permute-start.10 = (bf16[368,128]{1,0:T(8,128)(2,1)S(1)}, bf16[368,128]{1,0:T(8,128)(2,1)S(1)}, u32[]{:S(2)}, u32[]{:S(2)}) collective-permute-start(bf16[368,128]{1,0:T(8,128)(2,1)S(1)} %get-tuple-element.49), channel_id=1, source_target_pairs={{8,0},{16,8},{24,16},{9,1},{17,9},{25,17},{10,2},{18,10},{26,18},{... | collective-permute-start | bytes 282632 | tf_op jit(solution)/shard_map/ppermute | solution.py:519
  43.4 21.5 %copy-start = (bf16[32,64,512]{2,1,0:T(8,128)(2,1)S(1)}, bf16[32,64,512]{2,1,0:T(8,128)(2,1)}, u32[]{:S(2)}) copy-start(bf16[32,64,512]{2,1,0:T(8,128)(2,1)} %fine_ref.3) | copy-start | bytes 6291460
  43.4 21.5 %copy-start.1 = (s32[32,512]{1,0:T(8,128)S(1)}, s32[32,512]{1,0:T(8,128)}, u32[]{:S(2)}) copy-start(s32[32,512]{1,0:T(8,128)} %mask_ref.3) | copy-start | bytes 196612
  43.4 21.5 %copy-start.2 = (bf16[128,512]{1,0:T(8,128)(2,1)S(1)}, bf16[128,512]{1,0:T(8,128)(2,1)}, u32[]{:S(2)}) copy-start(bf16[128,512]{1,0:T(8,128)(2,1)} %w_ref.3) | copy-start | bytes 393220
  48.4 6.6 %collective-permute-start.14 = (bf16[256,128]{1,0:T(8,128)(2,1)S(1)}, bf16[256,128]{1,0:T(8,128)(2,1)S(1)}, u32[]{:S(2)}, u32[]{:S(2)}) collective-permute-start(bf16[256,128]{1,0:T(8,128)(2,1)S(1)} %get-tuple-element.59), channel_id=1, source_target_pairs={{0,6},{1,7},{2,0},{3,1},{4,2},{5,3},{6,4},{7,5},{8,14},{9,15},{10,... | collective-permute-start | bytes 196616 | tf_op jit(solution)/shard_map/ppermute | solution.py:512
  50.7 5.9 %collective-permute-start.15 = (bf16[256,128]{1,0:T(8,128)(2,1)S(1)}, bf16[256,128]{1,0:T(8,128)(2,1)S(1)}, u32[]{:S(2)}, u32[]{:S(2)}) collective-permute-start(bf16[256,128]{1,0:T(8,128)(2,1)S(1)} %get-tuple-element.60), channel_id=1, source_target_pairs={{0,5},{1,6},{2,7},{3,0},{4,1},{5,2},{6,3},{7,4},{8,13},{9,14},{10,... | collective-permute-start | bytes 196616 | tf_op jit(solution)/shard_map/ppermute | solution.py:512
  50.7 11.7 %collective-permute-start.16 = (bf16[256,128]{1,0:T(8,128)(2,1)S(1)}, bf16[256,128]{1,0:T(8,128)(2,1)S(1)}, u32[]{:S(2)}, u32[]{:S(2)}) collective-permute-start(bf16[256,128]{1,0:T(8,128)(2,1)S(1)} %get-tuple-element.61), channel_id=1, source_target_pairs={{0,4},{1,5},{2,6},{3,7},{4,0},{5,1},{6,2},{7,3},{8,12},{9,13},{10,... | collective-permute-start | bytes 196616 | tf_op jit(solution)/shard_map/ppermute | solution.py:512
  53.2 11.7 %collective-permute-start.17 = (bf16[256,128]{1,0:T(8,128)(2,1)S(1)}, bf16[256,128]{1,0:T(8,128)(2,1)S(1)}, u32[]{:S(2)}, u32[]{:S(2)}) collective-permute-start(bf16[256,128]{1,0:T(8,128)(2,1)S(1)} %get-tuple-element.62), channel_id=1, source_target_pairs={{0,3},{1,4},{2,5},{3,6},{4,7},{5,0},{6,1},{7,2},{8,11},{9,12},{10,... | collective-permute-start | bytes 196616 | tf_op jit(solution)/shard_map/ppermute | solution.py:512
  53.6 13.0 %collective-permute-start.11 = (bf16[256,128]{1,0:T(8,128)(2,1)S(1)}, bf16[256,128]{1,0:T(8,128)(2,1)S(1)}, u32[]{:S(2)}, u32[]{:S(2)}) collective-permute-start(bf16[256,128]{1,0:T(8,128)(2,1)S(1)} %get-tuple-element.55), channel_id=1, source_target_pairs={{0,2},{1,3},{2,4},{3,5},{4,6},{5,7},{6,0},{7,1},{8,10},{9,11},{10,... | collective-permute-start | bytes 196616 | tf_op jit(solution)/shard_map/ppermute | solution.py:512
  55.1 11.6 %collective-permute-start.12 = (bf16[256,128]{1,0:T(8,128)(2,1)S(1)}, bf16[256,128]{1,0:T(8,128)(2,1)S(1)}, u32[]{:S(2)}, u32[]{:S(2)}) collective-permute-start(bf16[256,128]{1,0:T(8,128)(2,1)S(1)} %get-tuple-element.56), channel_id=1, source_target_pairs={{0,1},{1,2},{2,3},{3,4},{4,5},{5,6},{6,7},{7,0},{8,9},{9,10},{10,1... | collective-permute-start | bytes 196616 | tf_op jit(solution)/shard_map/ppermute | solution.py:512
  56.6 10.1 %collective-permute-start.13 = (bf16[256,128]{1,0:T(8,128)(2,1)S(1)}, bf16[256,128]{1,0:T(8,128)(2,1)S(1)}, u32[]{:S(2)}, u32[]{:S(2)}) collective-permute-start(bf16[256,128]{1,0:T(8,128)(2,1)S(1)} %get-tuple-element.58), channel_id=1, source_target_pairs={{0,7},{1,0},{2,1},{3,2},{4,3},{5,4},{6,5},{7,6},{8,15},{9,8},{10,9... | collective-permute-start | bytes 196616 | tf_op jit(solution)/shard_map/ppermute | solution.py:512

commit v5 on v4

--- a/solution.py
+++ b/solution.py
@@ -18,8 +18,8 @@
 LATE = ((12, 3),)
 EARLY_PLANES = 11
 LATE_PLANES = 3
-FIRST_SENT = (4, 3, 5)
-LAST_SENT = (2, 6, 1, 7, 0)
+SENT = (4, 3, 5, 2, 6, 1, 7, 0)
+RETURNED = (1, 7, 6, 4, 2, 3, 5)
 UP_OFFSETS = 4
 DOWN_LIMIT = 62 * 1024 * 1024
 VMEM_LIMIT = 24 * 1024 * 1024
@@ -41,61 +41,91 @@
     return jnp.dot(spread, widen, preferred_element_type=jnp.float32)
 
 
-def down_kernel(offsets, fine_hbm, mask_hbm, w_hbm, *refs):
-    outs = refs[: len(offsets)]
-    fine_ref, mask_ref, w_ref, sems = refs[len(offsets) :]
-    count = len(offsets)
+def down_kernel(fine_hbm, mask_hbm, w_hbm, *refs):
+    outs = refs[:K]
+    fine_ref, mask_ref, w_ref, wide_ref, sems = refs[K:]
     first = [
-        pltpu.make_async_copy(mask_hbm, mask_ref, sems.at[count]),
-        pltpu.make_async_copy(w_hbm, w_ref, sems.at[count + 1]),
+        pltpu.make_async_copy(mask_hbm, mask_ref, sems.at[K]),
+        pltpu.make_async_copy(w_hbm, w_ref, sems.at[K + 1]),
     ]
-    chunks = [
-        pltpu.make_async_copy(fine_hbm.at[pl.ds(j * CAP, CAP)], fine_ref.at[k], sems.at[k])
-        for k, j in enumerate(offsets)
-    ]
-    for copy in first + chunks:
+    chunks = {
+        j: pltpu.make_async_copy(fine_hbm.at[pl.ds(j * CAP, CAP)], fine_ref.at[j], sems.at[j])
+        for j in SENT
+    }
+    for copy in first + list(chunks.values()):
         copy.start()
-    for copy in first:
-        copy.wait()
-    for k, j in enumerate(offsets):
-        mask = expand_mask(mask_ref[j * CAP : (j + 1) * CAP]).astype(jnp.bfloat16)
-        chunks[k].wait()
-        x = fine_ref[k].reshape(CAP * CELLS, -1) * mask
-        y = jnp.dot(x, w_ref[...], preferred_element_type=jnp.float32)
-        outs[k][...] = y.astype(jnp.bfloat16)
-
-
-def down_call(fine, mask, w, offsets):
-    cells, width = fine.shape[1:]
+    first[0].wait()
+    rows = CAP * CELLS
+    for part in range(K // 2):
+        wide_ref[part * 2 * rows : (part + 1) * 2 * rows] = expand_mask(
+            mask_ref[part * 2 * CAP : (part + 1) * 2 * CAP]
+        ).astype(jnp.bfloat16)
+    first[1].wait()
+    for part in range(K // 2):
+        pair = SENT[2 * part : 2 * part + 2]
+        for j in pair:
+            chunks[j].wait()
+        x = [
+            fine_ref[j].reshape(rows, -1) * wide_ref[j * rows : (j + 1) * rows] for j in pair
+        ]
+        y = jnp.dot(jnp.concatenate(x, axis=0), w_ref[...], preferred_element_type=jnp.float32)
+        y = y.astype(jnp.bfloat16)
+        for k, j in enumerate(pair):
+            outs[j][...] = y[k * rows : (k + 1) * rows]
+
+
+def down_call(fine, mask, w):
+    bricks, cells, width = fine.shape
     mid = w.shape[1]
-    count = len(offsets)
     hbm = pl.BlockSpec(memory_space=pltpu.HBM)
-    rows = count * CAP * cells
-    outs = pl.pallas_call(
-        functools.partial(down_kernel, offsets),
+    return pl.pallas_call(
+        down_kernel,
         in_specs=[hbm, hbm, hbm],
-        out_specs=[pl.BlockSpec(memory_space=pltpu.VMEM)] * count,
-        out_shape=[jax.ShapeDtypeStruct((CAP * cells, mid), jnp.bfloat16)] * count,
+        out_specs=[pl.BlockSpec(memory_space=pltpu.VMEM)] * K,
+        out_shape=[jax.ShapeDtypeStruct((CAP * cells, mid), jnp.bfloat16)] * K,
         scratch_shapes=[
-            pltpu.VMEM((count, CAP, cells, width), fine.dtype),
+            pltpu.VMEM((K, CAP, cells, width), fine.dtype),
             pltpu.VMEM(mask.shape, mask.dtype),
             pltpu.VMEM(w.shape, w.dtype),
-            pltpu.SemaphoreType.DMA((count + 2,)),
+            pltpu.VMEM((bricks * cells, width), jnp.bfloat16),
+            pltpu.SemaphoreType.DMA((K + 2,)),
         ],
         compiler_params=pltpu.CompilerParams(vmem_limit_bytes=DOWN_LIMIT),
-        cost_estimate=pl.CostEstimate(
-            flops=2 * rows * width * mid, bytes_accessed=rows * width * 2, transcendentals=0
-        ),
         name="down",
     )(fine, mask, w)
-    return dict(zip(offsets, outs))
+
+
+def prepare_kernel(mask_ref, w1_ref, w2_ref, mask_out, wide1_ref, wide2_ref):
+    gather_weights(w1_ref, wide1_ref)
+    gather_weights(w2_ref, wide2_ref)
+    step = 8
+    for part in range(mask_ref.shape[0] // step):
+        rows = slice(part * step * CELLS, (part + 1) * step * CELLS)
+        mask_out[rows] = expand_mask(mask_ref[part * step : (part + 1) * step]).astype(jnp.bfloat16)
+
+
+def prepare_call(mask, w_first, w_second):
+    mid = w_first.shape[1]
+    vmem = pl.BlockSpec(memory_space=pltpu.VMEM)
+    rows = mask.shape[0] * CELLS
+    wide = jax.ShapeDtypeStruct((9 * mid, 3 * mid), jnp.bfloat16)
+    return pl.pallas_call(
+        prepare_kernel,
+        in_specs=[vmem] * 3,
+        out_specs=[vmem] * 3,
+        out_shape=[jax.ShapeDtypeStruct((rows, mask.shape[1]), jnp.bfloat16), wide, wide],
+        compiler_params=pltpu.CompilerParams(vmem_limit_bytes=VMEM_LIMIT),
+        cost_estimate=pl.CostEstimate(
+            flops=2 * rows * mask.shape[1] * 128, bytes_accessed=rows * mask.shape[1] * 2, transcendentals=0
+        ),
+        name="prepare",
+    )(mask, w_first, w_second)
 
 
 def up_kernel(fine_ref, mask_ref, w_ref, *refs):
     out_ref = refs[-1]
     step = pl.program_id(0)
     bricks, cells, width = fine_ref.shape
-    mask = expand_mask(mask_ref[...])
     count = bricks // CAP
     steps = UP_OFFSETS // count
     for part in range(count):
@@ -105,7 +135,8 @@
         rows = slice(part * CAP * cells, (part + 1) * CAP * cells)
         up = jnp.dot(octant, w_ref[...], preferred_element_type=jnp.float32)
         fine = fine_ref[part * CAP : (part + 1) * CAP].reshape(CAP * cells, width)
-        out = jnp.where(mask[rows] > 0.5, fine.astype(jnp.float32) + up, 0.0)
+        mask = mask_ref[rows].astype(jnp.float32)
+        out = jnp.where(mask > 0.5, fine.astype(jnp.float32) + up, 0.0)
         out_ref[part * CAP : (part + 1) * CAP] = out.astype(jnp.bfloat16).reshape(CAP, cells, width)
 
 
@@ -124,7 +155,7 @@
         grid=(UP_OFFSETS * CAP // step,),
         in_specs=[
             pl.BlockSpec((step, cells, width), lambda i: (place(i), 0, 0)),
-            pl.BlockSpec((step, width), lambda i: (place(i), 0)),
+            pl.BlockSpec((step * cells, width), lambda i: (place(i), 0)),
             pl.BlockSpec((mid, width), lambda i: (0, 0)),
         ]
         + [pl.BlockSpec((CAP * cells, mid), lambda i: (0, 0))] * UP_OFFSETS
@@ -309,8 +340,7 @@
         ).astype(jnp.bfloat16)
 
 
-def inner_kernel(source_ref, block_ref, w1_ref, hidden_ref, wide1_ref, here, moved):
-    gather_weights(w1_ref, wide1_ref)
+def inner_kernel(source_ref, block_ref, wide1_ref, hidden_ref, here, moved):
     inner_planes(source_ref, block_ref, wide1_ref, hidden_ref, here, moved, EARLY)
 
 
@@ -320,7 +350,7 @@
     )
 
 
-def inner_call(source, block, w_first):
+def inner_call(source, block, wide1):
     mid = block.shape[1]
     smem = pl.BlockSpec(memory_space=pltpu.SMEM)
     vmem = pl.BlockSpec(memory_space=pltpu.VMEM)
@@ -328,16 +358,13 @@
     return pl.pallas_call(
         inner_kernel,
         in_specs=[smem, vmem, vmem],
-        out_specs=[vmem] * 2,
-        out_shape=[
-            jax.ShapeDtypeStruct((EARLY_PLANES, rows, mid), jnp.bfloat16),
-            jax.ShapeDtypeStruct((9 * mid, 3 * mid), jnp.bfloat16),
-        ],
+        out_specs=vmem,
+        out_shape=jax.ShapeDtypeStruct((EARLY_PLANES, rows, mid), jnp.bfloat16),
         scratch_shapes=[pltpu.VMEM((EARLY_PLANES + 2, SIDE * COLS, mid), jnp.bfloat16)] * 2,
         compiler_params=pltpu.CompilerParams(vmem_limit_bytes=VMEM_LIMIT),
         cost_estimate=conv_cost(EARLY_PLANES * rows, mid),
         name="inner",
-    )(source, block, w_first)
+    )(source, block, wide1)
 
 
 def side_kernel(
@@ -346,15 +373,12 @@
     before_ref,
     after_ref,
     wide1_ref,
-    w2_ref,
     hidden_ref,
     late_ref,
-    wide2_ref,
     mixed,
     here,
     moved,
 ):
-    gather_weights(w2_ref, wide2_ref)
     inner_planes(source_ref, block_ref, wide1_ref, late_ref, here, moved, LATE)
     width = block_ref.shape[1]
     for d in range(SIDE):
@@ -387,19 +411,18 @@
     hidden_ref[...] = value.reshape(2, inner, 16, width).astype(jnp.bfloat16)
 
 
-def side_call(source, block, before, after, wide1, w_second):
+def side_call(source, block, before, after, wide1):
     mid = block.shape[1]
     smem = pl.BlockSpec(memory_space=pltpu.SMEM)
     vmem = pl.BlockSpec(memory_space=pltpu.VMEM)
     inner = SIDE - 2
     return pl.pallas_call(
         side_kernel,
-        in_specs=[smem] + [vmem] * 5,
-        out_specs=[vmem] * 3,
+        in_specs=[smem] + [vmem] * 4,
+        out_specs=[vmem] * 2,
         out_shape=[
             jax.ShapeDtypeStruct((2, inner, 16, mid), jnp.bfloat16),
             jax.ShapeDtypeStruct((LATE_PLANES, inner * COLS, mid), jnp.bfloat16),
-            jax.ShapeDtypeStruct((9 * mid, 3 * mid), jnp.bfloat16),
         ],
         scratch_shapes=[
             pltpu.VMEM((2, SIDE * 16, mid), jnp.bfloat16),
@@ -409,7 +432,7 @@
         compiler_params=pltpu.CompilerParams(vmem_limit_bytes=VMEM_LIMIT),
         cost_estimate=conv_cost(inner * (4 + LATE_PLANES) * COLS, mid),
         name="side",
-    )(source, block, before, after, wide1, w_second)
+    )(source, block, before, after, wide1)
 
 
 def final_kernel(source_ref, *refs):
@@ -521,25 +544,26 @@
 
 def shards(fine, fine_mask, slot_source, w_down, w_first, w_second, w_up):
     mid = w_down.shape[1]
-    sent = down_call(fine, fine_mask, w_down, FIRST_SENT)
-    arrived = {j: from_behind(sent[j], "xy", j) for j in FIRST_SENT}
-    sent = down_call(fine, fine_mask, w_down, LAST_SENT)
-    arrived.update({j: from_behind(sent[j], "xy", j) for j in LAST_SENT if j})
-    arrived[0] = sent[0]
+    sent = down_call(fine, fine_mask, w_down)
+    arrived = {j: from_behind(sent[j], "xy", j) for j in SENT if j}
+    later_mask, own = lax.optimization_barrier((fine_mask, sent[0]))
+    mask, wide1, wide2 = prepare_call(later_mask, w_first, w_second)
+    own, mask, wide1, wide2 = lax.optimization_barrier((own, mask, wide1, wide2))
+    arrived[0] = own
     block, low, high = place_call(slot_source, [arrived[j] for j in range(K)])
     before, after = neighbours(low, high, "xy")
-    early, wide1 = inner_call(slot_source, block, w_first)
-    before, after, early, wide1 = lax.optimization_barrier((before, after, early, wide1))
+    early = inner_call(slot_source, block, wide1)
+    before, after, early = lax.optimization_barrier((before, after, early))
     under_send, over_send = edge_call(slot_source, block, before, after)
     under, over = neighbours(under_send, over_send, "gz")
-    side, late, wide2 = side_call(slot_source, block, before, after, wide1, w_second)
+    side, late = side_call(slot_source, block, before, after, wide1)
     coarse, *back = final_call(
         slot_source, block, (before, after, under, over), (early, late, side), wide1, wide2
     )
-    octant = {j: from_behind(back[j], "xy", -j) for j in FIRST_SENT + LAST_SENT if j}
+    octant = {j: from_behind(back[j], "xy", -j) for j in RETURNED}
     octant[0] = back[0]
-    fine_out = up_call(fine, fine_mask, w_up, [octant[j] for j in (2, 3, 4, 5)], 1, None)
-    fine_out = up_call(fine, fine_mask, w_up, [octant[j] for j in (6, 7, 0, 1)], 3, fine_out)
+    fine_out = up_call(fine, mask, w_up, [octant[j] for j in (6, 7, 0, 1)], 3, None)
+    fine_out = up_call(fine, mask, w_up, [octant[j] for j in (2, 3, 4, 5)], 1, fine_out)
     return fine_out, coarse.reshape(SIDE, SIDE, COLS, mid)
 
 

time: 68.7 us -> 66.4 us (0.967)
  Pallas kernels: 20.1 us -> 18.5 us
  starting transfers between devices: 34.3 us -> 32.9 us
    ppermute x14, starting transfers between devices: 26.1 us -> 25 us  [from_behind(): return lax.ppermute(value, axis, pairs)]
    pallas_call x4, Pallas kernels: 10.3 us -> 9.22 us  [the longest x1 4.1 us: down_call(): pl.pallas_call(down_kernel, in_specs=[hbm, hbm, hbm], out_specs=[pl.Block...]
  transfers between devices with their start and end apart: 18 -> 18, of which waited for: 6 -> 7; matrix products, arithmetic and copies ran while one was open for 0% -> 0% of each run, Pallas kernels for 14% -> 10%
where the time goes in v5:
time: 66.4 us; the launch traced here: 65.8 us
  starting transfers between devices  32.9 us (50%)
  Pallas kernels  18.5 us (28%)
  waiting for transfers between devices  12.7 us (19%)
  local copies, waits for them, and re-layouts  0.86 us (1%)
  between operations  0.79 us (1%)
    ppermute x14, starting transfers between devices, from_behind(): return lax.ppermute(value, axis, pairs)  25 us
    ppermute x14, waiting for transfers between devices, from_behind(): return lax.ppermute(value, axis, pairs)  8.23 us
    ppermute x2, starting transfers between devices, neighbours(): lax.ppermute(high, axis, forward)  5.36 us
    pallas_call x1, Pallas kernels, final_call(): pl.pallas_call(final_kernel, in_specs=[smem] + [vmem] * 10, out_specs=[vm...  5.02 us
    ppermute x2, waiting for transfers between devices, neighbours(): lax.ppermute(low, axis, backward)  4.42 us
    pallas_call x1, Pallas kernels, down_call(): pl.pallas_call(down_kernel, in_specs=[hbm, hbm, hbm], out_specs=[pl.Block...  4.1 us
    pallas_call x2, Pallas kernels, up_call(): pl.pallas_call(up_kernel, grid=(UP_OFFSETS * CAP // step,), in_specs=[pl....  2.99 us
    ppermute x2, starting transfers between devices, neighbours(): lax.ppermute(low, axis, backward)  2.58 us
  transfers between devices with their start and end apart: 18, of which 7 were waited for; matrix products, arithmetic and copies ran while one was open for 0% of the time, Pallas kernels for 10%

profile of v5, /device:TPU:0, one launch (start us, length us, event | category | flops | bytes accessed | tf_op | source)
XLA Modules:
  0.0 65.8 jit_solution(6640171239802775473)
XLA Ops:
  0.7 4.1 %down.1 = (bf16[256,128]{1,0:T(8,128)(2,1)}, bf16[256,128]{1,0:T(8,128)(2,1)}, bf16[256,128]{1,0:T(8,128)(2,1)}, bf16[256,128]{1,0:T(8,128)(2,1)}, bf16[256,128]...) custom-call(bf16[32,64,512]{2,1,0:T(8,128)(2,1)} %fine_ref.3, ...), custom_call_target="tpu_custom_call" | custom-call | tf_op jit(solution)/shard_map/down/pallas_call | solution.py:81
  4.8 3.0 %collective-permute-start = (bf16[256,128]{1,0:T(8,128)(2,1)}, bf16[256,128]{1,0:T(8,128)(2,1)S(1)}, u32[]{:S(2)}, u32[]{:S(2)}) collective-permute-start(bf16[256,128]{1,0:T(8,128)(2,1)} %get-tuple-element.46), channel_id=1, source_target_pairs={{0,1},{1,2},{2,3},{3,4},{4,5},{5,6},{6,7},{7,0},{8,9},{9,10},{10,1... | collective-permute-start | bytes 196616 | tf_op jit(solution)/shard_map/ppermute | solution.py:535
  7.8 1.6 %collective-permute-start.1 = (bf16[256,128]{1,0:T(8,128)(2,1)}, bf16[256,128]{1,0:T(8,128)(2,1)S(1)}, u32[]{:S(2)}, u32[]{:S(2)}) collective-permute-start(bf16[256,128]{1,0:T(8,128)(2,1)} %get-tuple-element.47), channel_id=1, source_target_pairs={{0,2},{1,3},{2,4},{3,5},{4,6},{5,7},{6,0},{7,1},{8,10},{9,11},{10,... | collective-permute-start | bytes 196616 | tf_op jit(solution)/shard_map/ppermute | solution.py:535
  9.3 2.6 %collective-permute-start.2 = (bf16[256,128]{1,0:T(8,128)(2,1)}, bf16[256,128]{1,0:T(8,128)(2,1)S(1)}, u32[]{:S(2)}, u32[]{:S(2)}) collective-permute-start(bf16[256,128]{1,0:T(8,128)(2,1)} %get-tuple-element.48), channel_id=1, source_target_pairs={{0,3},{1,4},{2,5},{3,6},{4,7},{5,0},{6,1},{7,2},{8,11},{9,12},{10,... | collective-permute-start | bytes 196616 | tf_op jit(solution)/shard_map/ppermute | solution.py:535
  11.9 1.2 %collective-permute-start.3 = (bf16[256,128]{1,0:T(8,128)(2,1)}, bf16[256,128]{1,0:T(8,128)(2,1)S(1)}, u32[]{:S(2)}, u32[]{:S(2)}) collective-permute-start(bf16[256,128]{1,0:T(8,128)(2,1)} %get-tuple-element.49), channel_id=1, source_target_pairs={{0,4},{1,5},{2,6},{3,7},{4,0},{5,1},{6,2},{7,3},{8,12},{9,13},{10,... | collective-permute-start | bytes 196616 | tf_op jit(solution)/shard_map/ppermute | solution.py:535
  13.1 2.6 %collective-permute-start.4 = (bf16[256,128]{1,0:T(8,128)(2,1)}, bf16[256,128]{1,0:T(8,128)(2,1)S(1)}, u32[]{:S(2)}, u32[]{:S(2)}) collective-permute-start(bf16[256,128]{1,0:T(8,128)(2,1)} %get-tuple-element.50), channel_id=1, source_target_pairs={{0,5},{1,6},{2,7},{3,0},{4,1},{5,2},{6,3},{7,4},{8,13},{9,14},{10,... | collective-permute-start | bytes 196616 | tf_op jit(solution)/shard_map/ppermute | solution.py:535
  15.8 1.3 %collective-permute-start.5 = (bf16[256,128]{1,0:T(8,128)(2,1)}, bf16[256,128]{1,0:T(8,128)(2,1)S(1)}, u32[]{:S(2)}, u32[]{:S(2)}) collective-permute-start(bf16[256,128]{1,0:T(8,128)(2,1)} %get-tuple-element.51), channel_id=1, source_target_pairs={{0,6},{1,7},{2,0},{3,1},{4,2},{5,3},{6,4},{7,5},{8,14},{9,15},{10,... | collective-permute-start | bytes 196616 | tf_op jit(solution)/shard_map/ppermute | solution.py:535
  17.1 1.4 %collective-permute-start.6 = (bf16[256,128]{1,0:T(8,128)(2,1)}, bf16[256,128]{1,0:T(8,128)(2,1)S(1)}, u32[]{:S(2)}, u32[]{:S(2)}) collective-permute-start(bf16[256,128]{1,0:T(8,128)(2,1)} %get-tuple-element.52), channel_id=1, source_target_pairs={{0,7},{1,0},{2,1},{3,2},{4,3},{5,4},{6,5},{7,6},{8,15},{9,8},{10,9... | collective-permute-start | bytes 196616 | tf_op jit(solution)/shard_map/ppermute | solution.py:535
  18.6 1.0 %prepare.1 = (bf16[2048,512]{1,0:T(8,128)(2,1)S(1)}, bf16[1152,384]{1,0:T(8,128)(2,1)S(1)}, bf16[1152,384]{1,0:T(8,128)(2,1)S(1)}) custom-call(s32[32,512]{1,0:T(8,128)S(1)} %copy-done.4, bf16[27,128,128]{2,1,0:T(8,128)(2,1)S(1)} %copy-done.1, bf16[27,128,128]{2,1,0:T(8,128)(2,1)S(1)} %copy-done.2), custom_call_target="tpu_custom_call" | custom-call | flops 268435456 | bytes 2097152 | tf_op jit(solution)/shard_map/prepare/pallas_call | solution.py:112
  19.9 0.8 %collective-permute-done.4.refs_5_ = bf16[256,128]{1,0:T(8,128)(2,1)S(1)} collective-permute-done((bf16[256,128]{1,0:T(8,128)(2,1)}, bf16[256,128]{1,0:T(8,128)(2,1)S(1)}, u32[]{:S(2)}, u32[]{:S(2)}) %collective-permute-start.4) | collective-permute-done | bytes 65568 | tf_op jit(solution)/shard_map/ppermute | solution.py:535
  20.7 1.3 %collective-permute-done.5.refs_6_ = bf16[256,128]{1,0:T(8,128)(2,1)S(1)} collective-permute-done((bf16[256,128]{1,0:T(8,128)(2,1)}, bf16[256,128]{1,0:T(8,128)(2,1)S(1)}, u32[]{:S(2)}, u32[]{:S(2)}) %collective-permute-start.5) | collective-permute-done | bytes 65568 | tf_op jit(solution)/shard_map/ppermute | solution.py:535
  21.9 0.8 %copy-done.5 = bf16[256,128]{1,0:T(8,128)(2,1)S(1)} copy-done((bf16[256,128]{1,0:T(8,128)(2,1)S(1)}, bf16[256,128]{1,0:T(8,128)(2,1)}, u32[]{:S(2)}) %copy-start.5) | copy-done | bytes 65560
  22.8 0.7 %place.1 = (bf16[2048,128]{1,0:T(8,128)(2,1)S(1)}, bf16[288,128]{1,0:T(8,128)(2,1)S(1)}, bf16[288,128]{1,0:T(8,128)(2,1)S(1)}) custom-call(s32[32]{0:T(128)S(1)} %copy-done.6, bf16[256,128]{1,0:T(8,128)(2,1)S(1)} %copy-done.5, bf16[256,128]{1,0:T(8,128)(2,1)S(1)} %collective-permute-done.refs_1_, bf16[256,128]{1,0:T(8,128)(2,1)S(1)} %collective-permute-done.1.refs_2_, ...), custom_call_target="tpu_custom_call" | custom-call | tf_op jit(solution)/shard_map/place/pallas_call | solution.py:226
  23.5 4.1 %collective-permute-start.7 = (bf16[288,128]{1,0:T(8,128)(2,1)S(1)}, bf16[288,128]{1,0:T(8,128)(2,1)S(1)}, u32[]{:S(2)}, u32[]{:S(2)}) collective-permute-start(bf16[288,128]{1,0:T(8,128)(2,1)S(1)} %get-tuple-element.54), channel_id=1, source_target_pairs={{0,1},{1,2},{2,3},{3,4},{4,5},{5,6},{6,7},{8,9},{9,10},{10,11},{11... | collective-permute-start | bytes 221192 | tf_op jit(solution)/shard_map/ppermute | solution.py:542
  27.6 1.3 %collective-permute-start.8 = (bf16[288,128]{1,0:T(8,128)(2,1)S(1)}, bf16[288,128]{1,0:T(8,128)(2,1)S(1)}, u32[]{:S(2)}, u32[]{:S(2)}) collective-permute-start(bf16[288,128]{1,0:T(8,128)(2,1)S(1)} %get-tuple-element.55), channel_id=1, source_target_pairs={{1,0},{2,1},{3,2},{4,3},{5,4},{6,5},{7,6},{9,8},{10,9},{11,10},{12... | collective-permute-start | bytes 221192 | tf_op jit(solution)/shard_map/ppermute | solution.py:542
  28.9 2.4 %inner.1.refs_5_ = bf16[11,112,128]{2,1,0:T(8,128)(2,1)S(1)} custom-call(s32[32]{0:T(128)S(1)} %copy-done.6, bf16[2048,128]{1,0:T(8,128)(2,1)S(1)} %get-tuple-element.53.block_ref.refs_0_, bf16[1152,384]{1,0:T(8,128)(2,1)S(1)} %get-tuple-element.56.wide1_ref.refs_8_), custom_call_target="tpu_custom_call" | custom-call | flops 1089994752 | bytes 1769472 | tf_op jit(solution)/shard_map/inner/pallas_call | solution.py:358
  31.3 2.6 %collective-permute-done.8.after_ref.refs_2_ = bf16[288,128]{1,0:T(8,128)(2,1)S(1)} collective-permute-done((bf16[288,128]{1,0:T(8,128)(2,1)S(1)}, bf16[288,128]{1,0:T(8,128)(2,1)S(1)}, u32[]{:S(2)}, u32[]{:S(2)}) %collective-permute-start.8) | collective-permute-done | bytes 73760 | tf_op jit(solution)/shard_map/ppermute | solution.py:542
  33.8 0.6 edge.1
  34.4 1.3 %collective-permute-start.9 = (bf16[368,128]{1,0:T(8,128)(2,1)S(1)}, bf16[368,128]{1,0:T(8,128)(2,1)S(1)}, u32[]{:S(2)}, u32[]{:S(2)}) collective-permute-start(bf16[368,128]{1,0:T(8,128)(2,1)S(1)} %get-tuple-element.59), channel_id=1, source_target_pairs={{0,8},{8,16},{16,24},{1,9},{9,17},{17,25},{2,10},{10,18},{18,26},{... | collective-permute-start | bytes 282632 | tf_op jit(solution)/shard_map/ppermute | solution.py:542
  35.7 1.3 %collective-permute-start.10 = (bf16[368,128]{1,0:T(8,128)(2,1)S(1)}, bf16[368,128]{1,0:T(8,128)(2,1)S(1)}, u32[]{:S(2)}, u32[]{:S(2)}) collective-permute-start(bf16[368,128]{1,0:T(8,128)(2,1)S(1)} %get-tuple-element.60), channel_id=1, source_target_pairs={{8,0},{16,8},{24,16},{9,1},{17,9},{25,17},{10,2},{18,10},{26,18},{... | collective-permute-start | bytes 282632 | tf_op jit(solution)/shard_map/ppermute | solution.py:542
  37.0 1.8 %side.1 = (bf16[2,14,16,128]{3,2,1,0:T(8,128)(2,1)S(1)}, bf16[3,112,128]{2,1,0:T(8,128)(2,1)S(1)}) custom-call(s32[32]{0:T(128)S(1)} %copy-done.6, bf16[2048,128]{1,0:T(8,128)(2,1)S(1)} %get-tuple-element.53.block_ref.refs_0_, bf16[288,128]{1,0:T(8,128)(2,1)S(1)} %collective-permute-done.7.before_ref.refs_1_, ...), custom_call_target="tpu_custom_call" | custom-call | flops 693633024 | bytes 1769472 | tf_op jit(solution)/shard_map/side/pallas_call | solution.py:419
  38.8 1.9 %collective-permute-done.10.refs_4_ = bf16[368,128]{1,0:T(8,128)(2,1)S(1)} collective-permute-done((bf16[368,128]{1,0:T(8,128)(2,1)S(1)}, bf16[368,128]{1,0:T(8,128)(2,1)S(1)}, u32[]{:S(2)}, u32[]{:S(2)}) %collective-permute-start.10) | collective-permute-done | bytes 94240 | tf_op jit(solution)/shard_map/ppermute | solution.py:542
  40.7 5.0 %final.1 = (bf16[2048,128]{1,0:T(8,128)(2,1)}, bf16[256,128]{1,0:T(8,128)(2,1)S(1)}, bf16[256,128]{1,0:T(8,128)(2,1)S(1)}, bf16[256,128]{1,0:T(8,128)(2,1)S(1)},...) custom-call(s32[32]{0:T(128)S(1)} %copy-done.6, ...), custom_call_target="tpu_custom_call" | custom-call | flops 1811939328 | bytes 1769472 | tf_op jit(solution)/shard_map/final/pallas_call | solution.py:511
  45.7 2.0 %collective-permute-start.15 = (bf16[256,128]{1,0:T(8,128)(2,1)S(1)}, bf16[256,128]{1,0:T(8,128)(2,1)S(1)}, u32[]{:S(2)}, u32[]{:S(2)}) collective-permute-start(bf16[256,128]{1,0:T(8,128)(2,1)S(1)} %get-tuple-element.69), channel_id=1, source_target_pairs={{0,2},{1,3},{2,4},{3,5},{4,6},{5,7},{6,0},{7,1},{8,10},{9,11},{10,... | collective-permute-start | bytes 196616 | tf_op jit(solution)/shard_map/ppermute | solution.py:535
  47.6 1.4 %collective-permute-start.16 = (bf16[256,128]{1,0:T(8,128)(2,1)S(1)}, bf16[256,128]{1,0:T(8,128)(2,1)S(1)}, u32[]{:S(2)}, u32[]{:S(2)}) collective-permute-start(bf16[256,128]{1,0:T(8,128)(2,1)S(1)} %get-tuple-element.70), channel_id=1, source_target_pairs={{0,1},{1,2},{2,3},{3,4},{4,5},{5,6},{6,7},{7,0},{8,9},{9,10},{10,1... | collective-permute-start | bytes 196616 | tf_op jit(solution)/shard_map/ppermute | solution.py:535
  49.0 3.4 %collective-permute-start.17 = (bf16[256,128]{1,0:T(8,128)(2,1)S(1)}, bf16[256,128]{1,0:T(8,128)(2,1)S(1)}, u32[]{:S(2)}, u32[]{:S(2)}) collective-permute-start(bf16[256,128]{1,0:T(8,128)(2,1)S(1)} %get-tuple-element.72), channel_id=1, source_target_pairs={{0,7},{1,0},{2,1},{3,2},{4,3},{5,4},{6,5},{7,6},{8,15},{9,8},{10,9... | collective-permute-start | bytes 196616 | tf_op jit(solution)/shard_map/ppermute | solution.py:535
  52.4 1.0 %collective-permute-start.12 = (bf16[256,128]{1,0:T(8,128)(2,1)S(1)}, bf16[256,128]{1,0:T(8,128)(2,1)S(1)}, u32[]{:S(2)}, u32[]{:S(2)}) collective-permute-start(bf16[256,128]{1,0:T(8,128)(2,1)S(1)} %get-tuple-element.66), channel_id=1, source_target_pairs={{0,5},{1,6},{2,7},{3,0},{4,1},{5,2},{6,3},{7,4},{8,13},{9,14},{10,... | collective-permute-start | bytes 196616 | tf_op jit(solution)/shard_map/ppermute | solution.py:535
  53.4 2.2 %collective-permute-start.13 = (bf16[256,128]{1,0:T(8,128)(2,1)S(1)}, bf16[256,128]{1,0:T(8,128)(2,1)S(1)}, u32[]{:S(2)}, u32[]{:S(2)}) collective-permute-start(bf16[256,128]{1,0:T(8,128)(2,1)S(1)} %get-tuple-element.67), channel_id=1, source_target_pairs={{0,4},{1,5},{2,6},{3,7},{4,0},{5,1},{6,2},{7,3},{8,12},{9,13},{10,... | collective-permute-start | bytes 196616 | tf_op jit(solution)/shard_map/ppermute | solution.py:535
  55.7 1.2 %collective-permute-start.14 = (bf16[256,128]{1,0:T(8,128)(2,1)S(1)}, bf16[256,128]{1,0:T(8,128)(2,1)S(1)}, u32[]{:S(2)}, u32[]{:S(2)}) collective-permute-start(bf16[256,128]{1,0:T(8,128)(2,1)S(1)} %get-tuple-element.68), channel_id=1, source_target_pairs={{0,3},{1,4},{2,5},{3,6},{4,7},{5,0},{6,1},{7,2},{8,11},{9,12},{10,... | collective-permute-start | bytes 196616 | tf_op jit(solution)/shard_map/ppermute | solution.py:535
  56.9 1.5 %up.2.refs_4_ = bf16[32,64,512]{2,1,0:T(8,128)(2,1)} custom-call(bf16[32,64,512]{2,1,0:T(8,128)(2,1)S(1)} %copy-done, bf16[2048,512]{1,0:T(8,128)(2,1)S(1)} %get-tuple-element.44.mask_ref, bf16[128,512]{1,0:T(8,128)(2,1)S(1)} %copy-done.3, bf16[256,128]{1,0:T(8,128)(2,1)S(1)} %collective-permute-done.15.refs_0_, ...), custom_call_target="tpu_custom_call" | custom-call | flops 134217728 | bytes 2097152 | tf_op jit(solution)/shard_map/up/pallas_call | solution.py:153
  58.4 5.5 %collective-permute-done.13.refs_2_ = bf16[256,128]{1,0:T(8,128)(2,1)S(1)} collective-permute-done((bf16[256,128]{1,0:T(8,128)(2,1)S(1)}, bf16[256,128]{1,0:T(8,128)(2,1)S(1)}, u32[]{:S(2)}, u32[]{:S(2)}) %collective-permute-start.13) | collective-permute-done | bytes 65568 | tf_op jit(solution)/shard_map/ppermute | solution.py:535
  64.3 1.5 %up.3 = bf16[32,64,512]{2,1,0:T(8,128)(2,1)} custom-call(bf16[32,64,512]{2,1,0:T(8,128)(2,1)S(1)} %copy-done, bf16[2048,512]{1,0:T(8,128)(2,1)S(1)} %get-tuple-element.44.mask_ref, bf16[128,512]{1,0:T(8,128)(2,1)S(1)} %copy-done.3, bf16[256,128]{1,0:T(8,128)(2,1)S(1)} %collective-permute-done.11.refs_0_, ...), custom_call_target="tpu_custom_call", output_to_operand_aliasing={{}: (7, {})} | custom-call | flops 134217728 | bytes 2097152 | tf_op jit(solution)/shard_map/up/pallas_call | solution.py:153
  (27 shorter events, 0.8 us)
Async XLA Ops:
  0.6 17.9 %copy-start.4 = (s32[32,512]{1,0:T(8,128)S(1)}, s32[32,512]{1,0:T(8,128)}, u32[]{:S(2)}) copy-start(s32[32,512]{1,0:T(8,128)} %mask_ref) | copy-start | bytes 196612
  0.6 17.9 %copy-start.2 = (bf16[27,128,128]{2,1,0:T(8,128)(2,1)S(1)}, bf16[27,128,128]{2,1,0:T(8,128)(2,1)}, u32[]{:S(2)}) copy-start(bf16[27,128,128]{2,1,0:T(8,128)(2,1)} %w2_ref.1) | copy-start | bytes 2654212
  0.7 17.9 %copy-start.1 = (bf16[27,128,128]{2,1,0:T(8,128)(2,1)S(1)}, bf16[27,128,128]{2,1,0:T(8,128)(2,1)}, u32[]{:S(2)}) copy-start(bf16[27,128,128]{2,1,0:T(8,128)(2,1)} %w1_ref.1) | copy-start | bytes 2654212
  0.7 21.3 %copy-start.6 = (s32[32]{0:T(128)S(1)}, s32[32]{0:T(128)}, u32[]{:S(2)}) copy-start(s32[32]{0:T(128)} %source_ref.9) | copy-start | bytes 388
  4.8 11.0 %collective-permute-start = (bf16[256,128]{1,0:T(8,128)(2,1)}, bf16[256,128]{1,0:T(8,128)(2,1)S(1)}, u32[]{:S(2)}, u32[]{:S(2)}) collective-permute-start(bf16[256,128]{1,0:T(8,128)(2,1)} %get-tuple-element.46), channel_id=1, source_target_pairs={{0,1},{1,2},{2,3},{3,4},{4,5},{5,6},{6,7},{7,0},{8,9},{9,10},{10,1... | collective-permute-start | bytes 196616 | tf_op jit(solution)/shard_map/ppermute | solution.py:535
  7.8 9.3 %collective-permute-start.1 = (bf16[256,128]{1,0:T(8,128)(2,1)}, bf16[256,128]{1,0:T(8,128)(2,1)S(1)}, u32[]{:S(2)}, u32[]{:S(2)}) collective-permute-start(bf16[256,128]{1,0:T(8,128)(2,1)} %get-tuple-element.47), channel_id=1, source_target_pairs={{0,2},{1,3},{2,4},{3,5},{4,6},{5,7},{6,0},{7,1},{8,10},{9,11},{10,... | collective-permute-start | bytes 196616 | tf_op jit(solution)/shard_map/ppermute | solution.py:535
  9.3 10.2 %collective-permute-start.2 = (bf16[256,128]{1,0:T(8,128)(2,1)}, bf16[256,128]{1,0:T(8,128)(2,1)S(1)}, u32[]{:S(2)}, u32[]{:S(2)}) collective-permute-start(bf16[256,128]{1,0:T(8,128)(2,1)} %get-tuple-element.48), channel_id=1, source_target_pairs={{0,3},{1,4},{2,5},{3,6},{4,7},{5,0},{6,1},{7,2},{8,11},{9,12},{10,... | collective-permute-start | bytes 196616 | tf_op jit(solution)/shard_map/ppermute | solution.py:535
  11.9 8.0 %collective-permute-start.3 = (bf16[256,128]{1,0:T(8,128)(2,1)}, bf16[256,128]{1,0:T(8,128)(2,1)S(1)}, u32[]{:S(2)}, u32[]{:S(2)}) collective-permute-start(bf16[256,128]{1,0:T(8,128)(2,1)} %get-tuple-element.49), channel_id=1, source_target_pairs={{0,4},{1,5},{2,6},{3,7},{4,0},{5,1},{6,2},{7,3},{8,12},{9,13},{10,... | collective-permute-start | bytes 196616 | tf_op jit(solution)/shard_map/ppermute | solution.py:535
  13.1 7.5 %collective-permute-start.4 = (bf16[256,128]{1,0:T(8,128)(2,1)}, bf16[256,128]{1,0:T(8,128)(2,1)S(1)}, u32[]{:S(2)}, u32[]{:S(2)}) collective-permute-start(bf16[256,128]{1,0:T(8,128)(2,1)} %get-tuple-element.50), channel_id=1, source_target_pairs={{0,5},{1,6},{2,7},{3,0},{4,1},{5,2},{6,3},{7,4},{8,13},{9,14},{10,... | collective-permute-start | bytes 196616 | tf_op jit(solution)/shard_map/ppermute | solution.py:535
  15.8 6.2 %collective-permute-start.5 = (bf16[256,128]{1,0:T(8,128)(2,1)}, bf16[256,128]{1,0:T(8,128)(2,1)S(1)}, u32[]{:S(2)}, u32[]{:S(2)}) collective-permute-start(bf16[256,128]{1,0:T(8,128)(2,1)} %get-tuple-element.51), channel_id=1, source_target_pairs={{0,6},{1,7},{2,0},{3,1},{4,2},{5,3},{6,4},{7,5},{8,14},{9,15},{10,... | collective-permute-start | bytes 196616 | tf_op jit(solution)/shard_map/ppermute | solution.py:535
  17.1 4.8 %collective-permute-start.6 = (bf16[256,128]{1,0:T(8,128)(2,1)}, bf16[256,128]{1,0:T(8,128)(2,1)S(1)}, u32[]{:S(2)}, u32[]{:S(2)}) collective-permute-start(bf16[256,128]{1,0:T(8,128)(2,1)} %get-tuple-element.52), channel_id=1, source_target_pairs={{0,7},{1,0},{2,1},{3,2},{4,3},{5,4},{6,5},{7,6},{8,15},{9,8},{10,9... | collective-permute-start | bytes 196616 | tf_op jit(solution)/shard_map/ppermute | solution.py:535
  21.9 0.8 %copy-start.5 = (bf16[256,128]{1,0:T(8,128)(2,1)S(1)}, bf16[256,128]{1,0:T(8,128)(2,1)}, u32[]{:S(2)}) copy-start(bf16[256,128]{1,0:T(8,128)(2,1)} %get-tuple-element.45.refs_0_) | copy-start | bytes 196612
  23.5 7.8 %collective-permute-start.7 = (bf16[288,128]{1,0:T(8,128)(2,1)S(1)}, bf16[288,128]{1,0:T(8,128)(2,1)S(1)}, u32[]{:S(2)}, u32[]{:S(2)}) collective-permute-start(bf16[288,128]{1,0:T(8,128)(2,1)S(1)} %get-tuple-element.54), channel_id=1, source_target_pairs={{0,1},{1,2},{2,3},{3,4},{4,5},{5,6},{6,7},{8,9},{9,10},{10,11},{11... | collective-permute-start | bytes 221192 | tf_op jit(solution)/shard_map/ppermute | solution.py:542
  27.6 6.2 %collective-permute-start.8 = (bf16[288,128]{1,0:T(8,128)(2,1)S(1)}, bf16[288,128]{1,0:T(8,128)(2,1)S(1)}, u32[]{:S(2)}, u32[]{:S(2)}) collective-permute-start(bf16[288,128]{1,0:T(8,128)(2,1)S(1)} %get-tuple-element.55), channel_id=1, source_target_pairs={{1,0},{2,1},{3,2},{4,3},{5,4},{6,5},{7,6},{9,8},{10,9},{11,10},{12... | collective-permute-start | bytes 221192 | tf_op jit(solution)/shard_map/ppermute | solution.py:542
  34.4 4.4 %collective-permute-start.9 = (bf16[368,128]{1,0:T(8,128)(2,1)S(1)}, bf16[368,128]{1,0:T(8,128)(2,1)S(1)}, u32[]{:S(2)}, u32[]{:S(2)}) collective-permute-start(bf16[368,128]{1,0:T(8,128)(2,1)S(1)} %get-tuple-element.59), channel_id=1, source_target_pairs={{0,8},{8,16},{16,24},{1,9},{9,17},{17,25},{2,10},{10,18},{18,26},{... | collective-permute-start | bytes 282632 | tf_op jit(solution)/shard_map/ppermute | solution.py:542
  35.7 4.9 %collective-permute-start.10 = (bf16[368,128]{1,0:T(8,128)(2,1)S(1)}, bf16[368,128]{1,0:T(8,128)(2,1)S(1)}, u32[]{:S(2)}, u32[]{:S(2)}) collective-permute-start(bf16[368,128]{1,0:T(8,128)(2,1)S(1)} %get-tuple-element.60), channel_id=1, source_target_pairs={{8,0},{16,8},{24,16},{9,1},{17,9},{25,17},{10,2},{18,10},{26,18},{... | collective-permute-start | bytes 282632 | tf_op jit(solution)/shard_map/ppermute | solution.py:542
  40.7 16.2 %copy-start = (bf16[32,64,512]{2,1,0:T(8,128)(2,1)S(1)}, bf16[32,64,512]{2,1,0:T(8,128)(2,1)}, u32[]{:S(2)}) copy-start(bf16[32,64,512]{2,1,0:T(8,128)(2,1)} %fine_ref.3) | copy-start | bytes 6291460
  40.7 16.2 %copy-start.3 = (bf16[128,512]{1,0:T(8,128)(2,1)S(1)}, bf16[128,512]{1,0:T(8,128)(2,1)}, u32[]{:S(2)}) copy-start(bf16[128,512]{1,0:T(8,128)(2,1)} %w_ref.3) | copy-start | bytes 393220
  45.7 7.7 %collective-permute-start.15 = (bf16[256,128]{1,0:T(8,128)(2,1)S(1)}, bf16[256,128]{1,0:T(8,128)(2,1)S(1)}, u32[]{:S(2)}, u32[]{:S(2)}) collective-permute-start(bf16[256,128]{1,0:T(8,128)(2,1)S(1)} %get-tuple-element.69), channel_id=1, source_target_pairs={{0,2},{1,3},{2,4},{3,5},{4,6},{5,7},{6,0},{7,1},{8,10},{9,11},{10,... | collective-permute-start | bytes 196616 | tf_op jit(solution)/shard_map/ppermute | solution.py:535
  47.6 8.0 %collective-permute-start.16 = (bf16[256,128]{1,0:T(8,128)(2,1)S(1)}, bf16[256,128]{1,0:T(8,128)(2,1)S(1)}, u32[]{:S(2)}, u32[]{:S(2)}) collective-permute-start(bf16[256,128]{1,0:T(8,128)(2,1)S(1)} %get-tuple-element.70), channel_id=1, source_target_pairs={{0,1},{1,2},{2,3},{3,4},{4,5},{5,6},{6,7},{7,0},{8,9},{9,10},{10,1... | collective-permute-start | bytes 196616 | tf_op jit(solution)/shard_map/ppermute | solution.py:535
  49.0 7.9 %collective-permute-start.17 = (bf16[256,128]{1,0:T(8,128)(2,1)S(1)}, bf16[256,128]{1,0:T(8,128)(2,1)S(1)}, u32[]{:S(2)}, u32[]{:S(2)}) collective-permute-start(bf16[256,128]{1,0:T(8,128)(2,1)S(1)} %get-tuple-element.72), channel_id=1, source_target_pairs={{0,7},{1,0},{2,1},{3,2},{4,3},{5,4},{6,5},{7,6},{8,15},{9,8},{10,9... | collective-permute-start | bytes 196616 | tf_op jit(solution)/shard_map/ppermute | solution.py:535
  52.4 6.0 %collective-permute-start.11 = (bf16[256,128]{1,0:T(8,128)(2,1)S(1)}, bf16[256,128]{1,0:T(8,128)(2,1)S(1)}, u32[]{:S(2)}, u32[]{:S(2)}) collective-permute-start(bf16[256,128]{1,0:T(8,128)(2,1)S(1)} %get-tuple-element.65), channel_id=1, source_target_pairs={{0,6},{1,7},{2,0},{3,1},{4,2},{5,3},{6,4},{7,5},{8,14},{9,15},{10,... | collective-permute-start | bytes 196616 | tf_op jit(solution)/shard_map/ppermute | solution.py:535
  52.4 6.0 %collective-permute-start.12 = (bf16[256,128]{1,0:T(8,128)(2,1)S(1)}, bf16[256,128]{1,0:T(8,128)(2,1)S(1)}, u32[]{:S(2)}, u32[]{:S(2)}) collective-permute-start(bf16[256,128]{1,0:T(8,128)(2,1)S(1)} %get-tuple-element.66), channel_id=1, source_target_pairs={{0,5},{1,6},{2,7},{3,0},{4,1},{5,2},{6,3},{7,4},{8,13},{9,14},{10,... | collective-permute-start | bytes 196616 | tf_op jit(solution)/shard_map/ppermute | solution.py:535
  53.4 10.5 %collective-permute-start.13 = (bf16[256,128]{1,0:T(8,128)(2,1)S(1)}, bf16[256,128]{1,0:T(8,128)(2,1)S(1)}, u32[]{:S(2)}, u32[]{:S(2)}) collective-permute-start(bf16[256,128]{1,0:T(8,128)(2,1)S(1)} %get-tuple-element.67), channel_id=1, source_target_pairs={{0,4},{1,5},{2,6},{3,7},{4,0},{5,1},{6,2},{7,3},{8,12},{9,13},{10,... | collective-permute-start | bytes 196616 | tf_op jit(solution)/shard_map/ppermute | solution.py:535
  55.7 8.6 %collective-permute-start.14 = (bf16[256,128]{1,0:T(8,128)(2,1)S(1)}, bf16[256,128]{1,0:T(8,128)(2,1)S(1)}, u32[]{:S(2)}, u32[]{:S(2)}) collective-permute-start(bf16[256,128]{1,0:T(8,128)(2,1)S(1)} %get-tuple-element.68), channel_id=1, source_target_pairs={{0,3},{1,4},{2,5},{3,6},{4,7},{5,0},{6,1},{7,2},{8,11},{9,12},{10,... | collective-permute-start | bytes 196616 | tf_op jit(solution)/shard_map/ppermute | solution.py:535

commit v6 on v5

--- a/solution.py
+++ b/solution.py
@@ -18,7 +18,8 @@
 LATE = ((12, 3),)
 EARLY_PLANES = 11
 LATE_PLANES = 3
-SENT = (4, 3, 5, 2, 6, 1, 7, 0)
+FIRST_SENT = (4,)
+LAST_SENT = (3, 5, 2, 6, 1, 7)
 RETURNED = (1, 7, 6, 4, 2, 3, 5)
 UP_OFFSETS = 4
 DOWN_LIMIT = 62 * 1024 * 1024
@@ -41,85 +42,104 @@
     return jnp.dot(spread, widen, preferred_element_type=jnp.float32)
 
 
-def down_kernel(fine_hbm, mask_hbm, w_hbm, *refs):
-    outs = refs[:K]
-    fine_ref, mask_ref, w_ref, wide_ref, sems = refs[K:]
+def down_kernel(offsets, fine_hbm, mask_hbm, w_hbm, *refs):
+    count = len(offsets)
+    outs = refs[:count]
+    fine_ref, mask_ref, w_ref, wide_ref, sems = refs[count:]
     first = [
-        pltpu.make_async_copy(mask_hbm, mask_ref, sems.at[K]),
-        pltpu.make_async_copy(w_hbm, w_ref, sems.at[K + 1]),
+        pltpu.make_async_copy(mask_hbm, mask_ref, sems.at[count]),
+        pltpu.make_async_copy(w_hbm, w_ref, sems.at[count + 1]),
     ]
-    chunks = {
-        j: pltpu.make_async_copy(fine_hbm.at[pl.ds(j * CAP, CAP)], fine_ref.at[j], sems.at[j])
-        for j in SENT
-    }
-    for copy in first + list(chunks.values()):
+    chunks = [
+        pltpu.make_async_copy(fine_hbm.at[pl.ds(j * CAP, CAP)], fine_ref.at[k], sems.at[k])
+        for k, j in enumerate(offsets)
+    ]
+    for copy in first + chunks:
         copy.start()
     first[0].wait()
     rows = CAP * CELLS
-    for part in range(K // 2):
-        wide_ref[part * 2 * rows : (part + 1) * 2 * rows] = expand_mask(
-            mask_ref[part * 2 * CAP : (part + 1) * 2 * CAP]
+    for k, j in enumerate(offsets):
+        wide_ref[k * rows : (k + 1) * rows] = expand_mask(
+            mask_ref[j * CAP : (j + 1) * CAP]
         ).astype(jnp.bfloat16)
     first[1].wait()
-    for part in range(K // 2):
-        pair = SENT[2 * part : 2 * part + 2]
-        for j in pair:
-            chunks[j].wait()
+    for start in range(0, count, 2):
+        group = range(start, min(start + 2, count))
+        for k in group:
+            chunks[k].wait()
         x = [
-            fine_ref[j].reshape(rows, -1) * wide_ref[j * rows : (j + 1) * rows] for j in pair
+            fine_ref[k].reshape(rows, -1) * wide_ref[k * rows : (k + 1) * rows] for k in group
         ]
         y = jnp.dot(jnp.concatenate(x, axis=0), w_ref[...], preferred_element_type=jnp.float32)
         y = y.astype(jnp.bfloat16)
-        for k, j in enumerate(pair):
-            outs[j][...] = y[k * rows : (k + 1) * rows]
-
-
-def down_call(fine, mask, w):
-    bricks, cells, width = fine.shape
+        for part, k in enumerate(group):
+            outs[k][...] = y[part * rows : (part + 1) * rows]
+
+
+def down_call(fine, mask, w, offsets):
+    cells, width = fine.shape[1:]
     mid = w.shape[1]
+    count = len(offsets)
+    rows = count * CAP * cells
     hbm = pl.BlockSpec(memory_space=pltpu.HBM)
-    return pl.pallas_call(
-        down_kernel,
+    outs = pl.pallas_call(
+        functools.partial(down_kernel, offsets),
         in_specs=[hbm, hbm, hbm],
-        out_specs=[pl.BlockSpec(memory_space=pltpu.VMEM)] * K,
-        out_shape=[jax.ShapeDtypeStruct((CAP * cells, mid), jnp.bfloat16)] * K,
+        out_specs=[pl.BlockSpec(memory_space=pltpu.VMEM)] * count,
+        out_shape=[jax.ShapeDtypeStruct((CAP * cells, mid), jnp.bfloat16)] * count,
         scratch_shapes=[
-            pltpu.VMEM((K, CAP, cells, width), fine.dtype),
+            pltpu.VMEM((count, CAP, cells, width), fine.dtype),
             pltpu.VMEM(mask.shape, mask.dtype),
             pltpu.VMEM(w.shape, w.dtype),
-            pltpu.VMEM((bricks * cells, width), jnp.bfloat16),
-            pltpu.SemaphoreType.DMA((K + 2,)),
+            pltpu.VMEM((rows, width), jnp.bfloat16),
+            pltpu.SemaphoreType.DMA((count + 2,)),
         ],
         compiler_params=pltpu.CompilerParams(vmem_limit_bytes=DOWN_LIMIT),
+        cost_estimate=pl.CostEstimate(
+            flops=2 * rows * width * mid, bytes_accessed=rows * width * 2, transcendentals=0
+        ),
         name="down",
     )(fine, mask, w)
-
-
-def prepare_kernel(mask_ref, w1_ref, w2_ref, mask_out, wide1_ref, wide2_ref):
+    return dict(zip(offsets, outs))
+
+
+def prepare_kernel(
+    fine_ref, mask_ref, w_down_ref, w1_ref, w2_ref, own_ref, mask_out, wide1_ref, wide2_ref
+):
     gather_weights(w1_ref, wide1_ref)
     gather_weights(w2_ref, wide2_ref)
     step = 8
     for part in range(mask_ref.shape[0] // step):
         rows = slice(part * step * CELLS, (part + 1) * step * CELLS)
         mask_out[rows] = expand_mask(mask_ref[part * step : (part + 1) * step]).astype(jnp.bfloat16)
-
-
-def prepare_call(mask, w_first, w_second):
+    rows = CAP * CELLS
+    own = fine_ref[...].reshape(rows, -1) * mask_out[:rows]
+    own = jnp.dot(own, w_down_ref[...], preferred_element_type=jnp.float32)
+    own_ref[...] = own.astype(jnp.bfloat16)
+
+
+def prepare_call(fine, mask, w_down, w_first, w_second):
     mid = w_first.shape[1]
     vmem = pl.BlockSpec(memory_space=pltpu.VMEM)
     rows = mask.shape[0] * CELLS
     wide = jax.ShapeDtypeStruct((9 * mid, 3 * mid), jnp.bfloat16)
     return pl.pallas_call(
         prepare_kernel,
-        in_specs=[vmem] * 3,
-        out_specs=[vmem] * 3,
-        out_shape=[jax.ShapeDtypeStruct((rows, mask.shape[1]), jnp.bfloat16), wide, wide],
+        grid=(1,),
+        in_specs=[pl.BlockSpec((CAP,) + fine.shape[1:], lambda i: (0, 0, 0))] + [vmem] * 4,
+        out_specs=[vmem] * 4,
+        out_shape=[
+            jax.ShapeDtypeStruct((CAP * CELLS, mid), jnp.bfloat16),
+            jax.ShapeDtypeStruct((rows, mask.shape[1]), jnp.bfloat16),
+            wide,
+            wide,
+        ],
         compiler_params=pltpu.CompilerParams(vmem_limit_bytes=VMEM_LIMIT),
         cost_estimate=pl.CostEstimate(
             flops=2 * rows * mask.shape[1] * 128, bytes_accessed=rows * mask.shape[1] * 2, transcendentals=0
         ),
         name="prepare",
-    )(mask, w_first, w_second)
+    )(fine, mask, w_down, w_first, w_second)
 
 
 def up_kernel(fine_ref, mask_ref, w_ref, *refs):
@@ -193,8 +213,8 @@
     return jnp.where(value >= 0, brick, 0.0).reshape(8, 8, 128)
 
 
-def place_kernel(source_ref, *refs):
-    block_ref, low_ref, high_ref, arrived = refs[K:]
+def place_kernel(base_ref, source_ref, *refs):
+    block_ref, even_ref, odd_ref, low_ref, high_ref, arrived = refs[K:]
     for j in range(K):
         arrived[j * CAP * CELLS : (j + 1) * CAP * CELLS] = refs[j][...]
     half = low_half((8, 8, 128))
@@ -217,51 +237,89 @@
     for row_brick, ref in ((0, low_ref), (3, high_ref)):
         flags = [slot_flags(source_ref, slot_index(d, row_brick)) for d in range(4)]
         ref[256:288] = jnp.concatenate(flags, axis=0).astype(jnp.bfloat16)
-
-
-def place_call(source, arrived):
+    face_out(base_ref[0], low_ref, high_ref, even_ref, odd_ref)
+
+
+def face_out(index, low_ref, high_ref, even_ref, odd_ref):
+    is_even = index % 2 == 0
+    even_ref[...] = jnp.where(is_even, high_ref[...], low_ref[...])
+    odd_ref[...] = jnp.where(is_even, low_ref[...], high_ref[...])
+
+
+def face_in(index, count, even_ref, odd_ref, low_ref, high_ref):
+    is_even = index % 2 == 0
+    empty = jnp.zeros(low_ref.shape, low_ref.dtype)
+    low = jnp.where(is_even, odd_ref[...], even_ref[...])
+    high = jnp.where(is_even, even_ref[...], odd_ref[...])
+    low_ref[...] = jnp.where(index == 0, empty, low)
+    high_ref[...] = jnp.where(index == count - 1, empty, high)
+
+
+def place_call(base, source, arrived):
     mid = arrived[0].shape[1]
     smem = pl.BlockSpec(memory_space=pltpu.SMEM)
     vmem = pl.BlockSpec(memory_space=pltpu.VMEM)
     return pl.pallas_call(
         place_kernel,
-        in_specs=[smem] + [vmem] * K,
+        in_specs=[smem, smem] + [vmem] * K,
         out_specs=[vmem] * 3,
         out_shape=[
             jax.ShapeDtypeStruct((rows, mid), jnp.bfloat16)
             for rows in (SIDE * SIDE * COLS, 288, 288)
         ],
-        scratch_shapes=[pltpu.VMEM((K * CAP * CELLS, mid), jnp.bfloat16)],
+        scratch_shapes=[
+            pltpu.VMEM((288, mid), jnp.bfloat16),
+            pltpu.VMEM((288, mid), jnp.bfloat16),
+            pltpu.VMEM((K * CAP * CELLS, mid), jnp.bfloat16),
+        ],
         compiler_params=pltpu.CompilerParams(vmem_limit_bytes=VMEM_LIMIT),
         name="place",
-    )(source, *arrived)
-
-
-def edge_kernel(source_ref, block_ref, before_ref, after_ref, low_ref, high_ref):
+    )(base, source, *arrived)
+
+
+def edge_kernel(
+    counts,
+    base_ref,
+    source_ref,
+    block_ref,
+    even_ref,
+    odd_ref,
+    before_ref,
+    after_ref,
+    even_out,
+    odd_out,
+    low_ref,
+    high_ref,
+):
+    face_in(base_ref[0], counts[1], even_ref, odd_ref, before_ref, after_ref)
     for ref, planes, brick in ((low_ref, (0, 1), 0), (high_ref, (SIDE - 2, SIDE - 1), 3)):
         for k, plane in enumerate(planes):
             start = k * WIDE * COLS
             ref[start : start + 16] = before_ref[plane * 16 : plane * 16 + 16]
             ref[start + 16 : start + 144] = block_ref[plane * 128 : plane * 128 + 128]
             ref[start + 144 : start + 160] = after_ref[plane * 16 : plane * 16 + 16]
-        first = 256 + brick * 8
         flags = [before_ref[256:288].astype(jnp.float32)[brick * 8 : brick * 8 + 8]]
         flags += [slot_flags(source_ref, slot_index(brick, r)) for r in range(4)]
         flags += [after_ref[256:288].astype(jnp.float32)[brick * 8 : brick * 8 + 8]]
         ref[320:368] = jnp.concatenate(flags, axis=0).astype(jnp.bfloat16)
-
-
-def edge_call(source, block, before, after):
+    face_out(base_ref[1], low_ref, high_ref, even_out, odd_out)
+
+
+def edge_call(counts, base, source, block, even, odd):
     smem = pl.BlockSpec(memory_space=pltpu.SMEM)
     vmem = pl.BlockSpec(memory_space=pltpu.VMEM)
+    mid = block.shape[1]
     return pl.pallas_call(
-        edge_kernel,
-        in_specs=[smem, vmem, vmem, vmem],
-        out_specs=[vmem] * 2,
-        out_shape=[jax.ShapeDtypeStruct((368, block.shape[1]), jnp.bfloat16)] * 2,
+        functools.partial(edge_kernel, counts),
+        in_specs=[smem, smem, vmem, vmem, vmem],
+        out_specs=[vmem] * 4,
+        out_shape=[
+            jax.ShapeDtypeStruct((rows, mid), jnp.bfloat16) for rows in (288, 288, 368, 368)
+        ],
+        scratch_shapes=[pltpu.VMEM((368, mid), jnp.bfloat16)] * 2,
         compiler_params=pltpu.CompilerParams(vmem_limit_bytes=VMEM_LIMIT),
         name="edge",
-    )(source, block, before, after)
+    )(base, source, block, even, odd)
 
 
 def gather_weights(w_ref, wide_ref):
@@ -435,11 +493,12 @@
     )(source, block, before, after, wide1)
 
 
-def final_kernel(source_ref, *refs):
-    block_ref, before_ref, after_ref, under_ref, over_ref = refs[:5]
+def final_kernel(count, base_ref, source_ref, *refs):
+    block_ref, before_ref, after_ref, even_ref, odd_ref = refs[:5]
     early_ref, late_ref, side_ref, wide1_ref, wide2_ref, coarse_ref = refs[5:11]
     backs = refs[11 : 11 + K]
-    x_here, x_next, h_here, h_next, stage = refs[11 + K :]
+    x_here, x_next, h_here, h_next, stage, under_ref, over_ref = refs[11 + K :]
+    face_in(base_ref[1], count, even_ref, odd_ref, under_ref, over_ref)
     width = block_ref.shape[1]
     flags_before = as_rows(before_ref[256:288])
     flags_after = as_rows(after_ref[256:288])
@@ -504,13 +563,13 @@
         backs[j][...] = stage[j * CAP * CELLS : (j + 1) * CAP * CELLS]
 
 
-def final_call(source, block, halo, hidden, wide1, wide2):
+def final_call(count, base, source, block, halo, hidden, wide1, wide2):
     mid = block.shape[1]
     smem = pl.BlockSpec(memory_space=pltpu.SMEM)
     vmem = pl.BlockSpec(memory_space=pltpu.VMEM)
     return pl.pallas_call(
-        final_kernel,
-        in_specs=[smem] + [vmem] * 10,
+        functools.partial(final_kernel, count),
+        in_specs=[smem, smem] + [vmem] * 10,
         out_specs=[vmem] * (1 + K),
         out_shape=[
             jax.ShapeDtypeStruct(block.shape, jnp.bfloat16),
@@ -522,11 +581,13 @@
             pltpu.VMEM((HID, HID * COLS, mid), jnp.bfloat16),
             pltpu.VMEM((HID, HID * COLS, mid), jnp.bfloat16),
             pltpu.VMEM(((K * CAP + 1) * CELLS, mid), jnp.bfloat16),
+            pltpu.VMEM((368, mid), jnp.bfloat16),
+            pltpu.VMEM((368, mid), jnp.bfloat16),
         ],
         compiler_params=pltpu.CompilerParams(vmem_limit_bytes=VMEM_LIMIT),
         cost_estimate=conv_cost(SIDE * SIDE * COLS, mid),
         name="final",
-    )(source, block, *halo, *hidden, wide1, wide2)
+    )(base, source, block, *halo, *hidden, wide1, wide2)
 
 
 def from_behind(value, axis, steps):
@@ -535,30 +596,47 @@
     return lax.ppermute(value, axis, pairs)
 
 
-def neighbours(low, high, axis):
+def swap_faces(even, odd, axis):
     count = lax.axis_size(axis)
-    forward = [(i, i + 1) for i in range(count - 1)]
-    backward = [(target, source) for source, target in forward]
-    return lax.ppermute(high, axis, forward), lax.ppermute(low, axis, backward)
+    swapped = []
+    for face, first in ((even, 0), (odd, 1)):
+        partner = list(range(count))
+        for i in range(first, count - 1, 2):
+            partner[i], partner[i + 1] = i + 1, i
+        swapped.append(lax.ppermute(face, axis, list(enumerate(partner))))
+    return swapped
 
 
 def shards(fine, fine_mask, slot_source, w_down, w_first, w_second, w_up):
     mid = w_down.shape[1]
-    sent = down_call(fine, fine_mask, w_down)
-    arrived = {j: from_behind(sent[j], "xy", j) for j in SENT if j}
-    later_mask, own = lax.optimization_barrier((fine_mask, sent[0]))
-    mask, wide1, wide2 = prepare_call(later_mask, w_first, w_second)
-    own, mask, wide1, wide2 = lax.optimization_barrier((own, mask, wide1, wide2))
-    arrived[0] = own
-    block, low, high = place_call(slot_source, [arrived[j] for j in range(K)])
-    before, after = neighbours(low, high, "xy")
+    base = jnp.stack([lax.axis_index("xy"), lax.axis_index("gz")]).astype(jnp.int32)
+    counts = (lax.axis_size("gz"), lax.axis_size("xy"))
+    sent = down_call(fine, fine_mask, w_down, FIRST_SENT)
+    arrived = {j: from_behind(sent[j], "xy", j) for j in FIRST_SENT}
+    fine_again, sent[FIRST_SENT[0]] = lax.optimization_barrier((fine, sent[FIRST_SENT[0]]))
+    sent = down_call(fine_again, fine_mask, w_down, LAST_SENT)
+    arrived.update({j: from_behind(sent[j], "xy", j) for j in LAST_SENT})
+    middle = LAST_SENT[1]
+    later = (arrived[middle], fine, fine_mask, w_down, w_first, w_second)
+    arrived[middle], *later = lax.optimization_barrier(later)
+    prepared = lax.optimization_barrier(tuple(prepare_call(*later)))
+    arrived[0], mask, wide1, wide2 = prepared
+    block, even, odd = place_call(base, slot_source, [arrived[j] for j in range(K)])
+    even, odd = swap_faces(even, odd, "xy")
     early = inner_call(slot_source, block, wide1)
-    before, after, early = lax.optimization_barrier((before, after, early))
-    under_send, over_send = edge_call(slot_source, block, before, after)
-    under, over = neighbours(under_send, over_send, "gz")
+    even, odd, early = lax.optimization_barrier((even, odd, early))
+    before, after, even, odd = edge_call(counts, base, slot_source, block, even, odd)
+    even, odd = swap_faces(even, odd, "gz")
     side, late = side_call(slot_source, block, before, after, wide1)
     coarse, *back = final_call(
-        slot_source, block, (before, after, under, over), (early, late, side), wide1, wide2
+        counts[0],
+        base,
+        slot_source,
+        block,
+        (before, after, even, odd),
+        (early, late, side),
+        wide1,
+        wide2,
     )
     octant = {j: from_behind(back[j], "xy", -j) for j in RETURNED}
     octant[0] = back[0]

time: 66.4 us -> 61.4 us (0.925)
  waiting for transfers between devices: 12.7 us -> 8.86 us
  starting transfers between devices: 32.9 us -> 29.8 us
  Pallas kernels: 18.5 us -> 20 us
  local copies, waits for them, and re-layouts: 0.86 us -> 1.63 us
    ppermute x4, starting transfers between devices: 7.95 us -> 2.7 us  [swap_faces(): swapped.append(lax.ppermute(face, axis, list(enumerate(partner))))]
    ppermute x4, waiting for transfers between devices: 4.42 us -> 0.09 us  [swap_faces(): swapped.append(lax.ppermute(face, axis, list(enumerate(partner))))]
    ppermute x14, starting transfers between devices: 25 us -> 27.1 us  [from_behind(): return lax.ppermute(value, axis, pairs)]
    pallas_call x5 -> x6, Pallas kernels: 11.4 us -> 12.9 us  [the longest x2 5.31 us: down_call(): pl.pallas_call(functools.partial(down_kernel, offsets), in_specs=[hbm, hb...]
    unnamed x14 -> x16, local copies, waits for them, and re-layouts: 0.86 us -> 1.63 us
  transfers between devices with their start and end apart: 18 -> 18, of which waited for: 7 -> 5; matrix products, arithmetic and copies ran while one was open for 0% -> 0% of each run, Pallas kernels for 10% -> 16%
where the time goes in v6:
time: 61.4 us; the launch traced here: 61.2 us
  starting transfers between devices  29.8 us (49%)
  Pallas kernels  20 us (33%)
  waiting for transfers between devices  8.86 us (14%)
  local copies, waits for them, and re-layouts  1.63 us (3%)
  between operations  0.84 us (1%)
    ppermute x14, starting transfers between devices, from_behind(): return lax.ppermute(value, axis, pairs)  27.1 us
    ppermute x14, waiting for transfers between devices, from_behind(): return lax.ppermute(value, axis, pairs)  8.77 us
    pallas_call x2, Pallas kernels, down_call(): pl.pallas_call(functools.partial(down_kernel, offsets), in_specs=[hbm, hb...  5.31 us
    pallas_call x1, Pallas kernels, final_call(): pl.pallas_call(functools.partial(final_kernel, count), in_specs=[smem, sm...  5.07 us
    pallas_call x2, Pallas kernels, up_call(): pl.pallas_call(up_kernel, grid=(UP_OFFSETS * CAP // step,), in_specs=[pl....  3 us
    ppermute x4, starting transfers between devices, swap_faces(): swapped.append(lax.ppermute(face, axis, list(enumerate(partner))))  2.7 us
    pallas_call x1, Pallas kernels, inner_call(): pl.pallas_call(inner_kernel, in_specs=[smem, vmem, vmem], out_specs=vmem,...  2.36 us
    pallas_call x1, Pallas kernels, side_call(): pl.pallas_call(side_kernel, in_specs=[smem] + [vmem] * 4, out_specs=[vmem...  1.77 us
  transfers between devices with their start and end apart: 18, of which 5 were waited for; matrix products, arithmetic and copies ran while one was open for 0% of the time, Pallas kernels for 16%

profile of v6, /device:TPU:0, one launch (start us, length us, event | category | flops | bytes accessed | tf_op | source)
XLA Modules:
  0.0 61.2 jit_solution(3348322572988438)
XLA Ops:
  0.7 2.1 %down.2 = bf16[256,128]{1,0:T(8,128)(2,1)} custom-call(bf16[32,64,512]{2,1,0:T(8,128)(2,1)} %fine_ref.4, s32[32,512]{1,0:T(8,128)} %mask_ref, bf16[512,128]{1,0:T(8,128)(2,1)} %w_down_ref), custom_call_target="tpu_custom_call" | custom-call | flops 33554432 | bytes 262144 | tf_op jit(solution)/shard_map/down/pallas_call | solution.py:85
  2.7 4.1 %collective-permute-start.4 = (bf16[256,128]{1,0:T(8,128)(2,1)}, bf16[256,128]{1,0:T(8,128)(2,1)S(1)}, u32[]{:S(2)}, u32[]{:S(2)}) collective-permute-start(bf16[256,128]{1,0:T(8,128)(2,1)} %down.2), channel_id=1, source_target_pairs={{0,4},{1,5},{2,6},{3,7},{4,0},{5,1},{6,2},{7,3},{8,12},{9,13},{10,... | collective-permute-start | bytes 196616 | tf_op jit(solution)/shard_map/ppermute | solution.py:596
  6.8 3.3 %down.3 = (bf16[256,128]{1,0:T(8,128)(2,1)}, bf16[256,128]{1,0:T(8,128)(2,1)}, bf16[256,128]{1,0:T(8,128)(2,1)}, bf16[256,128]{1,0:T(8,128)(2,1)}, bf16[256,128]{1,0:T(8,128)(2,1)}, /*index=5*/bf16[256,128]{1,0:T(8,128)(2,1)}) custom-call(bf16[32,64,512]{2,1,0:T(8,128)(2,1)} %fine_ref.4, s32[32,512]{1,0:T(8,128)} %mask_ref, bf16[512,128]{1,0:T(8,128)(2,1)} %w_down_ref), custom_call_target="tpu_custom_call" | custom-call | flops 201326592 | bytes 1572864 | tf_op jit(solution)/shard_map/down/pallas_call | solution.py:85
  10.1 1.3 %collective-permute-start = (bf16[256,128]{1,0:T(8,128)(2,1)}, bf16[256,128]{1,0:T(8,128)(2,1)S(1)}, u32[]{:S(2)}, u32[]{:S(2)}) collective-permute-start(bf16[256,128]{1,0:T(8,128)(2,1)} %get-tuple-element.41), channel_id=1, source_target_pairs={{0,5},{1,6},{2,7},{3,0},{4,1},{5,2},{6,3},{7,4},{8,13},{9,14},{10,... | collective-permute-start | bytes 196616 | tf_op jit(solution)/shard_map/ppermute | solution.py:596
  11.4 1.5 %collective-permute-start.1 = (bf16[256,128]{1,0:T(8,128)(2,1)}, bf16[256,128]{1,0:T(8,128)(2,1)S(1)}, u32[]{:S(2)}, u32[]{:S(2)}) collective-permute-start(bf16[256,128]{1,0:T(8,128)(2,1)} %get-tuple-element.49), channel_id=1, source_target_pairs={{0,1},{1,2},{2,3},{3,4},{4,5},{5,6},{6,7},{7,0},{8,9},{9,10},{10,1... | collective-permute-start | bytes 196616 | tf_op jit(solution)/shard_map/ppermute | solution.py:596
  13.0 0.7 %collective-permute-start.2 = (bf16[256,128]{1,0:T(8,128)(2,1)}, bf16[256,128]{1,0:T(8,128)(2,1)S(1)}, u32[]{:S(2)}, u32[]{:S(2)}) collective-permute-start(bf16[256,128]{1,0:T(8,128)(2,1)} %get-tuple-element.50), channel_id=1, source_target_pairs={{0,2},{1,3},{2,4},{3,5},{4,6},{5,7},{6,0},{7,1},{8,10},{9,11},{10,... | collective-permute-start | bytes 196616 | tf_op jit(solution)/shard_map/ppermute | solution.py:596
  13.7 3.4 %collective-permute-start.3 = (bf16[256,128]{1,0:T(8,128)(2,1)}, bf16[256,128]{1,0:T(8,128)(2,1)S(1)}, u32[]{:S(2)}, u32[]{:S(2)}) collective-permute-start(bf16[256,128]{1,0:T(8,128)(2,1)} %get-tuple-element.51), channel_id=1, source_target_pairs={{0,3},{1,4},{2,5},{3,6},{4,7},{5,0},{6,1},{7,2},{8,11},{9,12},{10,... | collective-permute-start | bytes 196616 | tf_op jit(solution)/shard_map/ppermute | solution.py:596
  17.1 2.3 %collective-permute-start.5 = (bf16[256,128]{1,0:T(8,128)(2,1)}, bf16[256,128]{1,0:T(8,128)(2,1)S(1)}, u32[]{:S(2)}, u32[]{:S(2)}) collective-permute-start(bf16[256,128]{1,0:T(8,128)(2,1)} %get-tuple-element.53), channel_id=1, source_target_pairs={{0,6},{1,7},{2,0},{3,1},{4,2},{5,3},{6,4},{7,5},{8,14},{9,15},{10,... | collective-permute-start | bytes 196616 | tf_op jit(solution)/shard_map/ppermute | solution.py:596
  19.3 0.6 %collective-permute-start.6 = (bf16[256,128]{1,0:T(8,128)(2,1)}, bf16[256,128]{1,0:T(8,128)(2,1)S(1)}, u32[]{:S(2)}, u32[]{:S(2)}) collective-permute-start(bf16[256,128]{1,0:T(8,128)(2,1)} %get-tuple-element.54), channel_id=1, source_target_pairs={{0,7},{1,0},{2,1},{3,2},{4,3},{5,4},{6,5},{7,6},{8,15},{9,8},{10,9... | collective-permute-start | bytes 196616 | tf_op jit(solution)/shard_map/ppermute | solution.py:596
  20.1 1.6 %copy-done = bf16[32,64,512]{2,1,0:T(8,128)(2,1)S(1)} copy-done((bf16[32,64,512]{2,1,0:T(8,128)(2,1)S(1)}, bf16[32,64,512]{2,1,0:T(8,128)(2,1)}, u32[]{:S(2)}) %copy-start) | copy-done | bytes 2097176
  21.6 1.1 %prepare.1 = (bf16[256,128]{1,0:T(8,128)(2,1)S(1)}, bf16[2048,512]{1,0:T(8,128)(2,1)S(1)}, bf16[1152,384]{1,0:T(8,128)(2,1)S(1)}, bf16[1152,384]{1,0:T(8,128)(2,1)S(1)}) custom-call(bf16[32,64,512]{2,1,0:T(8,128)(2,1)S(1)} %copy-done, s32[32,512]{1,0:T(8,128)S(1)} %copy-done.5, bf16[512,128]{1,0:T(8,128)(2,1)S(1)} %copy-done.2, ...), custom_call_target="tpu_custom_call" | custom-call | flops 268435456 | bytes 2097152 | tf_op jit(solution)/shard_map/prepare/pallas_call | solution.py:126
  22.8 1.1 %collective-permute-done.6.refs_7_ = bf16[256,128]{1,0:T(8,128)(2,1)S(1)} collective-permute-done((bf16[256,128]{1,0:T(8,128)(2,1)}, bf16[256,128]{1,0:T(8,128)(2,1)S(1)}, u32[]{:S(2)}, u32[]{:S(2)}) %collective-permute-start.6) | collective-permute-done | bytes 65568 | tf_op jit(solution)/shard_map/ppermute | solution.py:596
  23.8 0.8 %place.1 = (bf16[2048,128]{1,0:T(8,128)(2,1)S(1)}, bf16[288,128]{1,0:T(8,128)(2,1)S(1)}, bf16[288,128]{1,0:T(8,128)(2,1)S(1)}) custom-call(s32[2]{0:T(128)S(1)} %pad_add_fusion.base_ref, s32[32]{0:T(128)S(1)} %copy-done.7, bf16[256,128]{1,0:T(8,128)(2,1)S(1)} %get-tuple-element.48.refs_0_, bf16[256,128]{1,0:T(8,128)(2,1)S(1)} %collective-permute-done.1.refs_1_, ...), custom_call_target="tpu_custom_call" | custom-call | tf_op jit(solution)/shard_map/place/pallas_call | solution.py:262
  24.6 1.3 %collective-permute-start.7 = (bf16[288,128]{1,0:T(8,128)(2,1)S(1)}, bf16[288,128]{1,0:T(8,128)(2,1)S(1)}, u32[]{:S(2)}, u32[]{:S(2)}) collective-permute-start(bf16[288,128]{1,0:T(8,128)(2,1)S(1)} %get-tuple-element.56), channel_id=1, source_target_pairs={{0,1},{1,0},{2,3},{3,2},{4,5},{5,4},{6,7},{7,6},{8,9},{9,8},{10,11... | collective-permute-start | bytes 221192 | tf_op jit(solution)/shard_map/ppermute | solution.py:606
  25.9 0.7 %collective-permute-start.8 = (bf16[288,128]{1,0:T(8,128)(2,1)S(1)}, bf16[288,128]{1,0:T(8,128)(2,1)S(1)}, u32[]{:S(2)}, u32[]{:S(2)}) collective-permute-start(bf16[288,128]{1,0:T(8,128)(2,1)S(1)} %get-tuple-element.57), channel_id=1, source_target_pairs={{0,0},{1,2},{2,1},{3,4},{4,3},{5,6},{6,5},{7,7},{8,8},{9,10},{10,9... | collective-permute-start | bytes 221192 | tf_op jit(solution)/shard_map/ppermute | solution.py:606
  26.5 2.4 %inner.1.refs_5_ = bf16[11,112,128]{2,1,0:T(8,128)(2,1)S(1)} custom-call(s32[32]{0:T(128)S(1)} %copy-done.7, bf16[2048,128]{1,0:T(8,128)(2,1)S(1)} %get-tuple-element.55.block_ref.refs_0_, bf16[1152,384]{1,0:T(8,128)(2,1)S(1)} %get-tuple-element.58.wide1_ref.refs_8_), custom_call_target="tpu_custom_call" | custom-call | flops 1089994752 | bytes 1769472 | tf_op jit(solution)/shard_map/inner/pallas_call | solution.py:416
  29.0 0.6 %edge.1 = (bf16[288,128]{1,0:T(8,128)(2,1)S(1)}, bf16[288,128]{1,0:T(8,128)(2,1)S(1)}, bf16[368,128]{1,0:T(8,128)(2,1)S(1)}, bf16[368,128]{1,0:T(8,128)(2,1)S(1)}) custom-call(s32[2]{0:T(128)S(1)} %pad_add_fusion.base_ref, s32[32]{0:T(128)S(1)} %copy-done.7, bf16[2048,128]{1,0:T(8,128)(2,1)S(1)} %get-tuple-element.55.block_ref.refs_0_, ...), custom_call_target="tpu_custom_call" | custom-call | tf_op jit(solution)/shard_map/edge/pallas_call | solution.py:312
  29.7 0.7 %collective-permute-start.10 = (bf16[368,128]{1,0:T(8,128)(2,1)S(1)}, bf16[368,128]{1,0:T(8,128)(2,1)S(1)}, u32[]{:S(2)}, u32[]{:S(2)}) collective-permute-start(bf16[368,128]{1,0:T(8,128)(2,1)S(1)} %get-tuple-element.64), channel_id=1, source_target_pairs={{0,0},{8,16},{16,8},{24,24},{1,1},{9,17},{17,9},{25,25},{2,2},{10,... | collective-permute-start | bytes 282632 | tf_op jit(solution)/shard_map/ppermute | solution.py:606
  30.4 1.8 %side.1 = (bf16[2,14,16,128]{3,2,1,0:T(8,128)(2,1)S(1)}, bf16[3,112,128]{2,1,0:T(8,128)(2,1)S(1)}) custom-call(s32[32]{0:T(128)S(1)} %copy-done.7, bf16[2048,128]{1,0:T(8,128)(2,1)S(1)} %get-tuple-element.55.block_ref.refs_0_, bf16[288,128]{1,0:T(8,128)(2,1)S(1)} %get-tuple-element.61.before_ref.refs_1_, ...), custom_call_target="tpu_custom_call" | custom-call | flops 693633024 | bytes 1769472 | tf_op jit(solution)/shard_map/side/pallas_call | solution.py:477
  32.2 5.1 %final.1 = (bf16[2048,128]{1,0:T(8,128)(2,1)}, bf16[256,128]{1,0:T(8,128)(2,1)S(1)}, bf16[256,128]{1,0:T(8,128)(2,1)S(1)}, bf16[256,128]{1,0:T(8,128)(2,1)S(1)},...) custom-call(s32[2]{0:T(128)S(1)} %pad_add_fusion.base_ref, ...), custom_call_target="tpu_custom_call" | custom-call | flops 1811939328 | bytes 1769472 | tf_op jit(solution)/shard_map/final/pallas_call | solution.py:570
  37.3 4.5 %collective-permute-start.15 = (bf16[256,128]{1,0:T(8,128)(2,1)S(1)}, bf16[256,128]{1,0:T(8,128)(2,1)S(1)}, u32[]{:S(2)}, u32[]{:S(2)}) collective-permute-start(bf16[256,128]{1,0:T(8,128)(2,1)S(1)} %get-tuple-element.73), channel_id=1, source_target_pairs={{0,2},{1,3},{2,4},{3,5},{4,6},{5,7},{6,0},{7,1},{8,10},{9,11},{10,... | collective-permute-start | bytes 196616 | tf_op jit(solution)/shard_map/ppermute | solution.py:596
  41.8 0.4 collective-permute-start.16
  42.2 4.3 %collective-permute-start.17 = (bf16[256,128]{1,0:T(8,128)(2,1)S(1)}, bf16[256,128]{1,0:T(8,128)(2,1)S(1)}, u32[]{:S(2)}, u32[]{:S(2)}) collective-permute-start(bf16[256,128]{1,0:T(8,128)(2,1)S(1)} %get-tuple-element.76), channel_id=1, source_target_pairs={{0,7},{1,0},{2,1},{3,2},{4,3},{5,4},{6,5},{7,6},{8,15},{9,8},{10,9... | collective-permute-start | bytes 196616 | tf_op jit(solution)/shard_map/ppermute | solution.py:596
  46.5 0.4 collective-permute-start.11
  47.0 0.6 collective-permute-start.12
  47.5 2.8 %collective-permute-start.13 = (bf16[256,128]{1,0:T(8,128)(2,1)S(1)}, bf16[256,128]{1,0:T(8,128)(2,1)S(1)}, u32[]{:S(2)}, u32[]{:S(2)}) collective-permute-start(bf16[256,128]{1,0:T(8,128)(2,1)S(1)} %get-tuple-element.71), channel_id=1, source_target_pairs={{0,4},{1,5},{2,6},{3,7},{4,0},{5,1},{6,2},{7,3},{8,12},{9,13},{10,... | collective-permute-start | bytes 196616 | tf_op jit(solution)/shard_map/ppermute | solution.py:596
  50.3 0.1 collective-permute-start.14
  50.5 1.5 %up.2.refs_4_ = bf16[32,64,512]{2,1,0:T(8,128)(2,1)} custom-call(bf16[32,64,512]{2,1,0:T(8,128)(2,1)S(1)} %copy-done.1, bf16[2048,512]{1,0:T(8,128)(2,1)S(1)} %get-tuple-element.47.mask_ref, bf16[128,512]{1,0:T(8,128)(2,1)S(1)} %copy-done.6, bf16[256,128]{1,0:T(8,128)(2,1)S(1)} %collective-permute-done.15.refs_0_, ...), custom_call_target="tpu_custom_call" | custom-call | flops 134217728 | bytes 2097152 | tf_op jit(solution)/shard_map/up/pallas_call | solution.py:173
  52.0 0.6 %collective-permute-done.12.refs_1_ = bf16[256,128]{1,0:T(8,128)(2,1)S(1)} collective-permute-done((bf16[256,128]{1,0:T(8,128)(2,1)S(1)}, bf16[256,128]{1,0:T(8,128)(2,1)S(1)}, u32[]{:S(2)}, u32[]{:S(2)}) %collective-permute-start.12) | collective-permute-done | bytes 65568 | tf_op jit(solution)/shard_map/ppermute | solution.py:596
  52.6 6.0 %collective-permute-done.13.refs_2_ = bf16[256,128]{1,0:T(8,128)(2,1)S(1)} collective-permute-done((bf16[256,128]{1,0:T(8,128)(2,1)S(1)}, bf16[256,128]{1,0:T(8,128)(2,1)S(1)}, u32[]{:S(2)}, u32[]{:S(2)}) %collective-permute-start.13) | collective-permute-done | bytes 65568 | tf_op jit(solution)/shard_map/ppermute | solution.py:596
  58.6 1.0 %collective-permute-done.14.refs_3_ = bf16[256,128]{1,0:T(8,128)(2,1)S(1)} collective-permute-done((bf16[256,128]{1,0:T(8,128)(2,1)S(1)}, bf16[256,128]{1,0:T(8,128)(2,1)S(1)}, u32[]{:S(2)}, u32[]{:S(2)}) %collective-permute-start.14) | collective-permute-done | bytes 65568 | tf_op jit(solution)/shard_map/ppermute | solution.py:596
  59.7 1.5 %up.3 = bf16[32,64,512]{2,1,0:T(8,128)(2,1)} custom-call(bf16[32,64,512]{2,1,0:T(8,128)(2,1)S(1)} %copy-done.1, bf16[2048,512]{1,0:T(8,128)(2,1)S(1)} %get-tuple-element.47.mask_ref, bf16[128,512]{1,0:T(8,128)(2,1)S(1)} %copy-done.6, bf16[256,128]{1,0:T(8,128)(2,1)S(1)} %collective-permute-done.11.refs_0_, ...), custom_call_target="tpu_custom_call", output_to_operand_aliasing={{}: (7, {})} | custom-call | flops 134217728 | bytes 2097152 | tf_op jit(solution)/shard_map/up/pallas_call | solution.py:173
  (31 shorter events, 0.3 us)
Async XLA Ops:
  0.6 19.4 %copy-start.2 = (bf16[512,128]{1,0:T(8,128)(2,1)S(1)}, bf16[512,128]{1,0:T(8,128)(2,1)}, u32[]{:S(2)}) copy-start(bf16[512,128]{1,0:T(8,128)(2,1)} %w_down_ref) | copy-start | bytes 393220
  0.6 19.4 %copy-start.5 = (s32[32,512]{1,0:T(8,128)S(1)}, s32[32,512]{1,0:T(8,128)}, u32[]{:S(2)}) copy-start(s32[32,512]{1,0:T(8,128)} %mask_ref) | copy-start | bytes 196612
  0.7 19.4 %copy-start.4 = (bf16[27,128,128]{2,1,0:T(8,128)(2,1)S(1)}, bf16[27,128,128]{2,1,0:T(8,128)(2,1)}, u32[]{:S(2)}) copy-start(bf16[27,128,128]{2,1,0:T(8,128)(2,1)} %w2_ref) | copy-start | bytes 2654212
  0.7 19.4 %copy-start.3 = (bf16[27,128,128]{2,1,0:T(8,128)(2,1)S(1)}, bf16[27,128,128]{2,1,0:T(8,128)(2,1)}, u32[]{:S(2)}) copy-start(bf16[27,128,128]{2,1,0:T(8,128)(2,1)} %w1_ref) | copy-start | bytes 2654212
  2.7 14.3 %collective-permute-start.4 = (bf16[256,128]{1,0:T(8,128)(2,1)}, bf16[256,128]{1,0:T(8,128)(2,1)S(1)}, u32[]{:S(2)}, u32[]{:S(2)}) collective-permute-start(bf16[256,128]{1,0:T(8,128)(2,1)} %down.2), channel_id=1, source_target_pairs={{0,4},{1,5},{2,6},{3,7},{4,0},{5,1},{6,2},{7,3},{8,12},{9,13},{10,... | collective-permute-start | bytes 196616 | tf_op jit(solution)/shard_map/ppermute | solution.py:596
  10.1 13.7 %copy-start.7 = (s32[32]{0:T(128)S(1)}, s32[32]{0:T(128)}, u32[]{:S(2)}) copy-start(s32[32]{0:T(128)} %source_ref.9) | copy-start | bytes 388
  10.1 9.2 %collective-permute-start = (bf16[256,128]{1,0:T(8,128)(2,1)}, bf16[256,128]{1,0:T(8,128)(2,1)S(1)}, u32[]{:S(2)}, u32[]{:S(2)}) collective-permute-start(bf16[256,128]{1,0:T(8,128)(2,1)} %get-tuple-element.41), channel_id=1, source_target_pairs={{0,5},{1,6},{2,7},{3,0},{4,1},{5,2},{6,3},{7,4},{8,13},{9,14},{10,... | collective-permute-start | bytes 196616 | tf_op jit(solution)/shard_map/ppermute | solution.py:596
  11.4 11.3 %collective-permute-start.1 = (bf16[256,128]{1,0:T(8,128)(2,1)}, bf16[256,128]{1,0:T(8,128)(2,1)S(1)}, u32[]{:S(2)}, u32[]{:S(2)}) collective-permute-start(bf16[256,128]{1,0:T(8,128)(2,1)} %get-tuple-element.49), channel_id=1, source_target_pairs={{0,1},{1,2},{2,3},{3,4},{4,5},{5,6},{6,7},{7,0},{8,9},{9,10},{10,1... | collective-permute-start | bytes 196616 | tf_op jit(solution)/shard_map/ppermute | solution.py:596
  13.0 9.7 %collective-permute-start.2 = (bf16[256,128]{1,0:T(8,128)(2,1)}, bf16[256,128]{1,0:T(8,128)(2,1)S(1)}, u32[]{:S(2)}, u32[]{:S(2)}) collective-permute-start(bf16[256,128]{1,0:T(8,128)(2,1)} %get-tuple-element.50), channel_id=1, source_target_pairs={{0,2},{1,3},{2,4},{3,5},{4,6},{5,7},{6,0},{7,1},{8,10},{9,11},{10,... | collective-permute-start | bytes 196616 | tf_op jit(solution)/shard_map/ppermute | solution.py:596
  13.7 9.1 %collective-permute-start.3 = (bf16[256,128]{1,0:T(8,128)(2,1)}, bf16[256,128]{1,0:T(8,128)(2,1)S(1)}, u32[]{:S(2)}, u32[]{:S(2)}) collective-permute-start(bf16[256,128]{1,0:T(8,128)(2,1)} %get-tuple-element.51), channel_id=1, source_target_pairs={{0,3},{1,4},{2,5},{3,6},{4,7},{5,0},{6,1},{7,2},{8,11},{9,12},{10,... | collective-permute-start | bytes 196616 | tf_op jit(solution)/shard_map/ppermute | solution.py:596
  17.1 5.7 %collective-permute-start.5 = (bf16[256,128]{1,0:T(8,128)(2,1)}, bf16[256,128]{1,0:T(8,128)(2,1)S(1)}, u32[]{:S(2)}, u32[]{:S(2)}) collective-permute-start(bf16[256,128]{1,0:T(8,128)(2,1)} %get-tuple-element.53), channel_id=1, source_target_pairs={{0,6},{1,7},{2,0},{3,1},{4,2},{5,3},{6,4},{7,5},{8,14},{9,15},{10,... | collective-permute-start | bytes 196616 | tf_op jit(solution)/shard_map/ppermute | solution.py:596
  19.3 4.5 %collective-permute-start.6 = (bf16[256,128]{1,0:T(8,128)(2,1)}, bf16[256,128]{1,0:T(8,128)(2,1)S(1)}, u32[]{:S(2)}, u32[]{:S(2)}) collective-permute-start(bf16[256,128]{1,0:T(8,128)(2,1)} %get-tuple-element.54), channel_id=1, source_target_pairs={{0,7},{1,0},{2,1},{3,2},{4,3},{5,4},{6,5},{7,6},{8,15},{9,8},{10,9... | collective-permute-start | bytes 196616 | tf_op jit(solution)/shard_map/ppermute | solution.py:596
  20.0 1.6 %copy-start = (bf16[32,64,512]{2,1,0:T(8,128)(2,1)S(1)}, bf16[32,64,512]{2,1,0:T(8,128)(2,1)}, u32[]{:S(2)}) copy-start(bf16[32,64,512]{2,1,0:T(8,128)(2,1)} %fine_ref.4) | copy-start | bytes 6291460
  24.6 4.4 %collective-permute-start.7 = (bf16[288,128]{1,0:T(8,128)(2,1)S(1)}, bf16[288,128]{1,0:T(8,128)(2,1)S(1)}, u32[]{:S(2)}, u32[]{:S(2)}) collective-permute-start(bf16[288,128]{1,0:T(8,128)(2,1)S(1)} %get-tuple-element.56), channel_id=1, source_target_pairs={{0,1},{1,0},{2,3},{3,2},{4,5},{5,4},{6,7},{7,6},{8,9},{9,8},{10,11... | collective-permute-start | bytes 221192 | tf_op jit(solution)/shard_map/ppermute | solution.py:606
  25.9 3.1 %collective-permute-start.8 = (bf16[288,128]{1,0:T(8,128)(2,1)S(1)}, bf16[288,128]{1,0:T(8,128)(2,1)S(1)}, u32[]{:S(2)}, u32[]{:S(2)}) collective-permute-start(bf16[288,128]{1,0:T(8,128)(2,1)S(1)} %get-tuple-element.57), channel_id=1, source_target_pairs={{0,0},{1,2},{2,1},{3,4},{4,3},{5,6},{6,5},{7,7},{8,8},{9,10},{10,9... | collective-permute-start | bytes 221192 | tf_op jit(solution)/shard_map/ppermute | solution.py:606
  29.7 2.5 %collective-permute-start.9 = (bf16[368,128]{1,0:T(8,128)(2,1)S(1)}, bf16[368,128]{1,0:T(8,128)(2,1)S(1)}, u32[]{:S(2)}, u32[]{:S(2)}) collective-permute-start(bf16[368,128]{1,0:T(8,128)(2,1)S(1)} %get-tuple-element.63), channel_id=1, source_target_pairs={{0,8},{8,0},{16,24},{24,16},{1,9},{9,1},{17,25},{25,17},{2,10},{10... | collective-permute-start | bytes 282632 | tf_op jit(solution)/shard_map/ppermute | solution.py:606
  29.7 2.5 %collective-permute-start.10 = (bf16[368,128]{1,0:T(8,128)(2,1)S(1)}, bf16[368,128]{1,0:T(8,128)(2,1)S(1)}, u32[]{:S(2)}, u32[]{:S(2)}) collective-permute-start(bf16[368,128]{1,0:T(8,128)(2,1)S(1)} %get-tuple-element.64), channel_id=1, source_target_pairs={{0,0},{8,16},{16,8},{24,24},{1,1},{9,17},{17,9},{25,25},{2,2},{10,... | collective-permute-start | bytes 282632 | tf_op jit(solution)/shard_map/ppermute | solution.py:606
  32.2 18.3 %copy-start.1 = (bf16[32,64,512]{2,1,0:T(8,128)(2,1)S(1)}, bf16[32,64,512]{2,1,0:T(8,128)(2,1)}, u32[]{:S(2)}) copy-start(bf16[32,64,512]{2,1,0:T(8,128)(2,1)} %fine_ref.4) | copy-start | bytes 6291460
  32.2 18.2 %copy-start.6 = (bf16[128,512]{1,0:T(8,128)(2,1)S(1)}, bf16[128,512]{1,0:T(8,128)(2,1)}, u32[]{:S(2)}) copy-start(bf16[128,512]{1,0:T(8,128)(2,1)} %w_ref.3) | copy-start | bytes 393220
  37.3 10.2 %collective-permute-start.15 = (bf16[256,128]{1,0:T(8,128)(2,1)S(1)}, bf16[256,128]{1,0:T(8,128)(2,1)S(1)}, u32[]{:S(2)}, u32[]{:S(2)}) collective-permute-start(bf16[256,128]{1,0:T(8,128)(2,1)S(1)} %get-tuple-element.73), channel_id=1, source_target_pairs={{0,2},{1,3},{2,4},{3,5},{4,6},{5,7},{6,0},{7,1},{8,10},{9,11},{10,... | collective-permute-start | bytes 196616 | tf_op jit(solution)/shard_map/ppermute | solution.py:596
  41.8 8.5 %collective-permute-start.16 = (bf16[256,128]{1,0:T(8,128)(2,1)S(1)}, bf16[256,128]{1,0:T(8,128)(2,1)S(1)}, u32[]{:S(2)}, u32[]{:S(2)}) collective-permute-start(bf16[256,128]{1,0:T(8,128)(2,1)S(1)} %get-tuple-element.74), channel_id=1, source_target_pairs={{0,1},{1,2},{2,3},{3,4},{4,5},{5,6},{6,7},{7,0},{8,9},{9,10},{10,1... | collective-permute-start | bytes 196616 | tf_op jit(solution)/shard_map/ppermute | solution.py:596
  42.2 8.2 %collective-permute-start.17 = (bf16[256,128]{1,0:T(8,128)(2,1)S(1)}, bf16[256,128]{1,0:T(8,128)(2,1)S(1)}, u32[]{:S(2)}, u32[]{:S(2)}) collective-permute-start(bf16[256,128]{1,0:T(8,128)(2,1)S(1)} %get-tuple-element.76), channel_id=1, source_target_pairs={{0,7},{1,0},{2,1},{3,2},{4,3},{5,4},{6,5},{7,6},{8,15},{9,8},{10,9... | collective-permute-start | bytes 196616 | tf_op jit(solution)/shard_map/ppermute | solution.py:596
  46.5 5.5 %collective-permute-start.11 = (bf16[256,128]{1,0:T(8,128)(2,1)S(1)}, bf16[256,128]{1,0:T(8,128)(2,1)S(1)}, u32[]{:S(2)}, u32[]{:S(2)}) collective-permute-start(bf16[256,128]{1,0:T(8,128)(2,1)S(1)} %get-tuple-element.69), channel_id=1, source_target_pairs={{0,6},{1,7},{2,0},{3,1},{4,2},{5,3},{6,4},{7,5},{8,14},{9,15},{10,... | collective-permute-start | bytes 196616 | tf_op jit(solution)/shard_map/ppermute | solution.py:596
  47.0 5.6 %collective-permute-start.12 = (bf16[256,128]{1,0:T(8,128)(2,1)S(1)}, bf16[256,128]{1,0:T(8,128)(2,1)S(1)}, u32[]{:S(2)}, u32[]{:S(2)}) collective-permute-start(bf16[256,128]{1,0:T(8,128)(2,1)S(1)} %get-tuple-element.70), channel_id=1, source_target_pairs={{0,5},{1,6},{2,7},{3,0},{4,1},{5,2},{6,3},{7,4},{8,13},{9,14},{10,... | collective-permute-start | bytes 196616 | tf_op jit(solution)/shard_map/ppermute | solution.py:596
  47.5 11.1 %collective-permute-start.13 = (bf16[256,128]{1,0:T(8,128)(2,1)S(1)}, bf16[256,128]{1,0:T(8,128)(2,1)S(1)}, u32[]{:S(2)}, u32[]{:S(2)}) collective-permute-start(bf16[256,128]{1,0:T(8,128)(2,1)S(1)} %get-tuple-element.71), channel_id=1, source_target_pairs={{0,4},{1,5},{2,6},{3,7},{4,0},{5,1},{6,2},{7,3},{8,12},{9,13},{10,... | collective-permute-start | bytes 196616 | tf_op jit(solution)/shard_map/ppermute | solution.py:596
  50.3 9.4 %collective-permute-start.14 = (bf16[256,128]{1,0:T(8,128)(2,1)S(1)}, bf16[256,128]{1,0:T(8,128)(2,1)S(1)}, u32[]{:S(2)}, u32[]{:S(2)}) collective-permute-start(bf16[256,128]{1,0:T(8,128)(2,1)S(1)} %get-tuple-element.72), channel_id=1, source_target_pairs={{0,3},{1,4},{2,5},{3,6},{4,7},{5,0},{6,1},{7,2},{8,11},{9,12},{10,... | collective-permute-start | bytes 196616 | tf_op jit(solution)/shard_map/ppermute | solution.py:596

commit v7 on v6

--- a/solution.py
+++ b/solution.py
@@ -18,10 +18,8 @@
 LATE = ((12, 3),)
 EARLY_PLANES = 11
 LATE_PLANES = 3
-FIRST_SENT = (4,)
-LAST_SENT = (3, 5, 2, 6, 1, 7)
-RETURNED = (1, 7, 6, 4, 2, 3, 5)
-UP_OFFSETS = 4
+SENT = (4, 3, 5, 2, 6, 1, 7)
+UP_GROUPS = ((3, 4, 5, 0), (6, 7, 1, 2))
 DOWN_LIMIT = 62 * 1024 * 1024
 VMEM_LIMIT = 24 * 1024 * 1024
 
@@ -146,46 +144,46 @@
     out_ref = refs[-1]
     step = pl.program_id(0)
     bricks, cells, width = fine_ref.shape
-    count = bricks // CAP
-    steps = UP_OFFSETS // count
-    for part in range(count):
-        octant = refs[part][...]
-        for other in range(1, steps):
-            octant = jnp.where(step == other, refs[other * count + part][...], octant)
-        rows = slice(part * CAP * cells, (part + 1) * CAP * cells)
-        up = jnp.dot(octant, w_ref[...], preferred_element_type=jnp.float32)
-        fine = fine_ref[part * CAP : (part + 1) * CAP].reshape(CAP * cells, width)
-        mask = mask_ref[rows].astype(jnp.float32)
-        out = jnp.where(mask > 0.5, fine.astype(jnp.float32) + up, 0.0)
-        out_ref[part * CAP : (part + 1) * CAP] = out.astype(jnp.bfloat16).reshape(CAP, cells, width)
-
-
-def up_call(fine, mask, w, octants, first, partial):
+    octant = refs[0][...]
+    for other in range(1, len(UP_GROUPS[0])):
+        octant = jnp.where(step == other, refs[other][...], octant)
+    up = jnp.dot(octant, w_ref[...], preferred_element_type=jnp.float32)
+    fine = fine_ref[...].reshape(bricks * cells, width)
+    mask = mask_ref[...].astype(jnp.float32)
+    out = jnp.where(mask > 0.5, fine.astype(jnp.float32) + up, 0.0)
+    out_ref[...] = out.astype(jnp.bfloat16).reshape(bricks, cells, width)
+
+
+def up_call(fine, mask, w, octants, offsets, partial):
     bricks, cells, width = fine.shape
     mid = w.shape[0]
-    step = 8
-    blocks = bricks // step
+    count = len(offsets)
 
     def place(i):
-        return (first + i) % blocks
+        index = offsets[0]
+        for k in range(1, count):
+            index = jnp.where(i == k, offsets[k], index)
+        return index
 
     partials = [] if partial is None else [partial]
     return pl.pallas_call(
         up_kernel,
-        grid=(UP_OFFSETS * CAP // step,),
+        grid=(count,),
         in_specs=[
-            pl.BlockSpec((step, cells, width), lambda i: (place(i), 0, 0)),
-            pl.BlockSpec((step * cells, width), lambda i: (place(i), 0)),
+            pl.BlockSpec((CAP, cells, width), lambda i: (place(i), 0, 0)),
+            pl.BlockSpec((CAP * cells, width), lambda i: (place(i), 0)),
             pl.BlockSpec((mid, width), lambda i: (0, 0)),
         ]
-        + [pl.BlockSpec((CAP * cells, mid), lambda i: (0, 0))] * UP_OFFSETS
+        + [pl.BlockSpec((CAP * cells, mid), lambda i: (0, 0))] * count
         + [pl.BlockSpec(memory_space=pl.ANY)] * len(partials),
-        out_specs=pl.BlockSpec((step, cells, width), lambda i: (place(i), 0, 0)),
+        out_specs=pl.BlockSpec((CAP, cells, width), lambda i: (place(i), 0, 0)),
         out_shape=jax.ShapeDtypeStruct(fine.shape, jnp.bfloat16),
-        input_output_aliases={3 + UP_OFFSETS: 0} if partials else {},
+        input_output_aliases={3 + count: 0} if partials else {},
         compiler_params=pltpu.CompilerParams(vmem_limit_bytes=VMEM_LIMIT),
         cost_estimate=pl.CostEstimate(
-            flops=bricks * cells * width * mid, bytes_accessed=bricks * cells * width * 2, transcendentals=0
+            flops=2 * count * CAP * cells * width * mid,
+            bytes_accessed=count * CAP * cells * width * 4,
+            transcendentals=0,
         ),
         name="up",
     )(fine, mask, w, *octants, *partials)
@@ -214,7 +212,8 @@
 
 
 def place_kernel(base_ref, source_ref, *refs):
-    block_ref, even_ref, odd_ref, low_ref, high_ref, arrived = refs[K:]
+    block_ref, even_ref, odd_ref, gz_even_ref, gz_odd_ref = refs[K : K + 5]
+    low_ref, high_ref, under_ref, over_ref, arrived = refs[K + 5 :]
     for j in range(K):
         arrived[j * CAP * CELLS : (j + 1) * CAP * CELLS] = refs[j][...]
     half = low_half((8, 8, 128))
@@ -238,6 +237,12 @@
         flags = [slot_flags(source_ref, slot_index(d, row_brick)) for d in range(4)]
         ref[256:288] = jnp.concatenate(flags, axis=0).astype(jnp.bfloat16)
     face_out(base_ref[0], low_ref, high_ref, even_ref, odd_ref)
+    for depth_brick, ref in ((0, under_ref), (3, over_ref)):
+        first = 0 if depth_brick == 0 else (SIDE - 2) * 128
+        ref[0:256] = block_ref[first : first + 256]
+        flags = [slot_flags(source_ref, slot_index(depth_brick, r)) for r in range(4)]
+        ref[256:288] = jnp.concatenate(flags, axis=0).astype(jnp.bfloat16)
+    face_out(base_ref[1], under_ref, over_ref, gz_even_ref, gz_odd_ref)
 
 
 def face_out(index, low_ref, high_ref, even_ref, odd_ref):
@@ -262,14 +267,16 @@
     return pl.pallas_call(
         place_kernel,
         in_specs=[smem, smem] + [vmem] * K,
-        out_specs=[vmem] * 3,
+        out_specs=[vmem] * 5,
         out_shape=[
             jax.ShapeDtypeStruct((rows, mid), jnp.bfloat16)
-            for rows in (SIDE * SIDE * COLS, 288, 288)
+            for rows in (SIDE * SIDE * COLS, 288, 288, 288, 288)
         ],
         scratch_shapes=[
             pltpu.VMEM((288, mid), jnp.bfloat16),
             pltpu.VMEM((288, mid), jnp.bfloat16),
+            pltpu.VMEM((288, mid), jnp.bfloat16),
+            pltpu.VMEM((288, mid), jnp.bfloat16),
             pltpu.VMEM((K * CAP * CELLS, mid), jnp.bfloat16),
         ],
         compiler_params=pltpu.CompilerParams(vmem_limit_bytes=VMEM_LIMIT),
@@ -277,49 +284,35 @@
     )(base, source, *arrived)
 
 
-def edge_kernel(
-    counts,
-    base_ref,
-    source_ref,
-    block_ref,
-    even_ref,
-    odd_ref,
-    before_ref,
-    after_ref,
-    even_out,
-    odd_out,
-    low_ref,
-    high_ref,
-):
-    face_in(base_ref[0], counts[1], even_ref, odd_ref, before_ref, after_ref)
-    for ref, planes, brick in ((low_ref, (0, 1), 0), (high_ref, (SIDE - 2, SIDE - 1), 3)):
-        for k, plane in enumerate(planes):
-            start = k * WIDE * COLS
-            ref[start : start + 16] = before_ref[plane * 16 : plane * 16 + 16]
-            ref[start + 16 : start + 144] = block_ref[plane * 128 : plane * 128 + 128]
-            ref[start + 144 : start + 160] = after_ref[plane * 16 : plane * 16 + 16]
-        flags = [before_ref[256:288].astype(jnp.float32)[brick * 8 : brick * 8 + 8]]
-        flags += [slot_flags(source_ref, slot_index(brick, r)) for r in range(4)]
-        flags += [after_ref[256:288].astype(jnp.float32)[brick * 8 : brick * 8 + 8]]
-        ref[320:368] = jnp.concatenate(flags, axis=0).astype(jnp.bfloat16)
+def corner_kernel(counts, base_ref, *refs):
+    faces = refs[:4]
+    before_ref, after_ref, under_ref, over_ref, even_out, odd_out, low_ref, high_ref = refs[4:]
+    face_in(base_ref[0], counts[1], faces[0], faces[1], before_ref, after_ref)
+    face_in(base_ref[1], counts[0], faces[2], faces[3], under_ref, over_ref)
+    flags_before = as_rows(before_ref[256:288])
+    flags_after = as_rows(after_ref[256:288])
+    for ref, first, brick in ((low_ref, 0, 0), (high_ref, (SIDE - 2) * 16, 3)):
+        ref[0:32] = before_ref[first : first + 32]
+        ref[32:64] = after_ref[first : first + 32]
+        ref[64:80] = as_tiles(jnp.stack([flags_before[brick], flags_after[brick]], axis=0))
     face_out(base_ref[1], low_ref, high_ref, even_out, odd_out)
 
 
-def edge_call(counts, base, source, block, even, odd):
+def corner_call(counts, base, faces):
     smem = pl.BlockSpec(memory_space=pltpu.SMEM)
     vmem = pl.BlockSpec(memory_space=pltpu.VMEM)
-    mid = block.shape[1]
+    mid = faces[0].shape[1]
     return pl.pallas_call(
-        functools.partial(edge_kernel, counts),
-        in_specs=[smem, smem, vmem, vmem, vmem],
-        out_specs=[vmem] * 4,
+        functools.partial(corner_kernel, counts),
+        in_specs=[smem] + [vmem] * 4,
+        out_specs=[vmem] * 6,
         out_shape=[
-            jax.ShapeDtypeStruct((rows, mid), jnp.bfloat16) for rows in (288, 288, 368, 368)
-        ],
-        scratch_shapes=[pltpu.VMEM((368, mid), jnp.bfloat16)] * 2,
+            jax.ShapeDtypeStruct((rows, mid), jnp.bfloat16) for rows in (288, 288, 288, 288, 80, 80)
+        ],
+        scratch_shapes=[pltpu.VMEM((80, mid), jnp.bfloat16)] * 2,
         compiler_params=pltpu.CompilerParams(vmem_limit_bytes=VMEM_LIMIT),
-        name="edge",
-    )(base, source, block, even, odd)
+        name="corner",
+    )(base, *faces)
 
 
 def gather_weights(w_ref, wide_ref):
@@ -355,7 +348,7 @@
     return left + wide[:, :, width : 2 * width] + right
 
 
-def conv_planes(here_ref, next_ref, wide_ref, first, planes, rows):
+def plane_taps(here_ref, next_ref, first, planes, rows):
     taps = []
     for dd in range(3):
         span = slice(first + dd, first + dd + planes)
@@ -365,7 +358,11 @@
             here_ref[span, 16 : rows + 16, :],
         ]
     lhs = jnp.concatenate(taps, axis=2)
-    return multiply_taps(lhs.reshape(planes * rows, lhs.shape[2]), wide_ref)
+    return lhs.reshape(planes * rows, lhs.shape[2])
+
+
+def conv_planes(here_ref, next_ref, wide_ref, first, planes, rows):
+    return multiply_taps(plane_taps(here_ref, next_ref, first, planes, rows), wide_ref)
 
 
 def activate(value, flags):
@@ -425,169 +422,215 @@
     )(source, block, wide1)
 
 
-def side_kernel(
-    source_ref,
-    block_ref,
-    before_ref,
-    after_ref,
-    wide1_ref,
-    hidden_ref,
-    late_ref,
-    mixed,
-    here,
-    moved,
-):
-    inner_planes(source_ref, block_ref, wide1_ref, late_ref, here, moved, LATE)
+def side_taps(low, high):
+    mixed = as_tiles(
+        jnp.concatenate(
+            [as_rows(low).reshape(-1, 2, COLS, 128)[:, 1:], as_rows(high).reshape(-1, 2, COLS, 128)[:, :1]],
+            axis=1,
+        ).reshape(-1, COLS, 128)
+    )
+    return low, mixed, high
+
+
+def depth_taps(taps, planes):
+    parts = [tap[dd * 16 : (dd + planes) * 16] for dd in range(3) for tap in taps]
+    return jnp.concatenate(parts, axis=1)
+
+
+def coarse_rows(source_ref, block_ref, value, depth_brick):
     width = block_ref.shape[1]
-    for d in range(SIDE):
-        edge = slice(d * 16, (d + 1) * 16)
-        low = as_rows(block_ref[d * 128 : d * 128 + 16])
-        high = as_rows(block_ref[d * 128 + 112 : d * 128 + 128])
-        before = as_rows(before_ref[edge])
-        after = as_rows(after_ref[edge])
-        mixed[0, edge] = as_tiles(jnp.concatenate([before[1:], low[:1]], axis=0))
-        mixed[1, edge] = as_tiles(jnp.concatenate([high[1:], after[:1]], axis=0))
+    value = value.reshape(4, SIDE, COLS, width)
+    rows = slice(depth_brick * 512, (depth_brick + 1) * 512)
+    own = block_ref[rows].astype(jnp.float32).reshape(4, SIDE, COLS, width)
+    flags = [slot_flags(source_ref, slot_index(depth_brick, r)) for r in range(4)]
+    return (value + own) * spread_flags(flags, (4, 4, 4, 4))[None]
+
+
+def middle_kernel(source_ref, *refs):
+    block_ref, before_ref, after_ref, under_ref, over_ref, early_ref, wide1_ref, wide2_ref = refs[:8]
+    border_ref, h_here, h_next, coarse_ref, side, late, ends, ends_moved, here, moved = refs[8:]
+    width = block_ref.shape[1]
     inner = SIDE - 2
-    taps = []
-    for dd in range(3):
-        span = slice(dd * 16, (dd + inner) * 16)
-        low = [block_ref[(d + dd) * 128 : (d + dd) * 128 + 16] for d in range(inner)]
-        high = [block_ref[(d + dd) * 128 + 112 : (d + dd) * 128 + 128] for d in range(inner)]
-        taps.append(jnp.concatenate([before_ref[span]] + high, axis=0))
-        taps.append(jnp.concatenate([mixed[0, span], mixed[1, span]], axis=0))
-        taps.append(jnp.concatenate(low + [after_ref[span]], axis=0))
-    value = multiply_taps(jnp.concatenate(taps, axis=1), wide1_ref)
+    inner_planes(source_ref, block_ref, wide1_ref, late, here, moved, LATE)
+
+    low = jnp.concatenate([block_ref[d * 128 : d * 128 + 16] for d in range(SIDE)], axis=0)
+    high = jnp.concatenate([block_ref[d * 128 + 112 : d * 128 + 128] for d in range(SIDE)], axis=0)
+    left = depth_taps(side_taps(before_ref[0:256], low), inner)
+    right = depth_taps(side_taps(high, after_ref[0:256]), inner)
+    value = multiply_taps(jnp.concatenate([left, right], axis=0), wide1_ref)
     depths = (3, 4, 4, 3)
     edge_flags = (as_rows(before_ref[256:288]), as_rows(after_ref[256:288]))
     flags = []
-    for side, row_brick in ((0, 0), (1, 3)):
+    for end, row_brick in ((0, 0), (1, 3)):
         own = [slot_flags(source_ref, slot_index(d, row_brick)) for d in range(4)]
-        pairs = [jnp.stack([edge_flags[side][d], own[d]][:: 1 - 2 * side], axis=0) for d in range(4)]
+        pairs = [jnp.stack([edge_flags[end][d], own[d]][:: 1 - 2 * end], axis=0) for d in range(4)]
         flags.append(spread_flags(pairs, depths))
-    flags = jnp.stack(flags, axis=0)
-    value = activate(value.reshape(2, inner, 2, COLS, width), flags)
-    hidden_ref[...] = value.reshape(2, inner, 16, width).astype(jnp.bfloat16)
-
-
-def side_call(source, block, before, after, wide1):
+    value = activate(value.reshape(2, inner, 2, COLS, width), jnp.stack(flags, axis=0))
+    side[...] = value.reshape(2, inner, 16, width).astype(jnp.bfloat16)
+    for d in range(inner):
+        centre = early_ref[d] if d < EARLY_PLANES else late[d - EARLY_PLANES]
+        plane = jnp.concatenate([side[0, d], centre, side[1, d]], axis=0)
+        h_here[d] = plane
+        h_next[d] = as_tiles(moved_rows(as_rows(plane)))
+
+    for k in range(2):
+        planes = (
+            (k, under_ref[k * 128 : (k + 1) * 128]),
+            (2 + k, block_ref[k * 128 : (k + 1) * 128]),
+            (4 + k, block_ref[(SIDE - 2 + k) * 128 : (SIDE - 1 + k) * 128]),
+            (6 + k, over_ref[k * 128 : (k + 1) * 128]),
+        )
+        for index, plane in planes:
+            ends[index] = plane
+            ends_moved[index] = as_tiles(moved_rows(as_rows(plane)))
+    lhs = [plane_taps(ends, ends_moved, first, 2, inner * COLS) for first in (0, 4)]
+    value = multiply_taps(jnp.concatenate(lhs, axis=0), wide1_ref)
+    far = (as_rows(under_ref[256:288]), as_rows(over_ref[256:288]))
+    flags = []
+    for end, brick in ((0, 0), (1, 3)):
+        outer = [far[end][r] for r in range(4)]
+        own = [slot_flags(source_ref, slot_index(brick, r)) for r in range(4)]
+        for chosen in (outer, own) if end == 0 else (own, outer):
+            flags.append(spread_flags(chosen, (3, 4, 4, 3)))
+    value = activate(value.reshape(4, inner, COLS, width), jnp.stack(flags, axis=0))
+    border_ref[...] = value.reshape(4, inner * COLS, width).astype(jnp.bfloat16)
+
+    for depth_brick in (1, 2):
+        value = conv_planes(h_here, h_next, wide2_ref, depth_brick * 4 - 2, 4, SIDE * COLS)
+        value = coarse_rows(source_ref, block_ref, value, depth_brick)
+        rows = slice((depth_brick - 1) * 512, depth_brick * 512)
+        coarse_ref[rows] = value.reshape(512, width).astype(jnp.bfloat16)
+
+
+def middle_call(source, block, before, after, under, over, early, wide1, wide2):
     mid = block.shape[1]
     smem = pl.BlockSpec(memory_space=pltpu.SMEM)
     vmem = pl.BlockSpec(memory_space=pltpu.VMEM)
     inner = SIDE - 2
+    hidden = (inner, HID * COLS, mid)
     return pl.pallas_call(
-        side_kernel,
-        in_specs=[smem] + [vmem] * 4,
-        out_specs=[vmem] * 2,
+        middle_kernel,
+        in_specs=[smem] + [vmem] * 8,
+        out_specs=[vmem] * 4,
         out_shape=[
-            jax.ShapeDtypeStruct((2, inner, 16, mid), jnp.bfloat16),
-            jax.ShapeDtypeStruct((LATE_PLANES, inner * COLS, mid), jnp.bfloat16),
+            jax.ShapeDtypeStruct(shape, jnp.bfloat16)
+            for shape in ((4, inner * COLS, mid), hidden, hidden, (1024, mid))
         ],
         scratch_shapes=[
-            pltpu.VMEM((2, SIDE * 16, mid), jnp.bfloat16),
+            pltpu.VMEM((2, inner, 16, mid), jnp.bfloat16),
+            pltpu.VMEM((LATE_PLANES, inner * COLS, mid), jnp.bfloat16),
+            pltpu.VMEM((8, SIDE * COLS, mid), jnp.bfloat16),
+            pltpu.VMEM((8, SIDE * COLS, mid), jnp.bfloat16),
             pltpu.VMEM((LATE_PLANES + 2, SIDE * COLS, mid), jnp.bfloat16),
             pltpu.VMEM((LATE_PLANES + 2, SIDE * COLS, mid), jnp.bfloat16),
         ],
         compiler_params=pltpu.CompilerParams(vmem_limit_bytes=VMEM_LIMIT),
-        cost_estimate=conv_cost(inner * (4 + LATE_PLANES) * COLS, mid),
-        name="side",
-    )(source, block, before, after, wide1)
+        cost_estimate=conv_cost(inner * (8 + LATE_PLANES) * COLS + 1024, mid),
+        name="middle",
+    )(source, block, before, after, under, over, early, wide1, wide2)
+
+
+def scatter_bricks(source_ref, stage, value, depth_brick):
+    width = value.shape[3]
+    half = low_half((4, 2, COLS, width))
+    for r in range(4):
+        part = value[:, r * 4 : (r + 1) * 4].reshape(4, 2, 2, COLS, width)
+        even, odd = part[:, :, 0], part[:, :, 1]
+        b0 = jnp.where(half, even, pltpu.roll(odd, 4, 2))
+        b1 = jnp.where(half, pltpu.roll(even, 4, 2), odd)
+        slot = slot_index(depth_brick, r)
+        for k, brick in enumerate((b0, b1)):
+            source = source_ref[slot + k]
+            row = pl.multiple_of(jnp.where(source >= 0, source, K * CAP) * CELLS, CELLS)
+            stage[pl.ds(row, CELLS), :] = brick.reshape(CELLS, width).astype(jnp.bfloat16)
 
 
 def final_kernel(count, base_ref, source_ref, *refs):
-    block_ref, before_ref, after_ref, even_ref, odd_ref = refs[:5]
-    early_ref, late_ref, side_ref, wide1_ref, wide2_ref, coarse_ref = refs[5:11]
-    backs = refs[11 : 11 + K]
-    x_here, x_next, h_here, h_next, stage, under_ref, over_ref = refs[11 + K :]
-    face_in(base_ref[1], count, even_ref, odd_ref, under_ref, over_ref)
+    block_ref, before_ref, after_ref, under_ref, over_ref, even_ref, odd_ref = refs[:7]
+    border_ref, mid_here, mid_next, mid_ref, wide1_ref, wide2_ref, coarse_ref = refs[7:14]
+    backs = refs[14 : 14 + K]
+    h_here, h_next, stage, low_ref, high_ref = refs[14 + K :]
     width = block_ref.shape[1]
+    stage[...] = jnp.zeros(stage.shape, jnp.bfloat16)
+    face_in(base_ref[1], count, even_ref, odd_ref, low_ref, high_ref)
     flags_before = as_rows(before_ref[256:288])
     flags_after = as_rows(after_ref[256:288])
-    for end, ref in ((0, under_ref), (1, over_ref)):
-        planes = []
-        own = [0, 1] if end == 0 else [SIDE - 2, SIDE - 1]
-        for d in own:
-            edge = slice(d * 16, (d + 1) * 16)
-            planes.append(
-                jnp.concatenate(
-                    [before_ref[edge], block_ref[d * 128 : (d + 1) * 128], after_ref[edge]], axis=0
-                )
+    lhs = []
+    flags = []
+    for end, far, corner in ((0, under_ref, low_ref), (1, over_ref, high_ref)):
+        first = 0 if end == 0 else SIDE - 2
+        brick = 0 if end == 0 else 3
+        far_flags = as_rows(far[256:288])
+        corner_flags = as_rows(corner[64:80])
+        for which, line, lines in ((0, before_ref, flags_before), (1, after_ref, flags_after)):
+            row = 0 if which == 0 else 112
+            outer = [corner[which * 32 + k * 16 : which * 32 + k * 16 + 16] for k in range(2)]
+            outer_own = [line[(first + k) * 16 : (first + k) * 16 + 16] for k in range(2)]
+            near = [far[k * 128 + row : k * 128 + row + 16] for k in range(2)]
+            near_own = [
+                block_ref[(first + k) * 128 + row : (first + k) * 128 + row + 16] for k in range(2)
+            ]
+            outer = jnp.concatenate(outer + outer_own if end == 0 else outer_own + outer, axis=0)
+            near = jnp.concatenate(near + near_own if end == 0 else near_own + near, axis=0)
+            taps = side_taps(outer, near) if which == 0 else side_taps(near, outer)
+            lhs.append(depth_taps(taps, 2))
+            own_flag = slot_flags(source_ref, slot_index(brick, which * 3))
+            far_pair = [corner_flags[which], far_flags[which * 3]]
+            own_pair = [lines[brick], own_flag]
+            for pair in (far_pair, own_pair) if end == 0 else (own_pair, far_pair):
+                flags += pair if which == 0 else pair[::-1]
+    value = multiply_taps(jnp.concatenate(lhs, axis=0), wide1_ref)
+    corners = activate(value, jnp.stack(flags, axis=0))
+    corners = corners.reshape(2, 2, 2, 16, width).astype(jnp.bfloat16)
+    for end in range(2):
+        for k in range(2):
+            plane = jnp.concatenate(
+                [corners[end, 0, k], border_ref[end * 2 + k], corners[end, 1, k]], axis=0
             )
-        far = [ref[k * 160 : (k + 1) * 160] for k in range(2)]
-        for index, plane in enumerate(far + planes if end == 0 else planes + far):
-            x_here[index] = plane
-            x_next[index] = as_tiles(moved_rows(as_rows(plane)))
-        value = conv_planes(x_here, x_next, wide1_ref, 0, 2, HID * COLS)
-        value = value.reshape(2, HID, COLS, width)
-        far_flags = as_rows(ref[320:368])
-        brick = 0 if end == 0 else 3
-        own_flags = [flags_before[brick]]
-        own_flags += [slot_flags(source_ref, slot_index(brick, r)) for r in range(4)]
-        own_flags += [flags_after[brick]]
-        spread = [
-            spread_flags([far_flags[r] for r in range(6)], (1, 4, 4, 4, 4, 1)),
-            spread_flags(own_flags, (1, 4, 4, 4, 4, 1)),
-        ]
-        for k in range(2):
-            flags = spread[k if end == 0 else 1 - k]
-            rows = activate(value[k], flags)
-            index = k if end == 0 else HID - 2 + k
-            h_here[index] = as_tiles(rows)
-            h_next[index] = as_tiles(moved_rows(rows))
-    for d in range(SIDE - 2):
-        middle = early_ref[d] if d < EARLY_PLANES else late_ref[d - EARLY_PLANES]
-        plane = jnp.concatenate([side_ref[0, d], middle, side_ref[1, d]], axis=0)
-        h_here[d + 2] = plane
-        h_next[d + 2] = as_tiles(moved_rows(as_rows(plane)))
-
-    stage[...] = jnp.zeros(stage.shape, jnp.bfloat16)
-    for depth_brick in range(4):
-        value = conv_planes(h_here, h_next, wide2_ref, depth_brick * 4, 4, SIDE * COLS)
-        value = value.reshape(4, SIDE, COLS, width)
+            index = k if end == 0 else 10 + k
+            h_here[index] = plane
+            h_next[index] = as_tiles(moved_rows(as_rows(plane)))
+    for k in range(4):
+        for index, source in ((2 + k, k), (6 + k, SIDE - 6 + k)):
+            h_here[index] = mid_here[source]
+            h_next[index] = mid_next[source]
+    for depth_brick in (1, 2):
+        rows = slice((depth_brick - 1) * 512, depth_brick * 512)
+        done = mid_ref[rows]
+        coarse_ref[depth_brick * 512 : (depth_brick + 1) * 512] = done
+        done = done.astype(jnp.float32).reshape(4, SIDE, COLS, width)
+        scatter_bricks(source_ref, stage, done, depth_brick)
+    for depth_brick in (0, 3):
+        value = conv_planes(h_here, h_next, wide2_ref, depth_brick * 2, 4, SIDE * COLS)
+        value = coarse_rows(source_ref, block_ref, value, depth_brick)
         rows = slice(depth_brick * 512, (depth_brick + 1) * 512)
-        own = block_ref[rows].astype(jnp.float32).reshape(4, SIDE, COLS, width)
-        flags = [slot_flags(source_ref, slot_index(depth_brick, r)) for r in range(4)]
-        value = (value + own) * spread_flags(flags, (4, 4, 4, 4))[None]
-        coarse_ref[rows] = value.reshape(4 * SIDE * COLS, width).astype(jnp.bfloat16)
-        half = low_half((4, 2, COLS, width))
-        for r in range(4):
-            part = value[:, r * 4 : (r + 1) * 4].reshape(4, 2, 2, COLS, width)
-            even, odd = part[:, :, 0], part[:, :, 1]
-            b0 = jnp.where(half, even, pltpu.roll(odd, 4, 2))
-            b1 = jnp.where(half, pltpu.roll(even, 4, 2), odd)
-            slot = slot_index(depth_brick, r)
-            for k, brick in enumerate((b0, b1)):
-                source = source_ref[slot + k]
-                row = pl.multiple_of(jnp.where(source >= 0, source, K * CAP) * CELLS, CELLS)
-                stage[pl.ds(row, CELLS), :] = brick.reshape(CELLS, width).astype(jnp.bfloat16)
+        coarse_ref[rows] = value.reshape(512, width).astype(jnp.bfloat16)
+        scatter_bricks(source_ref, stage, value, depth_brick)
     for j in range(K):
         backs[j][...] = stage[j * CAP * CELLS : (j + 1) * CAP * CELLS]
 
 
-def final_call(count, base, source, block, halo, hidden, wide1, wide2):
+def final_call(count, base, source, block, halo, middle, wide1, wide2):
     mid = block.shape[1]
     smem = pl.BlockSpec(memory_space=pltpu.SMEM)
     vmem = pl.BlockSpec(memory_space=pltpu.VMEM)
     return pl.pallas_call(
         functools.partial(final_kernel, count),
-        in_specs=[smem, smem] + [vmem] * 10,
+        in_specs=[smem, smem] + [vmem] * 13,
         out_specs=[vmem] * (1 + K),
-        out_shape=[
-            jax.ShapeDtypeStruct(block.shape, jnp.bfloat16),
-        ]
+        out_shape=[jax.ShapeDtypeStruct(block.shape, jnp.bfloat16)]
         + [jax.ShapeDtypeStruct((CAP * CELLS, mid), jnp.bfloat16)] * K,
         scratch_shapes=[
-            pltpu.VMEM((4, WIDE * COLS, mid), jnp.bfloat16),
-            pltpu.VMEM((4, WIDE * COLS, mid), jnp.bfloat16),
-            pltpu.VMEM((HID, HID * COLS, mid), jnp.bfloat16),
-            pltpu.VMEM((HID, HID * COLS, mid), jnp.bfloat16),
+            pltpu.VMEM((12, HID * COLS, mid), jnp.bfloat16),
+            pltpu.VMEM((12, HID * COLS, mid), jnp.bfloat16),
             pltpu.VMEM(((K * CAP + 1) * CELLS, mid), jnp.bfloat16),
-            pltpu.VMEM((368, mid), jnp.bfloat16),
-            pltpu.VMEM((368, mid), jnp.bfloat16),
+            pltpu.VMEM((80, mid), jnp.bfloat16),
+            pltpu.VMEM((80, mid), jnp.bfloat16),
         ],
         compiler_params=pltpu.CompilerParams(vmem_limit_bytes=VMEM_LIMIT),
-        cost_estimate=conv_cost(SIDE * SIDE * COLS, mid),
+        cost_estimate=conv_cost(1152, mid),
         name="final",
-    )(base, source, block, *halo, *hidden, wide1, wide2)
+    )(base, source, block, *halo, *middle, wide1, wide2)
 
 
 def from_behind(value, axis, steps):
@@ -611,37 +654,28 @@
     mid = w_down.shape[1]
     base = jnp.stack([lax.axis_index("xy"), lax.axis_index("gz")]).astype(jnp.int32)
     counts = (lax.axis_size("gz"), lax.axis_size("xy"))
-    sent = down_call(fine, fine_mask, w_down, FIRST_SENT)
-    arrived = {j: from_behind(sent[j], "xy", j) for j in FIRST_SENT}
-    fine_again, sent[FIRST_SENT[0]] = lax.optimization_barrier((fine, sent[FIRST_SENT[0]]))
-    sent = down_call(fine_again, fine_mask, w_down, LAST_SENT)
-    arrived.update({j: from_behind(sent[j], "xy", j) for j in LAST_SENT})
-    middle = LAST_SENT[1]
-    later = (arrived[middle], fine, fine_mask, w_down, w_first, w_second)
-    arrived[middle], *later = lax.optimization_barrier(later)
+    sent = down_call(fine, fine_mask, w_down, SENT)
+    arrived = {j: from_behind(sent[j], "xy", j) for j in SENT}
+    later = (arrived[SENT[2]], fine, fine_mask, w_down, w_first, w_second)
+    arrived[SENT[2]], *later = lax.optimization_barrier(later)
     prepared = lax.optimization_barrier(tuple(prepare_call(*later)))
     arrived[0], mask, wide1, wide2 = prepared
-    block, even, odd = place_call(base, slot_source, [arrived[j] for j in range(K)])
-    even, odd = swap_faces(even, odd, "xy")
+    block, *faces = place_call(base, slot_source, [arrived[j] for j in range(K)])
+    gz_even, gz_odd = swap_faces(*faces[2:], "gz")
+    even, odd = swap_faces(*faces[:2], "xy")
     early = inner_call(slot_source, block, wide1)
-    even, odd, early = lax.optimization_barrier((even, odd, early))
-    before, after, even, odd = edge_call(counts, base, slot_source, block, even, odd)
+    even, odd, gz_even, gz_odd, early = lax.optimization_barrier((even, odd, gz_even, gz_odd, early))
+    *halo, even, odd = corner_call(counts, base, (even, odd, gz_even, gz_odd))
     even, odd = swap_faces(even, odd, "gz")
-    side, late = side_call(slot_source, block, before, after, wide1)
+    middle = middle_call(slot_source, block, *halo, early, wide1, wide2)
     coarse, *back = final_call(
-        counts[0],
-        base,
-        slot_source,
-        block,
-        (before, after, even, odd),
-        (early, late, side),
-        wide1,
-        wide2,
+        counts[0], base, slot_source, block, (*halo, even, odd), middle, wide1, wide2
     )
-    octant = {j: from_behind(back[j], "xy", -j) for j in RETURNED}
+    octant = {j: from_behind(back[j], "xy", -j) for j in SENT}
     octant[0] = back[0]
-    fine_out = up_call(fine, mask, w_up, [octant[j] for j in (6, 7, 0, 1)], 3, None)
-    fine_out = up_call(fine, mask, w_up, [octant[j] for j in (2, 3, 4, 5)], 1, fine_out)
+    fine_out = None
+    for group in UP_GROUPS:
+        fine_out = up_call(fine, mask, w_up, [octant[j] for j in group], group, fine_out)
     return fine_out, coarse.reshape(SIDE, SIDE, COLS, mid)
 
 

time: 61.4 us -> 63.3 us (1.031)
  starting transfers between devices: 29.8 us -> 33.8 us
  waiting for transfers between devices: 8.86 us -> 6.81 us
    ppermute x4 -> x6, starting transfers between devices: 2.7 us -> 7.29 us  [swap_faces(): swapped.append(lax.ppermute(face, axis, list(enumerate(partner))))]
    pallas_call x4, Pallas kernels: 5.42 us -> 8.63 us  [the longest x2 4.25 us: up_call(): pl.pallas_call(up_kernel, grid=(count,), in_specs=[pl.BlockSpec((CAP, cel...]
    ppermute x14, waiting for transfers between devices: 8.77 us -> 6.79 us  [from_behind(): return lax.ppermute(value, axis, pairs)]
    pallas_call x1, Pallas kernels: 5.07 us -> 3.22 us  [final_call(): pl.pallas_call(functools.partial(final_kernel, count), in_specs=[smem, sm...]
    pallas_call x2 -> x1, Pallas kernels: 5.31 us -> 3.91 us  [down_call(): pl.pallas_call(functools.partial(down_kernel, offsets), in_specs=[hbm, hb...]
  transfers between devices with their start and end apart: 18 -> 20, of which waited for: 5 -> 5; matrix products, arithmetic and copies ran while one was open for 0% -> 0% of each run, Pallas kernels for 16% -> 15%
where the time goes in v7:
time: 63.3 us; the launch traced here: 63.1 us
  starting transfers between devices  33.8 us (53%)
  Pallas kernels  20 us (32%)
  waiting for transfers between devices  6.81 us (11%)
  local copies, waits for them, and re-layouts  1.62 us (3%)
  between operations  0.85 us (1%)
    ppermute x14, starting transfers between devices, from_behind(): return lax.ppermute(value, axis, pairs)  26.5 us
    ppermute x6, starting transfers between devices, swap_faces(): swapped.append(lax.ppermute(face, axis, list(enumerate(partner))))  7.29 us
    ppermute x14, waiting for transfers between devices, from_behind(): return lax.ppermute(value, axis, pairs)  6.79 us
    pallas_call x2, Pallas kernels, up_call(): pl.pallas_call(up_kernel, grid=(count,), in_specs=[pl.BlockSpec((CAP, cel...  4.25 us
    pallas_call x1, Pallas kernels, down_call(): pl.pallas_call(functools.partial(down_kernel, offsets), in_specs=[hbm, hb...  3.91 us
    pallas_call x1, Pallas kernels, middle_call(): pl.pallas_call(middle_kernel, in_specs=[smem] + [vmem] * 8, out_specs=[vm...  3.74 us
    pallas_call x1, Pallas kernels, final_call(): pl.pallas_call(functools.partial(final_kernel, count), in_specs=[smem, sm...  3.22 us
    pallas_call x1, Pallas kernels, inner_call(): pl.pallas_call(inner_kernel, in_specs=[smem, vmem, vmem], out_specs=vmem,...  2.34 us
  transfers between devices with their start and end apart: 20, of which 5 were waited for; matrix products, arithmetic and copies ran while one was open for 0% of the time, Pallas kernels for 15%

profile of v7, /device:TPU:0, one launch (start us, length us, event | category | flops | bytes accessed | tf_op | source)
XLA Modules:
  0.0 63.1 jit_solution(8168267829286741131)
XLA Ops:
  0.7 3.9 %down.1 = (bf16[256,128]{1,0:T(8,128)(2,1)}, bf16[256,128]{1,0:T(8,128)(2,1)}, bf16[256,128]{1,0:T(8,128)(2,1)}, bf16[256,128]{1,0:T(8,128)(2,1)}, bf16[256,128]...) custom-call(bf16[32,64,512]{2,1,0:T(8,128)(2,1)} %fine_ref.4, s32[32,512]{1,0:T(8,128)} %mask_ref, ...), custom_call_target="tpu_custom_call" | custom-call | flops 234881024 | bytes 1835008 | tf_op jit(solution)/shard_map/down/pallas_call | solution.py:83
  4.6 5.0 %collective-permute-start = (bf16[256,128]{1,0:T(8,128)(2,1)}, bf16[256,128]{1,0:T(8,128)(2,1)S(1)}, u32[]{:S(2)}, u32[]{:S(2)}) collective-permute-start(bf16[256,128]{1,0:T(8,128)(2,1)} %get-tuple-element.48), channel_id=1, source_target_pairs={{0,5},{1,6},{2,7},{3,0},{4,1},{5,2},{6,3},{7,4},{8,13},{9,14},{10,... | collective-permute-start | bytes 196616 | tf_op jit(solution)/shard_map/ppermute | solution.py:639
  9.6 1.5 %collective-permute-start.1 = (bf16[256,128]{1,0:T(8,128)(2,1)}, bf16[256,128]{1,0:T(8,128)(2,1)S(1)}, u32[]{:S(2)}, u32[]{:S(2)}) collective-permute-start(bf16[256,128]{1,0:T(8,128)(2,1)} %get-tuple-element.56), channel_id=1, source_target_pairs={{0,1},{1,2},{2,3},{3,4},{4,5},{5,6},{6,7},{7,0},{8,9},{9,10},{10,1... | collective-permute-start | bytes 196616 | tf_op jit(solution)/shard_map/ppermute | solution.py:639
  11.2 1.8 %collective-permute-start.3 = (bf16[256,128]{1,0:T(8,128)(2,1)}, bf16[256,128]{1,0:T(8,128)(2,1)S(1)}, u32[]{:S(2)}, u32[]{:S(2)}) collective-permute-start(bf16[256,128]{1,0:T(8,128)(2,1)} %get-tuple-element.58), channel_id=1, source_target_pairs={{0,3},{1,4},{2,5},{3,6},{4,7},{5,0},{6,1},{7,2},{8,11},{9,12},{10,... | collective-permute-start | bytes 196616 | tf_op jit(solution)/shard_map/ppermute | solution.py:639
  13.0 3.5 %collective-permute-start.4 = (bf16[256,128]{1,0:T(8,128)(2,1)}, bf16[256,128]{1,0:T(8,128)(2,1)S(1)}, u32[]{:S(2)}, u32[]{:S(2)}) collective-permute-start(bf16[256,128]{1,0:T(8,128)(2,1)} %get-tuple-element.59), channel_id=1, source_target_pairs={{0,4},{1,5},{2,6},{3,7},{4,0},{5,1},{6,2},{7,3},{8,12},{9,13},{10,... | collective-permute-start | bytes 196616 | tf_op jit(solution)/shard_map/ppermute | solution.py:639
  16.5 1.4 %collective-permute-start.5 = (bf16[256,128]{1,0:T(8,128)(2,1)}, bf16[256,128]{1,0:T(8,128)(2,1)S(1)}, u32[]{:S(2)}, u32[]{:S(2)}) collective-permute-start(bf16[256,128]{1,0:T(8,128)(2,1)} %get-tuple-element.61), channel_id=1, source_target_pairs={{0,6},{1,7},{2,0},{3,1},{4,2},{5,3},{6,4},{7,5},{8,14},{9,15},{10,... | collective-permute-start | bytes 196616 | tf_op jit(solution)/shard_map/ppermute | solution.py:639
  17.8 1.0 %collective-permute-start.6 = (bf16[256,128]{1,0:T(8,128)(2,1)}, bf16[256,128]{1,0:T(8,128)(2,1)S(1)}, u32[]{:S(2)}, u32[]{:S(2)}) collective-permute-start(bf16[256,128]{1,0:T(8,128)(2,1)} %get-tuple-element.62), channel_id=1, source_target_pairs={{0,7},{1,0},{2,1},{3,2},{4,3},{5,4},{6,5},{7,6},{8,15},{9,8},{10,9... | collective-permute-start | bytes 196616 | tf_op jit(solution)/shard_map/ppermute | solution.py:639
  18.9 0.1 pad_add_fusion.base_ref
  19.0 1.6 %copy-done = bf16[32,64,512]{2,1,0:T(8,128)(2,1)S(1)} copy-done((bf16[32,64,512]{2,1,0:T(8,128)(2,1)S(1)}, bf16[32,64,512]{2,1,0:T(8,128)(2,1)}, u32[]{:S(2)}) %copy-start) | copy-done | bytes 2097176
  20.6 1.1 %prepare.1 = (bf16[256,128]{1,0:T(8,128)(2,1)S(1)}, bf16[2048,512]{1,0:T(8,128)(2,1)S(1)}, bf16[1152,384]{1,0:T(8,128)(2,1)S(1)}, bf16[1152,384]{1,0:T(8,128)(2,1)S(1)}) custom-call(bf16[32,64,512]{2,1,0:T(8,128)(2,1)S(1)} %copy-done, s32[32,512]{1,0:T(8,128)S(1)} %copy-done.6, bf16[512,128]{1,0:T(8,128)(2,1)S(1)} %copy-done.5, ...), custom_call_target="tpu_custom_call" | custom-call | flops 268435456 | bytes 2097152 | tf_op jit(solution)/shard_map/prepare/pallas_call | solution.py:124
  21.6 0.8 %collective-permute-done.3.refs_3_ = bf16[256,128]{1,0:T(8,128)(2,1)S(1)} collective-permute-done((bf16[256,128]{1,0:T(8,128)(2,1)}, bf16[256,128]{1,0:T(8,128)(2,1)S(1)}, u32[]{:S(2)}, u32[]{:S(2)}) %collective-permute-start.3) | collective-permute-done | bytes 65568 | tf_op jit(solution)/shard_map/ppermute | solution.py:639
  22.5 0.3 collective-permute-done.6.refs_7_
  22.7 0.8 %place.1 = (bf16[2048,128]{1,0:T(8,128)(2,1)S(1)}, bf16[288,128]{1,0:T(8,128)(2,1)S(1)}, bf16[288,128]{1,0:T(8,128)(2,1)S(1)}, bf16[288,128]{1,0:T(8,128)(2,1)S(1)}, bf16[288,128]{1,0:T(8,128)(2,1)S(1)}) custom-call(s32[2]{0:T(128)S(1)} %pad_add_fusion.base_ref, s32[32]{0:T(128)S(1)} %copy-done.7, bf16[256,128]{1,0:T(8,128)(2,1)S(1)} %get-tuple-element.55.refs_0_, ...), custom_call_target="tpu_custom_call" | custom-call | tf_op jit(solution)/shard_map/place/pallas_call | solution.py:267
  23.5 2.1 %collective-permute-start.7 = (bf16[288,128]{1,0:T(8,128)(2,1)S(1)}, bf16[288,128]{1,0:T(8,128)(2,1)S(1)}, u32[]{:S(2)}, u32[]{:S(2)}) collective-permute-start(bf16[288,128]{1,0:T(8,128)(2,1)S(1)} %get-tuple-element.64), channel_id=1, source_target_pairs={{0,1},{1,0},{2,3},{3,2},{4,5},{5,4},{6,7},{7,6},{8,9},{9,8},{10,11... | collective-permute-start | bytes 221192 | tf_op jit(solution)/shard_map/ppermute | solution.py:649
  25.6 0.7 %collective-permute-start.8 = (bf16[288,128]{1,0:T(8,128)(2,1)S(1)}, bf16[288,128]{1,0:T(8,128)(2,1)S(1)}, u32[]{:S(2)}, u32[]{:S(2)}) collective-permute-start(bf16[288,128]{1,0:T(8,128)(2,1)S(1)} %get-tuple-element.65), channel_id=1, source_target_pairs={{0,0},{1,2},{2,1},{3,4},{4,3},{5,6},{6,5},{7,7},{8,8},{9,10},{10,9... | collective-permute-start | bytes 221192 | tf_op jit(solution)/shard_map/ppermute | solution.py:649
  26.4 0.7 %collective-permute-start.10 = (bf16[288,128]{1,0:T(8,128)(2,1)S(1)}, bf16[288,128]{1,0:T(8,128)(2,1)S(1)}, u32[]{:S(2)}, u32[]{:S(2)}) collective-permute-start(bf16[288,128]{1,0:T(8,128)(2,1)S(1)} %get-tuple-element.67), channel_id=1, source_target_pairs={{0,0},{8,16},{16,8},{24,24},{1,1},{9,17},{17,9},{25,25},{2,2},{10,... | collective-permute-start | bytes 221192 | tf_op jit(solution)/shard_map/ppermute | solution.py:649
  27.1 2.3 %inner.1.refs_5_ = bf16[11,112,128]{2,1,0:T(8,128)(2,1)S(1)} custom-call(s32[32]{0:T(128)S(1)} %copy-done.7, bf16[2048,128]{1,0:T(8,128)(2,1)S(1)} %get-tuple-element.63.block_ref.refs_0_, bf16[1152,384]{1,0:T(8,128)(2,1)S(1)} %get-tuple-element.68.wide1_ref.refs_6_.refs_11_), custom_call_target="tpu_custom_call" | custom-call | flops 1089994752 | bytes 1769472 | tf_op jit(solution)/shard_map/inner/pallas_call | solution.py:413
  29.4 0.6 %corner.1 = (bf16[288,128]{1,0:T(8,128)(2,1)S(1)}, bf16[288,128]{1,0:T(8,128)(2,1)S(1)}, bf16[288,128]{1,0:T(8,128)(2,1)S(1)}, bf16[288,128]{1,0:T(8,128)(2,1)S(...) custom-call(s32[2]{0:T(128)S(1)} %pad_add_fusion.base_ref, ...), custom_call_target="tpu_custom_call" | custom-call | tf_op jit(solution)/shard_map/corner/pallas_call | solution.py:305
  30.1 3.2 %collective-permute-start.11 = (bf16[80,128]{1,0:T(8,128)(2,1)S(1)}, bf16[80,128]{1,0:T(8,128)(2,1)S(1)}, u32[]{:S(2)}, u32[]{:S(2)}) collective-permute-start(bf16[80,128]{1,0:T(8,128)(2,1)S(1)} %get-tuple-element.77), channel_id=1, source_target_pairs={{0,8},{8,0},{16,24},{24,16},{1,9},{9,1},{17,25},{25,17},{2,10},{10... | collective-permute-start | bytes 61448 | tf_op jit(solution)/shard_map/ppermute | solution.py:649
  33.2 0.7 %collective-permute-start.12 = (bf16[80,128]{1,0:T(8,128)(2,1)S(1)}, bf16[80,128]{1,0:T(8,128)(2,1)S(1)}, u32[]{:S(2)}, u32[]{:S(2)}) collective-permute-start(bf16[80,128]{1,0:T(8,128)(2,1)S(1)} %get-tuple-element.78), channel_id=1, source_target_pairs={{0,0},{8,16},{16,8},{24,24},{1,1},{9,17},{17,9},{25,25},{2,2},{10,... | collective-permute-start | bytes 61448 | tf_op jit(solution)/shard_map/ppermute | solution.py:649
  33.9 3.7 %middle.1 = (bf16[4,112,128]{2,1,0:T(8,128)(2,1)S(1)}, bf16[14,144,128]{2,1,0:T(8,128)(2,1)S(1)}, bf16[14,144,128]{2,1,0:T(8,128)(2,1)S(1)}, bf16[1024,128]{1,0:T(8,128)(2,1)S(1)}) custom-call(s32[32]{0:T(128)S(1)} %copy-done.7, bf16[2048,128]{1,0:T(8,128)(2,1)S(1)} %get-tuple-element.63.block_ref.refs_0_, bf16[288,128]{1,0:T(8,128)(2,1)S(1)} %get-tuple-element.73.refs_1_, ...), custom_call_target="tpu_custom_call" | custom-call | flops 1995964416 | bytes 1769472 | tf_op jit(solution)/shard_map/middle/pallas_call | solution.py:511
  37.7 3.2 %final.1 = (bf16[2048,128]{1,0:T(8,128)(2,1)}, bf16[256,128]{1,0:T(8,128)(2,1)S(1)}, bf16[256,128]{1,0:T(8,128)(2,1)S(1)}, bf16[256,128]{1,0:T(8,128)(2,1)S(1)},...) custom-call(s32[2]{0:T(128)S(1)} %pad_add_fusion.base_ref, ...), custom_call_target="tpu_custom_call" | custom-call | flops 1019215872 | bytes 1769472 | tf_op jit(solution)/shard_map/final/pallas_call | solution.py:617
  40.9 4.6 %collective-permute-start.17 = (bf16[256,128]{1,0:T(8,128)(2,1)S(1)}, bf16[256,128]{1,0:T(8,128)(2,1)S(1)}, u32[]{:S(2)}, u32[]{:S(2)}) collective-permute-start(bf16[256,128]{1,0:T(8,128)(2,1)S(1)} %get-tuple-element.89), channel_id=1, source_target_pairs={{0,5},{1,6},{2,7},{3,0},{4,1},{5,2},{6,3},{7,4},{8,13},{9,14},{10,... | collective-permute-start | bytes 196616 | tf_op jit(solution)/shard_map/ppermute | solution.py:639
  45.5 1.5 %collective-permute-start.18 = (bf16[256,128]{1,0:T(8,128)(2,1)S(1)}, bf16[256,128]{1,0:T(8,128)(2,1)S(1)}, u32[]{:S(2)}, u32[]{:S(2)}) collective-permute-start(bf16[256,128]{1,0:T(8,128)(2,1)S(1)} %get-tuple-element.90), channel_id=1, source_target_pairs={{0,4},{1,5},{2,6},{3,7},{4,0},{5,1},{6,2},{7,3},{8,12},{9,13},{10,... | collective-permute-start | bytes 196616 | tf_op jit(solution)/shard_map/ppermute | solution.py:639
  47.0 1.4 %collective-permute-start.13 = (bf16[256,128]{1,0:T(8,128)(2,1)S(1)}, bf16[256,128]{1,0:T(8,128)(2,1)S(1)}, u32[]{:S(2)}, u32[]{:S(2)}) collective-permute-start(bf16[256,128]{1,0:T(8,128)(2,1)S(1)} %get-tuple-element.85), channel_id=1, source_target_pairs={{0,2},{1,3},{2,4},{3,5},{4,6},{5,7},{6,0},{7,1},{8,10},{9,11},{10,... | collective-permute-start | bytes 196616 | tf_op jit(solution)/shard_map/ppermute | solution.py:639
  48.4 1.5 %collective-permute-start.14 = (bf16[256,128]{1,0:T(8,128)(2,1)S(1)}, bf16[256,128]{1,0:T(8,128)(2,1)S(1)}, u32[]{:S(2)}, u32[]{:S(2)}) collective-permute-start(bf16[256,128]{1,0:T(8,128)(2,1)S(1)} %get-tuple-element.86), channel_id=1, source_target_pairs={{0,1},{1,2},{2,3},{3,4},{4,5},{5,6},{6,7},{7,0},{8,9},{9,10},{10,1... | collective-permute-start | bytes 196616 | tf_op jit(solution)/shard_map/ppermute | solution.py:639
  49.9 3.3 %collective-permute-start.15 = (bf16[256,128]{1,0:T(8,128)(2,1)S(1)}, bf16[256,128]{1,0:T(8,128)(2,1)S(1)}, u32[]{:S(2)}, u32[]{:S(2)}) collective-permute-start(bf16[256,128]{1,0:T(8,128)(2,1)S(1)} %get-tuple-element.87), channel_id=1, source_target_pairs={{0,7},{1,0},{2,1},{3,2},{4,3},{5,4},{6,5},{7,6},{8,15},{9,8},{10,9... | collective-permute-start | bytes 196616 | tf_op jit(solution)/shard_map/ppermute | solution.py:639
  53.1 2.7 %collective-permute-done.18.refs_1_ = bf16[256,128]{1,0:T(8,128)(2,1)S(1)} collective-permute-done((bf16[256,128]{1,0:T(8,128)(2,1)S(1)}, bf16[256,128]{1,0:T(8,128)(2,1)S(1)}, u32[]{:S(2)}, u32[]{:S(2)}) %collective-permute-start.18) | collective-permute-done | bytes 65568 | tf_op jit(solution)/shard_map/ppermute | solution.py:639
  55.8 2.1 %up.2.refs_4_ = bf16[32,64,512]{2,1,0:T(8,128)(2,1)} custom-call(bf16[32,64,512]{2,1,0:T(8,128)(2,1)S(1)} %copy-done.1, bf16[2048,512]{1,0:T(8,128)(2,1)S(1)} %get-tuple-element.54.mask_ref, bf16[128,512]{1,0:T(8,128)(2,1)S(1)} %copy-done.4, bf16[256,128]{1,0:T(8,128)(2,1)S(1)} %collective-permute-done.17.refs_0_, ...), custom_call_target="tpu_custom_call" | custom-call | flops 134217728 | bytes 2097152 | tf_op jit(solution)/shard_map/up/pallas_call | solution.py:169
  58.0 1.2 %collective-permute-done.15.refs_2_ = bf16[256,128]{1,0:T(8,128)(2,1)S(1)} collective-permute-done((bf16[256,128]{1,0:T(8,128)(2,1)S(1)}, bf16[256,128]{1,0:T(8,128)(2,1)S(1)}, u32[]{:S(2)}, u32[]{:S(2)}) %collective-permute-start.15) | collective-permute-done | bytes 65568 | tf_op jit(solution)/shard_map/ppermute | solution.py:639
  59.2 1.8 %collective-permute-done.16.refs_3_ = bf16[256,128]{1,0:T(8,128)(2,1)S(1)} collective-permute-done((bf16[256,128]{1,0:T(8,128)(2,1)S(1)}, bf16[256,128]{1,0:T(8,128)(2,1)S(1)}, u32[]{:S(2)}, u32[]{:S(2)}) %collective-permute-start.16) | collective-permute-done | bytes 65568 | tf_op jit(solution)/shard_map/ppermute | solution.py:639
  61.0 2.1 %up.3 = bf16[32,64,512]{2,1,0:T(8,128)(2,1)} custom-call(bf16[32,64,512]{2,1,0:T(8,128)(2,1)S(1)} %copy-done.1, bf16[2048,512]{1,0:T(8,128)(2,1)S(1)} %get-tuple-element.54.mask_ref, bf16[128,512]{1,0:T(8,128)(2,1)S(1)} %copy-done.4, bf16[256,128]{1,0:T(8,128)(2,1)S(1)} %collective-permute-done.13.refs_0_, ...), custom_call_target="tpu_custom_call", output_to_operand_aliasing={{}: (7, {})} | custom-call | flops 134217728 | bytes 2097152 | tf_op jit(solution)/shard_map/up/pallas_call | solution.py:169
  (34 shorter events, 0.2 us)
Async XLA Ops:
  0.6 18.3 %copy-start.5 = (bf16[512,128]{1,0:T(8,128)(2,1)S(1)}, bf16[512,128]{1,0:T(8,128)(2,1)}, u32[]{:S(2)}) copy-start(bf16[512,128]{1,0:T(8,128)(2,1)} %w_down_ref) | copy-start | bytes 393220
  0.6 18.3 %copy-start.6 = (s32[32,512]{1,0:T(8,128)S(1)}, s32[32,512]{1,0:T(8,128)}, u32[]{:S(2)}) copy-start(s32[32,512]{1,0:T(8,128)} %mask_ref) | copy-start | bytes 196612
  0.7 18.3 %copy-start.3 = (bf16[27,128,128]{2,1,0:T(8,128)(2,1)S(1)}, bf16[27,128,128]{2,1,0:T(8,128)(2,1)}, u32[]{:S(2)}) copy-start(bf16[27,128,128]{2,1,0:T(8,128)(2,1)} %w2_ref) | copy-start | bytes 2654212
  0.7 18.3 %copy-start.2 = (bf16[27,128,128]{2,1,0:T(8,128)(2,1)S(1)}, bf16[27,128,128]{2,1,0:T(8,128)(2,1)}, u32[]{:S(2)}) copy-start(bf16[27,128,128]{2,1,0:T(8,128)(2,1)} %w1_ref) | copy-start | bytes 2654212
  4.6 18.1 %copy-start.7 = (s32[32]{0:T(128)S(1)}, s32[32]{0:T(128)}, u32[]{:S(2)}) copy-start(s32[32]{0:T(128)} %source_ref.7) | copy-start | bytes 388
  4.6 11.9 %collective-permute-start = (bf16[256,128]{1,0:T(8,128)(2,1)}, bf16[256,128]{1,0:T(8,128)(2,1)S(1)}, u32[]{:S(2)}, u32[]{:S(2)}) collective-permute-start(bf16[256,128]{1,0:T(8,128)(2,1)} %get-tuple-element.48), channel_id=1, source_target_pairs={{0,5},{1,6},{2,7},{3,0},{4,1},{5,2},{6,3},{7,4},{8,13},{9,14},{10,... | collective-permute-start | bytes 196616 | tf_op jit(solution)/shard_map/ppermute | solution.py:639
  9.6 8.2 %collective-permute-start.1 = (bf16[256,128]{1,0:T(8,128)(2,1)}, bf16[256,128]{1,0:T(8,128)(2,1)S(1)}, u32[]{:S(2)}, u32[]{:S(2)}) collective-permute-start(bf16[256,128]{1,0:T(8,128)(2,1)} %get-tuple-element.56), channel_id=1, source_target_pairs={{0,1},{1,2},{2,3},{3,4},{4,5},{5,6},{6,7},{7,0},{8,9},{9,10},{10,1... | collective-permute-start | bytes 196616 | tf_op jit(solution)/shard_map/ppermute | solution.py:639
  11.2 10.5 %collective-permute-start.2 = (bf16[256,128]{1,0:T(8,128)(2,1)}, bf16[256,128]{1,0:T(8,128)(2,1)S(1)}, u32[]{:S(2)}, u32[]{:S(2)}) collective-permute-start(bf16[256,128]{1,0:T(8,128)(2,1)} %get-tuple-element.57), channel_id=1, source_target_pairs={{0,2},{1,3},{2,4},{3,5},{4,6},{5,7},{6,0},{7,1},{8,10},{9,11},{10,... | collective-permute-start | bytes 196616 | tf_op jit(solution)/shard_map/ppermute | solution.py:639
  11.2 11.3 %collective-permute-start.3 = (bf16[256,128]{1,0:T(8,128)(2,1)}, bf16[256,128]{1,0:T(8,128)(2,1)S(1)}, u32[]{:S(2)}, u32[]{:S(2)}) collective-permute-start(bf16[256,128]{1,0:T(8,128)(2,1)} %get-tuple-element.58), channel_id=1, source_target_pairs={{0,3},{1,4},{2,5},{3,6},{4,7},{5,0},{6,1},{7,2},{8,11},{9,12},{10,... | collective-permute-start | bytes 196616 | tf_op jit(solution)/shard_map/ppermute | solution.py:639
  13.0 9.5 %collective-permute-start.4 = (bf16[256,128]{1,0:T(8,128)(2,1)}, bf16[256,128]{1,0:T(8,128)(2,1)S(1)}, u32[]{:S(2)}, u32[]{:S(2)}) collective-permute-start(bf16[256,128]{1,0:T(8,128)(2,1)} %get-tuple-element.59), channel_id=1, source_target_pairs={{0,4},{1,5},{2,6},{3,7},{4,0},{5,1},{6,2},{7,3},{8,12},{9,13},{10,... | collective-permute-start | bytes 196616 | tf_op jit(solution)/shard_map/ppermute | solution.py:639
  16.5 6.0 %collective-permute-start.5 = (bf16[256,128]{1,0:T(8,128)(2,1)}, bf16[256,128]{1,0:T(8,128)(2,1)S(1)}, u32[]{:S(2)}, u32[]{:S(2)}) collective-permute-start(bf16[256,128]{1,0:T(8,128)(2,1)} %get-tuple-element.61), channel_id=1, source_target_pairs={{0,6},{1,7},{2,0},{3,1},{4,2},{5,3},{6,4},{7,5},{8,14},{9,15},{10,... | collective-permute-start | bytes 196616 | tf_op jit(solution)/shard_map/ppermute | solution.py:639
  17.8 4.9 %collective-permute-start.6 = (bf16[256,128]{1,0:T(8,128)(2,1)}, bf16[256,128]{1,0:T(8,128)(2,1)S(1)}, u32[]{:S(2)}, u32[]{:S(2)}) collective-permute-start(bf16[256,128]{1,0:T(8,128)(2,1)} %get-tuple-element.62), channel_id=1, source_target_pairs={{0,7},{1,0},{2,1},{3,2},{4,3},{5,4},{6,5},{7,6},{8,15},{9,8},{10,9... | collective-permute-start | bytes 196616 | tf_op jit(solution)/shard_map/ppermute | solution.py:639
  19.0 1.6 %copy-start = (bf16[32,64,512]{2,1,0:T(8,128)(2,1)S(1)}, bf16[32,64,512]{2,1,0:T(8,128)(2,1)}, u32[]{:S(2)}) copy-start(bf16[32,64,512]{2,1,0:T(8,128)(2,1)} %fine_ref.4) | copy-start | bytes 6291460
  23.5 5.9 %collective-permute-start.7 = (bf16[288,128]{1,0:T(8,128)(2,1)S(1)}, bf16[288,128]{1,0:T(8,128)(2,1)S(1)}, u32[]{:S(2)}, u32[]{:S(2)}) collective-permute-start(bf16[288,128]{1,0:T(8,128)(2,1)S(1)} %get-tuple-element.64), channel_id=1, source_target_pairs={{0,1},{1,0},{2,3},{3,2},{4,5},{5,4},{6,7},{7,6},{8,9},{9,8},{10,11... | collective-permute-start | bytes 221192 | tf_op jit(solution)/shard_map/ppermute | solution.py:649
  25.6 3.8 %collective-permute-start.8 = (bf16[288,128]{1,0:T(8,128)(2,1)S(1)}, bf16[288,128]{1,0:T(8,128)(2,1)S(1)}, u32[]{:S(2)}, u32[]{:S(2)}) collective-permute-start(bf16[288,128]{1,0:T(8,128)(2,1)S(1)} %get-tuple-element.65), channel_id=1, source_target_pairs={{0,0},{1,2},{2,1},{3,4},{4,3},{5,6},{6,5},{7,7},{8,8},{9,10},{10,9... | collective-permute-start | bytes 221192 | tf_op jit(solution)/shard_map/ppermute | solution.py:649
  26.3 3.1 %collective-permute-start.9 = (bf16[288,128]{1,0:T(8,128)(2,1)S(1)}, bf16[288,128]{1,0:T(8,128)(2,1)S(1)}, u32[]{:S(2)}, u32[]{:S(2)}) collective-permute-start(bf16[288,128]{1,0:T(8,128)(2,1)S(1)} %get-tuple-element.66), channel_id=1, source_target_pairs={{0,8},{8,0},{16,24},{24,16},{1,9},{9,1},{17,25},{25,17},{2,10},{10... | collective-permute-start | bytes 221192 | tf_op jit(solution)/shard_map/ppermute | solution.py:649
  26.4 3.1 %collective-permute-start.10 = (bf16[288,128]{1,0:T(8,128)(2,1)S(1)}, bf16[288,128]{1,0:T(8,128)(2,1)S(1)}, u32[]{:S(2)}, u32[]{:S(2)}) collective-permute-start(bf16[288,128]{1,0:T(8,128)(2,1)S(1)} %get-tuple-element.67), channel_id=1, source_target_pairs={{0,0},{8,16},{16,8},{24,24},{1,1},{9,17},{17,9},{25,25},{2,2},{10,... | collective-permute-start | bytes 221192 | tf_op jit(solution)/shard_map/ppermute | solution.py:649
  30.1 7.6 %collective-permute-start.11 = (bf16[80,128]{1,0:T(8,128)(2,1)S(1)}, bf16[80,128]{1,0:T(8,128)(2,1)S(1)}, u32[]{:S(2)}, u32[]{:S(2)}) collective-permute-start(bf16[80,128]{1,0:T(8,128)(2,1)S(1)} %get-tuple-element.77), channel_id=1, source_target_pairs={{0,8},{8,0},{16,24},{24,16},{1,9},{9,1},{17,25},{25,17},{2,10},{10... | collective-permute-start | bytes 61448 | tf_op jit(solution)/shard_map/ppermute | solution.py:649
  33.2 4.4 %collective-permute-start.12 = (bf16[80,128]{1,0:T(8,128)(2,1)S(1)}, bf16[80,128]{1,0:T(8,128)(2,1)S(1)}, u32[]{:S(2)}, u32[]{:S(2)}) collective-permute-start(bf16[80,128]{1,0:T(8,128)(2,1)S(1)} %get-tuple-element.78), channel_id=1, source_target_pairs={{0,0},{8,16},{16,8},{24,24},{1,1},{9,17},{17,9},{25,25},{2,2},{10,... | collective-permute-start | bytes 61448 | tf_op jit(solution)/shard_map/ppermute | solution.py:649
  37.7 18.2 %copy-start.1 = (bf16[32,64,512]{2,1,0:T(8,128)(2,1)S(1)}, bf16[32,64,512]{2,1,0:T(8,128)(2,1)}, u32[]{:S(2)}) copy-start(bf16[32,64,512]{2,1,0:T(8,128)(2,1)} %fine_ref.4) | copy-start | bytes 6291460
  37.7 18.2 %copy-start.4 = (bf16[128,512]{1,0:T(8,128)(2,1)S(1)}, bf16[128,512]{1,0:T(8,128)(2,1)}, u32[]{:S(2)}) copy-start(bf16[128,512]{1,0:T(8,128)(2,1)} %w_ref.3) | copy-start | bytes 393220
  40.9 9.0 %collective-permute-start.17 = (bf16[256,128]{1,0:T(8,128)(2,1)S(1)}, bf16[256,128]{1,0:T(8,128)(2,1)S(1)}, u32[]{:S(2)}, u32[]{:S(2)}) collective-permute-start(bf16[256,128]{1,0:T(8,128)(2,1)S(1)} %get-tuple-element.89), channel_id=1, source_target_pairs={{0,5},{1,6},{2,7},{3,0},{4,1},{5,2},{6,3},{7,4},{8,13},{9,14},{10,... | collective-permute-start | bytes 196616 | tf_op jit(solution)/shard_map/ppermute | solution.py:639
  45.5 10.3 %collective-permute-start.18 = (bf16[256,128]{1,0:T(8,128)(2,1)S(1)}, bf16[256,128]{1,0:T(8,128)(2,1)S(1)}, u32[]{:S(2)}, u32[]{:S(2)}) collective-permute-start(bf16[256,128]{1,0:T(8,128)(2,1)S(1)} %get-tuple-element.90), channel_id=1, source_target_pairs={{0,4},{1,5},{2,6},{3,7},{4,0},{5,1},{6,2},{7,3},{8,12},{9,13},{10,... | collective-permute-start | bytes 196616 | tf_op jit(solution)/shard_map/ppermute | solution.py:639
  47.0 8.8 %collective-permute-start.19 = (bf16[256,128]{1,0:T(8,128)(2,1)S(1)}, bf16[256,128]{1,0:T(8,128)(2,1)S(1)}, u32[]{:S(2)}, u32[]{:S(2)}) collective-permute-start(bf16[256,128]{1,0:T(8,128)(2,1)S(1)} %get-tuple-element.91), channel_id=1, source_target_pairs={{0,3},{1,4},{2,5},{3,6},{4,7},{5,0},{6,1},{7,2},{8,11},{9,12},{10,... | collective-permute-start | bytes 196616 | tf_op jit(solution)/shard_map/ppermute | solution.py:639
  47.0 11.0 %collective-permute-start.13 = (bf16[256,128]{1,0:T(8,128)(2,1)S(1)}, bf16[256,128]{1,0:T(8,128)(2,1)S(1)}, u32[]{:S(2)}, u32[]{:S(2)}) collective-permute-start(bf16[256,128]{1,0:T(8,128)(2,1)S(1)} %get-tuple-element.85), channel_id=1, source_target_pairs={{0,2},{1,3},{2,4},{3,5},{4,6},{5,7},{6,0},{7,1},{8,10},{9,11},{10,... | collective-permute-start | bytes 196616 | tf_op jit(solution)/shard_map/ppermute | solution.py:639
  48.4 9.6 %collective-permute-start.14 = (bf16[256,128]{1,0:T(8,128)(2,1)S(1)}, bf16[256,128]{1,0:T(8,128)(2,1)S(1)}, u32[]{:S(2)}, u32[]{:S(2)}) collective-permute-start(bf16[256,128]{1,0:T(8,128)(2,1)S(1)} %get-tuple-element.86), channel_id=1, source_target_pairs={{0,1},{1,2},{2,3},{3,4},{4,5},{5,6},{6,7},{7,0},{8,9},{9,10},{10,1... | collective-permute-start | bytes 196616 | tf_op jit(solution)/shard_map/ppermute | solution.py:639
  49.9 9.3 %collective-permute-start.15 = (bf16[256,128]{1,0:T(8,128)(2,1)S(1)}, bf16[256,128]{1,0:T(8,128)(2,1)S(1)}, u32[]{:S(2)}, u32[]{:S(2)}) collective-permute-start(bf16[256,128]{1,0:T(8,128)(2,1)S(1)} %get-tuple-element.87), channel_id=1, source_target_pairs={{0,7},{1,0},{2,1},{3,2},{4,3},{5,4},{6,5},{7,6},{8,15},{9,8},{10,9... | collective-permute-start | bytes 196616 | tf_op jit(solution)/shard_map/ppermute | solution.py:639
  55.8 5.2 %collective-permute-start.16 = (bf16[256,128]{1,0:T(8,128)(2,1)S(1)}, bf16[256,128]{1,0:T(8,128)(2,1)S(1)}, u32[]{:S(2)}, u32[]{:S(2)}) collective-permute-start(bf16[256,128]{1,0:T(8,128)(2,1)S(1)} %get-tuple-element.88), channel_id=1, source_target_pairs={{0,6},{1,7},{2,0},{3,1},{4,2},{5,3},{6,4},{7,5},{8,14},{9,15},{10,... | collective-permute-start | bytes 196616 | tf_op jit(solution)/shard_map/ppermute | solution.py:639

commit v8 on v6

--- a/solution.py
+++ b/solution.py
@@ -14,13 +14,11 @@
 COLS = 8
 WIDE = SIDE + 4
 HID = SIDE + 2
-EARLY = ((1, 3), (4, 4), (8, 4))
+EARLY = ((1, 3), (4, 4))
+LATER = ((8, 4),)
 LATE = ((12, 3),)
-EARLY_PLANES = 11
 LATE_PLANES = 3
-FIRST_SENT = (4,)
-LAST_SENT = (3, 5, 2, 6, 1, 7)
-RETURNED = (1, 7, 6, 4, 2, 3, 5)
+SENT = (4, 3, 5, 2, 6, 1, 7)
 UP_OFFSETS = 4
 DOWN_LIMIT = 62 * 1024 * 1024
 VMEM_LIMIT = 24 * 1024 * 1024
@@ -355,7 +353,7 @@
     return left + wide[:, :, width : 2 * width] + right
 
 
-def conv_planes(here_ref, next_ref, wide_ref, first, planes, rows):
+def plane_taps(here_ref, next_ref, first, planes, rows):
     taps = []
     for dd in range(3):
         span = slice(first + dd, first + dd + planes)
@@ -365,7 +363,11 @@
             here_ref[span, 16 : rows + 16, :],
         ]
     lhs = jnp.concatenate(taps, axis=2)
-    return multiply_taps(lhs.reshape(planes * rows, lhs.shape[2]), wide_ref)
+    return lhs.reshape(planes * rows, lhs.shape[2])
+
+
+def conv_planes(here_ref, next_ref, wide_ref, first, planes, rows):
+    return multiply_taps(plane_taps(here_ref, next_ref, first, planes, rows), wide_ref)
 
 
 def activate(value, flags):
@@ -398,8 +400,8 @@
         ).astype(jnp.bfloat16)
 
 
-def inner_kernel(source_ref, block_ref, wide1_ref, hidden_ref, here, moved):
-    inner_planes(source_ref, block_ref, wide1_ref, hidden_ref, here, moved, EARLY)
+def inner_kernel(groups, source_ref, block_ref, wide1_ref, hidden_ref, here, moved):
+    inner_planes(source_ref, block_ref, wide1_ref, hidden_ref, here, moved, groups)
 
 
 def conv_cost(rows, width):
@@ -408,162 +410,183 @@
     )
 
 
-def inner_call(source, block, wide1):
+def inner_call(source, block, wide1, groups):
     mid = block.shape[1]
     smem = pl.BlockSpec(memory_space=pltpu.SMEM)
     vmem = pl.BlockSpec(memory_space=pltpu.VMEM)
     rows = (SIDE - 2) * COLS
+    planes = sum(count for _, count in groups)
     return pl.pallas_call(
-        inner_kernel,
+        functools.partial(inner_kernel, groups),
         in_specs=[smem, vmem, vmem],
         out_specs=vmem,
-        out_shape=jax.ShapeDtypeStruct((EARLY_PLANES, rows, mid), jnp.bfloat16),
-        scratch_shapes=[pltpu.VMEM((EARLY_PLANES + 2, SIDE * COLS, mid), jnp.bfloat16)] * 2,
+        out_shape=jax.ShapeDtypeStruct((planes, rows, mid), jnp.bfloat16),
+        scratch_shapes=[pltpu.VMEM((planes + 2, SIDE * COLS, mid), jnp.bfloat16)] * 2,
         compiler_params=pltpu.CompilerParams(vmem_limit_bytes=VMEM_LIMIT),
-        cost_estimate=conv_cost(EARLY_PLANES * rows, mid),
+        cost_estimate=conv_cost(planes * rows, mid),
         name="inner",
     )(source, block, wide1)
 
 
-def side_kernel(
-    source_ref,
-    block_ref,
-    before_ref,
-    after_ref,
-    wide1_ref,
-    hidden_ref,
-    late_ref,
-    mixed,
-    here,
-    moved,
-):
-    inner_planes(source_ref, block_ref, wide1_ref, late_ref, here, moved, LATE)
+def side_taps(low, high):
+    mixed = as_tiles(
+        jnp.concatenate(
+            [as_rows(low).reshape(-1, 2, COLS, 128)[:, 1:], as_rows(high).reshape(-1, 2, COLS, 128)[:, :1]],
+            axis=1,
+        ).reshape(-1, COLS, 128)
+    )
+    return low, mixed, high
+
+
+def depth_taps(taps, planes):
+    parts = [tap[dd * 16 : (dd + planes) * 16] for dd in range(3) for tap in taps]
+    return jnp.concatenate(parts, axis=1)
+
+
+def coarse_rows(source_ref, block_ref, value, depth_brick):
     width = block_ref.shape[1]
-    for d in range(SIDE):
-        edge = slice(d * 16, (d + 1) * 16)
-        low = as_rows(block_ref[d * 128 : d * 128 + 16])
-        high = as_rows(block_ref[d * 128 + 112 : d * 128 + 128])
-        before = as_rows(before_ref[edge])
-        after = as_rows(after_ref[edge])
-        mixed[0, edge] = as_tiles(jnp.concatenate([before[1:], low[:1]], axis=0))
-        mixed[1, edge] = as_tiles(jnp.concatenate([high[1:], after[:1]], axis=0))
+    value = value.reshape(4, SIDE, COLS, width)
+    rows = slice(depth_brick * 512, (depth_brick + 1) * 512)
+    own = block_ref[rows].astype(jnp.float32).reshape(4, SIDE, COLS, width)
+    flags = [slot_flags(source_ref, slot_index(depth_brick, r)) for r in range(4)]
+    return (value + own) * spread_flags(flags, (4, 4, 4, 4))[None]
+
+
+def middle_kernel(source_ref, *refs):
+    block_ref, before_ref, after_ref, early_ref, later_ref, wide1_ref, wide2_ref = refs[:7]
+    h_here, h_next, coarse_ref, side, late, here, moved = refs[7:]
+    width = block_ref.shape[1]
     inner = SIDE - 2
-    taps = []
-    for dd in range(3):
-        span = slice(dd * 16, (dd + inner) * 16)
-        low = [block_ref[(d + dd) * 128 : (d + dd) * 128 + 16] for d in range(inner)]
-        high = [block_ref[(d + dd) * 128 + 112 : (d + dd) * 128 + 128] for d in range(inner)]
-        taps.append(jnp.concatenate([before_ref[span]] + high, axis=0))
-        taps.append(jnp.concatenate([mixed[0, span], mixed[1, span]], axis=0))
-        taps.append(jnp.concatenate(low + [after_ref[span]], axis=0))
-    value = multiply_taps(jnp.concatenate(taps, axis=1), wide1_ref)
+    inner_planes(source_ref, block_ref, wide1_ref, late, here, moved, LATE)
+
+    low = jnp.concatenate([block_ref[d * 128 : d * 128 + 16] for d in range(SIDE)], axis=0)
+    high = jnp.concatenate([block_ref[d * 128 + 112 : d * 128 + 128] for d in range(SIDE)], axis=0)
+    left = depth_taps(side_taps(before_ref[0:256], low), inner)
+    right = depth_taps(side_taps(high, after_ref[0:256]), inner)
+    value = multiply_taps(jnp.concatenate([left, right], axis=0), wide1_ref)
     depths = (3, 4, 4, 3)
     edge_flags = (as_rows(before_ref[256:288]), as_rows(after_ref[256:288]))
     flags = []
-    for side, row_brick in ((0, 0), (1, 3)):
+    for end, row_brick in ((0, 0), (1, 3)):
         own = [slot_flags(source_ref, slot_index(d, row_brick)) for d in range(4)]
-        pairs = [jnp.stack([edge_flags[side][d], own[d]][:: 1 - 2 * side], axis=0) for d in range(4)]
+        pairs = [jnp.stack([edge_flags[end][d], own[d]][:: 1 - 2 * end], axis=0) for d in range(4)]
         flags.append(spread_flags(pairs, depths))
-    flags = jnp.stack(flags, axis=0)
-    value = activate(value.reshape(2, inner, 2, COLS, width), flags)
-    hidden_ref[...] = value.reshape(2, inner, 16, width).astype(jnp.bfloat16)
-
-
-def side_call(source, block, before, after, wide1):
+    value = activate(value.reshape(2, inner, 2, COLS, width), jnp.stack(flags, axis=0))
+    side[...] = value.reshape(2, inner, 16, width).astype(jnp.bfloat16)
+    centres = [ref[k] for ref in (early_ref, later_ref, late) for k in range(ref.shape[0])]
+    for d in range(inner):
+        plane = jnp.concatenate([side[0, d], centres[d], side[1, d]], axis=0)
+        h_here[d] = plane
+        h_next[d] = as_tiles(moved_rows(as_rows(plane)))
+
+    for depth_brick in (1, 2):
+        value = conv_planes(h_here, h_next, wide2_ref, depth_brick * 4 - 2, 4, SIDE * COLS)
+        value = coarse_rows(source_ref, block_ref, value, depth_brick)
+        rows = slice((depth_brick - 1) * 512, depth_brick * 512)
+        coarse_ref[rows] = value.reshape(512, width).astype(jnp.bfloat16)
+
+
+def middle_call(source, block, before, after, early, later, wide1, wide2):
     mid = block.shape[1]
     smem = pl.BlockSpec(memory_space=pltpu.SMEM)
     vmem = pl.BlockSpec(memory_space=pltpu.VMEM)
     inner = SIDE - 2
+    hidden = (inner, HID * COLS, mid)
     return pl.pallas_call(
-        side_kernel,
-        in_specs=[smem] + [vmem] * 4,
-        out_specs=[vmem] * 2,
+        middle_kernel,
+        in_specs=[smem] + [vmem] * 7,
+        out_specs=[vmem] * 3,
         out_shape=[
-            jax.ShapeDtypeStruct((2, inner, 16, mid), jnp.bfloat16),
-            jax.ShapeDtypeStruct((LATE_PLANES, inner * COLS, mid), jnp.bfloat16),
+            jax.ShapeDtypeStruct(shape, jnp.bfloat16) for shape in (hidden, hidden, (1024, mid))
         ],
         scratch_shapes=[
-            pltpu.VMEM((2, SIDE * 16, mid), jnp.bfloat16),
+            pltpu.VMEM((2, inner, 16, mid), jnp.bfloat16),
+            pltpu.VMEM((LATE_PLANES, inner * COLS, mid), jnp.bfloat16),
             pltpu.VMEM((LATE_PLANES + 2, SIDE * COLS, mid), jnp.bfloat16),
             pltpu.VMEM((LATE_PLANES + 2, SIDE * COLS, mid), jnp.bfloat16),
         ],
         compiler_params=pltpu.CompilerParams(vmem_limit_bytes=VMEM_LIMIT),
-        cost_estimate=conv_cost(inner * (4 + LATE_PLANES) * COLS, mid),
-        name="side",
-    )(source, block, before, after, wide1)
+        cost_estimate=conv_cost(inner * (4 + LATE_PLANES) * COLS + 1024, mid),
+        name="middle",
+    )(source, block, before, after, early, later, wide1, wide2)
+
+
+def scatter_bricks(source_ref, stage, value, depth_brick):
+    width = value.shape[3]
+    half = low_half((4, 2, COLS, width))
+    for r in range(4):
+        part = value[:, r * 4 : (r + 1) * 4].reshape(4, 2, 2, COLS, width)
+        even, odd = part[:, :, 0], part[:, :, 1]
+        b0 = jnp.where(half, even, pltpu.roll(odd, 4, 2))
+        b1 = jnp.where(half, pltpu.roll(even, 4, 2), odd)
+        slot = slot_index(depth_brick, r)
+        for k, brick in enumerate((b0, b1)):
+            source = source_ref[slot + k]
+            row = pl.multiple_of(jnp.where(source >= 0, source, K * CAP) * CELLS, CELLS)
+            stage[pl.ds(row, CELLS), :] = brick.reshape(CELLS, width).astype(jnp.bfloat16)
 
 
 def final_kernel(count, base_ref, source_ref, *refs):
     block_ref, before_ref, after_ref, even_ref, odd_ref = refs[:5]
-    early_ref, late_ref, side_ref, wide1_ref, wide2_ref, coarse_ref = refs[5:11]
+    mid_here, mid_next, mid_ref, wide1_ref, wide2_ref, coarse_ref = refs[5:11]
     backs = refs[11 : 11 + K]
     x_here, x_next, h_here, h_next, stage, under_ref, over_ref = refs[11 + K :]
+    width = block_ref.shape[1]
+    stage[...] = jnp.zeros(stage.shape, jnp.bfloat16)
     face_in(base_ref[1], count, even_ref, odd_ref, under_ref, over_ref)
-    width = block_ref.shape[1]
     flags_before = as_rows(before_ref[256:288])
     flags_after = as_rows(after_ref[256:288])
+    spread = []
     for end, ref in ((0, under_ref), (1, over_ref)):
-        planes = []
-        own = [0, 1] if end == 0 else [SIDE - 2, SIDE - 1]
-        for d in own:
+        own = []
+        for d in (0, 1) if end == 0 else (SIDE - 2, SIDE - 1):
             edge = slice(d * 16, (d + 1) * 16)
-            planes.append(
+            own.append(
                 jnp.concatenate(
                     [before_ref[edge], block_ref[d * 128 : (d + 1) * 128], after_ref[edge]], axis=0
                 )
             )
         far = [ref[k * 160 : (k + 1) * 160] for k in range(2)]
-        for index, plane in enumerate(far + planes if end == 0 else planes + far):
-            x_here[index] = plane
-            x_next[index] = as_tiles(moved_rows(as_rows(plane)))
-        value = conv_planes(x_here, x_next, wide1_ref, 0, 2, HID * COLS)
-        value = value.reshape(2, HID, COLS, width)
+        for index, plane in enumerate(far + own if end == 0 else own + far):
+            x_here[end * 4 + index] = plane
+            x_next[end * 4 + index] = as_tiles(moved_rows(as_rows(plane)))
         far_flags = as_rows(ref[320:368])
         brick = 0 if end == 0 else 3
         own_flags = [flags_before[brick]]
         own_flags += [slot_flags(source_ref, slot_index(brick, r)) for r in range(4)]
         own_flags += [flags_after[brick]]
-        spread = [
+        pair = [
             spread_flags([far_flags[r] for r in range(6)], (1, 4, 4, 4, 4, 1)),
             spread_flags(own_flags, (1, 4, 4, 4, 4, 1)),
         ]
-        for k in range(2):
-            flags = spread[k if end == 0 else 1 - k]
-            rows = activate(value[k], flags)
-            index = k if end == 0 else HID - 2 + k
-            h_here[index] = as_tiles(rows)
-            h_next[index] = as_tiles(moved_rows(rows))
-    for d in range(SIDE - 2):
-        middle = early_ref[d] if d < EARLY_PLANES else late_ref[d - EARLY_PLANES]
-        plane = jnp.concatenate([side_ref[0, d], middle, side_ref[1, d]], axis=0)
-        h_here[d + 2] = plane
-        h_next[d + 2] = as_tiles(moved_rows(as_rows(plane)))
-
-    stage[...] = jnp.zeros(stage.shape, jnp.bfloat16)
-    for depth_brick in range(4):
-        value = conv_planes(h_here, h_next, wide2_ref, depth_brick * 4, 4, SIDE * COLS)
-        value = value.reshape(4, SIDE, COLS, width)
+        spread += pair if end == 0 else pair[::-1]
+    lhs = [plane_taps(x_here, x_next, first, 2, HID * COLS) for first in (0, 4)]
+    value = multiply_taps(jnp.concatenate(lhs, axis=0), wide1_ref)
+    value = activate(value.reshape(4, HID, COLS, width), jnp.stack(spread, axis=0))
+    for k, index in enumerate((0, 1, 10, 11)):
+        h_here[index] = as_tiles(value[k])
+        h_next[index] = as_tiles(moved_rows(value[k]))
+    for k in range(4):
+        for index, source in ((2 + k, k), (6 + k, SIDE - 6 + k)):
+            h_here[index] = mid_here[source]
+            h_next[index] = mid_next[source]
+    for depth_brick in (1, 2):
+        rows = slice((depth_brick - 1) * 512, depth_brick * 512)
+        done = mid_ref[rows]
+        coarse_ref[depth_brick * 512 : (depth_brick + 1) * 512] = done
+        done = done.astype(jnp.float32).reshape(4, SIDE, COLS, width)
+        scatter_bricks(source_ref, stage, done, depth_brick)
+    for depth_brick in (0, 3):
+        value = conv_planes(h_here, h_next, wide2_ref, depth_brick * 2, 4, SIDE * COLS)
+        value = coarse_rows(source_ref, block_ref, value, depth_brick)
         rows = slice(depth_brick * 512, (depth_brick + 1) * 512)
-        own = block_ref[rows].astype(jnp.float32).reshape(4, SIDE, COLS, width)
-        flags = [slot_flags(source_ref, slot_index(depth_brick, r)) for r in range(4)]
-        value = (value + own) * spread_flags(flags, (4, 4, 4, 4))[None]
-        coarse_ref[rows] = value.reshape(4 * SIDE * COLS, width).astype(jnp.bfloat16)
-        half = low_half((4, 2, COLS, width))
-        for r in range(4):
-            part = value[:, r * 4 : (r + 1) * 4].reshape(4, 2, 2, COLS, width)
-            even, odd = part[:, :, 0], part[:, :, 1]
-            b0 = jnp.where(half, even, pltpu.roll(odd, 4, 2))
-            b1 = jnp.where(half, pltpu.roll(even, 4, 2), odd)
-            slot = slot_index(depth_brick, r)
-            for k, brick in enumerate((b0, b1)):
-                source = source_ref[slot + k]
-                row = pl.multiple_of(jnp.where(source >= 0, source, K * CAP) * CELLS, CELLS)
-                stage[pl.ds(row, CELLS), :] = brick.reshape(CELLS, width).astype(jnp.bfloat16)
+        coarse_ref[rows] = value.reshape(512, width).astype(jnp.bfloat16)
+        scatter_bricks(source_ref, stage, value, depth_brick)
     for j in range(K):
         backs[j][...] = stage[j * CAP * CELLS : (j + 1) * CAP * CELLS]
 
 
-def final_call(count, base, source, block, halo, hidden, wide1, wide2):
+def final_call(count, base, source, block, halo, middle, wide1, wide2):
     mid = block.shape[1]
     smem = pl.BlockSpec(memory_space=pltpu.SMEM)
     vmem = pl.BlockSpec(memory_space=pltpu.VMEM)
@@ -571,23 +594,21 @@
         functools.partial(final_kernel, count),
         in_specs=[smem, smem] + [vmem] * 10,
         out_specs=[vmem] * (1 + K),
-        out_shape=[
-            jax.ShapeDtypeStruct(block.shape, jnp.bfloat16),
-        ]
+        out_shape=[jax.ShapeDtypeStruct(block.shape, jnp.bfloat16)]
         + [jax.ShapeDtypeStruct((CAP * CELLS, mid), jnp.bfloat16)] * K,
         scratch_shapes=[
-            pltpu.VMEM((4, WIDE * COLS, mid), jnp.bfloat16),
-            pltpu.VMEM((4, WIDE * COLS, mid), jnp.bfloat16),
-            pltpu.VMEM((HID, HID * COLS, mid), jnp.bfloat16),
-            pltpu.VMEM((HID, HID * COLS, mid), jnp.bfloat16),
+            pltpu.VMEM((8, WIDE * COLS, mid), jnp.bfloat16),
+            pltpu.VMEM((8, WIDE * COLS, mid), jnp.bfloat16),
+            pltpu.VMEM((12, HID * COLS, mid), jnp.bfloat16),
+            pltpu.VMEM((12, HID * COLS, mid), jnp.bfloat16),
             pltpu.VMEM(((K * CAP + 1) * CELLS, mid), jnp.bfloat16),
             pltpu.VMEM((368, mid), jnp.bfloat16),
             pltpu.VMEM((368, mid), jnp.bfloat16),
         ],
         compiler_params=pltpu.CompilerParams(vmem_limit_bytes=VMEM_LIMIT),
-        cost_estimate=conv_cost(SIDE * SIDE * COLS, mid),
+        cost_estimate=conv_cost(1600, mid),
         name="final",
-    )(base, source, block, *halo, *hidden, wide1, wide2)
+    )(base, source, block, *halo, *middle, wide1, wide2)
 
 
 def from_behind(value, axis, steps):
@@ -596,52 +617,42 @@
     return lax.ppermute(value, axis, pairs)
 
 
-def swap_faces(even, odd, axis):
+def swap_face(face, axis, first):
     count = lax.axis_size(axis)
-    swapped = []
-    for face, first in ((even, 0), (odd, 1)):
-        partner = list(range(count))
-        for i in range(first, count - 1, 2):
-            partner[i], partner[i + 1] = i + 1, i
-        swapped.append(lax.ppermute(face, axis, list(enumerate(partner))))
-    return swapped
+    partner = list(range(count))
+    for i in range(first, count - 1, 2):
+        partner[i], partner[i + 1] = i + 1, i
+    return lax.ppermute(face, axis, list(enumerate(partner)))
 
 
 def shards(fine, fine_mask, slot_source, w_down, w_first, w_second, w_up):
     mid = w_down.shape[1]
     base = jnp.stack([lax.axis_index("xy"), lax.axis_index("gz")]).astype(jnp.int32)
     counts = (lax.axis_size("gz"), lax.axis_size("xy"))
-    sent = down_call(fine, fine_mask, w_down, FIRST_SENT)
-    arrived = {j: from_behind(sent[j], "xy", j) for j in FIRST_SENT}
-    fine_again, sent[FIRST_SENT[0]] = lax.optimization_barrier((fine, sent[FIRST_SENT[0]]))
-    sent = down_call(fine_again, fine_mask, w_down, LAST_SENT)
-    arrived.update({j: from_behind(sent[j], "xy", j) for j in LAST_SENT})
-    middle = LAST_SENT[1]
-    later = (arrived[middle], fine, fine_mask, w_down, w_first, w_second)
-    arrived[middle], *later = lax.optimization_barrier(later)
+    sent = down_call(fine, fine_mask, w_down, SENT)
+    arrived = {j: from_behind(sent[j], "xy", j) for j in SENT}
+    later = (arrived[SENT[2]], fine, fine_mask, w_down, w_first, w_second)
+    arrived[SENT[2]], *later = lax.optimization_barrier(later)
     prepared = lax.optimization_barrier(tuple(prepare_call(*later)))
     arrived[0], mask, wide1, wide2 = prepared
     block, even, odd = place_call(base, slot_source, [arrived[j] for j in range(K)])
-    even, odd = swap_faces(even, odd, "xy")
-    early = inner_call(slot_source, block, wide1)
-    even, odd, early = lax.optimization_barrier((even, odd, early))
+    odd = swap_face(odd, "xy", 1)
+    early = inner_call(slot_source, block, wide1, EARLY)
+    even, early = lax.optimization_barrier((even, early))
+    even = swap_face(even, "xy", 0)
+    later = inner_call(slot_source, block, wide1, LATER)
+    even, odd, later = lax.optimization_barrier((even, odd, later))
     before, after, even, odd = edge_call(counts, base, slot_source, block, even, odd)
-    even, odd = swap_faces(even, odd, "gz")
-    side, late = side_call(slot_source, block, before, after, wide1)
+    even = swap_face(even, "gz", 0)
+    odd = swap_face(odd, "gz", 1)
+    middle = middle_call(slot_source, block, before, after, early, later, wide1, wide2)
     coarse, *back = final_call(
-        counts[0],
-        base,
-        slot_source,
-        block,
-        (before, after, even, odd),
-        (early, late, side),
-        wide1,
-        wide2,
+        counts[0], base, slot_source, block, (before, after, even, odd), middle, wide1, wide2
     )
-    octant = {j: from_behind(back[j], "xy", -j) for j in RETURNED}
+    octant = {j: from_behind(back[j], "xy", -j) for j in SENT}
     octant[0] = back[0]
-    fine_out = up_call(fine, mask, w_up, [octant[j] for j in (6, 7, 0, 1)], 3, None)
-    fine_out = up_call(fine, mask, w_up, [octant[j] for j in (2, 3, 4, 5)], 1, fine_out)
+    fine_out = up_call(fine, mask, w_up, [octant[j] for j in (2, 3, 4, 5)], 1, None)
+    fine_out = up_call(fine, mask, w_up, [octant[j] for j in (6, 7, 0, 1)], 3, fine_out)
     return fine_out, coarse.reshape(SIDE, SIDE, COLS, mid)
 
 

time: 61.4 us -> 61.7 us (level)
  starting transfers between devices: 29.8 us -> 34.7 us
  waiting for transfers between devices: 8.86 us -> 4.43 us
    ppermute x14, waiting for transfers between devices: 8.77 us -> 3.42 us  [from_behind(): return lax.ppermute(value, axis, pairs)]
    ppermute x14, starting transfers between devices: 27.1 us -> 29.6 us  [from_behind(): return lax.ppermute(value, axis, pairs)]
    ppermute x4, starting transfers between devices: 2.7 us -> 5.11 us  [swap_face(): return lax.ppermute(face, axis, list(enumerate(partner)))]
    pallas_call x2 -> x3, Pallas kernels: 4.13 us -> 6.3 us  [the longest x1 3.22 us: middle_call(): pl.pallas_call(middle_kernel, in_specs=[smem] + [vmem] * 7, out_specs=[vm...]
    pallas_call x2 -> x1, Pallas kernels: 5.31 us -> 3.9 us  [down_call(): pl.pallas_call(functools.partial(down_kernel, offsets), in_specs=[hbm, hb...]
    pallas_call x1, Pallas kernels: 5.07 us -> 4.03 us  [final_call(): pl.pallas_call(functools.partial(final_kernel, count), in_specs=[smem, sm...]
    ppermute x4, waiting for transfers between devices: 0.09 us -> 1.01 us  [swap_face(): return lax.ppermute(face, axis, list(enumerate(partner)))]
  transfers between devices with their start and end apart: 18 -> 18, of which waited for: 5 -> 4; matrix products, arithmetic and copies ran while one was open for 0% -> 0% of each run, Pallas kernels for 16% -> 14%
where the time goes in v8:
time: 61.7 us; the launch traced here: 61.4 us
  starting transfers between devices  34.7 us (56%)
  Pallas kernels  19.7 us (32%)
  waiting for transfers between devices  4.43 us (7%)
  local copies, waits for them, and re-layouts  1.62 us (3%)
  between operations  0.83 us (1%)
    ppermute x14, starting transfers between devices, from_behind(): return lax.ppermute(value, axis, pairs)  29.6 us
    ppermute x4, starting transfers between devices, swap_face(): return lax.ppermute(face, axis, list(enumerate(partner)))  5.11 us
    pallas_call x1, Pallas kernels, final_call(): pl.pallas_call(functools.partial(final_kernel, count), in_specs=[smem, sm...  4.03 us
    pallas_call x1, Pallas kernels, down_call(): pl.pallas_call(functools.partial(down_kernel, offsets), in_specs=[hbm, hb...  3.9 us
    ppermute x14, waiting for transfers between devices, from_behind(): return lax.ppermute(value, axis, pairs)  3.42 us
    pallas_call x1, Pallas kernels, middle_call(): pl.pallas_call(middle_kernel, in_specs=[smem] + [vmem] * 7, out_specs=[vm...  3.22 us
    pallas_call x2, Pallas kernels, inner_call(): pl.pallas_call(functools.partial(inner_kernel, groups), in_specs=[smem, v...  3.07 us
    pallas_call x2, Pallas kernels, up_call(): pl.pallas_call(up_kernel, grid=(UP_OFFSETS * CAP // step,), in_specs=[pl....  3.02 us
  transfers between devices with their start and end apart: 18, of which 4 were waited for; matrix products, arithmetic and copies ran while one was open for 0% of the time, Pallas kernels for 14%

profile of v8, /device:TPU:0, one launch (start us, length us, event | category | flops | bytes accessed | tf_op | source)
XLA Modules:
  0.0 61.4 jit_solution(13719499214221512496)
XLA Ops:
  0.7 3.9 %down.1 = (bf16[256,128]{1,0:T(8,128)(2,1)}, bf16[256,128]{1,0:T(8,128)(2,1)}, bf16[256,128]{1,0:T(8,128)(2,1)}, bf16[256,128]{1,0:T(8,128)(2,1)}, bf16[256,128]...) custom-call(bf16[32,64,512]{2,1,0:T(8,128)(2,1)} %fine_ref.4, s32[32,512]{1,0:T(8,128)} %mask_ref, ...), custom_call_target="tpu_custom_call" | custom-call | flops 234881024 | bytes 1835008 | tf_op jit(solution)/shard_map/down/pallas_call | solution.py:83
  4.6 5.0 %collective-permute-start = (bf16[256,128]{1,0:T(8,128)(2,1)}, bf16[256,128]{1,0:T(8,128)(2,1)S(1)}, u32[]{:S(2)}, u32[]{:S(2)}) collective-permute-start(bf16[256,128]{1,0:T(8,128)(2,1)} %get-tuple-element.43), channel_id=1, source_target_pairs={{0,5},{1,6},{2,7},{3,0},{4,1},{5,2},{6,3},{7,4},{8,13},{9,14},{10,... | collective-permute-start | bytes 196616 | tf_op jit(solution)/shard_map/ppermute | solution.py:617
  9.6 1.5 %collective-permute-start.1 = (bf16[256,128]{1,0:T(8,128)(2,1)}, bf16[256,128]{1,0:T(8,128)(2,1)S(1)}, u32[]{:S(2)}, u32[]{:S(2)}) collective-permute-start(bf16[256,128]{1,0:T(8,128)(2,1)} %get-tuple-element.51), channel_id=1, source_target_pairs={{0,1},{1,2},{2,3},{3,4},{4,5},{5,6},{6,7},{7,0},{8,9},{9,10},{10,1... | collective-permute-start | bytes 196616 | tf_op jit(solution)/shard_map/ppermute | solution.py:617
  11.2 1.8 %collective-permute-start.3 = (bf16[256,128]{1,0:T(8,128)(2,1)}, bf16[256,128]{1,0:T(8,128)(2,1)S(1)}, u32[]{:S(2)}, u32[]{:S(2)}) collective-permute-start(bf16[256,128]{1,0:T(8,128)(2,1)} %get-tuple-element.53), channel_id=1, source_target_pairs={{0,3},{1,4},{2,5},{3,6},{4,7},{5,0},{6,1},{7,2},{8,11},{9,12},{10,... | collective-permute-start | bytes 196616 | tf_op jit(solution)/shard_map/ppermute | solution.py:617
  13.0 3.5 %collective-permute-start.4 = (bf16[256,128]{1,0:T(8,128)(2,1)}, bf16[256,128]{1,0:T(8,128)(2,1)S(1)}, u32[]{:S(2)}, u32[]{:S(2)}) collective-permute-start(bf16[256,128]{1,0:T(8,128)(2,1)} %get-tuple-element.54), channel_id=1, source_target_pairs={{0,4},{1,5},{2,6},{3,7},{4,0},{5,1},{6,2},{7,3},{8,12},{9,13},{10,... | collective-permute-start | bytes 196616 | tf_op jit(solution)/shard_map/ppermute | solution.py:617
  16.5 1.4 %collective-permute-start.5 = (bf16[256,128]{1,0:T(8,128)(2,1)}, bf16[256,128]{1,0:T(8,128)(2,1)S(1)}, u32[]{:S(2)}, u32[]{:S(2)}) collective-permute-start(bf16[256,128]{1,0:T(8,128)(2,1)} %get-tuple-element.56), channel_id=1, source_target_pairs={{0,6},{1,7},{2,0},{3,1},{4,2},{5,3},{6,4},{7,5},{8,14},{9,15},{10,... | collective-permute-start | bytes 196616 | tf_op jit(solution)/shard_map/ppermute | solution.py:617
  17.8 1.0 %collective-permute-start.6 = (bf16[256,128]{1,0:T(8,128)(2,1)}, bf16[256,128]{1,0:T(8,128)(2,1)S(1)}, u32[]{:S(2)}, u32[]{:S(2)}) collective-permute-start(bf16[256,128]{1,0:T(8,128)(2,1)} %get-tuple-element.57), channel_id=1, source_target_pairs={{0,7},{1,0},{2,1},{3,2},{4,3},{5,4},{6,5},{7,6},{8,15},{9,8},{10,9... | collective-permute-start | bytes 196616 | tf_op jit(solution)/shard_map/ppermute | solution.py:617
  18.9 0.1 pad_add_fusion.base_ref
  19.0 1.6 %copy-done = bf16[32,64,512]{2,1,0:T(8,128)(2,1)S(1)} copy-done((bf16[32,64,512]{2,1,0:T(8,128)(2,1)S(1)}, bf16[32,64,512]{2,1,0:T(8,128)(2,1)}, u32[]{:S(2)}) %copy-start) | copy-done | bytes 2097176
  20.6 1.1 %prepare.1 = (bf16[256,128]{1,0:T(8,128)(2,1)S(1)}, bf16[2048,512]{1,0:T(8,128)(2,1)S(1)}, bf16[1152,384]{1,0:T(8,128)(2,1)S(1)}, bf16[1152,384]{1,0:T(8,128)(2,1)S(1)}) custom-call(bf16[32,64,512]{2,1,0:T(8,128)(2,1)S(1)} %copy-done, s32[32,512]{1,0:T(8,128)S(1)} %copy-done.6, bf16[512,128]{1,0:T(8,128)(2,1)S(1)} %copy-done.5, ...), custom_call_target="tpu_custom_call" | custom-call | flops 268435456 | bytes 2097152 | tf_op jit(solution)/shard_map/prepare/pallas_call | solution.py:124
  21.6 0.8 %collective-permute-done.3.refs_3_ = bf16[256,128]{1,0:T(8,128)(2,1)S(1)} collective-permute-done((bf16[256,128]{1,0:T(8,128)(2,1)}, bf16[256,128]{1,0:T(8,128)(2,1)S(1)}, u32[]{:S(2)}, u32[]{:S(2)}) %collective-permute-start.3) | collective-permute-done | bytes 65568 | tf_op jit(solution)/shard_map/ppermute | solution.py:617
  22.5 0.3 collective-permute-done.6.refs_7_
  22.7 0.8 %place.1 = (bf16[2048,128]{1,0:T(8,128)(2,1)S(1)}, bf16[288,128]{1,0:T(8,128)(2,1)S(1)}, bf16[288,128]{1,0:T(8,128)(2,1)S(1)}) custom-call(s32[2]{0:T(128)S(1)} %pad_add_fusion.base_ref, s32[32]{0:T(128)S(1)} %copy-done.7, bf16[256,128]{1,0:T(8,128)(2,1)S(1)} %get-tuple-element.50.refs_0_, bf16[256,128]{1,0:T(8,128)(2,1)S(1)} %collective-permute-done.1.refs_1_, ...), custom_call_target="tpu_custom_call" | custom-call | tf_op jit(solution)/shard_map/place/pallas_call | solution.py:260
  23.5 0.7 %collective-permute-start.8 = (bf16[288,128]{1,0:T(8,128)(2,1)S(1)}, bf16[288,128]{1,0:T(8,128)(2,1)S(1)}, u32[]{:S(2)}, u32[]{:S(2)}) collective-permute-start(bf16[288,128]{1,0:T(8,128)(2,1)S(1)} %get-tuple-element.62), channel_id=1, source_target_pairs={{0,0},{1,2},{2,1},{3,4},{4,3},{5,6},{6,5},{7,7},{8,8},{9,10},{10,9... | collective-permute-start | bytes 221192 | tf_op jit(solution)/shard_map/ppermute | solution.py:625
  24.2 1.8 %inner.2.refs_3_ = bf16[7,112,128]{2,1,0:T(8,128)(2,1)S(1)} custom-call(s32[32]{0:T(128)S(1)} %copy-done.7, bf16[2048,128]{1,0:T(8,128)(2,1)S(1)} %get-tuple-element.58.block_ref.refs_0_, bf16[1152,384]{1,0:T(8,128)(2,1)S(1)} %get-tuple-element.60.wide1_ref.refs_5_.refs_8_), custom_call_target="tpu_custom_call" | custom-call | flops 693633024 | bytes 1769472 | tf_op jit(solution)/shard_map/inner/pallas_call | solution.py:419
  25.9 3.7 %collective-permute-start.7 = (bf16[288,128]{1,0:T(8,128)(2,1)S(1)}, bf16[288,128]{1,0:T(8,128)(2,1)S(1)}, u32[]{:S(2)}, u32[]{:S(2)}) collective-permute-start(bf16[288,128]{1,0:T(8,128)(2,1)S(1)} %get-tuple-element.61), channel_id=1, source_target_pairs={{0,1},{1,0},{2,3},{3,2},{4,5},{5,4},{6,7},{7,6},{8,9},{9,8},{10,11... | collective-permute-start | bytes 221192 | tf_op jit(solution)/shard_map/ppermute | solution.py:625
  29.7 1.3 %inner.3.refs_4_ = bf16[4,112,128]{2,1,0:T(8,128)(2,1)S(1)} custom-call(s32[32]{0:T(128)S(1)} %copy-done.7, bf16[2048,128]{1,0:T(8,128)(2,1)S(1)} %get-tuple-element.58.block_ref.refs_0_, bf16[1152,384]{1,0:T(8,128)(2,1)S(1)} %get-tuple-element.60.wide1_ref.refs_5_.refs_8_), custom_call_target="tpu_custom_call" | custom-call | flops 396361728 | bytes 1769472 | tf_op jit(solution)/shard_map/inner/pallas_call | solution.py:419
  31.0 1.0 %collective-permute-done.7.even_ref = bf16[288,128]{1,0:T(8,128)(2,1)S(1)} collective-permute-done((bf16[288,128]{1,0:T(8,128)(2,1)S(1)}, bf16[288,128]{1,0:T(8,128)(2,1)S(1)}, u32[]{:S(2)}, u32[]{:S(2)}) %collective-permute-start.7) | collective-permute-done | bytes 73760 | tf_op jit(solution)/shard_map/ppermute | solution.py:625
  32.0 0.6 %edge.1 = (bf16[288,128]{1,0:T(8,128)(2,1)S(1)}, bf16[288,128]{1,0:T(8,128)(2,1)S(1)}, bf16[368,128]{1,0:T(8,128)(2,1)S(1)}, bf16[368,128]{1,0:T(8,128)(2,1)S(1)}) custom-call(s32[2]{0:T(128)S(1)} %pad_add_fusion.base_ref, s32[32]{0:T(128)S(1)} %copy-done.7, bf16[2048,128]{1,0:T(8,128)(2,1)S(1)} %get-tuple-element.58.block_ref.refs_0_, ...), custom_call_target="tpu_custom_call" | custom-call | tf_op jit(solution)/shard_map/edge/pallas_call | solution.py:310
  32.7 0.7 %collective-permute-start.10 = (bf16[368,128]{1,0:T(8,128)(2,1)S(1)}, bf16[368,128]{1,0:T(8,128)(2,1)S(1)}, u32[]{:S(2)}, u32[]{:S(2)}) collective-permute-start(bf16[368,128]{1,0:T(8,128)(2,1)S(1)} %get-tuple-element.68), channel_id=1, source_target_pairs={{0,0},{8,16},{16,8},{24,24},{1,1},{9,17},{17,9},{25,25},{2,2},{10,... | collective-permute-start | bytes 282632 | tf_op jit(solution)/shard_map/ppermute | solution.py:625
  33.4 3.2 %middle.1 = (bf16[14,144,128]{2,1,0:T(8,128)(2,1)S(1)}, bf16[14,144,128]{2,1,0:T(8,128)(2,1)S(1)}, bf16[1024,128]{1,0:T(8,128)(2,1)S(1)}) custom-call(s32[32]{0:T(128)S(1)} %copy-done.7, bf16[2048,128]{1,0:T(8,128)(2,1)S(1)} %get-tuple-element.58.block_ref.refs_0_, bf16[288,128]{1,0:T(8,128)(2,1)S(1)} %get-tuple-element.65.refs_1_, ...), custom_call_target="tpu_custom_call" | custom-call | flops 1599602688 | bytes 1769472 | tf_op jit(solution)/shard_map/middle/pallas_call | solution.py:495
  36.7 4.0 %final.1 = (bf16[2048,128]{1,0:T(8,128)(2,1)}, bf16[256,128]{1,0:T(8,128)(2,1)S(1)}, bf16[256,128]{1,0:T(8,128)(2,1)S(1)}, bf16[256,128]{1,0:T(8,128)(2,1)S(1)},...) custom-call(s32[2]{0:T(128)S(1)} %pad_add_fusion.base_ref, ...), custom_call_target="tpu_custom_call" | custom-call | flops 1415577600 | bytes 1769472 | tf_op jit(solution)/shard_map/final/pallas_call | solution.py:593
  40.7 2.5 %collective-permute-start.14 = (bf16[256,128]{1,0:T(8,128)(2,1)S(1)}, bf16[256,128]{1,0:T(8,128)(2,1)S(1)}, u32[]{:S(2)}, u32[]{:S(2)}) collective-permute-start(bf16[256,128]{1,0:T(8,128)(2,1)S(1)} %get-tuple-element.79), channel_id=1, source_target_pairs={{0,6},{1,7},{2,0},{3,1},{4,2},{5,3},{6,4},{7,5},{8,14},{9,15},{10,... | collective-permute-start | bytes 196616 | tf_op jit(solution)/shard_map/ppermute | solution.py:617
  43.2 1.7 %collective-permute-start.15 = (bf16[256,128]{1,0:T(8,128)(2,1)S(1)}, bf16[256,128]{1,0:T(8,128)(2,1)S(1)}, u32[]{:S(2)}, u32[]{:S(2)}) collective-permute-start(bf16[256,128]{1,0:T(8,128)(2,1)S(1)} %get-tuple-element.80), channel_id=1, source_target_pairs={{0,5},{1,6},{2,7},{3,0},{4,1},{5,2},{6,3},{7,4},{8,13},{9,14},{10,... | collective-permute-start | bytes 196616 | tf_op jit(solution)/shard_map/ppermute | solution.py:617
  44.9 0.7 %collective-permute-start.16 = (bf16[256,128]{1,0:T(8,128)(2,1)S(1)}, bf16[256,128]{1,0:T(8,128)(2,1)S(1)}, u32[]{:S(2)}, u32[]{:S(2)}) collective-permute-start(bf16[256,128]{1,0:T(8,128)(2,1)S(1)} %get-tuple-element.81), channel_id=1, source_target_pairs={{0,4},{1,5},{2,6},{3,7},{4,0},{5,1},{6,2},{7,3},{8,12},{9,13},{10,... | collective-permute-start | bytes 196616 | tf_op jit(solution)/shard_map/ppermute | solution.py:617
  45.6 2.6 %collective-permute-start.17 = (bf16[256,128]{1,0:T(8,128)(2,1)S(1)}, bf16[256,128]{1,0:T(8,128)(2,1)S(1)}, u32[]{:S(2)}, u32[]{:S(2)}) collective-permute-start(bf16[256,128]{1,0:T(8,128)(2,1)S(1)} %get-tuple-element.82), channel_id=1, source_target_pairs={{0,3},{1,4},{2,5},{3,6},{4,7},{5,0},{6,1},{7,2},{8,11},{9,12},{10,... | collective-permute-start | bytes 196616 | tf_op jit(solution)/shard_map/ppermute | solution.py:617
  48.2 1.9 %collective-permute-start.11 = (bf16[256,128]{1,0:T(8,128)(2,1)S(1)}, bf16[256,128]{1,0:T(8,128)(2,1)S(1)}, u32[]{:S(2)}, u32[]{:S(2)}) collective-permute-start(bf16[256,128]{1,0:T(8,128)(2,1)S(1)} %get-tuple-element.75), channel_id=1, source_target_pairs={{0,2},{1,3},{2,4},{3,5},{4,6},{5,7},{6,0},{7,1},{8,10},{9,11},{10,... | collective-permute-start | bytes 196616 | tf_op jit(solution)/shard_map/ppermute | solution.py:617
  50.1 0.7 %collective-permute-start.12 = (bf16[256,128]{1,0:T(8,128)(2,1)S(1)}, bf16[256,128]{1,0:T(8,128)(2,1)S(1)}, u32[]{:S(2)}, u32[]{:S(2)}) collective-permute-start(bf16[256,128]{1,0:T(8,128)(2,1)S(1)} %get-tuple-element.76), channel_id=1, source_target_pairs={{0,1},{1,2},{2,3},{3,4},{4,5},{5,6},{6,7},{7,0},{8,9},{9,10},{10,1... | collective-permute-start | bytes 196616 | tf_op jit(solution)/shard_map/ppermute | solution.py:617
  50.8 5.3 %collective-permute-start.13 = (bf16[256,128]{1,0:T(8,128)(2,1)S(1)}, bf16[256,128]{1,0:T(8,128)(2,1)S(1)}, u32[]{:S(2)}, u32[]{:S(2)}) collective-permute-start(bf16[256,128]{1,0:T(8,128)(2,1)S(1)} %get-tuple-element.78), channel_id=1, source_target_pairs={{0,7},{1,0},{2,1},{3,2},{4,3},{5,4},{6,5},{7,6},{8,15},{9,8},{10,9... | collective-permute-start | bytes 196616 | tf_op jit(solution)/shard_map/ppermute | solution.py:617
  56.0 2.3 %collective-permute-done.17.refs_3_ = bf16[256,128]{1,0:T(8,128)(2,1)S(1)} collective-permute-done((bf16[256,128]{1,0:T(8,128)(2,1)S(1)}, bf16[256,128]{1,0:T(8,128)(2,1)S(1)}, u32[]{:S(2)}, u32[]{:S(2)}) %collective-permute-start.17) | collective-permute-done | bytes 65568 | tf_op jit(solution)/shard_map/ppermute | solution.py:617
  58.4 1.5 %up.2.refs_4_ = bf16[32,64,512]{2,1,0:T(8,128)(2,1)} custom-call(bf16[32,64,512]{2,1,0:T(8,128)(2,1)S(1)} %copy-done.1, bf16[2048,512]{1,0:T(8,128)(2,1)S(1)} %get-tuple-element.49.mask_ref, bf16[128,512]{1,0:T(8,128)(2,1)S(1)} %copy-done.4, bf16[256,128]{1,0:T(8,128)(2,1)S(1)} %collective-permute-done.14.refs_0_, ...), custom_call_target="tpu_custom_call" | custom-call | flops 134217728 | bytes 2097152 | tf_op jit(solution)/shard_map/up/pallas_call | solution.py:171
  59.9 1.5 %up.3 = bf16[32,64,512]{2,1,0:T(8,128)(2,1)} custom-call(bf16[32,64,512]{2,1,0:T(8,128)(2,1)S(1)} %copy-done.1, bf16[2048,512]{1,0:T(8,128)(2,1)S(1)} %get-tuple-element.49.mask_ref, bf16[128,512]{1,0:T(8,128)(2,1)S(1)} %copy-done.4, bf16[256,128]{1,0:T(8,128)(2,1)S(1)} %collective-permute-done.11.refs_0_, ...), custom_call_target="tpu_custom_call", output_to_operand_aliasing={{}: (7, {})} | custom-call | flops 134217728 | bytes 2097152 | tf_op jit(solution)/shard_map/up/pallas_call | solution.py:171
  (31 shorter events, 0.2 us)
Async XLA Ops:
  0.6 18.3 %copy-start.5 = (bf16[512,128]{1,0:T(8,128)(2,1)S(1)}, bf16[512,128]{1,0:T(8,128)(2,1)}, u32[]{:S(2)}) copy-start(bf16[512,128]{1,0:T(8,128)(2,1)} %w_down_ref) | copy-start | bytes 393220
  0.6 18.3 %copy-start.6 = (s32[32,512]{1,0:T(8,128)S(1)}, s32[32,512]{1,0:T(8,128)}, u32[]{:S(2)}) copy-start(s32[32,512]{1,0:T(8,128)} %mask_ref) | copy-start | bytes 196612
  0.7 18.3 %copy-start.3 = (bf16[27,128,128]{2,1,0:T(8,128)(2,1)S(1)}, bf16[27,128,128]{2,1,0:T(8,128)(2,1)}, u32[]{:S(2)}) copy-start(bf16[27,128,128]{2,1,0:T(8,128)(2,1)} %w2_ref) | copy-start | bytes 2654212
  0.7 18.3 %copy-start.2 = (bf16[27,128,128]{2,1,0:T(8,128)(2,1)S(1)}, bf16[27,128,128]{2,1,0:T(8,128)(2,1)}, u32[]{:S(2)}) copy-start(bf16[27,128,128]{2,1,0:T(8,128)(2,1)} %w1_ref) | copy-start | bytes 2654212
  4.6 18.1 %copy-start.7 = (s32[32]{0:T(128)S(1)}, s32[32]{0:T(128)}, u32[]{:S(2)}) copy-start(s32[32]{0:T(128)} %source_ref.11) | copy-start | bytes 388
  4.6 11.9 %collective-permute-start = (bf16[256,128]{1,0:T(8,128)(2,1)}, bf16[256,128]{1,0:T(8,128)(2,1)S(1)}, u32[]{:S(2)}, u32[]{:S(2)}) collective-permute-start(bf16[256,128]{1,0:T(8,128)(2,1)} %get-tuple-element.43), channel_id=1, source_target_pairs={{0,5},{1,6},{2,7},{3,0},{4,1},{5,2},{6,3},{7,4},{8,13},{9,14},{10,... | collective-permute-start | bytes 196616 | tf_op jit(solution)/shard_map/ppermute | solution.py:617
  9.6 8.2 %collective-permute-start.1 = (bf16[256,128]{1,0:T(8,128)(2,1)}, bf16[256,128]{1,0:T(8,128)(2,1)S(1)}, u32[]{:S(2)}, u32[]{:S(2)}) collective-permute-start(bf16[256,128]{1,0:T(8,128)(2,1)} %get-tuple-element.51), channel_id=1, source_target_pairs={{0,1},{1,2},{2,3},{3,4},{4,5},{5,6},{6,7},{7,0},{8,9},{9,10},{10,1... | collective-permute-start | bytes 196616 | tf_op jit(solution)/shard_map/ppermute | solution.py:617
  11.2 10.5 %collective-permute-start.2 = (bf16[256,128]{1,0:T(8,128)(2,1)}, bf16[256,128]{1,0:T(8,128)(2,1)S(1)}, u32[]{:S(2)}, u32[]{:S(2)}) collective-permute-start(bf16[256,128]{1,0:T(8,128)(2,1)} %get-tuple-element.52), channel_id=1, source_target_pairs={{0,2},{1,3},{2,4},{3,5},{4,6},{5,7},{6,0},{7,1},{8,10},{9,11},{10,... | collective-permute-start | bytes 196616 | tf_op jit(solution)/shard_map/ppermute | solution.py:617
  11.2 11.3 %collective-permute-start.3 = (bf16[256,128]{1,0:T(8,128)(2,1)}, bf16[256,128]{1,0:T(8,128)(2,1)S(1)}, u32[]{:S(2)}, u32[]{:S(2)}) collective-permute-start(bf16[256,128]{1,0:T(8,128)(2,1)} %get-tuple-element.53), channel_id=1, source_target_pairs={{0,3},{1,4},{2,5},{3,6},{4,7},{5,0},{6,1},{7,2},{8,11},{9,12},{10,... | collective-permute-start | bytes 196616 | tf_op jit(solution)/shard_map/ppermute | solution.py:617
  13.0 9.5 %collective-permute-start.4 = (bf16[256,128]{1,0:T(8,128)(2,1)}, bf16[256,128]{1,0:T(8,128)(2,1)S(1)}, u32[]{:S(2)}, u32[]{:S(2)}) collective-permute-start(bf16[256,128]{1,0:T(8,128)(2,1)} %get-tuple-element.54), channel_id=1, source_target_pairs={{0,4},{1,5},{2,6},{3,7},{4,0},{5,1},{6,2},{7,3},{8,12},{9,13},{10,... | collective-permute-start | bytes 196616 | tf_op jit(solution)/shard_map/ppermute | solution.py:617
  16.5 6.0 %collective-permute-start.5 = (bf16[256,128]{1,0:T(8,128)(2,1)}, bf16[256,128]{1,0:T(8,128)(2,1)S(1)}, u32[]{:S(2)}, u32[]{:S(2)}) collective-permute-start(bf16[256,128]{1,0:T(8,128)(2,1)} %get-tuple-element.56), channel_id=1, source_target_pairs={{0,6},{1,7},{2,0},{3,1},{4,2},{5,3},{6,4},{7,5},{8,14},{9,15},{10,... | collective-permute-start | bytes 196616 | tf_op jit(solution)/shard_map/ppermute | solution.py:617
  17.8 4.9 %collective-permute-start.6 = (bf16[256,128]{1,0:T(8,128)(2,1)}, bf16[256,128]{1,0:T(8,128)(2,1)S(1)}, u32[]{:S(2)}, u32[]{:S(2)}) collective-permute-start(bf16[256,128]{1,0:T(8,128)(2,1)} %get-tuple-element.57), channel_id=1, source_target_pairs={{0,7},{1,0},{2,1},{3,2},{4,3},{5,4},{6,5},{7,6},{8,15},{9,8},{10,9... | collective-permute-start | bytes 196616 | tf_op jit(solution)/shard_map/ppermute | solution.py:617
  19.0 1.6 %copy-start = (bf16[32,64,512]{2,1,0:T(8,128)(2,1)S(1)}, bf16[32,64,512]{2,1,0:T(8,128)(2,1)}, u32[]{:S(2)}) copy-start(bf16[32,64,512]{2,1,0:T(8,128)(2,1)} %fine_ref.4) | copy-start | bytes 6291460
  23.5 7.5 %collective-permute-start.8 = (bf16[288,128]{1,0:T(8,128)(2,1)S(1)}, bf16[288,128]{1,0:T(8,128)(2,1)S(1)}, u32[]{:S(2)}, u32[]{:S(2)}) collective-permute-start(bf16[288,128]{1,0:T(8,128)(2,1)S(1)} %get-tuple-element.62), channel_id=1, source_target_pairs={{0,0},{1,2},{2,1},{3,4},{4,3},{5,6},{6,5},{7,7},{8,8},{9,10},{10,9... | collective-permute-start | bytes 221192 | tf_op jit(solution)/shard_map/ppermute | solution.py:625
  25.9 6.0 %collective-permute-start.7 = (bf16[288,128]{1,0:T(8,128)(2,1)S(1)}, bf16[288,128]{1,0:T(8,128)(2,1)S(1)}, u32[]{:S(2)}, u32[]{:S(2)}) collective-permute-start(bf16[288,128]{1,0:T(8,128)(2,1)S(1)} %get-tuple-element.61), channel_id=1, source_target_pairs={{0,1},{1,0},{2,3},{3,2},{4,5},{5,4},{6,7},{7,6},{8,9},{9,8},{10,11... | collective-permute-start | bytes 221192 | tf_op jit(solution)/shard_map/ppermute | solution.py:625
  32.6 4.0 %collective-permute-start.9 = (bf16[368,128]{1,0:T(8,128)(2,1)S(1)}, bf16[368,128]{1,0:T(8,128)(2,1)S(1)}, u32[]{:S(2)}, u32[]{:S(2)}) collective-permute-start(bf16[368,128]{1,0:T(8,128)(2,1)S(1)} %get-tuple-element.67), channel_id=1, source_target_pairs={{0,8},{8,0},{16,24},{24,16},{1,9},{9,1},{17,25},{25,17},{2,10},{10... | collective-permute-start | bytes 282632 | tf_op jit(solution)/shard_map/ppermute | solution.py:625
  32.7 3.9 %collective-permute-start.10 = (bf16[368,128]{1,0:T(8,128)(2,1)S(1)}, bf16[368,128]{1,0:T(8,128)(2,1)S(1)}, u32[]{:S(2)}, u32[]{:S(2)}) collective-permute-start(bf16[368,128]{1,0:T(8,128)(2,1)S(1)} %get-tuple-element.68), channel_id=1, source_target_pairs={{0,0},{8,16},{16,8},{24,24},{1,1},{9,17},{17,9},{25,25},{2,2},{10,... | collective-permute-start | bytes 282632 | tf_op jit(solution)/shard_map/ppermute | solution.py:625
  36.6 21.7 %copy-start.1 = (bf16[32,64,512]{2,1,0:T(8,128)(2,1)S(1)}, bf16[32,64,512]{2,1,0:T(8,128)(2,1)}, u32[]{:S(2)}) copy-start(bf16[32,64,512]{2,1,0:T(8,128)(2,1)} %fine_ref.4) | copy-start | bytes 6291460
  36.7 21.7 %copy-start.4 = (bf16[128,512]{1,0:T(8,128)(2,1)S(1)}, bf16[128,512]{1,0:T(8,128)(2,1)}, u32[]{:S(2)}) copy-start(bf16[128,512]{1,0:T(8,128)(2,1)} %w_ref.3) | copy-start | bytes 393220
  40.7 9.4 %collective-permute-start.14 = (bf16[256,128]{1,0:T(8,128)(2,1)S(1)}, bf16[256,128]{1,0:T(8,128)(2,1)S(1)}, u32[]{:S(2)}, u32[]{:S(2)}) collective-permute-start(bf16[256,128]{1,0:T(8,128)(2,1)S(1)} %get-tuple-element.79), channel_id=1, source_target_pairs={{0,6},{1,7},{2,0},{3,1},{4,2},{5,3},{6,4},{7,5},{8,14},{9,15},{10,... | collective-permute-start | bytes 196616 | tf_op jit(solution)/shard_map/ppermute | solution.py:617
  43.2 7.6 %collective-permute-start.15 = (bf16[256,128]{1,0:T(8,128)(2,1)S(1)}, bf16[256,128]{1,0:T(8,128)(2,1)S(1)}, u32[]{:S(2)}, u32[]{:S(2)}) collective-permute-start(bf16[256,128]{1,0:T(8,128)(2,1)S(1)} %get-tuple-element.80), channel_id=1, source_target_pairs={{0,5},{1,6},{2,7},{3,0},{4,1},{5,2},{6,3},{7,4},{8,13},{9,14},{10,... | collective-permute-start | bytes 196616 | tf_op jit(solution)/shard_map/ppermute | solution.py:617
  44.9 11.2 %collective-permute-start.16 = (bf16[256,128]{1,0:T(8,128)(2,1)S(1)}, bf16[256,128]{1,0:T(8,128)(2,1)S(1)}, u32[]{:S(2)}, u32[]{:S(2)}) collective-permute-start(bf16[256,128]{1,0:T(8,128)(2,1)S(1)} %get-tuple-element.81), channel_id=1, source_target_pairs={{0,4},{1,5},{2,6},{3,7},{4,0},{5,1},{6,2},{7,3},{8,12},{9,13},{10,... | collective-permute-start | bytes 196616 | tf_op jit(solution)/shard_map/ppermute | solution.py:617
  45.6 12.8 %collective-permute-start.17 = (bf16[256,128]{1,0:T(8,128)(2,1)S(1)}, bf16[256,128]{1,0:T(8,128)(2,1)S(1)}, u32[]{:S(2)}, u32[]{:S(2)}) collective-permute-start(bf16[256,128]{1,0:T(8,128)(2,1)S(1)} %get-tuple-element.82), channel_id=1, source_target_pairs={{0,3},{1,4},{2,5},{3,6},{4,7},{5,0},{6,1},{7,2},{8,11},{9,12},{10,... | collective-permute-start | bytes 196616 | tf_op jit(solution)/shard_map/ppermute | solution.py:617
  48.2 11.7 %collective-permute-start.11 = (bf16[256,128]{1,0:T(8,128)(2,1)S(1)}, bf16[256,128]{1,0:T(8,128)(2,1)S(1)}, u32[]{:S(2)}, u32[]{:S(2)}) collective-permute-start(bf16[256,128]{1,0:T(8,128)(2,1)S(1)} %get-tuple-element.75), channel_id=1, source_target_pairs={{0,2},{1,3},{2,4},{3,5},{4,6},{5,7},{6,0},{7,1},{8,10},{9,11},{10,... | collective-permute-start | bytes 196616 | tf_op jit(solution)/shard_map/ppermute | solution.py:617
  50.1 9.8 %collective-permute-start.12 = (bf16[256,128]{1,0:T(8,128)(2,1)S(1)}, bf16[256,128]{1,0:T(8,128)(2,1)S(1)}, u32[]{:S(2)}, u32[]{:S(2)}) collective-permute-start(bf16[256,128]{1,0:T(8,128)(2,1)S(1)} %get-tuple-element.76), channel_id=1, source_target_pairs={{0,1},{1,2},{2,3},{3,4},{4,5},{5,6},{6,7},{7,0},{8,9},{9,10},{10,1... | collective-permute-start | bytes 196616 | tf_op jit(solution)/shard_map/ppermute | solution.py:617
  50.8 9.1 %collective-permute-start.13 = (bf16[256,128]{1,0:T(8,128)(2,1)S(1)}, bf16[256,128]{1,0:T(8,128)(2,1)S(1)}, u32[]{:S(2)}, u32[]{:S(2)}) collective-permute-start(bf16[256,128]{1,0:T(8,128)(2,1)S(1)} %get-tuple-element.78), channel_id=1, source_target_pairs={{0,7},{1,0},{2,1},{3,2},{4,3},{5,4},{6,5},{7,6},{8,15},{9,8},{10,9... | collective-permute-start | bytes 196616 | tf_op jit(solution)/shard_map/ppermute | solution.py:617

commit v9 on v8

--- a/solution.py
+++ b/solution.py
@@ -14,8 +14,8 @@
 COLS = 8
 WIDE = SIDE + 4
 HID = SIDE + 2
-EARLY = ((1, 3), (4, 4))
-LATER = ((8, 4),)
+EARLY = ((1, 3),)
+LATER = ((4, 4), (8, 4))
 LATE = ((12, 3),)
 LATE_PLANES = 3
 SENT = (4, 3, 5, 2, 6, 1, 7)
@@ -452,9 +452,9 @@
     return (value + own) * spread_flags(flags, (4, 4, 4, 4))[None]
 
 
-def middle_kernel(source_ref, *refs):
-    block_ref, before_ref, after_ref, early_ref, later_ref, wide1_ref, wide2_ref = refs[:7]
-    h_here, h_next, coarse_ref, side, late, here, moved = refs[7:]
+def side_kernel(source_ref, *refs):
+    block_ref, before_ref, after_ref, early_ref, later_ref, wide1_ref = refs[:6]
+    h_here, h_next, side, late, here, moved = refs[6:]
     width = block_ref.shape[1]
     inner = SIDE - 2
     inner_planes(source_ref, block_ref, wide1_ref, late, here, moved, LATE)
@@ -479,6 +479,9 @@
         h_here[d] = plane
         h_next[d] = as_tiles(moved_rows(as_rows(plane)))
 
+
+def half_kernel(source_ref, block_ref, h_here, h_next, wide2_ref, coarse_ref):
+    width = block_ref.shape[1]
     for depth_brick in (1, 2):
         value = conv_planes(h_here, h_next, wide2_ref, depth_brick * 4 - 2, 4, SIDE * COLS)
         value = coarse_rows(source_ref, block_ref, value, depth_brick)
@@ -486,19 +489,17 @@
         coarse_ref[rows] = value.reshape(512, width).astype(jnp.bfloat16)
 
 
-def middle_call(source, block, before, after, early, later, wide1, wide2):
+def side_call(source, block, before, after, early, later, wide1):
     mid = block.shape[1]
     smem = pl.BlockSpec(memory_space=pltpu.SMEM)
     vmem = pl.BlockSpec(memory_space=pltpu.VMEM)
     inner = SIDE - 2
     hidden = (inner, HID * COLS, mid)
     return pl.pallas_call(
-        middle_kernel,
-        in_specs=[smem] + [vmem] * 7,
-        out_specs=[vmem] * 3,
-        out_shape=[
-            jax.ShapeDtypeStruct(shape, jnp.bfloat16) for shape in (hidden, hidden, (1024, mid))
-        ],
+        side_kernel,
+        in_specs=[smem] + [vmem] * 6,
+        out_specs=[vmem] * 2,
+        out_shape=[jax.ShapeDtypeStruct(hidden, jnp.bfloat16)] * 2,
         scratch_shapes=[
             pltpu.VMEM((2, inner, 16, mid), jnp.bfloat16),
             pltpu.VMEM((LATE_PLANES, inner * COLS, mid), jnp.bfloat16),
@@ -506,9 +507,23 @@
             pltpu.VMEM((LATE_PLANES + 2, SIDE * COLS, mid), jnp.bfloat16),
         ],
         compiler_params=pltpu.CompilerParams(vmem_limit_bytes=VMEM_LIMIT),
-        cost_estimate=conv_cost(inner * (4 + LATE_PLANES) * COLS + 1024, mid),
-        name="middle",
-    )(source, block, before, after, early, later, wide1, wide2)
+        cost_estimate=conv_cost(inner * (4 + LATE_PLANES) * COLS, mid),
+        name="side",
+    )(source, block, before, after, early, later, wide1)
+
+
+def half_call(source, block, here, moved, wide2):
+    mid = block.shape[1]
+    vmem = pl.BlockSpec(memory_space=pltpu.VMEM)
+    return pl.pallas_call(
+        half_kernel,
+        in_specs=[pl.BlockSpec(memory_space=pltpu.SMEM)] + [vmem] * 4,
+        out_specs=vmem,
+        out_shape=jax.ShapeDtypeStruct((1024, mid), jnp.bfloat16),
+        compiler_params=pltpu.CompilerParams(vmem_limit_bytes=VMEM_LIMIT),
+        cost_estimate=conv_cost(1024, mid),
+        name="half",
+    )(source, block, here, moved, wide2)
 
 
 def scatter_bricks(source_ref, stage, value, depth_brick):
@@ -643,9 +658,11 @@
     later = inner_call(slot_source, block, wide1, LATER)
     even, odd, later = lax.optimization_barrier((even, odd, later))
     before, after, even, odd = edge_call(counts, base, slot_source, block, even, odd)
+    odd = swap_face(odd, "gz", 1)
+    here, moved = side_call(slot_source, block, before, after, early, later, wide1)
+    even, here, moved = lax.optimization_barrier((even, here, moved))
     even = swap_face(even, "gz", 0)
-    odd = swap_face(odd, "gz", 1)
-    middle = middle_call(slot_source, block, before, after, early, later, wide1, wide2)
+    middle = (here, moved, half_call(slot_source, block, here, moved, wide2))
     coarse, *back = final_call(
         counts[0], base, slot_source, block, (before, after, even, odd), middle, wide1, wide2
     )

time: 61.7 us -> 63.5 us (1.029)
  starting transfers between devices: 34.7 us -> 36.4 us
    ppermute x4, starting transfers between devices: 5.11 us -> 7.98 us  [swap_face(): return lax.ppermute(face, axis, list(enumerate(partner)))]
    ppermute x14, starting transfers between devices: 29.6 us -> 28.4 us  [from_behind(): return lax.ppermute(value, axis, pairs)]
    pallas_call x1 -> x2, Pallas kernels: 3.22 us -> 3.89 us  [the longest x1 2.01 us: half_call(): pl.pallas_call(half_kernel, in_specs=[pl.BlockSpec(memory_space=pltpu.SME...]
  transfers between devices with their start and end apart: 18 -> 18, of which waited for: 4 -> 6; matrix products, arithmetic and copies ran while one was open for 0% -> 0% of each run, Pallas kernels for 14% -> 15%
where the time goes in v9:
time: 63.5 us; the launch traced here: 63.4 us
  starting transfers between devices  36.4 us (57%)
  Pallas kernels  20.3 us (32%)
  waiting for transfers between devices  4.14 us (7%)
  local copies, waits for them, and re-layouts  1.62 us (3%)
  between operations  0.82 us (1%)
    ppermute x14, starting transfers between devices, from_behind(): return lax.ppermute(value, axis, pairs)  28.4 us
    ppermute x4, starting transfers between devices, swap_face(): return lax.ppermute(face, axis, list(enumerate(partner)))  7.98 us
    pallas_call x1, Pallas kernels, final_call(): pl.pallas_call(functools.partial(final_kernel, count), in_specs=[smem, sm...  4.03 us
    pallas_call x1, Pallas kernels, down_call(): pl.pallas_call(functools.partial(down_kernel, offsets), in_specs=[hbm, hb...  3.9 us
    ppermute x14, waiting for transfers between devices, from_behind(): return lax.ppermute(value, axis, pairs)  3.72 us
    pallas_call x2, Pallas kernels, inner_call(): pl.pallas_call(functools.partial(inner_kernel, groups), in_specs=[smem, v...  3.08 us
    pallas_call x2, Pallas kernels, up_call(): pl.pallas_call(up_kernel, grid=(UP_OFFSETS * CAP // step,), in_specs=[pl....  2.95 us
    pallas_call x1, Pallas kernels, half_call(): pl.pallas_call(half_kernel, in_specs=[pl.BlockSpec(memory_space=pltpu.SME...  2.01 us
  transfers between devices with their start and end apart: 18, of which 6 were waited for; matrix products, arithmetic and copies ran while one was open for 0% of the time, Pallas kernels for 15%

profile of v9, /device:TPU:0, one launch (start us, length us, event | category | flops | bytes accessed | tf_op | source)
XLA Modules:
  0.0 63.4 jit_solution(6478805001328128534)
XLA Ops:
  0.7 3.9 %down.1 = (bf16[256,128]{1,0:T(8,128)(2,1)}, bf16[256,128]{1,0:T(8,128)(2,1)}, bf16[256,128]{1,0:T(8,128)(2,1)}, bf16[256,128]{1,0:T(8,128)(2,1)}, bf16[256,128]...) custom-call(bf16[32,64,512]{2,1,0:T(8,128)(2,1)} %fine_ref.4, s32[32,512]{1,0:T(8,128)} %mask_ref, ...), custom_call_target="tpu_custom_call" | custom-call | flops 234881024 | bytes 1835008 | tf_op jit(solution)/shard_map/down/pallas_call | solution.py:83
  4.6 5.0 %collective-permute-start = (bf16[256,128]{1,0:T(8,128)(2,1)}, bf16[256,128]{1,0:T(8,128)(2,1)S(1)}, u32[]{:S(2)}, u32[]{:S(2)}) collective-permute-start(bf16[256,128]{1,0:T(8,128)(2,1)} %get-tuple-element.45), channel_id=1, source_target_pairs={{0,5},{1,6},{2,7},{3,0},{4,1},{5,2},{6,3},{7,4},{8,13},{9,14},{10,... | collective-permute-start | bytes 196616 | tf_op jit(solution)/shard_map/ppermute | solution.py:632
  9.6 1.5 %collective-permute-start.1 = (bf16[256,128]{1,0:T(8,128)(2,1)}, bf16[256,128]{1,0:T(8,128)(2,1)S(1)}, u32[]{:S(2)}, u32[]{:S(2)}) collective-permute-start(bf16[256,128]{1,0:T(8,128)(2,1)} %get-tuple-element.53), channel_id=1, source_target_pairs={{0,1},{1,2},{2,3},{3,4},{4,5},{5,6},{6,7},{7,0},{8,9},{9,10},{10,1... | collective-permute-start | bytes 196616 | tf_op jit(solution)/shard_map/ppermute | solution.py:632
  11.2 1.8 %collective-permute-start.3 = (bf16[256,128]{1,0:T(8,128)(2,1)}, bf16[256,128]{1,0:T(8,128)(2,1)S(1)}, u32[]{:S(2)}, u32[]{:S(2)}) collective-permute-start(bf16[256,128]{1,0:T(8,128)(2,1)} %get-tuple-element.55), channel_id=1, source_target_pairs={{0,3},{1,4},{2,5},{3,6},{4,7},{5,0},{6,1},{7,2},{8,11},{9,12},{10,... | collective-permute-start | bytes 196616 | tf_op jit(solution)/shard_map/ppermute | solution.py:632
  13.0 3.5 %collective-permute-start.4 = (bf16[256,128]{1,0:T(8,128)(2,1)}, bf16[256,128]{1,0:T(8,128)(2,1)S(1)}, u32[]{:S(2)}, u32[]{:S(2)}) collective-permute-start(bf16[256,128]{1,0:T(8,128)(2,1)} %get-tuple-element.56), channel_id=1, source_target_pairs={{0,4},{1,5},{2,6},{3,7},{4,0},{5,1},{6,2},{7,3},{8,12},{9,13},{10,... | collective-permute-start | bytes 196616 | tf_op jit(solution)/shard_map/ppermute | solution.py:632
  16.5 1.4 %collective-permute-start.5 = (bf16[256,128]{1,0:T(8,128)(2,1)}, bf16[256,128]{1,0:T(8,128)(2,1)S(1)}, u32[]{:S(2)}, u32[]{:S(2)}) collective-permute-start(bf16[256,128]{1,0:T(8,128)(2,1)} %get-tuple-element.58), channel_id=1, source_target_pairs={{0,6},{1,7},{2,0},{3,1},{4,2},{5,3},{6,4},{7,5},{8,14},{9,15},{10,... | collective-permute-start | bytes 196616 | tf_op jit(solution)/shard_map/ppermute | solution.py:632
  17.8 1.0 %collective-permute-start.6 = (bf16[256,128]{1,0:T(8,128)(2,1)}, bf16[256,128]{1,0:T(8,128)(2,1)S(1)}, u32[]{:S(2)}, u32[]{:S(2)}) collective-permute-start(bf16[256,128]{1,0:T(8,128)(2,1)} %get-tuple-element.59), channel_id=1, source_target_pairs={{0,7},{1,0},{2,1},{3,2},{4,3},{5,4},{6,5},{7,6},{8,15},{9,8},{10,9... | collective-permute-start | bytes 196616 | tf_op jit(solution)/shard_map/ppermute | solution.py:632
  19.0 1.6 %copy-done = bf16[32,64,512]{2,1,0:T(8,128)(2,1)S(1)} copy-done((bf16[32,64,512]{2,1,0:T(8,128)(2,1)S(1)}, bf16[32,64,512]{2,1,0:T(8,128)(2,1)}, u32[]{:S(2)}) %copy-start) | copy-done | bytes 2097176
  20.6 1.1 %prepare.1 = (bf16[256,128]{1,0:T(8,128)(2,1)S(1)}, bf16[2048,512]{1,0:T(8,128)(2,1)S(1)}, bf16[1152,384]{1,0:T(8,128)(2,1)S(1)}, bf16[1152,384]{1,0:T(8,128)(2,1)S(1)}) custom-call(bf16[32,64,512]{2,1,0:T(8,128)(2,1)S(1)} %copy-done, s32[32,512]{1,0:T(8,128)S(1)} %copy-done.6, bf16[512,128]{1,0:T(8,128)(2,1)S(1)} %copy-done.5, ...), custom_call_target="tpu_custom_call" | custom-call | flops 268435456 | bytes 2097152 | tf_op jit(solution)/shard_map/prepare/pallas_call | solution.py:124
  21.6 0.8 %collective-permute-done.3.refs_3_ = bf16[256,128]{1,0:T(8,128)(2,1)S(1)} collective-permute-done((bf16[256,128]{1,0:T(8,128)(2,1)}, bf16[256,128]{1,0:T(8,128)(2,1)S(1)}, u32[]{:S(2)}, u32[]{:S(2)}) %collective-permute-start.3) | collective-permute-done | bytes 65568 | tf_op jit(solution)/shard_map/ppermute | solution.py:632
  22.7 0.8 %place.1 = (bf16[2048,128]{1,0:T(8,128)(2,1)S(1)}, bf16[288,128]{1,0:T(8,128)(2,1)S(1)}, bf16[288,128]{1,0:T(8,128)(2,1)S(1)}) custom-call(s32[2]{0:T(128)S(1)} %pad_add_fusion.base_ref, s32[32]{0:T(128)S(1)} %copy-done.7, bf16[256,128]{1,0:T(8,128)(2,1)S(1)} %get-tuple-element.52.refs_0_, bf16[256,128]{1,0:T(8,128)(2,1)S(1)} %collective-permute-done.1.refs_1_, ...), custom_call_target="tpu_custom_call" | custom-call | tf_op jit(solution)/shard_map/place/pallas_call | solution.py:260
  23.5 0.7 %collective-permute-start.8 = (bf16[288,128]{1,0:T(8,128)(2,1)S(1)}, bf16[288,128]{1,0:T(8,128)(2,1)S(1)}, u32[]{:S(2)}, u32[]{:S(2)}) collective-permute-start(bf16[288,128]{1,0:T(8,128)(2,1)S(1)} %get-tuple-element.64), channel_id=1, source_target_pairs={{0,0},{1,2},{2,1},{3,4},{4,3},{5,6},{6,5},{7,7},{8,8},{9,10},{10,9... | collective-permute-start | bytes 221192 | tf_op jit(solution)/shard_map/ppermute | solution.py:640
  24.2 1.2 %inner.2.refs_3_ = bf16[3,112,128]{2,1,0:T(8,128)(2,1)S(1)} custom-call(s32[32]{0:T(128)S(1)} %copy-done.7, bf16[2048,128]{1,0:T(8,128)(2,1)S(1)} %get-tuple-element.60.block_ref.refs_0_, bf16[1152,384]{1,0:T(8,128)(2,1)S(1)} %get-tuple-element.62.wide1_ref.refs_5_.refs_8_), custom_call_target="tpu_custom_call" | custom-call | flops 297271296 | bytes 1769472 | tf_op jit(solution)/shard_map/inner/pallas_call | solution.py:419
  25.4 3.7 %collective-permute-start.7 = (bf16[288,128]{1,0:T(8,128)(2,1)S(1)}, bf16[288,128]{1,0:T(8,128)(2,1)S(1)}, u32[]{:S(2)}, u32[]{:S(2)}) collective-permute-start(bf16[288,128]{1,0:T(8,128)(2,1)S(1)} %get-tuple-element.63), channel_id=1, source_target_pairs={{0,1},{1,0},{2,3},{3,2},{4,5},{5,4},{6,7},{7,6},{8,9},{9,8},{10,11... | collective-permute-start | bytes 221192 | tf_op jit(solution)/shard_map/ppermute | solution.py:640
  29.1 1.9 %inner.3.refs_4_ = bf16[8,112,128]{2,1,0:T(8,128)(2,1)S(1)} custom-call(s32[32]{0:T(128)S(1)} %copy-done.7, bf16[2048,128]{1,0:T(8,128)(2,1)S(1)} %get-tuple-element.60.block_ref.refs_0_, bf16[1152,384]{1,0:T(8,128)(2,1)S(1)} %get-tuple-element.62.wide1_ref.refs_5_.refs_8_), custom_call_target="tpu_custom_call" | custom-call | flops 792723456 | bytes 1769472 | tf_op jit(solution)/shard_map/inner/pallas_call | solution.py:419
  31.0 0.4 collective-permute-done.7.even_ref
  31.4 0.6 %edge.1 = (bf16[288,128]{1,0:T(8,128)(2,1)S(1)}, bf16[288,128]{1,0:T(8,128)(2,1)S(1)}, bf16[368,128]{1,0:T(8,128)(2,1)S(1)}, bf16[368,128]{1,0:T(8,128)(2,1)S(1)}) custom-call(s32[2]{0:T(128)S(1)} %pad_add_fusion.base_ref, s32[32]{0:T(128)S(1)} %copy-done.7, bf16[2048,128]{1,0:T(8,128)(2,1)S(1)} %get-tuple-element.60.block_ref.refs_0_, ...), custom_call_target="tpu_custom_call" | custom-call | tf_op jit(solution)/shard_map/edge/pallas_call | solution.py:310
  32.0 0.7 %collective-permute-start.10 = (bf16[368,128]{1,0:T(8,128)(2,1)S(1)}, bf16[368,128]{1,0:T(8,128)(2,1)S(1)}, u32[]{:S(2)}, u32[]{:S(2)}) collective-permute-start(bf16[368,128]{1,0:T(8,128)(2,1)S(1)} %get-tuple-element.75), channel_id=1, source_target_pairs={{0,0},{8,16},{16,8},{24,24},{1,1},{9,17},{17,9},{25,25},{2,2},{10,... | collective-permute-start | bytes 282632 | tf_op jit(solution)/shard_map/ppermute | solution.py:640
  32.7 1.9 %side.1 = (bf16[14,144,128]{2,1,0:T(8,128)(2,1)S(1)}, bf16[14,144,128]{2,1,0:T(8,128)(2,1)S(1)}) custom-call(s32[32]{0:T(128)S(1)} %copy-done.7, bf16[2048,128]{1,0:T(8,128)(2,1)S(1)} %get-tuple-element.60.block_ref.refs_0_, bf16[288,128]{1,0:T(8,128)(2,1)S(1)} %get-tuple-element.67.refs_1_, bf16[288,128]{1,0:T(8,128)(2,1)S(1)} %get-tuple-element.68.refs_2_, ...), custom_call_target="tpu_custom_call" | custom-call | flops 693633024 | bytes 1769472 | tf_op jit(solution)/shard_map/side/pallas_call | solution.py:498
  34.6 2.9 %collective-permute-start.9 = (bf16[368,128]{1,0:T(8,128)(2,1)S(1)}, bf16[368,128]{1,0:T(8,128)(2,1)S(1)}, u32[]{:S(2)}, u32[]{:S(2)}) collective-permute-start(bf16[368,128]{1,0:T(8,128)(2,1)S(1)} %get-tuple-element.74), channel_id=1, source_target_pairs={{0,8},{8,0},{16,24},{24,16},{1,9},{9,1},{17,25},{25,17},{2,10},{10... | collective-permute-start | bytes 282632 | tf_op jit(solution)/shard_map/ppermute | solution.py:640
  37.5 2.0 %half.1.refs_7_ = bf16[1024,128]{1,0:T(8,128)(2,1)S(1)} custom-call(s32[32]{0:T(128)S(1)} %copy-done.7, bf16[2048,128]{1,0:T(8,128)(2,1)S(1)} %get-tuple-element.60.block_ref.refs_0_, bf16[14,144,128]{2,1,0:T(8,128)(2,1)S(1)} %get-tuple-element.76.h_here.refs_5_, bf16[14,144,128]{2,1,0:T(8,128)(2,1)S(1)} %get-tuple-element.77.h_next.refs_6_, ...), custom_call_target="tpu_custom_call" | custom-call | flops 905969664 | bytes 1769472 | tf_op jit(solution)/shard_map/half/pallas_call | solution.py:518
  39.6 4.0 %final.1 = (bf16[2048,128]{1,0:T(8,128)(2,1)}, bf16[256,128]{1,0:T(8,128)(2,1)S(1)}, bf16[256,128]{1,0:T(8,128)(2,1)S(1)}, bf16[256,128]{1,0:T(8,128)(2,1)S(1)},...) custom-call(s32[2]{0:T(128)S(1)} %pad_add_fusion.base_ref, ...), custom_call_target="tpu_custom_call" | custom-call | flops 1415577600 | bytes 1769472 | tf_op jit(solution)/shard_map/final/pallas_call | solution.py:608
  43.6 2.6 %collective-permute-start.14 = (bf16[256,128]{1,0:T(8,128)(2,1)S(1)}, bf16[256,128]{1,0:T(8,128)(2,1)S(1)}, u32[]{:S(2)}, u32[]{:S(2)}) collective-permute-start(bf16[256,128]{1,0:T(8,128)(2,1)S(1)} %get-tuple-element.83), channel_id=1, source_target_pairs={{0,6},{1,7},{2,0},{3,1},{4,2},{5,3},{6,4},{7,5},{8,14},{9,15},{10,... | collective-permute-start | bytes 196616 | tf_op jit(solution)/shard_map/ppermute | solution.py:632
  46.3 2.0 %collective-permute-start.15 = (bf16[256,128]{1,0:T(8,128)(2,1)S(1)}, bf16[256,128]{1,0:T(8,128)(2,1)S(1)}, u32[]{:S(2)}, u32[]{:S(2)}) collective-permute-start(bf16[256,128]{1,0:T(8,128)(2,1)S(1)} %get-tuple-element.84), channel_id=1, source_target_pairs={{0,5},{1,6},{2,7},{3,0},{4,1},{5,2},{6,3},{7,4},{8,13},{9,14},{10,... | collective-permute-start | bytes 196616 | tf_op jit(solution)/shard_map/ppermute | solution.py:632
  48.5 2.6 %collective-permute-start.17 = (bf16[256,128]{1,0:T(8,128)(2,1)S(1)}, bf16[256,128]{1,0:T(8,128)(2,1)S(1)}, u32[]{:S(2)}, u32[]{:S(2)}) collective-permute-start(bf16[256,128]{1,0:T(8,128)(2,1)S(1)} %get-tuple-element.86), channel_id=1, source_target_pairs={{0,3},{1,4},{2,5},{3,6},{4,7},{5,0},{6,1},{7,2},{8,11},{9,12},{10,... | collective-permute-start | bytes 196616 | tf_op jit(solution)/shard_map/ppermute | solution.py:632
  51.1 1.9 %collective-permute-start.11 = (bf16[256,128]{1,0:T(8,128)(2,1)S(1)}, bf16[256,128]{1,0:T(8,128)(2,1)S(1)}, u32[]{:S(2)}, u32[]{:S(2)}) collective-permute-start(bf16[256,128]{1,0:T(8,128)(2,1)S(1)} %get-tuple-element.79), channel_id=1, source_target_pairs={{0,2},{1,3},{2,4},{3,5},{4,6},{5,7},{6,0},{7,1},{8,10},{9,11},{10,... | collective-permute-start | bytes 196616 | tf_op jit(solution)/shard_map/ppermute | solution.py:632
  53.0 0.7 %collective-permute-start.12 = (bf16[256,128]{1,0:T(8,128)(2,1)S(1)}, bf16[256,128]{1,0:T(8,128)(2,1)S(1)}, u32[]{:S(2)}, u32[]{:S(2)}) collective-permute-start(bf16[256,128]{1,0:T(8,128)(2,1)S(1)} %get-tuple-element.80), channel_id=1, source_target_pairs={{0,1},{1,2},{2,3},{3,4},{4,5},{5,6},{6,7},{7,0},{8,9},{9,10},{10,1... | collective-permute-start | bytes 196616 | tf_op jit(solution)/shard_map/ppermute | solution.py:632
  53.7 4.1 %collective-permute-start.13 = (bf16[256,128]{1,0:T(8,128)(2,1)S(1)}, bf16[256,128]{1,0:T(8,128)(2,1)S(1)}, u32[]{:S(2)}, u32[]{:S(2)}) collective-permute-start(bf16[256,128]{1,0:T(8,128)(2,1)S(1)} %get-tuple-element.82), channel_id=1, source_target_pairs={{0,7},{1,0},{2,1},{3,2},{4,3},{5,4},{6,5},{7,6},{8,15},{9,8},{10,9... | collective-permute-start | bytes 196616 | tf_op jit(solution)/shard_map/ppermute | solution.py:632
  57.8 1.6 %collective-permute-done.16.refs_2_ = bf16[256,128]{1,0:T(8,128)(2,1)S(1)} collective-permute-done((bf16[256,128]{1,0:T(8,128)(2,1)S(1)}, bf16[256,128]{1,0:T(8,128)(2,1)S(1)}, u32[]{:S(2)}, u32[]{:S(2)}) %collective-permute-start.16) | collective-permute-done | bytes 65568 | tf_op jit(solution)/shard_map/ppermute | solution.py:632
  59.3 1.0 %collective-permute-done.17.refs_3_ = bf16[256,128]{1,0:T(8,128)(2,1)S(1)} collective-permute-done((bf16[256,128]{1,0:T(8,128)(2,1)S(1)}, bf16[256,128]{1,0:T(8,128)(2,1)S(1)}, u32[]{:S(2)}, u32[]{:S(2)}) %collective-permute-start.17) | collective-permute-done | bytes 65568 | tf_op jit(solution)/shard_map/ppermute | solution.py:632
  60.3 1.5 %up.2.refs_4_ = bf16[32,64,512]{2,1,0:T(8,128)(2,1)} custom-call(bf16[32,64,512]{2,1,0:T(8,128)(2,1)S(1)} %copy-done.1, bf16[2048,512]{1,0:T(8,128)(2,1)S(1)} %get-tuple-element.51.mask_ref, bf16[128,512]{1,0:T(8,128)(2,1)S(1)} %copy-done.4, bf16[256,128]{1,0:T(8,128)(2,1)S(1)} %collective-permute-done.14.refs_0_, ...), custom_call_target="tpu_custom_call" | custom-call | flops 134217728 | bytes 2097152 | tf_op jit(solution)/shard_map/up/pallas_call | solution.py:171
  61.9 1.5 %up.3 = bf16[32,64,512]{2,1,0:T(8,128)(2,1)} custom-call(bf16[32,64,512]{2,1,0:T(8,128)(2,1)S(1)} %copy-done.1, bf16[2048,512]{1,0:T(8,128)(2,1)S(1)} %get-tuple-element.51.mask_ref, bf16[128,512]{1,0:T(8,128)(2,1)S(1)} %copy-done.4, bf16[256,128]{1,0:T(8,128)(2,1)S(1)} %collective-permute-done.11.refs_0_, ...), custom_call_target="tpu_custom_call", output_to_operand_aliasing={{}: (7, {})} | custom-call | flops 134217728 | bytes 2097152 | tf_op jit(solution)/shard_map/up/pallas_call | solution.py:171
  (32 shorter events, 0.8 us)
Async XLA Ops:
  0.6 18.3 %copy-start.5 = (bf16[512,128]{1,0:T(8,128)(2,1)S(1)}, bf16[512,128]{1,0:T(8,128)(2,1)}, u32[]{:S(2)}) copy-start(bf16[512,128]{1,0:T(8,128)(2,1)} %w_down_ref) | copy-start | bytes 393220
  0.6 18.3 %copy-start.6 = (s32[32,512]{1,0:T(8,128)S(1)}, s32[32,512]{1,0:T(8,128)}, u32[]{:S(2)}) copy-start(s32[32,512]{1,0:T(8,128)} %mask_ref) | copy-start | bytes 196612
  0.7 18.3 %copy-start.3 = (bf16[27,128,128]{2,1,0:T(8,128)(2,1)S(1)}, bf16[27,128,128]{2,1,0:T(8,128)(2,1)}, u32[]{:S(2)}) copy-start(bf16[27,128,128]{2,1,0:T(8,128)(2,1)} %w2_ref) | copy-start | bytes 2654212
  0.7 18.3 %copy-start.2 = (bf16[27,128,128]{2,1,0:T(8,128)(2,1)S(1)}, bf16[27,128,128]{2,1,0:T(8,128)(2,1)}, u32[]{:S(2)}) copy-start(bf16[27,128,128]{2,1,0:T(8,128)(2,1)} %w1_ref) | copy-start | bytes 2654212
  4.6 18.1 %copy-start.7 = (s32[32]{0:T(128)S(1)}, s32[32]{0:T(128)}, u32[]{:S(2)}) copy-start(s32[32]{0:T(128)} %source_ref.13) | copy-start | bytes 388
  4.6 11.9 %collective-permute-start = (bf16[256,128]{1,0:T(8,128)(2,1)}, bf16[256,128]{1,0:T(8,128)(2,1)S(1)}, u32[]{:S(2)}, u32[]{:S(2)}) collective-permute-start(bf16[256,128]{1,0:T(8,128)(2,1)} %get-tuple-element.45), channel_id=1, source_target_pairs={{0,5},{1,6},{2,7},{3,0},{4,1},{5,2},{6,3},{7,4},{8,13},{9,14},{10,... | collective-permute-start | bytes 196616 | tf_op jit(solution)/shard_map/ppermute | solution.py:632
  9.6 8.2 %collective-permute-start.1 = (bf16[256,128]{1,0:T(8,128)(2,1)}, bf16[256,128]{1,0:T(8,128)(2,1)S(1)}, u32[]{:S(2)}, u32[]{:S(2)}) collective-permute-start(bf16[256,128]{1,0:T(8,128)(2,1)} %get-tuple-element.53), channel_id=1, source_target_pairs={{0,1},{1,2},{2,3},{3,4},{4,5},{5,6},{6,7},{7,0},{8,9},{9,10},{10,1... | collective-permute-start | bytes 196616 | tf_op jit(solution)/shard_map/ppermute | solution.py:632
  11.2 10.5 %collective-permute-start.2 = (bf16[256,128]{1,0:T(8,128)(2,1)}, bf16[256,128]{1,0:T(8,128)(2,1)S(1)}, u32[]{:S(2)}, u32[]{:S(2)}) collective-permute-start(bf16[256,128]{1,0:T(8,128)(2,1)} %get-tuple-element.54), channel_id=1, source_target_pairs={{0,2},{1,3},{2,4},{3,5},{4,6},{5,7},{6,0},{7,1},{8,10},{9,11},{10,... | collective-permute-start | bytes 196616 | tf_op jit(solution)/shard_map/ppermute | solution.py:632
  11.2 11.3 %collective-permute-start.3 = (bf16[256,128]{1,0:T(8,128)(2,1)}, bf16[256,128]{1,0:T(8,128)(2,1)S(1)}, u32[]{:S(2)}, u32[]{:S(2)}) collective-permute-start(bf16[256,128]{1,0:T(8,128)(2,1)} %get-tuple-element.55), channel_id=1, source_target_pairs={{0,3},{1,4},{2,5},{3,6},{4,7},{5,0},{6,1},{7,2},{8,11},{9,12},{10,... | collective-permute-start | bytes 196616 | tf_op jit(solution)/shard_map/ppermute | solution.py:632
  13.0 9.5 %collective-permute-start.4 = (bf16[256,128]{1,0:T(8,128)(2,1)}, bf16[256,128]{1,0:T(8,128)(2,1)S(1)}, u32[]{:S(2)}, u32[]{:S(2)}) collective-permute-start(bf16[256,128]{1,0:T(8,128)(2,1)} %get-tuple-element.56), channel_id=1, source_target_pairs={{0,4},{1,5},{2,6},{3,7},{4,0},{5,1},{6,2},{7,3},{8,12},{9,13},{10,... | collective-permute-start | bytes 196616 | tf_op jit(solution)/shard_map/ppermute | solution.py:632
  16.5 6.0 %collective-permute-start.5 = (bf16[256,128]{1,0:T(8,128)(2,1)}, bf16[256,128]{1,0:T(8,128)(2,1)S(1)}, u32[]{:S(2)}, u32[]{:S(2)}) collective-permute-start(bf16[256,128]{1,0:T(8,128)(2,1)} %get-tuple-element.58), channel_id=1, source_target_pairs={{0,6},{1,7},{2,0},{3,1},{4,2},{5,3},{6,4},{7,5},{8,14},{9,15},{10,... | collective-permute-start | bytes 196616 | tf_op jit(solution)/shard_map/ppermute | solution.py:632
  17.8 4.9 %collective-permute-start.6 = (bf16[256,128]{1,0:T(8,128)(2,1)}, bf16[256,128]{1,0:T(8,128)(2,1)S(1)}, u32[]{:S(2)}, u32[]{:S(2)}) collective-permute-start(bf16[256,128]{1,0:T(8,128)(2,1)} %get-tuple-element.59), channel_id=1, source_target_pairs={{0,7},{1,0},{2,1},{3,2},{4,3},{5,4},{6,5},{7,6},{8,15},{9,8},{10,9... | collective-permute-start | bytes 196616 | tf_op jit(solution)/shard_map/ppermute | solution.py:632
  19.0 1.6 %copy-start = (bf16[32,64,512]{2,1,0:T(8,128)(2,1)S(1)}, bf16[32,64,512]{2,1,0:T(8,128)(2,1)}, u32[]{:S(2)}) copy-start(bf16[32,64,512]{2,1,0:T(8,128)(2,1)} %fine_ref.4) | copy-start | bytes 6291460
  23.5 7.5 %collective-permute-start.8 = (bf16[288,128]{1,0:T(8,128)(2,1)S(1)}, bf16[288,128]{1,0:T(8,128)(2,1)S(1)}, u32[]{:S(2)}, u32[]{:S(2)}) collective-permute-start(bf16[288,128]{1,0:T(8,128)(2,1)S(1)} %get-tuple-element.64), channel_id=1, source_target_pairs={{0,0},{1,2},{2,1},{3,4},{4,3},{5,6},{6,5},{7,7},{8,8},{9,10},{10,9... | collective-permute-start | bytes 221192 | tf_op jit(solution)/shard_map/ppermute | solution.py:640
  25.4 6.0 %collective-permute-start.7 = (bf16[288,128]{1,0:T(8,128)(2,1)S(1)}, bf16[288,128]{1,0:T(8,128)(2,1)S(1)}, u32[]{:S(2)}, u32[]{:S(2)}) collective-permute-start(bf16[288,128]{1,0:T(8,128)(2,1)S(1)} %get-tuple-element.63), channel_id=1, source_target_pairs={{0,1},{1,0},{2,3},{3,2},{4,5},{5,4},{6,7},{7,6},{8,9},{9,8},{10,11... | collective-permute-start | bytes 221192 | tf_op jit(solution)/shard_map/ppermute | solution.py:640
  32.0 7.5 %collective-permute-start.10 = (bf16[368,128]{1,0:T(8,128)(2,1)S(1)}, bf16[368,128]{1,0:T(8,128)(2,1)S(1)}, u32[]{:S(2)}, u32[]{:S(2)}) collective-permute-start(bf16[368,128]{1,0:T(8,128)(2,1)S(1)} %get-tuple-element.75), channel_id=1, source_target_pairs={{0,0},{8,16},{16,8},{24,24},{1,1},{9,17},{17,9},{25,25},{2,2},{10,... | collective-permute-start | bytes 282632 | tf_op jit(solution)/shard_map/ppermute | solution.py:640
  34.6 5.0 %collective-permute-start.9 = (bf16[368,128]{1,0:T(8,128)(2,1)S(1)}, bf16[368,128]{1,0:T(8,128)(2,1)S(1)}, u32[]{:S(2)}, u32[]{:S(2)}) collective-permute-start(bf16[368,128]{1,0:T(8,128)(2,1)S(1)} %get-tuple-element.74), channel_id=1, source_target_pairs={{0,8},{8,0},{16,24},{24,16},{1,9},{9,1},{17,25},{25,17},{2,10},{10... | collective-permute-start | bytes 282632 | tf_op jit(solution)/shard_map/ppermute | solution.py:640
  39.6 20.8 %copy-start.1 = (bf16[32,64,512]{2,1,0:T(8,128)(2,1)S(1)}, bf16[32,64,512]{2,1,0:T(8,128)(2,1)}, u32[]{:S(2)}) copy-start(bf16[32,64,512]{2,1,0:T(8,128)(2,1)} %fine_ref.4) | copy-start | bytes 6291460
  39.6 20.7 %copy-start.4 = (bf16[128,512]{1,0:T(8,128)(2,1)S(1)}, bf16[128,512]{1,0:T(8,128)(2,1)}, u32[]{:S(2)}) copy-start(bf16[128,512]{1,0:T(8,128)(2,1)} %w_ref.3) | copy-start | bytes 393220
  43.6 9.4 %collective-permute-start.14 = (bf16[256,128]{1,0:T(8,128)(2,1)S(1)}, bf16[256,128]{1,0:T(8,128)(2,1)S(1)}, u32[]{:S(2)}, u32[]{:S(2)}) collective-permute-start(bf16[256,128]{1,0:T(8,128)(2,1)S(1)} %get-tuple-element.83), channel_id=1, source_target_pairs={{0,6},{1,7},{2,0},{3,1},{4,2},{5,3},{6,4},{7,5},{8,14},{9,15},{10,... | collective-permute-start | bytes 196616 | tf_op jit(solution)/shard_map/ppermute | solution.py:632
  46.3 7.5 %collective-permute-start.15 = (bf16[256,128]{1,0:T(8,128)(2,1)S(1)}, bf16[256,128]{1,0:T(8,128)(2,1)S(1)}, u32[]{:S(2)}, u32[]{:S(2)}) collective-permute-start(bf16[256,128]{1,0:T(8,128)(2,1)S(1)} %get-tuple-element.84), channel_id=1, source_target_pairs={{0,5},{1,6},{2,7},{3,0},{4,1},{5,2},{6,3},{7,4},{8,13},{9,14},{10,... | collective-permute-start | bytes 196616 | tf_op jit(solution)/shard_map/ppermute | solution.py:632
  48.2 11.1 %collective-permute-start.16 = (bf16[256,128]{1,0:T(8,128)(2,1)S(1)}, bf16[256,128]{1,0:T(8,128)(2,1)S(1)}, u32[]{:S(2)}, u32[]{:S(2)}) collective-permute-start(bf16[256,128]{1,0:T(8,128)(2,1)S(1)} %get-tuple-element.85), channel_id=1, source_target_pairs={{0,4},{1,5},{2,6},{3,7},{4,0},{5,1},{6,2},{7,3},{8,12},{9,13},{10,... | collective-permute-start | bytes 196616 | tf_op jit(solution)/shard_map/ppermute | solution.py:632
  48.5 11.8 %collective-permute-start.17 = (bf16[256,128]{1,0:T(8,128)(2,1)S(1)}, bf16[256,128]{1,0:T(8,128)(2,1)S(1)}, u32[]{:S(2)}, u32[]{:S(2)}) collective-permute-start(bf16[256,128]{1,0:T(8,128)(2,1)S(1)} %get-tuple-element.86), channel_id=1, source_target_pairs={{0,3},{1,4},{2,5},{3,6},{4,7},{5,0},{6,1},{7,2},{8,11},{9,12},{10,... | collective-permute-start | bytes 196616 | tf_op jit(solution)/shard_map/ppermute | solution.py:632
  51.1 10.6 %collective-permute-start.11 = (bf16[256,128]{1,0:T(8,128)(2,1)S(1)}, bf16[256,128]{1,0:T(8,128)(2,1)S(1)}, u32[]{:S(2)}, u32[]{:S(2)}) collective-permute-start(bf16[256,128]{1,0:T(8,128)(2,1)S(1)} %get-tuple-element.79), channel_id=1, source_target_pairs={{0,2},{1,3},{2,4},{3,5},{4,6},{5,7},{6,0},{7,1},{8,10},{9,11},{10,... | collective-permute-start | bytes 196616 | tf_op jit(solution)/shard_map/ppermute | solution.py:632
  53.0 8.7 %collective-permute-start.12 = (bf16[256,128]{1,0:T(8,128)(2,1)S(1)}, bf16[256,128]{1,0:T(8,128)(2,1)S(1)}, u32[]{:S(2)}, u32[]{:S(2)}) collective-permute-start(bf16[256,128]{1,0:T(8,128)(2,1)S(1)} %get-tuple-element.80), channel_id=1, source_target_pairs={{0,1},{1,2},{2,3},{3,4},{4,5},{5,6},{6,7},{7,0},{8,9},{9,10},{10,1... | collective-permute-start | bytes 196616 | tf_op jit(solution)/shard_map/ppermute | solution.py:632
  53.7 8.2 %collective-permute-start.13 = (bf16[256,128]{1,0:T(8,128)(2,1)S(1)}, bf16[256,128]{1,0:T(8,128)(2,1)S(1)}, u32[]{:S(2)}, u32[]{:S(2)}) collective-permute-start(bf16[256,128]{1,0:T(8,128)(2,1)S(1)} %get-tuple-element.82), channel_id=1, source_target_pairs={{0,7},{1,0},{2,1},{3,2},{4,3},{5,4},{6,5},{7,6},{8,15},{9,8},{10,9... | collective-permute-start | bytes 196616 | tf_op jit(solution)/shard_map/ppermute | solution.py:632

commit v10 on v8

--- a/solution.py
+++ b/solution.py
@@ -14,11 +14,11 @@
 COLS = 8
 WIDE = SIDE + 4
 HID = SIDE + 2
-EARLY = ((1, 3), (4, 4))
-LATER = ((8, 4),)
+EARLY = ((1, 3), (4, 4), (8, 4))
 LATE = ((12, 3),)
 LATE_PLANES = 3
 SENT = (4, 3, 5, 2, 6, 1, 7)
+RETURNED = (1, 7, 6, 4, 2, 3, 5)
 UP_OFFSETS = 4
 DOWN_LIMIT = 62 * 1024 * 1024
 VMEM_LIMIT = 24 * 1024 * 1024
@@ -453,8 +453,8 @@
 
 
 def middle_kernel(source_ref, *refs):
-    block_ref, before_ref, after_ref, early_ref, later_ref, wide1_ref, wide2_ref = refs[:7]
-    h_here, h_next, coarse_ref, side, late, here, moved = refs[7:]
+    block_ref, before_ref, after_ref, early_ref, wide1_ref, wide2_ref = refs[:6]
+    h_here, h_next, coarse_ref, side, late, here, moved = refs[6:]
     width = block_ref.shape[1]
     inner = SIDE - 2
     inner_planes(source_ref, block_ref, wide1_ref, late, here, moved, LATE)
@@ -473,7 +473,7 @@
         flags.append(spread_flags(pairs, depths))
     value = activate(value.reshape(2, inner, 2, COLS, width), jnp.stack(flags, axis=0))
     side[...] = value.reshape(2, inner, 16, width).astype(jnp.bfloat16)
-    centres = [ref[k] for ref in (early_ref, later_ref, late) for k in range(ref.shape[0])]
+    centres = [ref[k] for ref in (early_ref, late) for k in range(ref.shape[0])]
     for d in range(inner):
         plane = jnp.concatenate([side[0, d], centres[d], side[1, d]], axis=0)
         h_here[d] = plane
@@ -486,7 +486,7 @@
         coarse_ref[rows] = value.reshape(512, width).astype(jnp.bfloat16)
 
 
-def middle_call(source, block, before, after, early, later, wide1, wide2):
+def middle_call(source, block, before, after, early, wide1, wide2):
     mid = block.shape[1]
     smem = pl.BlockSpec(memory_space=pltpu.SMEM)
     vmem = pl.BlockSpec(memory_space=pltpu.VMEM)
@@ -494,7 +494,7 @@
     hidden = (inner, HID * COLS, mid)
     return pl.pallas_call(
         middle_kernel,
-        in_specs=[smem] + [vmem] * 7,
+        in_specs=[smem] + [vmem] * 6,
         out_specs=[vmem] * 3,
         out_shape=[
             jax.ShapeDtypeStruct(shape, jnp.bfloat16) for shape in (hidden, hidden, (1024, mid))
@@ -508,7 +508,7 @@
         compiler_params=pltpu.CompilerParams(vmem_limit_bytes=VMEM_LIMIT),
         cost_estimate=conv_cost(inner * (4 + LATE_PLANES) * COLS + 1024, mid),
         name="middle",
-    )(source, block, before, after, early, later, wide1, wide2)
+    )(source, block, before, after, early, wide1, wide2)
 
 
 def scatter_bricks(source_ref, stage, value, depth_brick):
@@ -636,23 +636,21 @@
     prepared = lax.optimization_barrier(tuple(prepare_call(*later)))
     arrived[0], mask, wide1, wide2 = prepared
     block, even, odd = place_call(base, slot_source, [arrived[j] for j in range(K)])
+    even = swap_face(even, "xy", 0)
     odd = swap_face(odd, "xy", 1)
     early = inner_call(slot_source, block, wide1, EARLY)
-    even, early = lax.optimization_barrier((even, early))
-    even = swap_face(even, "xy", 0)
-    later = inner_call(slot_source, block, wide1, LATER)
-    even, odd, later = lax.optimization_barrier((even, odd, later))
+    even, odd, early = lax.optimization_barrier((even, odd, early))
     before, after, even, odd = edge_call(counts, base, slot_source, block, even, odd)
     even = swap_face(even, "gz", 0)
     odd = swap_face(odd, "gz", 1)
-    middle = middle_call(slot_source, block, before, after, early, later, wide1, wide2)
+    middle = middle_call(slot_source, block, before, after, early, wide1, wide2)
     coarse, *back = final_call(
         counts[0], base, slot_source, block, (before, after, even, odd), middle, wide1, wide2
     )
-    octant = {j: from_behind(back[j], "xy", -j) for j in SENT}
+    octant = {j: from_behind(back[j], "xy", -j) for j in RETURNED}
     octant[0] = back[0]
-    fine_out = up_call(fine, mask, w_up, [octant[j] for j in (2, 3, 4, 5)], 1, None)
-    fine_out = up_call(fine, mask, w_up, [octant[j] for j in (6, 7, 0, 1)], 3, fine_out)
+    fine_out = up_call(fine, mask, w_up, [octant[j] for j in (6, 7, 0, 1)], 3, None)
+    fine_out = up_call(fine, mask, w_up, [octant[j] for j in (2, 3, 4, 5)], 1, fine_out)
     return fine_out, coarse.reshape(SIDE, SIDE, COLS, mid)
 
 

time: 61.7 us -> 61.1 us (level)
  waiting for transfers between devices: 4.43 us -> 8.77 us
  starting transfers between devices: 34.7 us -> 30.5 us
  Pallas kernels: 19.7 us -> 19 us
    ppermute x14, waiting for transfers between devices: 3.42 us -> 8.76 us  [from_behind(): return lax.ppermute(value, axis, pairs)]
    ppermute x14, starting transfers between devices: 29.6 us -> 27.1 us  [from_behind(): return lax.ppermute(value, axis, pairs)]
    ppermute x4, starting transfers between devices: 5.11 us -> 3.49 us  [swap_face(): return lax.ppermute(face, axis, list(enumerate(partner)))]
    ppermute x4, waiting for transfers between devices: 1.01 us -> 0.01 us  [swap_face(): return lax.ppermute(face, axis, list(enumerate(partner)))]
    pallas_call x2 -> x1, Pallas kernels: 3.07 us -> 2.36 us  [inner_call(): pl.pallas_call(functools.partial(inner_kernel, groups), in_specs=[smem, v...]
  transfers between devices with their start and end apart: 18 -> 18, of which waited for: 4 -> 5; matrix products, arithmetic and copies ran while one was open for 0% -> 0% of each run, Pallas kernels for 14% -> 13%
where the time goes in v10:
time: 61.1 us; the launch traced here: 60.8 us
  starting transfers between devices  30.5 us (50%)
  Pallas kernels  19 us (31%)
  waiting for transfers between devices  8.77 us (14%)
  local copies, waits for them, and re-layouts  1.62 us (3%)
  between operations  0.82 us (1%)
    ppermute x14, starting transfers between devices, from_behind(): return lax.ppermute(value, axis, pairs)  27.1 us
    ppermute x14, waiting for transfers between devices, from_behind(): return lax.ppermute(value, axis, pairs)  8.76 us
    pallas_call x1, Pallas kernels, final_call(): pl.pallas_call(functools.partial(final_kernel, count), in_specs=[smem, sm...  4.03 us
    pallas_call x1, Pallas kernels, down_call(): pl.pallas_call(functools.partial(down_kernel, offsets), in_specs=[hbm, hb...  3.9 us
    ppermute x4, starting transfers between devices, swap_face(): return lax.ppermute(face, axis, list(enumerate(partner)))  3.49 us
    pallas_call x1, Pallas kernels, middle_call(): pl.pallas_call(middle_kernel, in_specs=[smem] + [vmem] * 6, out_specs=[vm...  3.23 us
    pallas_call x2, Pallas kernels, up_call(): pl.pallas_call(up_kernel, grid=(UP_OFFSETS * CAP // step,), in_specs=[pl....  2.99 us
    pallas_call x1, Pallas kernels, inner_call(): pl.pallas_call(functools.partial(inner_kernel, groups), in_specs=[smem, v...  2.36 us
  transfers between devices with their start and end apart: 18, of which 5 were waited for; matrix products, arithmetic and copies ran while one was open for 0% of the time, Pallas kernels for 13%

profile of v10, /device:TPU:0, one launch (start us, length us, event | category | flops | bytes accessed | tf_op | source)
XLA Modules:
  0.0 60.8 jit_solution(15404029204218518457)
XLA Ops:
  0.7 3.9 %down.1 = (bf16[256,128]{1,0:T(8,128)(2,1)}, bf16[256,128]{1,0:T(8,128)(2,1)}, bf16[256,128]{1,0:T(8,128)(2,1)}, bf16[256,128]{1,0:T(8,128)(2,1)}, bf16[256,128]...) custom-call(bf16[32,64,512]{2,1,0:T(8,128)(2,1)} %fine_ref.4, s32[32,512]{1,0:T(8,128)} %mask_ref, ...), custom_call_target="tpu_custom_call" | custom-call | flops 234881024 | bytes 1835008 | tf_op jit(solution)/shard_map/down/pallas_call | solution.py:83
  4.6 5.0 %collective-permute-start = (bf16[256,128]{1,0:T(8,128)(2,1)}, bf16[256,128]{1,0:T(8,128)(2,1)S(1)}, u32[]{:S(2)}, u32[]{:S(2)}) collective-permute-start(bf16[256,128]{1,0:T(8,128)(2,1)} %get-tuple-element.41), channel_id=1, source_target_pairs={{0,5},{1,6},{2,7},{3,0},{4,1},{5,2},{6,3},{7,4},{8,13},{9,14},{10,... | collective-permute-start | bytes 196616 | tf_op jit(solution)/shard_map/ppermute | solution.py:617
  9.6 1.5 %collective-permute-start.1 = (bf16[256,128]{1,0:T(8,128)(2,1)}, bf16[256,128]{1,0:T(8,128)(2,1)S(1)}, u32[]{:S(2)}, u32[]{:S(2)}) collective-permute-start(bf16[256,128]{1,0:T(8,128)(2,1)} %get-tuple-element.49), channel_id=1, source_target_pairs={{0,1},{1,2},{2,3},{3,4},{4,5},{5,6},{6,7},{7,0},{8,9},{9,10},{10,1... | collective-permute-start | bytes 196616 | tf_op jit(solution)/shard_map/ppermute | solution.py:617
  11.2 0.0 collective-permute-start.2
  11.2 1.8 %collective-permute-start.3 = (bf16[256,128]{1,0:T(8,128)(2,1)}, bf16[256,128]{1,0:T(8,128)(2,1)S(1)}, u32[]{:S(2)}, u32[]{:S(2)}) collective-permute-start(bf16[256,128]{1,0:T(8,128)(2,1)} %get-tuple-element.51), channel_id=1, source_target_pairs={{0,3},{1,4},{2,5},{3,6},{4,7},{5,0},{6,1},{7,2},{8,11},{9,12},{10,... | collective-permute-start | bytes 196616 | tf_op jit(solution)/shard_map/ppermute | solution.py:617
  13.0 3.5 %collective-permute-start.4 = (bf16[256,128]{1,0:T(8,128)(2,1)}, bf16[256,128]{1,0:T(8,128)(2,1)S(1)}, u32[]{:S(2)}, u32[]{:S(2)}) collective-permute-start(bf16[256,128]{1,0:T(8,128)(2,1)} %get-tuple-element.52), channel_id=1, source_target_pairs={{0,4},{1,5},{2,6},{3,7},{4,0},{5,1},{6,2},{7,3},{8,12},{9,13},{10,... | collective-permute-start | bytes 196616 | tf_op jit(solution)/shard_map/ppermute | solution.py:617
  16.5 1.4 %collective-permute-start.5 = (bf16[256,128]{1,0:T(8,128)(2,1)}, bf16[256,128]{1,0:T(8,128)(2,1)S(1)}, u32[]{:S(2)}, u32[]{:S(2)}) collective-permute-start(bf16[256,128]{1,0:T(8,128)(2,1)} %get-tuple-element.54), channel_id=1, source_target_pairs={{0,6},{1,7},{2,0},{3,1},{4,2},{5,3},{6,4},{7,5},{8,14},{9,15},{10,... | collective-permute-start | bytes 196616 | tf_op jit(solution)/shard_map/ppermute | solution.py:617
  17.8 1.0 %collective-permute-start.6 = (bf16[256,128]{1,0:T(8,128)(2,1)}, bf16[256,128]{1,0:T(8,128)(2,1)S(1)}, u32[]{:S(2)}, u32[]{:S(2)}) collective-permute-start(bf16[256,128]{1,0:T(8,128)(2,1)} %get-tuple-element.55), channel_id=1, source_target_pairs={{0,7},{1,0},{2,1},{3,2},{4,3},{5,4},{6,5},{7,6},{8,15},{9,8},{10,9... | collective-permute-start | bytes 196616 | tf_op jit(solution)/shard_map/ppermute | solution.py:617
  18.9 0.1 pad_add_fusion.base_ref
  19.0 1.6 %copy-done = bf16[32,64,512]{2,1,0:T(8,128)(2,1)S(1)} copy-done((bf16[32,64,512]{2,1,0:T(8,128)(2,1)S(1)}, bf16[32,64,512]{2,1,0:T(8,128)(2,1)}, u32[]{:S(2)}) %copy-start) | copy-done | bytes 2097176
  20.6 1.1 %prepare.1 = (bf16[256,128]{1,0:T(8,128)(2,1)S(1)}, bf16[2048,512]{1,0:T(8,128)(2,1)S(1)}, bf16[1152,384]{1,0:T(8,128)(2,1)S(1)}, bf16[1152,384]{1,0:T(8,128)(2,1)S(1)}) custom-call(bf16[32,64,512]{2,1,0:T(8,128)(2,1)S(1)} %copy-done, s32[32,512]{1,0:T(8,128)S(1)} %copy-done.6, bf16[512,128]{1,0:T(8,128)(2,1)S(1)} %copy-done.5, ...), custom_call_target="tpu_custom_call" | custom-call | flops 268435456 | bytes 2097152 | tf_op jit(solution)/shard_map/prepare/pallas_call | solution.py:124
  21.6 0.8 %collective-permute-done.3.refs_3_ = bf16[256,128]{1,0:T(8,128)(2,1)S(1)} collective-permute-done((bf16[256,128]{1,0:T(8,128)(2,1)}, bf16[256,128]{1,0:T(8,128)(2,1)S(1)}, u32[]{:S(2)}, u32[]{:S(2)}) %collective-permute-start.3) | collective-permute-done | bytes 65568 | tf_op jit(solution)/shard_map/ppermute | solution.py:617
  22.5 0.3 collective-permute-done.6.refs_7_
  22.7 0.8 %place.1 = (bf16[2048,128]{1,0:T(8,128)(2,1)S(1)}, bf16[288,128]{1,0:T(8,128)(2,1)S(1)}, bf16[288,128]{1,0:T(8,128)(2,1)S(1)}) custom-call(s32[2]{0:T(128)S(1)} %pad_add_fusion.base_ref, s32[32]{0:T(128)S(1)} %copy-done.7, bf16[256,128]{1,0:T(8,128)(2,1)S(1)} %get-tuple-element.48.refs_0_, bf16[256,128]{1,0:T(8,128)(2,1)S(1)} %collective-permute-done.1.refs_1_, ...), custom_call_target="tpu_custom_call" | custom-call | tf_op jit(solution)/shard_map/place/pallas_call | solution.py:260
  23.5 2.1 %collective-permute-start.7 = (bf16[288,128]{1,0:T(8,128)(2,1)S(1)}, bf16[288,128]{1,0:T(8,128)(2,1)S(1)}, u32[]{:S(2)}, u32[]{:S(2)}) collective-permute-start(bf16[288,128]{1,0:T(8,128)(2,1)S(1)} %get-tuple-element.57), channel_id=1, source_target_pairs={{0,1},{1,0},{2,3},{3,2},{4,5},{5,4},{6,7},{7,6},{8,9},{9,8},{10,11... | collective-permute-start | bytes 221192 | tf_op jit(solution)/shard_map/ppermute | solution.py:625
  25.6 0.7 %collective-permute-start.8 = (bf16[288,128]{1,0:T(8,128)(2,1)S(1)}, bf16[288,128]{1,0:T(8,128)(2,1)S(1)}, u32[]{:S(2)}, u32[]{:S(2)}) collective-permute-start(bf16[288,128]{1,0:T(8,128)(2,1)S(1)} %get-tuple-element.58), channel_id=1, source_target_pairs={{0,0},{1,2},{2,1},{3,4},{4,3},{5,6},{6,5},{7,7},{8,8},{9,10},{10,9... | collective-permute-start | bytes 221192 | tf_op jit(solution)/shard_map/ppermute | solution.py:625
  26.3 2.4 %inner.1.refs_3_ = bf16[11,112,128]{2,1,0:T(8,128)(2,1)S(1)} custom-call(s32[32]{0:T(128)S(1)} %copy-done.7, bf16[2048,128]{1,0:T(8,128)(2,1)S(1)} %get-tuple-element.56.block_ref.refs_0_, bf16[1152,384]{1,0:T(8,128)(2,1)S(1)} %get-tuple-element.59.wide1_ref.refs_4_.refs_8_), custom_call_target="tpu_custom_call" | custom-call | flops 1089994752 | bytes 1769472 | tf_op jit(solution)/shard_map/inner/pallas_call | solution.py:419
  28.7 0.6 %edge.1 = (bf16[288,128]{1,0:T(8,128)(2,1)S(1)}, bf16[288,128]{1,0:T(8,128)(2,1)S(1)}, bf16[368,128]{1,0:T(8,128)(2,1)S(1)}, bf16[368,128]{1,0:T(8,128)(2,1)S(1)}) custom-call(s32[2]{0:T(128)S(1)} %pad_add_fusion.base_ref, s32[32]{0:T(128)S(1)} %copy-done.7, bf16[2048,128]{1,0:T(8,128)(2,1)S(1)} %get-tuple-element.56.block_ref.refs_0_, ...), custom_call_target="tpu_custom_call" | custom-call | tf_op jit(solution)/shard_map/edge/pallas_call | solution.py:310
  29.3 0.1 collective-permute-start.9
  29.4 0.7 %collective-permute-start.10 = (bf16[368,128]{1,0:T(8,128)(2,1)S(1)}, bf16[368,128]{1,0:T(8,128)(2,1)S(1)}, u32[]{:S(2)}, u32[]{:S(2)}) collective-permute-start(bf16[368,128]{1,0:T(8,128)(2,1)S(1)} %get-tuple-element.65), channel_id=1, source_target_pairs={{0,0},{8,16},{16,8},{24,24},{1,1},{9,17},{17,9},{25,25},{2,2},{10,... | collective-permute-start | bytes 282632 | tf_op jit(solution)/shard_map/ppermute | solution.py:625
  30.1 3.2 %middle.1 = (bf16[14,144,128]{2,1,0:T(8,128)(2,1)S(1)}, bf16[14,144,128]{2,1,0:T(8,128)(2,1)S(1)}, bf16[1024,128]{1,0:T(8,128)(2,1)S(1)}) custom-call(s32[32]{0:T(128)S(1)} %copy-done.7, bf16[2048,128]{1,0:T(8,128)(2,1)S(1)} %get-tuple-element.56.block_ref.refs_0_, bf16[288,128]{1,0:T(8,128)(2,1)S(1)} %get-tuple-element.62.refs_1_, ...), custom_call_target="tpu_custom_call" | custom-call | flops 1599602688 | bytes 1769472 | tf_op jit(solution)/shard_map/middle/pallas_call | solution.py:495
  33.3 4.0 %final.1 = (bf16[2048,128]{1,0:T(8,128)(2,1)}, bf16[256,128]{1,0:T(8,128)(2,1)S(1)}, bf16[256,128]{1,0:T(8,128)(2,1)S(1)}, bf16[256,128]{1,0:T(8,128)(2,1)S(1)},...) custom-call(s32[2]{0:T(128)S(1)} %pad_add_fusion.base_ref, ...), custom_call_target="tpu_custom_call" | custom-call | flops 1415577600 | bytes 1769472 | tf_op jit(solution)/shard_map/final/pallas_call | solution.py:593
  37.4 5.1 %collective-permute-start.15 = (bf16[256,128]{1,0:T(8,128)(2,1)S(1)}, bf16[256,128]{1,0:T(8,128)(2,1)S(1)}, u32[]{:S(2)}, u32[]{:S(2)}) collective-permute-start(bf16[256,128]{1,0:T(8,128)(2,1)S(1)} %get-tuple-element.75), channel_id=1, source_target_pairs={{0,2},{1,3},{2,4},{3,5},{4,6},{5,7},{6,0},{7,1},{8,10},{9,11},{10,... | collective-permute-start | bytes 196616 | tf_op jit(solution)/shard_map/ppermute | solution.py:617
  42.4 0.0 collective-permute-start.16
  42.5 4.7 %collective-permute-start.17 = (bf16[256,128]{1,0:T(8,128)(2,1)S(1)}, bf16[256,128]{1,0:T(8,128)(2,1)S(1)}, u32[]{:S(2)}, u32[]{:S(2)}) collective-permute-start(bf16[256,128]{1,0:T(8,128)(2,1)S(1)} %get-tuple-element.78), channel_id=1, source_target_pairs={{0,7},{1,0},{2,1},{3,2},{4,3},{5,4},{6,5},{7,6},{8,15},{9,8},{10,9... | collective-permute-start | bytes 196616 | tf_op jit(solution)/shard_map/ppermute | solution.py:617
  47.2 2.9 %collective-permute-start.13 = (bf16[256,128]{1,0:T(8,128)(2,1)S(1)}, bf16[256,128]{1,0:T(8,128)(2,1)S(1)}, u32[]{:S(2)}, u32[]{:S(2)}) collective-permute-start(bf16[256,128]{1,0:T(8,128)(2,1)S(1)} %get-tuple-element.73), channel_id=1, source_target_pairs={{0,4},{1,5},{2,6},{3,7},{4,0},{5,1},{6,2},{7,3},{8,12},{9,13},{10,... | collective-permute-start | bytes 196616 | tf_op jit(solution)/shard_map/ppermute | solution.py:617
  50.1 0.1 collective-permute-start.14
  50.2 1.5 %up.2.refs_4_ = bf16[32,64,512]{2,1,0:T(8,128)(2,1)} custom-call(bf16[32,64,512]{2,1,0:T(8,128)(2,1)S(1)} %copy-done.1, bf16[2048,512]{1,0:T(8,128)(2,1)S(1)} %get-tuple-element.47.mask_ref, bf16[128,512]{1,0:T(8,128)(2,1)S(1)} %copy-done.4, bf16[256,128]{1,0:T(8,128)(2,1)S(1)} %collective-permute-done.15.refs_0_, ...), custom_call_target="tpu_custom_call" | custom-call | flops 134217728 | bytes 2097152 | tf_op jit(solution)/shard_map/up/pallas_call | solution.py:171
  51.7 0.6 %collective-permute-done.12.refs_1_ = bf16[256,128]{1,0:T(8,128)(2,1)S(1)} collective-permute-done((bf16[256,128]{1,0:T(8,128)(2,1)S(1)}, bf16[256,128]{1,0:T(8,128)(2,1)S(1)}, u32[]{:S(2)}, u32[]{:S(2)}) %collective-permute-start.12) | collective-permute-done | bytes 65568 | tf_op jit(solution)/shard_map/ppermute | solution.py:617
  52.3 4.1 %collective-permute-done.13.refs_2_ = bf16[256,128]{1,0:T(8,128)(2,1)S(1)} collective-permute-done((bf16[256,128]{1,0:T(8,128)(2,1)S(1)}, bf16[256,128]{1,0:T(8,128)(2,1)S(1)}, u32[]{:S(2)}, u32[]{:S(2)}) %collective-permute-start.13) | collective-permute-done | bytes 65568 | tf_op jit(solution)/shard_map/ppermute | solution.py:617
  56.5 2.9 %collective-permute-done.14.refs_3_ = bf16[256,128]{1,0:T(8,128)(2,1)S(1)} collective-permute-done((bf16[256,128]{1,0:T(8,128)(2,1)S(1)}, bf16[256,128]{1,0:T(8,128)(2,1)S(1)}, u32[]{:S(2)}, u32[]{:S(2)}) %collective-permute-start.14) | collective-permute-done | bytes 65568 | tf_op jit(solution)/shard_map/ppermute | solution.py:617
  59.4 1.5 %up.3 = bf16[32,64,512]{2,1,0:T(8,128)(2,1)} custom-call(bf16[32,64,512]{2,1,0:T(8,128)(2,1)S(1)} %copy-done.1, bf16[2048,512]{1,0:T(8,128)(2,1)S(1)} %get-tuple-element.47.mask_ref, bf16[128,512]{1,0:T(8,128)(2,1)S(1)} %copy-done.4, bf16[256,128]{1,0:T(8,128)(2,1)S(1)} %collective-permute-done.11.refs_0_, ...), custom_call_target="tpu_custom_call", output_to_operand_aliasing={{}: (7, {})} | custom-call | flops 134217728 | bytes 2097152 | tf_op jit(solution)/shard_map/up/pallas_call | solution.py:171
  (30 shorter events, 0.1 us)
Async XLA Ops:
  0.6 18.3 %copy-start.5 = (bf16[512,128]{1,0:T(8,128)(2,1)S(1)}, bf16[512,128]{1,0:T(8,128)(2,1)}, u32[]{:S(2)}) copy-start(bf16[512,128]{1,0:T(8,128)(2,1)} %w_down_ref) | copy-start | bytes 393220
  0.6 18.3 %copy-start.6 = (s32[32,512]{1,0:T(8,128)S(1)}, s32[32,512]{1,0:T(8,128)}, u32[]{:S(2)}) copy-start(s32[32,512]{1,0:T(8,128)} %mask_ref) | copy-start | bytes 196612
  0.7 18.3 %copy-start.3 = (bf16[27,128,128]{2,1,0:T(8,128)(2,1)S(1)}, bf16[27,128,128]{2,1,0:T(8,128)(2,1)}, u32[]{:S(2)}) copy-start(bf16[27,128,128]{2,1,0:T(8,128)(2,1)} %w2_ref) | copy-start | bytes 2654212
  0.7 18.3 %copy-start.2 = (bf16[27,128,128]{2,1,0:T(8,128)(2,1)S(1)}, bf16[27,128,128]{2,1,0:T(8,128)(2,1)}, u32[]{:S(2)}) copy-start(bf16[27,128,128]{2,1,0:T(8,128)(2,1)} %w1_ref) | copy-start | bytes 2654212
  4.6 18.1 %copy-start.7 = (s32[32]{0:T(128)S(1)}, s32[32]{0:T(128)}, u32[]{:S(2)}) copy-start(s32[32]{0:T(128)} %source_ref.9) | copy-start | bytes 388
  4.6 11.9 %collective-permute-start = (bf16[256,128]{1,0:T(8,128)(2,1)}, bf16[256,128]{1,0:T(8,128)(2,1)S(1)}, u32[]{:S(2)}, u32[]{:S(2)}) collective-permute-start(bf16[256,128]{1,0:T(8,128)(2,1)} %get-tuple-element.41), channel_id=1, source_target_pairs={{0,5},{1,6},{2,7},{3,0},{4,1},{5,2},{6,3},{7,4},{8,13},{9,14},{10,... | collective-permute-start | bytes 196616 | tf_op jit(solution)/shard_map/ppermute | solution.py:617
  9.6 8.2 %collective-permute-start.1 = (bf16[256,128]{1,0:T(8,128)(2,1)}, bf16[256,128]{1,0:T(8,128)(2,1)S(1)}, u32[]{:S(2)}, u32[]{:S(2)}) collective-permute-start(bf16[256,128]{1,0:T(8,128)(2,1)} %get-tuple-element.49), channel_id=1, source_target_pairs={{0,1},{1,2},{2,3},{3,4},{4,5},{5,6},{6,7},{7,0},{8,9},{9,10},{10,1... | collective-permute-start | bytes 196616 | tf_op jit(solution)/shard_map/ppermute | solution.py:617
  11.2 10.5 %collective-permute-start.2 = (bf16[256,128]{1,0:T(8,128)(2,1)}, bf16[256,128]{1,0:T(8,128)(2,1)S(1)}, u32[]{:S(2)}, u32[]{:S(2)}) collective-permute-start(bf16[256,128]{1,0:T(8,128)(2,1)} %get-tuple-element.50), channel_id=1, source_target_pairs={{0,2},{1,3},{2,4},{3,5},{4,6},{5,7},{6,0},{7,1},{8,10},{9,11},{10,... | collective-permute-start | bytes 196616 | tf_op jit(solution)/shard_map/ppermute | solution.py:617
  11.2 11.3 %collective-permute-start.3 = (bf16[256,128]{1,0:T(8,128)(2,1)}, bf16[256,128]{1,0:T(8,128)(2,1)S(1)}, u32[]{:S(2)}, u32[]{:S(2)}) collective-permute-start(bf16[256,128]{1,0:T(8,128)(2,1)} %get-tuple-element.51), channel_id=1, source_target_pairs={{0,3},{1,4},{2,5},{3,6},{4,7},{5,0},{6,1},{7,2},{8,11},{9,12},{10,... | collective-permute-start | bytes 196616 | tf_op jit(solution)/shard_map/ppermute | solution.py:617
  13.0 9.5 %collective-permute-start.4 = (bf16[256,128]{1,0:T(8,128)(2,1)}, bf16[256,128]{1,0:T(8,128)(2,1)S(1)}, u32[]{:S(2)}, u32[]{:S(2)}) collective-permute-start(bf16[256,128]{1,0:T(8,128)(2,1)} %get-tuple-element.52), channel_id=1, source_target_pairs={{0,4},{1,5},{2,6},{3,7},{4,0},{5,1},{6,2},{7,3},{8,12},{9,13},{10,... | collective-permute-start | bytes 196616 | tf_op jit(solution)/shard_map/ppermute | solution.py:617
  16.5 6.0 %collective-permute-start.5 = (bf16[256,128]{1,0:T(8,128)(2,1)}, bf16[256,128]{1,0:T(8,128)(2,1)S(1)}, u32[]{:S(2)}, u32[]{:S(2)}) collective-permute-start(bf16[256,128]{1,0:T(8,128)(2,1)} %get-tuple-element.54), channel_id=1, source_target_pairs={{0,6},{1,7},{2,0},{3,1},{4,2},{5,3},{6,4},{7,5},{8,14},{9,15},{10,... | collective-permute-start | bytes 196616 | tf_op jit(solution)/shard_map/ppermute | solution.py:617
  17.8 4.9 %collective-permute-start.6 = (bf16[256,128]{1,0:T(8,128)(2,1)}, bf16[256,128]{1,0:T(8,128)(2,1)S(1)}, u32[]{:S(2)}, u32[]{:S(2)}) collective-permute-start(bf16[256,128]{1,0:T(8,128)(2,1)} %get-tuple-element.55), channel_id=1, source_target_pairs={{0,7},{1,0},{2,1},{3,2},{4,3},{5,4},{6,5},{7,6},{8,15},{9,8},{10,9... | collective-permute-start | bytes 196616 | tf_op jit(solution)/shard_map/ppermute | solution.py:617
  19.0 1.6 %copy-start = (bf16[32,64,512]{2,1,0:T(8,128)(2,1)S(1)}, bf16[32,64,512]{2,1,0:T(8,128)(2,1)}, u32[]{:S(2)}) copy-start(bf16[32,64,512]{2,1,0:T(8,128)(2,1)} %fine_ref.4) | copy-start | bytes 6291460
  23.5 5.1 %collective-permute-start.7 = (bf16[288,128]{1,0:T(8,128)(2,1)S(1)}, bf16[288,128]{1,0:T(8,128)(2,1)S(1)}, u32[]{:S(2)}, u32[]{:S(2)}) collective-permute-start(bf16[288,128]{1,0:T(8,128)(2,1)S(1)} %get-tuple-element.57), channel_id=1, source_target_pairs={{0,1},{1,0},{2,3},{3,2},{4,5},{5,4},{6,7},{7,6},{8,9},{9,8},{10,11... | collective-permute-start | bytes 221192 | tf_op jit(solution)/shard_map/ppermute | solution.py:625
  25.6 3.0 %collective-permute-start.8 = (bf16[288,128]{1,0:T(8,128)(2,1)S(1)}, bf16[288,128]{1,0:T(8,128)(2,1)S(1)}, u32[]{:S(2)}, u32[]{:S(2)}) collective-permute-start(bf16[288,128]{1,0:T(8,128)(2,1)S(1)} %get-tuple-element.58), channel_id=1, source_target_pairs={{0,0},{1,2},{2,1},{3,4},{4,3},{5,6},{6,5},{7,7},{8,8},{9,10},{10,9... | collective-permute-start | bytes 221192 | tf_op jit(solution)/shard_map/ppermute | solution.py:625
  29.3 4.0 %collective-permute-start.9 = (bf16[368,128]{1,0:T(8,128)(2,1)S(1)}, bf16[368,128]{1,0:T(8,128)(2,1)S(1)}, u32[]{:S(2)}, u32[]{:S(2)}) collective-permute-start(bf16[368,128]{1,0:T(8,128)(2,1)S(1)} %get-tuple-element.64), channel_id=1, source_target_pairs={{0,8},{8,0},{16,24},{24,16},{1,9},{9,1},{17,25},{25,17},{2,10},{10... | collective-permute-start | bytes 282632 | tf_op jit(solution)/shard_map/ppermute | solution.py:625
  29.4 3.9 %collective-permute-start.10 = (bf16[368,128]{1,0:T(8,128)(2,1)S(1)}, bf16[368,128]{1,0:T(8,128)(2,1)S(1)}, u32[]{:S(2)}, u32[]{:S(2)}) collective-permute-start(bf16[368,128]{1,0:T(8,128)(2,1)S(1)} %get-tuple-element.65), channel_id=1, source_target_pairs={{0,0},{8,16},{16,8},{24,24},{1,1},{9,17},{17,9},{25,25},{2,2},{10,... | collective-permute-start | bytes 282632 | tf_op jit(solution)/shard_map/ppermute | solution.py:625
  33.3 16.9 %copy-start.1 = (bf16[32,64,512]{2,1,0:T(8,128)(2,1)S(1)}, bf16[32,64,512]{2,1,0:T(8,128)(2,1)}, u32[]{:S(2)}) copy-start(bf16[32,64,512]{2,1,0:T(8,128)(2,1)} %fine_ref.4) | copy-start | bytes 6291460
  33.3 16.8 %copy-start.4 = (bf16[128,512]{1,0:T(8,128)(2,1)S(1)}, bf16[128,512]{1,0:T(8,128)(2,1)}, u32[]{:S(2)}) copy-start(bf16[128,512]{1,0:T(8,128)(2,1)} %w_ref.3) | copy-start | bytes 393220
  37.4 9.8 %collective-permute-start.15 = (bf16[256,128]{1,0:T(8,128)(2,1)S(1)}, bf16[256,128]{1,0:T(8,128)(2,1)S(1)}, u32[]{:S(2)}, u32[]{:S(2)}) collective-permute-start(bf16[256,128]{1,0:T(8,128)(2,1)S(1)} %get-tuple-element.75), channel_id=1, source_target_pairs={{0,2},{1,3},{2,4},{3,5},{4,6},{5,7},{6,0},{7,1},{8,10},{9,11},{10,... | collective-permute-start | bytes 196616 | tf_op jit(solution)/shard_map/ppermute | solution.py:617
  42.4 7.7 %collective-permute-start.16 = (bf16[256,128]{1,0:T(8,128)(2,1)S(1)}, bf16[256,128]{1,0:T(8,128)(2,1)S(1)}, u32[]{:S(2)}, u32[]{:S(2)}) collective-permute-start(bf16[256,128]{1,0:T(8,128)(2,1)S(1)} %get-tuple-element.76), channel_id=1, source_target_pairs={{0,1},{1,2},{2,3},{3,4},{4,5},{5,6},{6,7},{7,0},{8,9},{9,10},{10,1... | collective-permute-start | bytes 196616 | tf_op jit(solution)/shard_map/ppermute | solution.py:617
  42.5 7.7 %collective-permute-start.17 = (bf16[256,128]{1,0:T(8,128)(2,1)S(1)}, bf16[256,128]{1,0:T(8,128)(2,1)S(1)}, u32[]{:S(2)}, u32[]{:S(2)}) collective-permute-start(bf16[256,128]{1,0:T(8,128)(2,1)S(1)} %get-tuple-element.78), channel_id=1, source_target_pairs={{0,7},{1,0},{2,1},{3,2},{4,3},{5,4},{6,5},{7,6},{8,15},{9,8},{10,9... | collective-permute-start | bytes 196616 | tf_op jit(solution)/shard_map/ppermute | solution.py:617
  47.2 4.5 %collective-permute-start.11 = (bf16[256,128]{1,0:T(8,128)(2,1)S(1)}, bf16[256,128]{1,0:T(8,128)(2,1)S(1)}, u32[]{:S(2)}, u32[]{:S(2)}) collective-permute-start(bf16[256,128]{1,0:T(8,128)(2,1)S(1)} %get-tuple-element.71), channel_id=1, source_target_pairs={{0,6},{1,7},{2,0},{3,1},{4,2},{5,3},{6,4},{7,5},{8,14},{9,15},{10,... | collective-permute-start | bytes 196616 | tf_op jit(solution)/shard_map/ppermute | solution.py:617
  47.2 5.2 %collective-permute-start.12 = (bf16[256,128]{1,0:T(8,128)(2,1)S(1)}, bf16[256,128]{1,0:T(8,128)(2,1)S(1)}, u32[]{:S(2)}, u32[]{:S(2)}) collective-permute-start(bf16[256,128]{1,0:T(8,128)(2,1)S(1)} %get-tuple-element.72), channel_id=1, source_target_pairs={{0,5},{1,6},{2,7},{3,0},{4,1},{5,2},{6,3},{7,4},{8,13},{9,14},{10,... | collective-permute-start | bytes 196616 | tf_op jit(solution)/shard_map/ppermute | solution.py:617
  47.2 9.3 %collective-permute-start.13 = (bf16[256,128]{1,0:T(8,128)(2,1)S(1)}, bf16[256,128]{1,0:T(8,128)(2,1)S(1)}, u32[]{:S(2)}, u32[]{:S(2)}) collective-permute-start(bf16[256,128]{1,0:T(8,128)(2,1)S(1)} %get-tuple-element.73), channel_id=1, source_target_pairs={{0,4},{1,5},{2,6},{3,7},{4,0},{5,1},{6,2},{7,3},{8,12},{9,13},{10,... | collective-permute-start | bytes 196616 | tf_op jit(solution)/shard_map/ppermute | solution.py:617
  50.1 9.3 %collective-permute-start.14 = (bf16[256,128]{1,0:T(8,128)(2,1)S(1)}, bf16[256,128]{1,0:T(8,128)(2,1)S(1)}, u32[]{:S(2)}, u32[]{:S(2)}) collective-permute-start(bf16[256,128]{1,0:T(8,128)(2,1)S(1)} %get-tuple-element.74), channel_id=1, source_target_pairs={{0,3},{1,4},{2,5},{3,6},{4,7},{5,0},{6,1},{7,2},{8,11},{9,12},{10,... | collective-permute-start | bytes 196616 | tf_op jit(solution)/shard_map/ppermute | solution.py:617

commit v11 on v10

--- a/solution.py
+++ b/solution.py
@@ -19,7 +19,6 @@
 LATE_PLANES = 3
 SENT = (4, 3, 5, 2, 6, 1, 7)
 RETURNED = (1, 7, 6, 4, 2, 3, 5)
-UP_OFFSETS = 4
 DOWN_LIMIT = 62 * 1024 * 1024
 VMEM_LIMIT = 24 * 1024 * 1024
 
@@ -43,7 +42,7 @@
 def down_kernel(offsets, fine_hbm, mask_hbm, w_hbm, *refs):
     count = len(offsets)
     outs = refs[:count]
-    fine_ref, mask_ref, w_ref, wide_ref, sems = refs[count:]
+    fine_ref, mask_ref, w_ref, wide_ref, result_ref, sems, out_sems = refs[count:]
     first = [
         pltpu.make_async_copy(mask_hbm, mask_ref, sems.at[count]),
         pltpu.make_async_copy(w_hbm, w_ref, sems.at[count + 1]),
@@ -71,7 +70,10 @@
         y = jnp.dot(jnp.concatenate(x, axis=0), w_ref[...], preferred_element_type=jnp.float32)
         y = y.astype(jnp.bfloat16)
         for part, k in enumerate(group):
-            outs[k][...] = y[part * rows : (part + 1) * rows]
+            result_ref[k] = y[part * rows : (part + 1) * rows]
+            pltpu.make_async_copy(result_ref.at[k], outs[k], out_sems.at[k]).start()
+    for k in range(count):
+        pltpu.make_async_copy(result_ref.at[k], outs[k], out_sems.at[k]).wait()
 
 
 def down_call(fine, mask, w, offsets):
@@ -83,14 +85,16 @@
     outs = pl.pallas_call(
         functools.partial(down_kernel, offsets),
         in_specs=[hbm, hbm, hbm],
-        out_specs=[pl.BlockSpec(memory_space=pltpu.VMEM)] * count,
+        out_specs=[pl.BlockSpec(memory_space=pl.ANY)] * count,
         out_shape=[jax.ShapeDtypeStruct((CAP * cells, mid), jnp.bfloat16)] * count,
         scratch_shapes=[
             pltpu.VMEM((count, CAP, cells, width), fine.dtype),
             pltpu.VMEM(mask.shape, mask.dtype),
             pltpu.VMEM(w.shape, w.dtype),
             pltpu.VMEM((rows, width), jnp.bfloat16),
+            pltpu.VMEM((count, CAP * cells, mid), jnp.bfloat16),
             pltpu.SemaphoreType.DMA((count + 2,)),
+            pltpu.SemaphoreType.DMA((count,)),
         ],
         compiler_params=pltpu.CompilerParams(vmem_limit_bytes=DOWN_LIMIT),
         cost_estimate=pl.CostEstimate(
@@ -140,12 +144,12 @@
     )(fine, mask, w_down, w_first, w_second)
 
 
-def up_kernel(fine_ref, mask_ref, w_ref, *refs):
+def up_kernel(offsets, fine_ref, mask_ref, w_ref, *refs):
     out_ref = refs[-1]
     step = pl.program_id(0)
     bricks, cells, width = fine_ref.shape
     count = bricks // CAP
-    steps = UP_OFFSETS // count
+    steps = offsets // count
     for part in range(count):
         octant = refs[part][...]
         for other in range(1, steps):
@@ -167,20 +171,21 @@
     def place(i):
         return (first + i) % blocks
 
+    count = len(octants)
     partials = [] if partial is None else [partial]
     return pl.pallas_call(
-        up_kernel,
-        grid=(UP_OFFSETS * CAP // step,),
+        functools.partial(up_kernel, count),
+        grid=(count * CAP // step,),
         in_specs=[
             pl.BlockSpec((step, cells, width), lambda i: (place(i), 0, 0)),
             pl.BlockSpec((step * cells, width), lambda i: (place(i), 0)),
             pl.BlockSpec((mid, width), lambda i: (0, 0)),
         ]
-        + [pl.BlockSpec((CAP * cells, mid), lambda i: (0, 0))] * UP_OFFSETS
+        + [pl.BlockSpec((CAP * cells, mid), lambda i: (0, 0))] * count
         + [pl.BlockSpec(memory_space=pl.ANY)] * len(partials),
         out_specs=pl.BlockSpec((step, cells, width), lambda i: (place(i), 0, 0)),
         out_shape=jax.ShapeDtypeStruct(fine.shape, jnp.bfloat16),
-        input_output_aliases={3 + UP_OFFSETS: 0} if partials else {},
+        input_output_aliases={3 + count: 0} if partials else {},
         compiler_params=pltpu.CompilerParams(vmem_limit_bytes=VMEM_LIMIT),
         cost_estimate=pl.CostEstimate(
             flops=bricks * cells * width * mid, bytes_accessed=bricks * cells * width * 2, transcendentals=0
@@ -528,9 +533,9 @@
 
 def final_kernel(count, base_ref, source_ref, *refs):
     block_ref, before_ref, after_ref, even_ref, odd_ref = refs[:5]
-    mid_here, mid_next, mid_ref, wide1_ref, wide2_ref, coarse_ref = refs[5:11]
-    backs = refs[11 : 11 + K]
-    x_here, x_next, h_here, h_next, stage, under_ref, over_ref = refs[11 + K :]
+    mid_here, mid_next, mid_ref, wide1_ref, wide2_ref, first_ref, last_ref = refs[5:12]
+    backs = refs[12 : 12 + K]
+    x_here, x_next, h_here, h_next, stage, under_ref, over_ref = refs[12 + K :]
     width = block_ref.shape[1]
     stage[...] = jnp.zeros(stage.shape, jnp.bfloat16)
     face_in(base_ref[1], count, even_ref, odd_ref, under_ref, over_ref)
@@ -572,15 +577,12 @@
             h_next[index] = mid_next[source]
     for depth_brick in (1, 2):
         rows = slice((depth_brick - 1) * 512, depth_brick * 512)
-        done = mid_ref[rows]
-        coarse_ref[depth_brick * 512 : (depth_brick + 1) * 512] = done
-        done = done.astype(jnp.float32).reshape(4, SIDE, COLS, width)
+        done = mid_ref[rows].astype(jnp.float32).reshape(4, SIDE, COLS, width)
         scatter_bricks(source_ref, stage, done, depth_brick)
-    for depth_brick in (0, 3):
+    for depth_brick, ref in ((0, first_ref), (3, last_ref)):
         value = conv_planes(h_here, h_next, wide2_ref, depth_brick * 2, 4, SIDE * COLS)
         value = coarse_rows(source_ref, block_ref, value, depth_brick)
-        rows = slice(depth_brick * 512, (depth_brick + 1) * 512)
-        coarse_ref[rows] = value.reshape(512, width).astype(jnp.bfloat16)
+        ref[...] = value.reshape(512, width).astype(jnp.bfloat16)
         scatter_bricks(source_ref, stage, value, depth_brick)
     for j in range(K):
         backs[j][...] = stage[j * CAP * CELLS : (j + 1) * CAP * CELLS]
@@ -593,8 +595,8 @@
     return pl.pallas_call(
         functools.partial(final_kernel, count),
         in_specs=[smem, smem] + [vmem] * 10,
-        out_specs=[vmem] * (1 + K),
-        out_shape=[jax.ShapeDtypeStruct(block.shape, jnp.bfloat16)]
+        out_specs=[vmem] * (2 + K),
+        out_shape=[jax.ShapeDtypeStruct((512, mid), jnp.bfloat16)] * 2
         + [jax.ShapeDtypeStruct((CAP * CELLS, mid), jnp.bfloat16)] * K,
         scratch_shapes=[
             pltpu.VMEM((8, WIDE * COLS, mid), jnp.bfloat16),
@@ -644,13 +646,17 @@
     even = swap_face(even, "gz", 0)
     odd = swap_face(odd, "gz", 1)
     middle = middle_call(slot_source, block, before, after, early, wide1, wide2)
-    coarse, *back = final_call(
+    first, last, *back = final_call(
         counts[0], base, slot_source, block, (before, after, even, odd), middle, wide1, wide2
     )
     octant = {j: from_behind(back[j], "xy", -j) for j in RETURNED}
     octant[0] = back[0]
-    fine_out = up_call(fine, mask, w_up, [octant[j] for j in (6, 7, 0, 1)], 3, None)
-    fine_out = up_call(fine, mask, w_up, [octant[j] for j in (2, 3, 4, 5)], 1, fine_out)
+    octant[6], *pieces = lax.optimization_barrier((octant[6], first, middle[2], last))
+    coarse = jnp.concatenate(pieces, axis=0)
+    fine_out = None
+    for group, block_index in (((6, 7, 0, 1), 3), ((2, 3), 1), ((4, 5), 2)):
+        octants = [octant[j] for j in group]
+        fine_out = up_call(fine, mask, w_up, octants, block_index, fine_out)
     return fine_out, coarse.reshape(SIDE, SIDE, COLS, mid)
 
 

time: 61.1 us -> 60.5 us (level)
  waiting for transfers between devices: 8.77 us -> 7.27 us
  other arithmetic: 0.07 us -> 0.9 us
    ppermute x14, waiting for transfers between devices: 8.76 us -> 7.26 us  [from_behind(): return lax.ppermute(value, axis, pairs)]
    concatenate x0 -> x1, other arithmetic: none -> 0.83 us  [shards(): coarse = jnp.concatenate(pieces, axis=0)]
    pallas_call x1, Pallas kernels: 4.03 us -> 3.21 us  [final_call(): pl.pallas_call(functools.partial(final_kernel, count), in_specs=[smem, sm...]
    pallas_call x2 -> x3, Pallas kernels: 2.99 us -> 3.74 us  [up_call(): pl.pallas_call(functools.partial(up_kernel, count), grid=(count * CAP //...]
  transfers between devices with their start and end apart: 18 -> 18, of which waited for: 5 -> 4; matrix products, arithmetic and copies ran while one was open for 0% -> 1% of each run, Pallas kernels for 13% -> 15%
where the time goes in v11:
time: 60.5 us; the launch traced here: 60.3 us
  starting transfers between devices  30.7 us (51%)
  Pallas kernels  19 us (31%)
  waiting for transfers between devices  7.27 us (12%)
  local copies, waits for them, and re-layouts  1.62 us (3%)
  other arithmetic  0.9 us (1%)
  between operations  0.83 us (1%)
    ppermute x14, starting transfers between devices, from_behind(): return lax.ppermute(value, axis, pairs)  27.2 us
    ppermute x14, waiting for transfers between devices, from_behind(): return lax.ppermute(value, axis, pairs)  7.26 us
    pallas_call x1, Pallas kernels, down_call(): pl.pallas_call(functools.partial(down_kernel, offsets), in_specs=[hbm, hb...  3.97 us
    pallas_call x3, Pallas kernels, up_call(): pl.pallas_call(functools.partial(up_kernel, count), grid=(count * CAP //...  3.74 us
    ppermute x4, starting transfers between devices, swap_face(): return lax.ppermute(face, axis, list(enumerate(partner)))  3.49 us
    pallas_call x1, Pallas kernels, middle_call(): pl.pallas_call(middle_kernel, in_specs=[smem] + [vmem] * 6, out_specs=[vm...  3.23 us
    pallas_call x1, Pallas kernels, final_call(): pl.pallas_call(functools.partial(final_kernel, count), in_specs=[smem, sm...  3.21 us
    pallas_call x1, Pallas kernels, inner_call(): pl.pallas_call(functools.partial(inner_kernel, groups), in_specs=[smem, v...  2.37 us
  transfers between devices with their start and end apart: 18, of which 4 were waited for; matrix products, arithmetic and copies ran while one was open for 1% of the time, Pallas kernels for 15%

profile of v11, /device:TPU:0, one launch (start us, length us, event | category | flops | bytes accessed | tf_op | source)
XLA Modules:
  0.0 60.3 jit_solution(819476258958026597)
XLA Ops:
  0.7 4.0 %down.1 = (bf16[256,128]{1,0:T(8,128)(2,1)}, bf16[256,128]{1,0:T(8,128)(2,1)}, bf16[256,128]{1,0:T(8,128)(2,1)}, bf16[256,128]{1,0:T(8,128)(2,1)}, bf16[256,128]...) custom-call(bf16[32,64,512]{2,1,0:T(8,128)(2,1)} %fine_ref.6, s32[32,512]{1,0:T(8,128)} %mask_ref, ...), custom_call_target="tpu_custom_call" | custom-call | flops 234881024 | bytes 1835008 | tf_op jit(solution)/shard_map/down/pallas_call | solution.py:85
  4.7 5.0 %collective-permute-start = (bf16[256,128]{1,0:T(8,128)(2,1)}, bf16[256,128]{1,0:T(8,128)(2,1)S(1)}, u32[]{:S(2)}, u32[]{:S(2)}) collective-permute-start(bf16[256,128]{1,0:T(8,128)(2,1)} %get-tuple-element.46), channel_id=1, source_target_pairs={{0,5},{1,6},{2,7},{3,0},{4,1},{5,2},{6,3},{7,4},{8,13},{9,14},{10,... | collective-permute-start | bytes 196616 | tf_op jit(solution)/shard_map/ppermute | solution.py:619
  9.7 1.5 %collective-permute-start.1 = (bf16[256,128]{1,0:T(8,128)(2,1)}, bf16[256,128]{1,0:T(8,128)(2,1)S(1)}, u32[]{:S(2)}, u32[]{:S(2)}) collective-permute-start(bf16[256,128]{1,0:T(8,128)(2,1)} %get-tuple-element.54), channel_id=1, source_target_pairs={{0,1},{1,2},{2,3},{3,4},{4,5},{5,6},{6,7},{7,0},{8,9},{9,10},{10,1... | collective-permute-start | bytes 196616 | tf_op jit(solution)/shard_map/ppermute | solution.py:619
  11.3 1.8 %collective-permute-start.3 = (bf16[256,128]{1,0:T(8,128)(2,1)}, bf16[256,128]{1,0:T(8,128)(2,1)S(1)}, u32[]{:S(2)}, u32[]{:S(2)}) collective-permute-start(bf16[256,128]{1,0:T(8,128)(2,1)} %get-tuple-element.56), channel_id=1, source_target_pairs={{0,3},{1,4},{2,5},{3,6},{4,7},{5,0},{6,1},{7,2},{8,11},{9,12},{10,... | collective-permute-start | bytes 196616 | tf_op jit(solution)/shard_map/ppermute | solution.py:619
  13.0 3.5 %collective-permute-start.4 = (bf16[256,128]{1,0:T(8,128)(2,1)}, bf16[256,128]{1,0:T(8,128)(2,1)S(1)}, u32[]{:S(2)}, u32[]{:S(2)}) collective-permute-start(bf16[256,128]{1,0:T(8,128)(2,1)} %get-tuple-element.57), channel_id=1, source_target_pairs={{0,4},{1,5},{2,6},{3,7},{4,0},{5,1},{6,2},{7,3},{8,12},{9,13},{10,... | collective-permute-start | bytes 196616 | tf_op jit(solution)/shard_map/ppermute | solution.py:619
  16.5 1.3 %collective-permute-start.5 = (bf16[256,128]{1,0:T(8,128)(2,1)}, bf16[256,128]{1,0:T(8,128)(2,1)S(1)}, u32[]{:S(2)}, u32[]{:S(2)}) collective-permute-start(bf16[256,128]{1,0:T(8,128)(2,1)} %get-tuple-element.59), channel_id=1, source_target_pairs={{0,6},{1,7},{2,0},{3,1},{4,2},{5,3},{6,4},{7,5},{8,14},{9,15},{10,... | collective-permute-start | bytes 196616 | tf_op jit(solution)/shard_map/ppermute | solution.py:619
  17.9 1.0 %collective-permute-start.6 = (bf16[256,128]{1,0:T(8,128)(2,1)}, bf16[256,128]{1,0:T(8,128)(2,1)S(1)}, u32[]{:S(2)}, u32[]{:S(2)}) collective-permute-start(bf16[256,128]{1,0:T(8,128)(2,1)} %get-tuple-element.60), channel_id=1, source_target_pairs={{0,7},{1,0},{2,1},{3,2},{4,3},{5,4},{6,5},{7,6},{8,15},{9,8},{10,9... | collective-permute-start | bytes 196616 | tf_op jit(solution)/shard_map/ppermute | solution.py:619
  18.9 0.1 pad_add_fusion.base_ref
  19.0 1.6 %copy-done = bf16[32,64,512]{2,1,0:T(8,128)(2,1)S(1)} copy-done((bf16[32,64,512]{2,1,0:T(8,128)(2,1)S(1)}, bf16[32,64,512]{2,1,0:T(8,128)(2,1)}, u32[]{:S(2)}) %copy-start) | copy-done | bytes 2097176
  20.6 1.1 %prepare.1 = (bf16[256,128]{1,0:T(8,128)(2,1)S(1)}, bf16[2048,512]{1,0:T(8,128)(2,1)S(1)}, bf16[1152,384]{1,0:T(8,128)(2,1)S(1)}, bf16[1152,384]{1,0:T(8,128)(2,1)S(1)}) custom-call(bf16[32,64,512]{2,1,0:T(8,128)(2,1)S(1)} %copy-done, s32[32,512]{1,0:T(8,128)S(1)} %copy-done.6, bf16[512,128]{1,0:T(8,128)(2,1)S(1)} %copy-done.5, ...), custom_call_target="tpu_custom_call" | custom-call | flops 268435456 | bytes 2097152 | tf_op jit(solution)/shard_map/prepare/pallas_call | solution.py:128
  21.7 0.8 %collective-permute-done.3.refs_3_ = bf16[256,128]{1,0:T(8,128)(2,1)S(1)} collective-permute-done((bf16[256,128]{1,0:T(8,128)(2,1)}, bf16[256,128]{1,0:T(8,128)(2,1)S(1)}, u32[]{:S(2)}, u32[]{:S(2)}) %collective-permute-start.3) | collective-permute-done | bytes 65568 | tf_op jit(solution)/shard_map/ppermute | solution.py:619
  22.5 0.3 collective-permute-done.6.refs_7_
  22.8 0.8 %place.1 = (bf16[2048,128]{1,0:T(8,128)(2,1)S(1)}, bf16[288,128]{1,0:T(8,128)(2,1)S(1)}, bf16[288,128]{1,0:T(8,128)(2,1)S(1)}) custom-call(s32[2]{0:T(128)S(1)} %pad_add_fusion.base_ref, s32[32]{0:T(128)S(1)} %copy-done.7, bf16[256,128]{1,0:T(8,128)(2,1)S(1)} %get-tuple-element.53.refs_0_, bf16[256,128]{1,0:T(8,128)(2,1)S(1)} %collective-permute-done.1.refs_1_, ...), custom_call_target="tpu_custom_call" | custom-call | tf_op jit(solution)/shard_map/place/pallas_call | solution.py:265
  23.6 2.1 %collective-permute-start.7 = (bf16[288,128]{1,0:T(8,128)(2,1)S(1)}, bf16[288,128]{1,0:T(8,128)(2,1)S(1)}, u32[]{:S(2)}, u32[]{:S(2)}) collective-permute-start(bf16[288,128]{1,0:T(8,128)(2,1)S(1)} %get-tuple-element.62), channel_id=1, source_target_pairs={{0,1},{1,0},{2,3},{3,2},{4,5},{5,4},{6,7},{7,6},{8,9},{9,8},{10,11... | collective-permute-start | bytes 221192 | tf_op jit(solution)/shard_map/ppermute | solution.py:627
  25.7 0.7 %collective-permute-start.8 = (bf16[288,128]{1,0:T(8,128)(2,1)S(1)}, bf16[288,128]{1,0:T(8,128)(2,1)S(1)}, u32[]{:S(2)}, u32[]{:S(2)}) collective-permute-start(bf16[288,128]{1,0:T(8,128)(2,1)S(1)} %get-tuple-element.63), channel_id=1, source_target_pairs={{0,0},{1,2},{2,1},{3,4},{4,3},{5,6},{6,5},{7,7},{8,8},{9,10},{10,9... | collective-permute-start | bytes 221192 | tf_op jit(solution)/shard_map/ppermute | solution.py:627
  26.3 2.4 %inner.1.refs_3_ = bf16[11,112,128]{2,1,0:T(8,128)(2,1)S(1)} custom-call(s32[32]{0:T(128)S(1)} %copy-done.7, bf16[2048,128]{1,0:T(8,128)(2,1)S(1)} %get-tuple-element.61.block_ref.refs_0_, bf16[1152,384]{1,0:T(8,128)(2,1)S(1)} %get-tuple-element.64.wide1_ref.refs_4_.refs_8_), custom_call_target="tpu_custom_call" | custom-call | flops 1089994752 | bytes 1769472 | tf_op jit(solution)/shard_map/inner/pallas_call | solution.py:424
  28.7 0.6 %edge.1 = (bf16[288,128]{1,0:T(8,128)(2,1)S(1)}, bf16[288,128]{1,0:T(8,128)(2,1)S(1)}, bf16[368,128]{1,0:T(8,128)(2,1)S(1)}, bf16[368,128]{1,0:T(8,128)(2,1)S(1)}) custom-call(s32[2]{0:T(128)S(1)} %pad_add_fusion.base_ref, s32[32]{0:T(128)S(1)} %copy-done.7, bf16[2048,128]{1,0:T(8,128)(2,1)S(1)} %get-tuple-element.61.block_ref.refs_0_, ...), custom_call_target="tpu_custom_call" | custom-call | tf_op jit(solution)/shard_map/edge/pallas_call | solution.py:315
  29.4 0.7 %collective-permute-start.10 = (bf16[368,128]{1,0:T(8,128)(2,1)S(1)}, bf16[368,128]{1,0:T(8,128)(2,1)S(1)}, u32[]{:S(2)}, u32[]{:S(2)}) collective-permute-start(bf16[368,128]{1,0:T(8,128)(2,1)S(1)} %get-tuple-element.70), channel_id=1, source_target_pairs={{0,0},{8,16},{16,8},{24,24},{1,1},{9,17},{17,9},{25,25},{2,2},{10,... | collective-permute-start | bytes 282632 | tf_op jit(solution)/shard_map/ppermute | solution.py:627
  30.1 3.2 %middle.1 = (bf16[14,144,128]{2,1,0:T(8,128)(2,1)S(1)}, bf16[14,144,128]{2,1,0:T(8,128)(2,1)S(1)}, bf16[1024,128]{1,0:T(8,128)(2,1)S(1)}) custom-call(s32[32]{0:T(128)S(1)} %copy-done.7, bf16[2048,128]{1,0:T(8,128)(2,1)S(1)} %get-tuple-element.61.block_ref.refs_0_, bf16[288,128]{1,0:T(8,128)(2,1)S(1)} %get-tuple-element.67.refs_1_, ...), custom_call_target="tpu_custom_call" | custom-call | flops 1599602688 | bytes 1769472 | tf_op jit(solution)/shard_map/middle/pallas_call | solution.py:500
  33.4 3.2 %final.1 = (bf16[512,128]{1,0:T(8,128)(2,1)S(1)}, bf16[512,128]{1,0:T(8,128)(2,1)S(1)}, bf16[256,128]{1,0:T(8,128)(2,1)S(1)}, bf16[256,128]{1,0:T(8,128)(2,1)S(1...) custom-call(s32[2]{0:T(128)S(1)} %pad_add_fusion.base_ref, ...), custom_call_target="tpu_custom_call" | custom-call | flops 1415577600 | bytes 1769472 | tf_op jit(solution)/shard_map/final/pallas_call | solution.py:595
  36.6 5.1 %collective-permute-start.15 = (bf16[256,128]{1,0:T(8,128)(2,1)S(1)}, bf16[256,128]{1,0:T(8,128)(2,1)S(1)}, u32[]{:S(2)}, u32[]{:S(2)}) collective-permute-start(bf16[256,128]{1,0:T(8,128)(2,1)S(1)} %get-tuple-element.80), channel_id=1, source_target_pairs={{0,2},{1,3},{2,4},{3,5},{4,6},{5,7},{6,0},{7,1},{8,10},{9,11},{10,... | collective-permute-start | bytes 196616 | tf_op jit(solution)/shard_map/ppermute | solution.py:619
  41.8 1.4 %collective-permute-start.11 = (bf16[256,128]{1,0:T(8,128)(2,1)S(1)}, bf16[256,128]{1,0:T(8,128)(2,1)S(1)}, u32[]{:S(2)}, u32[]{:S(2)}) collective-permute-start(bf16[256,128]{1,0:T(8,128)(2,1)S(1)} %get-tuple-element.76), channel_id=1, source_target_pairs={{0,4},{1,5},{2,6},{3,7},{4,0},{5,1},{6,2},{7,3},{8,12},{9,13},{10,... | collective-permute-start | bytes 196616 | tf_op jit(solution)/shard_map/ppermute | solution.py:619
  43.2 3.9 %collective-permute-start.12 = (bf16[256,128]{1,0:T(8,128)(2,1)S(1)}, bf16[256,128]{1,0:T(8,128)(2,1)S(1)}, u32[]{:S(2)}, u32[]{:S(2)}) collective-permute-start(bf16[256,128]{1,0:T(8,128)(2,1)S(1)} %get-tuple-element.77), channel_id=1, source_target_pairs={{0,3},{1,4},{2,5},{3,6},{4,7},{5,0},{6,1},{7,2},{8,11},{9,12},{10,... | collective-permute-start | bytes 196616 | tf_op jit(solution)/shard_map/ppermute | solution.py:619
  47.0 0.9 %collective-permute-start.13 = (bf16[256,128]{1,0:T(8,128)(2,1)S(1)}, bf16[256,128]{1,0:T(8,128)(2,1)S(1)}, u32[]{:S(2)}, u32[]{:S(2)}) collective-permute-start(bf16[256,128]{1,0:T(8,128)(2,1)S(1)} %get-tuple-element.78), channel_id=1, source_target_pairs={{0,6},{1,7},{2,0},{3,1},{4,2},{5,3},{6,4},{7,5},{8,14},{9,15},{10,... | collective-permute-start | bytes 196616 | tf_op jit(solution)/shard_map/ppermute | solution.py:619
  48.0 0.5 collective-permute-start.14
  48.5 0.5 collective-permute-done.16.refs_1_
  49.0 1.0 %collective-permute-start.17 = (bf16[256,128]{1,0:T(8,128)(2,1)S(1)}, bf16[256,128]{1,0:T(8,128)(2,1)S(1)}, u32[]{:S(2)}, u32[]{:S(2)}) collective-permute-start(bf16[256,128]{1,0:T(8,128)(2,1)S(1)} %get-tuple-element.86), channel_id=1, source_target_pairs={{0,7},{1,0},{2,1},{3,2},{4,3},{5,4},{6,5},{7,6},{8,15},{9,8},{10,9... | collective-permute-start | bytes 196616 | tf_op jit(solution)/shard_map/ppermute | solution.py:619
  50.0 0.8 %pad_maximum_fusion = bf16[2048,128]{1,0:T(8,128)(2,1)} fusion(bf16[512,128]{1,0:T(8,128)(2,1)S(1)} %get-tuple-element.89, bf16[1024,128]{1,0:T(8,128)(2,1)S(1)} %get-tuple-element.88.refs_7_, bf16[512,128]{1,0:T(8,128)(2,1)S(1)} %get-tuple-element.87), kind=kLoop, calls=%fused_computation | loop fusion | flops 1572864 | bytes 1048576 | tf_op jit(solution)/shard_map/concatenate | solution.py:655
  50.9 5.7 %collective-permute-done.17.refs_3_ = bf16[256,128]{1,0:T(8,128)(2,1)S(1)} collective-permute-done((bf16[256,128]{1,0:T(8,128)(2,1)S(1)}, bf16[256,128]{1,0:T(8,128)(2,1)S(1)}, u32[]{:S(2)}, u32[]{:S(2)}) %collective-permute-start.17) | collective-permute-done | bytes 65568 | tf_op jit(solution)/shard_map/ppermute | solution.py:619
  56.5 1.5 %up.3.refs_2_ = bf16[32,64,512]{2,1,0:T(8,128)(2,1)} custom-call(bf16[32,64,512]{2,1,0:T(8,128)(2,1)S(1)} %copy-done.1, bf16[2048,512]{1,0:T(8,128)(2,1)S(1)} %get-tuple-element.52.mask_ref, bf16[128,512]{1,0:T(8,128)(2,1)S(1)} %copy-done.2, bf16[256,128]{1,0:T(8,128)(2,1)S(1)} %collective-permute-done.15.refs_0_, ...), custom_call_target="tpu_custom_call" | custom-call | flops 134217728 | bytes 2097152 | tf_op jit(solution)/shard_map/up/pallas_call | solution.py:176
  58.0 1.1 %up.4.refs_2_ = bf16[32,64,512]{2,1,0:T(8,128)(2,1)} custom-call(bf16[32,64,512]{2,1,0:T(8,128)(2,1)S(1)} %copy-done.1, bf16[2048,512]{1,0:T(8,128)(2,1)S(1)} %get-tuple-element.52.mask_ref, bf16[128,512]{1,0:T(8,128)(2,1)S(1)} %copy-done.2, bf16[256,128]{1,0:T(8,128)(2,1)S(1)} %collective-permute-done.13.refs_0_, ...), custom_call_target="tpu_custom_call", output_to_operand_aliasing={{}: (5, {})} | custom-call | flops 134217728 | bytes 2097152 | tf_op jit(solution)/shard_map/up/pallas_call | solution.py:176
  59.2 1.1 %up.5 = bf16[32,64,512]{2,1,0:T(8,128)(2,1)} custom-call(bf16[32,64,512]{2,1,0:T(8,128)(2,1)S(1)} %copy-done.1, bf16[2048,512]{1,0:T(8,128)(2,1)S(1)} %get-tuple-element.52.mask_ref, bf16[128,512]{1,0:T(8,128)(2,1)S(1)} %copy-done.2, bf16[256,128]{1,0:T(8,128)(2,1)S(1)} %collective-permute-done.11.refs_0_, ...), custom_call_target="tpu_custom_call", output_to_operand_aliasing={{}: (5, {})} | custom-call | flops 134217728 | bytes 2097152 | tf_op jit(solution)/shard_map/up/pallas_call | solution.py:176
  (32 shorter events, 0.2 us)
Async XLA Ops:
  0.6 18.4 %copy-start.5 = (bf16[512,128]{1,0:T(8,128)(2,1)S(1)}, bf16[512,128]{1,0:T(8,128)(2,1)}, u32[]{:S(2)}) copy-start(bf16[512,128]{1,0:T(8,128)(2,1)} %w_down_ref) | copy-start | bytes 393220
  0.6 18.4 %copy-start.6 = (s32[32,512]{1,0:T(8,128)S(1)}, s32[32,512]{1,0:T(8,128)}, u32[]{:S(2)}) copy-start(s32[32,512]{1,0:T(8,128)} %mask_ref) | copy-start | bytes 196612
  0.7 18.4 %copy-start.4 = (bf16[27,128,128]{2,1,0:T(8,128)(2,1)S(1)}, bf16[27,128,128]{2,1,0:T(8,128)(2,1)}, u32[]{:S(2)}) copy-start(bf16[27,128,128]{2,1,0:T(8,128)(2,1)} %w2_ref) | copy-start | bytes 2654212
  0.7 18.4 %copy-start.3 = (bf16[27,128,128]{2,1,0:T(8,128)(2,1)S(1)}, bf16[27,128,128]{2,1,0:T(8,128)(2,1)}, u32[]{:S(2)}) copy-start(bf16[27,128,128]{2,1,0:T(8,128)(2,1)} %w1_ref) | copy-start | bytes 2654212
  4.6 18.1 %copy-start.7 = (s32[32]{0:T(128)S(1)}, s32[32]{0:T(128)}, u32[]{:S(2)}) copy-start(s32[32]{0:T(128)} %source_ref.9) | copy-start | bytes 388
  4.7 11.9 %collective-permute-start = (bf16[256,128]{1,0:T(8,128)(2,1)}, bf16[256,128]{1,0:T(8,128)(2,1)S(1)}, u32[]{:S(2)}, u32[]{:S(2)}) collective-permute-start(bf16[256,128]{1,0:T(8,128)(2,1)} %get-tuple-element.46), channel_id=1, source_target_pairs={{0,5},{1,6},{2,7},{3,0},{4,1},{5,2},{6,3},{7,4},{8,13},{9,14},{10,... | collective-permute-start | bytes 196616 | tf_op jit(solution)/shard_map/ppermute | solution.py:619
  9.7 8.2 %collective-permute-start.1 = (bf16[256,128]{1,0:T(8,128)(2,1)}, bf16[256,128]{1,0:T(8,128)(2,1)S(1)}, u32[]{:S(2)}, u32[]{:S(2)}) collective-permute-start(bf16[256,128]{1,0:T(8,128)(2,1)} %get-tuple-element.54), channel_id=1, source_target_pairs={{0,1},{1,2},{2,3},{3,4},{4,5},{5,6},{6,7},{7,0},{8,9},{9,10},{10,1... | collective-permute-start | bytes 196616 | tf_op jit(solution)/shard_map/ppermute | solution.py:619
  11.2 10.5 %collective-permute-start.2 = (bf16[256,128]{1,0:T(8,128)(2,1)}, bf16[256,128]{1,0:T(8,128)(2,1)S(1)}, u32[]{:S(2)}, u32[]{:S(2)}) collective-permute-start(bf16[256,128]{1,0:T(8,128)(2,1)} %get-tuple-element.55), channel_id=1, source_target_pairs={{0,2},{1,3},{2,4},{3,5},{4,6},{5,7},{6,0},{7,1},{8,10},{9,11},{10,... | collective-permute-start | bytes 196616 | tf_op jit(solution)/shard_map/ppermute | solution.py:619
  11.3 11.3 %collective-permute-start.3 = (bf16[256,128]{1,0:T(8,128)(2,1)}, bf16[256,128]{1,0:T(8,128)(2,1)S(1)}, u32[]{:S(2)}, u32[]{:S(2)}) collective-permute-start(bf16[256,128]{1,0:T(8,128)(2,1)} %get-tuple-element.56), channel_id=1, source_target_pairs={{0,3},{1,4},{2,5},{3,6},{4,7},{5,0},{6,1},{7,2},{8,11},{9,12},{10,... | collective-permute-start | bytes 196616 | tf_op jit(solution)/shard_map/ppermute | solution.py:619
  13.0 9.5 %collective-permute-start.4 = (bf16[256,128]{1,0:T(8,128)(2,1)}, bf16[256,128]{1,0:T(8,128)(2,1)S(1)}, u32[]{:S(2)}, u32[]{:S(2)}) collective-permute-start(bf16[256,128]{1,0:T(8,128)(2,1)} %get-tuple-element.57), channel_id=1, source_target_pairs={{0,4},{1,5},{2,6},{3,7},{4,0},{5,1},{6,2},{7,3},{8,12},{9,13},{10,... | collective-permute-start | bytes 196616 | tf_op jit(solution)/shard_map/ppermute | solution.py:619
  16.5 6.0 %collective-permute-start.5 = (bf16[256,128]{1,0:T(8,128)(2,1)}, bf16[256,128]{1,0:T(8,128)(2,1)S(1)}, u32[]{:S(2)}, u32[]{:S(2)}) collective-permute-start(bf16[256,128]{1,0:T(8,128)(2,1)} %get-tuple-element.59), channel_id=1, source_target_pairs={{0,6},{1,7},{2,0},{3,1},{4,2},{5,3},{6,4},{7,5},{8,14},{9,15},{10,... | collective-permute-start | bytes 196616 | tf_op jit(solution)/shard_map/ppermute | solution.py:619
  17.9 4.9 %collective-permute-start.6 = (bf16[256,128]{1,0:T(8,128)(2,1)}, bf16[256,128]{1,0:T(8,128)(2,1)S(1)}, u32[]{:S(2)}, u32[]{:S(2)}) collective-permute-start(bf16[256,128]{1,0:T(8,128)(2,1)} %get-tuple-element.60), channel_id=1, source_target_pairs={{0,7},{1,0},{2,1},{3,2},{4,3},{5,4},{6,5},{7,6},{8,15},{9,8},{10,9... | collective-permute-start | bytes 196616 | tf_op jit(solution)/shard_map/ppermute | solution.py:619
  19.0 1.6 %copy-start = (bf16[32,64,512]{2,1,0:T(8,128)(2,1)S(1)}, bf16[32,64,512]{2,1,0:T(8,128)(2,1)}, u32[]{:S(2)}) copy-start(bf16[32,64,512]{2,1,0:T(8,128)(2,1)} %fine_ref.6) | copy-start | bytes 6291460
  23.6 5.1 %collective-permute-start.7 = (bf16[288,128]{1,0:T(8,128)(2,1)S(1)}, bf16[288,128]{1,0:T(8,128)(2,1)S(1)}, u32[]{:S(2)}, u32[]{:S(2)}) collective-permute-start(bf16[288,128]{1,0:T(8,128)(2,1)S(1)} %get-tuple-element.62), channel_id=1, source_target_pairs={{0,1},{1,0},{2,3},{3,2},{4,5},{5,4},{6,7},{7,6},{8,9},{9,8},{10,11... | collective-permute-start | bytes 221192 | tf_op jit(solution)/shard_map/ppermute | solution.py:627
  25.7 3.0 %collective-permute-start.8 = (bf16[288,128]{1,0:T(8,128)(2,1)S(1)}, bf16[288,128]{1,0:T(8,128)(2,1)S(1)}, u32[]{:S(2)}, u32[]{:S(2)}) collective-permute-start(bf16[288,128]{1,0:T(8,128)(2,1)S(1)} %get-tuple-element.63), channel_id=1, source_target_pairs={{0,0},{1,2},{2,1},{3,4},{4,3},{5,6},{6,5},{7,7},{8,8},{9,10},{10,9... | collective-permute-start | bytes 221192 | tf_op jit(solution)/shard_map/ppermute | solution.py:627
  29.4 4.0 %collective-permute-start.9 = (bf16[368,128]{1,0:T(8,128)(2,1)S(1)}, bf16[368,128]{1,0:T(8,128)(2,1)S(1)}, u32[]{:S(2)}, u32[]{:S(2)}) collective-permute-start(bf16[368,128]{1,0:T(8,128)(2,1)S(1)} %get-tuple-element.69), channel_id=1, source_target_pairs={{0,8},{8,0},{16,24},{24,16},{1,9},{9,1},{17,25},{25,17},{2,10},{10... | collective-permute-start | bytes 282632 | tf_op jit(solution)/shard_map/ppermute | solution.py:627
  29.4 3.9 %collective-permute-start.10 = (bf16[368,128]{1,0:T(8,128)(2,1)S(1)}, bf16[368,128]{1,0:T(8,128)(2,1)S(1)}, u32[]{:S(2)}, u32[]{:S(2)}) collective-permute-start(bf16[368,128]{1,0:T(8,128)(2,1)S(1)} %get-tuple-element.70), channel_id=1, source_target_pairs={{0,0},{8,16},{16,8},{24,24},{1,1},{9,17},{17,9},{25,25},{2,2},{10,... | collective-permute-start | bytes 282632 | tf_op jit(solution)/shard_map/ppermute | solution.py:627
  33.4 23.2 %copy-start.1 = (bf16[32,64,512]{2,1,0:T(8,128)(2,1)S(1)}, bf16[32,64,512]{2,1,0:T(8,128)(2,1)}, u32[]{:S(2)}) copy-start(bf16[32,64,512]{2,1,0:T(8,128)(2,1)} %fine_ref.6) | copy-start | bytes 6291460
  33.4 23.1 %copy-start.2 = (bf16[128,512]{1,0:T(8,128)(2,1)S(1)}, bf16[128,512]{1,0:T(8,128)(2,1)}, u32[]{:S(2)}) copy-start(bf16[128,512]{1,0:T(8,128)(2,1)} %w_ref.5) | copy-start | bytes 393220
  36.6 11.3 %collective-permute-start.15 = (bf16[256,128]{1,0:T(8,128)(2,1)S(1)}, bf16[256,128]{1,0:T(8,128)(2,1)S(1)}, u32[]{:S(2)}, u32[]{:S(2)}) collective-permute-start(bf16[256,128]{1,0:T(8,128)(2,1)S(1)} %get-tuple-element.80), channel_id=1, source_target_pairs={{0,2},{1,3},{2,4},{3,5},{4,6},{5,7},{6,0},{7,1},{8,10},{9,11},{10,... | collective-permute-start | bytes 196616 | tf_op jit(solution)/shard_map/ppermute | solution.py:619
  41.7 7.2 %collective-permute-start.16 = (bf16[256,128]{1,0:T(8,128)(2,1)S(1)}, bf16[256,128]{1,0:T(8,128)(2,1)S(1)}, u32[]{:S(2)}, u32[]{:S(2)}) collective-permute-start(bf16[256,128]{1,0:T(8,128)(2,1)S(1)} %get-tuple-element.84), channel_id=1, source_target_pairs={{0,1},{1,2},{2,3},{3,4},{4,5},{5,6},{6,7},{7,0},{8,9},{9,10},{10,1... | collective-permute-start | bytes 196616 | tf_op jit(solution)/shard_map/ppermute | solution.py:619
  41.8 17.4 %collective-permute-start.11 = (bf16[256,128]{1,0:T(8,128)(2,1)S(1)}, bf16[256,128]{1,0:T(8,128)(2,1)S(1)}, u32[]{:S(2)}, u32[]{:S(2)}) collective-permute-start(bf16[256,128]{1,0:T(8,128)(2,1)S(1)} %get-tuple-element.76), channel_id=1, source_target_pairs={{0,4},{1,5},{2,6},{3,7},{4,0},{5,1},{6,2},{7,3},{8,12},{9,13},{10,... | collective-permute-start | bytes 196616 | tf_op jit(solution)/shard_map/ppermute | solution.py:619
  43.2 16.0 %collective-permute-start.12 = (bf16[256,128]{1,0:T(8,128)(2,1)S(1)}, bf16[256,128]{1,0:T(8,128)(2,1)S(1)}, u32[]{:S(2)}, u32[]{:S(2)}) collective-permute-start(bf16[256,128]{1,0:T(8,128)(2,1)S(1)} %get-tuple-element.77), channel_id=1, source_target_pairs={{0,3},{1,4},{2,5},{3,6},{4,7},{5,0},{6,1},{7,2},{8,11},{9,12},{10,... | collective-permute-start | bytes 196616 | tf_op jit(solution)/shard_map/ppermute | solution.py:619
  47.0 11.0 %collective-permute-start.13 = (bf16[256,128]{1,0:T(8,128)(2,1)S(1)}, bf16[256,128]{1,0:T(8,128)(2,1)S(1)}, u32[]{:S(2)}, u32[]{:S(2)}) collective-permute-start(bf16[256,128]{1,0:T(8,128)(2,1)S(1)} %get-tuple-element.78), channel_id=1, source_target_pairs={{0,6},{1,7},{2,0},{3,1},{4,2},{5,3},{6,4},{7,5},{8,14},{9,15},{10,... | collective-permute-start | bytes 196616 | tf_op jit(solution)/shard_map/ppermute | solution.py:619
  48.0 10.1 %collective-permute-start.14 = (bf16[256,128]{1,0:T(8,128)(2,1)S(1)}, bf16[256,128]{1,0:T(8,128)(2,1)S(1)}, u32[]{:S(2)}, u32[]{:S(2)}) collective-permute-start(bf16[256,128]{1,0:T(8,128)(2,1)S(1)} %get-tuple-element.79), channel_id=1, source_target_pairs={{0,5},{1,6},{2,7},{3,0},{4,1},{5,2},{6,3},{7,4},{8,13},{9,14},{10,... | collective-permute-start | bytes 196616 | tf_op jit(solution)/shard_map/ppermute | solution.py:619
  49.0 7.5 %collective-permute-start.17 = (bf16[256,128]{1,0:T(8,128)(2,1)S(1)}, bf16[256,128]{1,0:T(8,128)(2,1)S(1)}, u32[]{:S(2)}, u32[]{:S(2)}) collective-permute-start(bf16[256,128]{1,0:T(8,128)(2,1)S(1)} %get-tuple-element.86), channel_id=1, source_target_pairs={{0,7},{1,0},{2,1},{3,2},{4,3},{5,4},{6,5},{7,6},{8,15},{9,8},{10,9... | collective-permute-start | bytes 196616 | tf_op jit(solution)/shard_map/ppermute | solution.py:619

commit v12 on v11

--- a/solution.py
+++ b/solution.py
@@ -18,7 +18,7 @@
 LATE = ((12, 3),)
 LATE_PLANES = 3
 SENT = (4, 3, 5, 2, 6, 1, 7)
-RETURNED = (1, 7, 6, 4, 2, 3, 5)
+RETURNED = (6, 7, 4, 5, 2, 3, 1)
 DOWN_LIMIT = 62 * 1024 * 1024
 VMEM_LIMIT = 24 * 1024 * 1024
 
@@ -649,13 +649,16 @@
     first, last, *back = final_call(
         counts[0], base, slot_source, block, (before, after, even, odd), middle, wide1, wide2
     )
-    octant = {j: from_behind(back[j], "xy", -j) for j in RETURNED}
+    octant = {j: from_behind(back[j], "xy", -j) for j in RETURNED[:5]}
+    for done, j in zip(RETURNED, RETURNED[5:]):
+        octant[done], value = lax.optimization_barrier((octant[done], back[j]))
+        octant[j] = from_behind(value, "xy", -j)
     octant[0] = back[0]
-    octant[6], *pieces = lax.optimization_barrier((octant[6], first, middle[2], last))
+    octant[7], *pieces = lax.optimization_barrier((octant[7], first, middle[2], last))
     coarse = jnp.concatenate(pieces, axis=0)
     fine_out = None
-    for group, block_index in (((6, 7, 0, 1), 3), ((2, 3), 1), ((4, 5), 2)):
-        octants = [octant[j] for j in group]
+    for block_index in (3, 2, 1, 0):
+        octants = [octant[2 * block_index], octant[2 * block_index + 1]]
         fine_out = up_call(fine, mask, w_up, octants, block_index, fine_out)
     return fine_out, coarse.reshape(SIDE, SIDE, COLS, mid)
 

time: 60.5 us -> 59.9 us (0.990)
  waiting for transfers between devices: 7.27 us -> 5.67 us
  Pallas kernels: 19 us -> 19.8 us
    ppermute x14, waiting for transfers between devices: 7.26 us -> 5.66 us  [from_behind(): return lax.ppermute(value, axis, pairs)]
    pallas_call x3 -> x4, Pallas kernels: 3.74 us -> 4.52 us  [up_call(): pl.pallas_call(functools.partial(up_kernel, count), grid=(count * CAP //...]
  transfers between devices with their start and end apart: 18 -> 18, of which waited for: 4 -> 3; matrix products, arithmetic and copies ran while one was open for 1% -> 2% of each run, Pallas kernels for 15% -> 17%
where the time goes in v12:
time: 59.9 us; the launch traced here: 59.4 us
  starting transfers between devices  30.6 us (51%)
  Pallas kernels  19.8 us (33%)
  waiting for transfers between devices  5.67 us (9%)
  local copies, waits for them, and re-layouts  1.62 us (3%)
  other arithmetic  0.9 us (2%)
  between operations  0.83 us (1%)
    ppermute x14, starting transfers between devices, from_behind(): return lax.ppermute(value, axis, pairs)  27.1 us
    ppermute x14, waiting for transfers between devices, from_behind(): return lax.ppermute(value, axis, pairs)  5.66 us
    pallas_call x4, Pallas kernels, up_call(): pl.pallas_call(functools.partial(up_kernel, count), grid=(count * CAP //...  4.52 us
    pallas_call x1, Pallas kernels, down_call(): pl.pallas_call(functools.partial(down_kernel, offsets), in_specs=[hbm, hb...  3.97 us
    ppermute x4, starting transfers between devices, swap_face(): return lax.ppermute(face, axis, list(enumerate(partner)))  3.49 us
    pallas_call x1, Pallas kernels, middle_call(): pl.pallas_call(middle_kernel, in_specs=[smem] + [vmem] * 6, out_specs=[vm...  3.23 us
    pallas_call x1, Pallas kernels, final_call(): pl.pallas_call(functools.partial(final_kernel, count), in_specs=[smem, sm...  3.21 us
    pallas_call x1, Pallas kernels, inner_call(): pl.pallas_call(functools.partial(inner_kernel, groups), in_specs=[smem, v...  2.37 us
  transfers between devices with their start and end apart: 18, of which 3 were waited for; matrix products, arithmetic and copies ran while one was open for 2% of the time, Pallas kernels for 17%

profile of v12, /device:TPU:0, one launch (start us, length us, event | category | flops | bytes accessed | tf_op | source)
XLA Modules:
  0.0 59.4 jit_solution(4148178881177717955)
XLA Ops:
  0.7 4.0 %down.1 = (bf16[256,128]{1,0:T(8,128)(2,1)}, bf16[256,128]{1,0:T(8,128)(2,1)}, bf16[256,128]{1,0:T(8,128)(2,1)}, bf16[256,128]{1,0:T(8,128)(2,1)}, bf16[256,128]...) custom-call(bf16[32,64,512]{2,1,0:T(8,128)(2,1)} %fine_ref.8, s32[32,512]{1,0:T(8,128)} %mask_ref, ...), custom_call_target="tpu_custom_call" | custom-call | flops 234881024 | bytes 1835008 | tf_op jit(solution)/shard_map/down/pallas_call | solution.py:85
  4.7 5.0 %collective-permute-start = (bf16[256,128]{1,0:T(8,128)(2,1)}, bf16[256,128]{1,0:T(8,128)(2,1)S(1)}, u32[]{:S(2)}, u32[]{:S(2)}) collective-permute-start(bf16[256,128]{1,0:T(8,128)(2,1)} %get-tuple-element.50), channel_id=1, source_target_pairs={{0,5},{1,6},{2,7},{3,0},{4,1},{5,2},{6,3},{7,4},{8,13},{9,14},{10,... | collective-permute-start | bytes 196616 | tf_op jit(solution)/shard_map/ppermute | solution.py:619
  9.7 1.5 %collective-permute-start.1 = (bf16[256,128]{1,0:T(8,128)(2,1)}, bf16[256,128]{1,0:T(8,128)(2,1)S(1)}, u32[]{:S(2)}, u32[]{:S(2)}) collective-permute-start(bf16[256,128]{1,0:T(8,128)(2,1)} %get-tuple-element.58), channel_id=1, source_target_pairs={{0,1},{1,2},{2,3},{3,4},{4,5},{5,6},{6,7},{7,0},{8,9},{9,10},{10,1... | collective-permute-start | bytes 196616 | tf_op jit(solution)/shard_map/ppermute | solution.py:619
  11.3 1.8 %collective-permute-start.3 = (bf16[256,128]{1,0:T(8,128)(2,1)}, bf16[256,128]{1,0:T(8,128)(2,1)S(1)}, u32[]{:S(2)}, u32[]{:S(2)}) collective-permute-start(bf16[256,128]{1,0:T(8,128)(2,1)} %get-tuple-element.60), channel_id=1, source_target_pairs={{0,3},{1,4},{2,5},{3,6},{4,7},{5,0},{6,1},{7,2},{8,11},{9,12},{10,... | collective-permute-start | bytes 196616 | tf_op jit(solution)/shard_map/ppermute | solution.py:619
  13.0 3.5 %collective-permute-start.4 = (bf16[256,128]{1,0:T(8,128)(2,1)}, bf16[256,128]{1,0:T(8,128)(2,1)S(1)}, u32[]{:S(2)}, u32[]{:S(2)}) collective-permute-start(bf16[256,128]{1,0:T(8,128)(2,1)} %get-tuple-element.61), channel_id=1, source_target_pairs={{0,4},{1,5},{2,6},{3,7},{4,0},{5,1},{6,2},{7,3},{8,12},{9,13},{10,... | collective-permute-start | bytes 196616 | tf_op jit(solution)/shard_map/ppermute | solution.py:619
  16.5 1.3 %collective-permute-start.5 = (bf16[256,128]{1,0:T(8,128)(2,1)}, bf16[256,128]{1,0:T(8,128)(2,1)S(1)}, u32[]{:S(2)}, u32[]{:S(2)}) collective-permute-start(bf16[256,128]{1,0:T(8,128)(2,1)} %get-tuple-element.63), channel_id=1, source_target_pairs={{0,6},{1,7},{2,0},{3,1},{4,2},{5,3},{6,4},{7,5},{8,14},{9,15},{10,... | collective-permute-start | bytes 196616 | tf_op jit(solution)/shard_map/ppermute | solution.py:619
  17.9 1.0 %collective-permute-start.6 = (bf16[256,128]{1,0:T(8,128)(2,1)}, bf16[256,128]{1,0:T(8,128)(2,1)S(1)}, u32[]{:S(2)}, u32[]{:S(2)}) collective-permute-start(bf16[256,128]{1,0:T(8,128)(2,1)} %get-tuple-element.64), channel_id=1, source_target_pairs={{0,7},{1,0},{2,1},{3,2},{4,3},{5,4},{6,5},{7,6},{8,15},{9,8},{10,9... | collective-permute-start | bytes 196616 | tf_op jit(solution)/shard_map/ppermute | solution.py:619
  18.9 0.1 pad_add_fusion.base_ref
  19.0 1.6 %copy-done = bf16[32,64,512]{2,1,0:T(8,128)(2,1)S(1)} copy-done((bf16[32,64,512]{2,1,0:T(8,128)(2,1)S(1)}, bf16[32,64,512]{2,1,0:T(8,128)(2,1)}, u32[]{:S(2)}) %copy-start) | copy-done | bytes 2097176
  20.6 1.1 %prepare.1 = (bf16[256,128]{1,0:T(8,128)(2,1)S(1)}, bf16[2048,512]{1,0:T(8,128)(2,1)S(1)}, bf16[1152,384]{1,0:T(8,128)(2,1)S(1)}, bf16[1152,384]{1,0:T(8,128)(2,1)S(1)}) custom-call(bf16[32,64,512]{2,1,0:T(8,128)(2,1)S(1)} %copy-done, s32[32,512]{1,0:T(8,128)S(1)} %copy-done.6, bf16[512,128]{1,0:T(8,128)(2,1)S(1)} %copy-done.5, ...), custom_call_target="tpu_custom_call" | custom-call | flops 268435456 | bytes 2097152 | tf_op jit(solution)/shard_map/prepare/pallas_call | solution.py:128
  21.7 0.8 %collective-permute-done.3.refs_3_ = bf16[256,128]{1,0:T(8,128)(2,1)S(1)} collective-permute-done((bf16[256,128]{1,0:T(8,128)(2,1)}, bf16[256,128]{1,0:T(8,128)(2,1)S(1)}, u32[]{:S(2)}, u32[]{:S(2)}) %collective-permute-start.3) | collective-permute-done | bytes 65568 | tf_op jit(solution)/shard_map/ppermute | solution.py:619
  22.5 0.3 collective-permute-done.6.refs_7_
  22.8 0.8 %place.1 = (bf16[2048,128]{1,0:T(8,128)(2,1)S(1)}, bf16[288,128]{1,0:T(8,128)(2,1)S(1)}, bf16[288,128]{1,0:T(8,128)(2,1)S(1)}) custom-call(s32[2]{0:T(128)S(1)} %pad_add_fusion.base_ref, s32[32]{0:T(128)S(1)} %copy-done.7, bf16[256,128]{1,0:T(8,128)(2,1)S(1)} %get-tuple-element.57.refs_0_, bf16[256,128]{1,0:T(8,128)(2,1)S(1)} %collective-permute-done.1.refs_1_, ...), custom_call_target="tpu_custom_call" | custom-call | tf_op jit(solution)/shard_map/place/pallas_call | solution.py:265
  23.6 2.1 %collective-permute-start.7 = (bf16[288,128]{1,0:T(8,128)(2,1)S(1)}, bf16[288,128]{1,0:T(8,128)(2,1)S(1)}, u32[]{:S(2)}, u32[]{:S(2)}) collective-permute-start(bf16[288,128]{1,0:T(8,128)(2,1)S(1)} %get-tuple-element.66), channel_id=1, source_target_pairs={{0,1},{1,0},{2,3},{3,2},{4,5},{5,4},{6,7},{7,6},{8,9},{9,8},{10,11... | collective-permute-start | bytes 221192 | tf_op jit(solution)/shard_map/ppermute | solution.py:627
  25.7 0.7 %collective-permute-start.8 = (bf16[288,128]{1,0:T(8,128)(2,1)S(1)}, bf16[288,128]{1,0:T(8,128)(2,1)S(1)}, u32[]{:S(2)}, u32[]{:S(2)}) collective-permute-start(bf16[288,128]{1,0:T(8,128)(2,1)S(1)} %get-tuple-element.67), channel_id=1, source_target_pairs={{0,0},{1,2},{2,1},{3,4},{4,3},{5,6},{6,5},{7,7},{8,8},{9,10},{10,9... | collective-permute-start | bytes 221192 | tf_op jit(solution)/shard_map/ppermute | solution.py:627
  26.3 2.4 %inner.1.refs_3_ = bf16[11,112,128]{2,1,0:T(8,128)(2,1)S(1)} custom-call(s32[32]{0:T(128)S(1)} %copy-done.7, bf16[2048,128]{1,0:T(8,128)(2,1)S(1)} %get-tuple-element.65.block_ref.refs_0_, bf16[1152,384]{1,0:T(8,128)(2,1)S(1)} %get-tuple-element.68.wide1_ref.refs_4_.refs_8_), custom_call_target="tpu_custom_call" | custom-call | flops 1089994752 | bytes 1769472 | tf_op jit(solution)/shard_map/inner/pallas_call | solution.py:424
  28.7 0.6 %edge.1 = (bf16[288,128]{1,0:T(8,128)(2,1)S(1)}, bf16[288,128]{1,0:T(8,128)(2,1)S(1)}, bf16[368,128]{1,0:T(8,128)(2,1)S(1)}, bf16[368,128]{1,0:T(8,128)(2,1)S(1)}) custom-call(s32[2]{0:T(128)S(1)} %pad_add_fusion.base_ref, s32[32]{0:T(128)S(1)} %copy-done.7, bf16[2048,128]{1,0:T(8,128)(2,1)S(1)} %get-tuple-element.65.block_ref.refs_0_, ...), custom_call_target="tpu_custom_call" | custom-call | tf_op jit(solution)/shard_map/edge/pallas_call | solution.py:315
  29.4 0.7 %collective-permute-start.10 = (bf16[368,128]{1,0:T(8,128)(2,1)S(1)}, bf16[368,128]{1,0:T(8,128)(2,1)S(1)}, u32[]{:S(2)}, u32[]{:S(2)}) collective-permute-start(bf16[368,128]{1,0:T(8,128)(2,1)S(1)} %get-tuple-element.74), channel_id=1, source_target_pairs={{0,0},{8,16},{16,8},{24,24},{1,1},{9,17},{17,9},{25,25},{2,2},{10,... | collective-permute-start | bytes 282632 | tf_op jit(solution)/shard_map/ppermute | solution.py:627
  30.1 3.2 %middle.1 = (bf16[14,144,128]{2,1,0:T(8,128)(2,1)S(1)}, bf16[14,144,128]{2,1,0:T(8,128)(2,1)S(1)}, bf16[1024,128]{1,0:T(8,128)(2,1)S(1)}) custom-call(s32[32]{0:T(128)S(1)} %copy-done.7, bf16[2048,128]{1,0:T(8,128)(2,1)S(1)} %get-tuple-element.65.block_ref.refs_0_, bf16[288,128]{1,0:T(8,128)(2,1)S(1)} %get-tuple-element.71.refs_1_, ...), custom_call_target="tpu_custom_call" | custom-call | flops 1599602688 | bytes 1769472 | tf_op jit(solution)/shard_map/middle/pallas_call | solution.py:500
  33.4 3.2 %final.1 = (bf16[512,128]{1,0:T(8,128)(2,1)S(1)}, bf16[512,128]{1,0:T(8,128)(2,1)S(1)}, bf16[256,128]{1,0:T(8,128)(2,1)S(1)}, bf16[256,128]{1,0:T(8,128)(2,1)S(1...) custom-call(s32[2]{0:T(128)S(1)} %pad_add_fusion.base_ref, ...), custom_call_target="tpu_custom_call" | custom-call | flops 1415577600 | bytes 1769472 | tf_op jit(solution)/shard_map/final/pallas_call | solution.py:595
  36.6 4.1 %collective-permute-start.11 = (bf16[256,128]{1,0:T(8,128)(2,1)S(1)}, bf16[256,128]{1,0:T(8,128)(2,1)S(1)}, u32[]{:S(2)}, u32[]{:S(2)}) collective-permute-start(bf16[256,128]{1,0:T(8,128)(2,1)S(1)} %get-tuple-element.81), channel_id=1, source_target_pairs={{0,1},{1,2},{2,3},{3,4},{4,5},{5,6},{6,7},{7,0},{8,9},{9,10},{10,1... | collective-permute-start | bytes 196616 | tf_op jit(solution)/shard_map/ppermute | solution.py:619
  40.8 1.0 %collective-permute-start.14 = (bf16[256,128]{1,0:T(8,128)(2,1)S(1)}, bf16[256,128]{1,0:T(8,128)(2,1)S(1)}, u32[]{:S(2)}, u32[]{:S(2)}) collective-permute-start(bf16[256,128]{1,0:T(8,128)(2,1)S(1)} %get-tuple-element.85), channel_id=1, source_target_pairs={{0,2},{1,3},{2,4},{3,5},{4,6},{5,7},{6,0},{7,1},{8,10},{9,11},{10,... | collective-permute-start | bytes 196616 | tf_op jit(solution)/shard_map/ppermute | solution.py:619
  41.8 2.8 %collective-permute-start.13 = (bf16[256,128]{1,0:T(8,128)(2,1)S(1)}, bf16[256,128]{1,0:T(8,128)(2,1)S(1)}, u32[]{:S(2)}, u32[]{:S(2)}) collective-permute-start(bf16[256,128]{1,0:T(8,128)(2,1)S(1)} %get-tuple-element.84), channel_id=1, source_target_pairs={{0,6},{1,7},{2,0},{3,1},{4,2},{5,3},{6,4},{7,5},{8,14},{9,15},{10,... | collective-permute-start | bytes 196616 | tf_op jit(solution)/shard_map/ppermute | solution.py:619
  44.6 2.4 %collective-permute-start.17 = (bf16[256,128]{1,0:T(8,128)(2,1)S(1)}, bf16[256,128]{1,0:T(8,128)(2,1)S(1)}, u32[]{:S(2)}, u32[]{:S(2)}) collective-permute-start(bf16[256,128]{1,0:T(8,128)(2,1)S(1)} %get-tuple-element.89), channel_id=1, source_target_pairs={{0,3},{1,4},{2,5},{3,6},{4,7},{5,0},{6,1},{7,2},{8,11},{9,12},{10,... | collective-permute-start | bytes 196616 | tf_op jit(solution)/shard_map/ppermute | solution.py:619
  47.0 1.5 %collective-permute-start.12 = (bf16[256,128]{1,0:T(8,128)(2,1)S(1)}, bf16[256,128]{1,0:T(8,128)(2,1)S(1)}, u32[]{:S(2)}, u32[]{:S(2)}) collective-permute-start(bf16[256,128]{1,0:T(8,128)(2,1)S(1)} %get-tuple-element.83), channel_id=1, source_target_pairs={{0,7},{1,0},{2,1},{3,2},{4,3},{5,4},{6,5},{7,6},{8,15},{9,8},{10,9... | collective-permute-start | bytes 196616 | tf_op jit(solution)/shard_map/ppermute | solution.py:619
  48.5 0.9 %collective-permute-start.15 = (bf16[256,128]{1,0:T(8,128)(2,1)S(1)}, bf16[256,128]{1,0:T(8,128)(2,1)S(1)}, u32[]{:S(2)}, u32[]{:S(2)}) collective-permute-start(bf16[256,128]{1,0:T(8,128)(2,1)S(1)} %get-tuple-element.87), channel_id=1, source_target_pairs={{0,5},{1,6},{2,7},{3,0},{4,1},{5,2},{6,3},{7,4},{8,13},{9,14},{10,... | collective-permute-start | bytes 196616 | tf_op jit(solution)/shard_map/ppermute | solution.py:619
  49.5 0.8 %pad_maximum_fusion = bf16[2048,128]{1,0:T(8,128)(2,1)} fusion(bf16[512,128]{1,0:T(8,128)(2,1)S(1)} %get-tuple-element.97, bf16[1024,128]{1,0:T(8,128)(2,1)S(1)} %get-tuple-element.96.refs_7_, bf16[512,128]{1,0:T(8,128)(2,1)S(1)} %get-tuple-element.95), kind=kLoop, calls=%fused_computation | loop fusion | flops 1572864 | bytes 1048576 | tf_op jit(solution)/shard_map/concatenate | solution.py:658
  50.3 1.1 %up.4.refs_2_ = bf16[32,64,512]{2,1,0:T(8,128)(2,1)} custom-call(bf16[32,64,512]{2,1,0:T(8,128)(2,1)S(1)} %copy-done.1, bf16[2048,512]{1,0:T(8,128)(2,1)S(1)} %get-tuple-element.56.mask_ref, bf16[128,512]{1,0:T(8,128)(2,1)S(1)} %copy-done.2, bf16[256,128]{1,0:T(8,128)(2,1)S(1)} %collective-permute-done.14.refs_0_, ...), custom_call_target="tpu_custom_call" | custom-call | flops 134217728 | bytes 2097152 | tf_op jit(solution)/shard_map/up/pallas_call | solution.py:176
  51.4 4.6 %collective-permute-done.17.refs_1_ = bf16[256,128]{1,0:T(8,128)(2,1)S(1)} collective-permute-done((bf16[256,128]{1,0:T(8,128)(2,1)S(1)}, bf16[256,128]{1,0:T(8,128)(2,1)S(1)}, u32[]{:S(2)}, u32[]{:S(2)}) %collective-permute-start.17) | collective-permute-done | bytes 65568 | tf_op jit(solution)/shard_map/ppermute | solution.py:619
  56.0 1.1 %up.5.refs_2_ = bf16[32,64,512]{2,1,0:T(8,128)(2,1)} custom-call(bf16[32,64,512]{2,1,0:T(8,128)(2,1)S(1)} %copy-done.1, bf16[2048,512]{1,0:T(8,128)(2,1)S(1)} %get-tuple-element.56.mask_ref, bf16[128,512]{1,0:T(8,128)(2,1)S(1)} %copy-done.2, bf16[256,128]{1,0:T(8,128)(2,1)S(1)} %collective-permute-done.16.refs_0_, ...), custom_call_target="tpu_custom_call", output_to_operand_aliasing={{}: (5, {})} | custom-call | flops 134217728 | bytes 2097152 | tf_op jit(solution)/shard_map/up/pallas_call | solution.py:176
  57.1 1.1 %up.6.refs_2_ = bf16[32,64,512]{2,1,0:T(8,128)(2,1)} custom-call(bf16[32,64,512]{2,1,0:T(8,128)(2,1)S(1)} %copy-done.1, bf16[2048,512]{1,0:T(8,128)(2,1)S(1)} %get-tuple-element.56.mask_ref, bf16[128,512]{1,0:T(8,128)(2,1)S(1)} %copy-done.2, bf16[256,128]{1,0:T(8,128)(2,1)S(1)} %collective-permute-done.13.refs_0_, ...), custom_call_target="tpu_custom_call", output_to_operand_aliasing={{}: (5, {})} | custom-call | flops 134217728 | bytes 2097152 | tf_op jit(solution)/shard_map/up/pallas_call | solution.py:176
  58.3 1.1 %up.7 = bf16[32,64,512]{2,1,0:T(8,128)(2,1)} custom-call(bf16[32,64,512]{2,1,0:T(8,128)(2,1)S(1)} %copy-done.1, bf16[2048,512]{1,0:T(8,128)(2,1)S(1)} %get-tuple-element.56.mask_ref, bf16[128,512]{1,0:T(8,128)(2,1)S(1)} %copy-done.2, bf16[256,128]{1,0:T(8,128)(2,1)S(1)} %get-tuple-element.80.refs_0_, ...), custom_call_target="tpu_custom_call", output_to_operand_aliasing={{}: (5, {})} | custom-call | flops 134217728 | bytes 2097152 | tf_op jit(solution)/shard_map/up/pallas_call | solution.py:176
  (33 shorter events, 0.2 us)
Async XLA Ops:
  0.6 18.4 %copy-start.5 = (bf16[512,128]{1,0:T(8,128)(2,1)S(1)}, bf16[512,128]{1,0:T(8,128)(2,1)}, u32[]{:S(2)}) copy-start(bf16[512,128]{1,0:T(8,128)(2,1)} %w_down_ref) | copy-start | bytes 393220
  0.6 18.4 %copy-start.6 = (s32[32,512]{1,0:T(8,128)S(1)}, s32[32,512]{1,0:T(8,128)}, u32[]{:S(2)}) copy-start(s32[32,512]{1,0:T(8,128)} %mask_ref) | copy-start | bytes 196612
  0.7 18.4 %copy-start.4 = (bf16[27,128,128]{2,1,0:T(8,128)(2,1)S(1)}, bf16[27,128,128]{2,1,0:T(8,128)(2,1)}, u32[]{:S(2)}) copy-start(bf16[27,128,128]{2,1,0:T(8,128)(2,1)} %w2_ref) | copy-start | bytes 2654212
  0.7 18.4 %copy-start.3 = (bf16[27,128,128]{2,1,0:T(8,128)(2,1)S(1)}, bf16[27,128,128]{2,1,0:T(8,128)(2,1)}, u32[]{:S(2)}) copy-start(bf16[27,128,128]{2,1,0:T(8,128)(2,1)} %w1_ref) | copy-start | bytes 2654212
  4.6 18.1 %copy-start.7 = (s32[32]{0:T(128)S(1)}, s32[32]{0:T(128)}, u32[]{:S(2)}) copy-start(s32[32]{0:T(128)} %source_ref.9) | copy-start | bytes 388
  4.7 11.9 %collective-permute-start = (bf16[256,128]{1,0:T(8,128)(2,1)}, bf16[256,128]{1,0:T(8,128)(2,1)S(1)}, u32[]{:S(2)}, u32[]{:S(2)}) collective-permute-start(bf16[256,128]{1,0:T(8,128)(2,1)} %get-tuple-element.50), channel_id=1, source_target_pairs={{0,5},{1,6},{2,7},{3,0},{4,1},{5,2},{6,3},{7,4},{8,13},{9,14},{10,... | collective-permute-start | bytes 196616 | tf_op jit(solution)/shard_map/ppermute | solution.py:619
  9.7 8.2 %collective-permute-start.1 = (bf16[256,128]{1,0:T(8,128)(2,1)}, bf16[256,128]{1,0:T(8,128)(2,1)S(1)}, u32[]{:S(2)}, u32[]{:S(2)}) collective-permute-start(bf16[256,128]{1,0:T(8,128)(2,1)} %get-tuple-element.58), channel_id=1, source_target_pairs={{0,1},{1,2},{2,3},{3,4},{4,5},{5,6},{6,7},{7,0},{8,9},{9,10},{10,1... | collective-permute-start | bytes 196616 | tf_op jit(solution)/shard_map/ppermute | solution.py:619
  11.2 10.5 %collective-permute-start.2 = (bf16[256,128]{1,0:T(8,128)(2,1)}, bf16[256,128]{1,0:T(8,128)(2,1)S(1)}, u32[]{:S(2)}, u32[]{:S(2)}) collective-permute-start(bf16[256,128]{1,0:T(8,128)(2,1)} %get-tuple-element.59), channel_id=1, source_target_pairs={{0,2},{1,3},{2,4},{3,5},{4,6},{5,7},{6,0},{7,1},{8,10},{9,11},{10,... | collective-permute-start | bytes 196616 | tf_op jit(solution)/shard_map/ppermute | solution.py:619
  11.3 11.3 %collective-permute-start.3 = (bf16[256,128]{1,0:T(8,128)(2,1)}, bf16[256,128]{1,0:T(8,128)(2,1)S(1)}, u32[]{:S(2)}, u32[]{:S(2)}) collective-permute-start(bf16[256,128]{1,0:T(8,128)(2,1)} %get-tuple-element.60), channel_id=1, source_target_pairs={{0,3},{1,4},{2,5},{3,6},{4,7},{5,0},{6,1},{7,2},{8,11},{9,12},{10,... | collective-permute-start | bytes 196616 | tf_op jit(solution)/shard_map/ppermute | solution.py:619
  13.0 9.5 %collective-permute-start.4 = (bf16[256,128]{1,0:T(8,128)(2,1)}, bf16[256,128]{1,0:T(8,128)(2,1)S(1)}, u32[]{:S(2)}, u32[]{:S(2)}) collective-permute-start(bf16[256,128]{1,0:T(8,128)(2,1)} %get-tuple-element.61), channel_id=1, source_target_pairs={{0,4},{1,5},{2,6},{3,7},{4,0},{5,1},{6,2},{7,3},{8,12},{9,13},{10,... | collective-permute-start | bytes 196616 | tf_op jit(solution)/shard_map/ppermute | solution.py:619
  16.5 6.0 %collective-permute-start.5 = (bf16[256,128]{1,0:T(8,128)(2,1)}, bf16[256,128]{1,0:T(8,128)(2,1)S(1)}, u32[]{:S(2)}, u32[]{:S(2)}) collective-permute-start(bf16[256,128]{1,0:T(8,128)(2,1)} %get-tuple-element.63), channel_id=1, source_target_pairs={{0,6},{1,7},{2,0},{3,1},{4,2},{5,3},{6,4},{7,5},{8,14},{9,15},{10,... | collective-permute-start | bytes 196616 | tf_op jit(solution)/shard_map/ppermute | solution.py:619
  17.9 4.9 %collective-permute-start.6 = (bf16[256,128]{1,0:T(8,128)(2,1)}, bf16[256,128]{1,0:T(8,128)(2,1)S(1)}, u32[]{:S(2)}, u32[]{:S(2)}) collective-permute-start(bf16[256,128]{1,0:T(8,128)(2,1)} %get-tuple-element.64), channel_id=1, source_target_pairs={{0,7},{1,0},{2,1},{3,2},{4,3},{5,4},{6,5},{7,6},{8,15},{9,8},{10,9... | collective-permute-start | bytes 196616 | tf_op jit(solution)/shard_map/ppermute | solution.py:619
  19.0 1.6 %copy-start = (bf16[32,64,512]{2,1,0:T(8,128)(2,1)S(1)}, bf16[32,64,512]{2,1,0:T(8,128)(2,1)}, u32[]{:S(2)}) copy-start(bf16[32,64,512]{2,1,0:T(8,128)(2,1)} %fine_ref.8) | copy-start | bytes 6291460
  23.6 5.1 %collective-permute-start.7 = (bf16[288,128]{1,0:T(8,128)(2,1)S(1)}, bf16[288,128]{1,0:T(8,128)(2,1)S(1)}, u32[]{:S(2)}, u32[]{:S(2)}) collective-permute-start(bf16[288,128]{1,0:T(8,128)(2,1)S(1)} %get-tuple-element.66), channel_id=1, source_target_pairs={{0,1},{1,0},{2,3},{3,2},{4,5},{5,4},{6,7},{7,6},{8,9},{9,8},{10,11... | collective-permute-start | bytes 221192 | tf_op jit(solution)/shard_map/ppermute | solution.py:627
  25.7 3.0 %collective-permute-start.8 = (bf16[288,128]{1,0:T(8,128)(2,1)S(1)}, bf16[288,128]{1,0:T(8,128)(2,1)S(1)}, u32[]{:S(2)}, u32[]{:S(2)}) collective-permute-start(bf16[288,128]{1,0:T(8,128)(2,1)S(1)} %get-tuple-element.67), channel_id=1, source_target_pairs={{0,0},{1,2},{2,1},{3,4},{4,3},{5,6},{6,5},{7,7},{8,8},{9,10},{10,9... | collective-permute-start | bytes 221192 | tf_op jit(solution)/shard_map/ppermute | solution.py:627
  29.4 4.0 %collective-permute-start.9 = (bf16[368,128]{1,0:T(8,128)(2,1)S(1)}, bf16[368,128]{1,0:T(8,128)(2,1)S(1)}, u32[]{:S(2)}, u32[]{:S(2)}) collective-permute-start(bf16[368,128]{1,0:T(8,128)(2,1)S(1)} %get-tuple-element.73), channel_id=1, source_target_pairs={{0,8},{8,0},{16,24},{24,16},{1,9},{9,1},{17,25},{25,17},{2,10},{10... | collective-permute-start | bytes 282632 | tf_op jit(solution)/shard_map/ppermute | solution.py:627
  29.4 3.9 %collective-permute-start.10 = (bf16[368,128]{1,0:T(8,128)(2,1)S(1)}, bf16[368,128]{1,0:T(8,128)(2,1)S(1)}, u32[]{:S(2)}, u32[]{:S(2)}) collective-permute-start(bf16[368,128]{1,0:T(8,128)(2,1)S(1)} %get-tuple-element.74), channel_id=1, source_target_pairs={{0,0},{8,16},{16,8},{24,24},{1,1},{9,17},{17,9},{25,25},{2,2},{10,... | collective-permute-start | bytes 282632 | tf_op jit(solution)/shard_map/ppermute | solution.py:627
  33.4 16.9 %copy-start.1 = (bf16[32,64,512]{2,1,0:T(8,128)(2,1)S(1)}, bf16[32,64,512]{2,1,0:T(8,128)(2,1)}, u32[]{:S(2)}) copy-start(bf16[32,64,512]{2,1,0:T(8,128)(2,1)} %fine_ref.8) | copy-start | bytes 6291460
  33.4 16.9 %copy-start.2 = (bf16[128,512]{1,0:T(8,128)(2,1)S(1)}, bf16[128,512]{1,0:T(8,128)(2,1)}, u32[]{:S(2)}) copy-start(bf16[128,512]{1,0:T(8,128)(2,1)} %w_ref.7) | copy-start | bytes 393220
  36.6 10.4 %collective-permute-start.11 = (bf16[256,128]{1,0:T(8,128)(2,1)S(1)}, bf16[256,128]{1,0:T(8,128)(2,1)S(1)}, u32[]{:S(2)}, u32[]{:S(2)}) collective-permute-start(bf16[256,128]{1,0:T(8,128)(2,1)S(1)} %get-tuple-element.81), channel_id=1, source_target_pairs={{0,1},{1,2},{2,3},{3,4},{4,5},{5,6},{6,7},{7,0},{8,9},{9,10},{10,1... | collective-permute-start | bytes 196616 | tf_op jit(solution)/shard_map/ppermute | solution.py:619
  40.8 7.8 %collective-permute-start.14 = (bf16[256,128]{1,0:T(8,128)(2,1)S(1)}, bf16[256,128]{1,0:T(8,128)(2,1)S(1)}, u32[]{:S(2)}, u32[]{:S(2)}) collective-permute-start(bf16[256,128]{1,0:T(8,128)(2,1)S(1)} %get-tuple-element.85), channel_id=1, source_target_pairs={{0,2},{1,3},{2,4},{3,5},{4,6},{5,7},{6,0},{7,1},{8,10},{9,11},{10,... | collective-permute-start | bytes 196616 | tf_op jit(solution)/shard_map/ppermute | solution.py:619
  41.8 15.3 %collective-permute-start.13 = (bf16[256,128]{1,0:T(8,128)(2,1)S(1)}, bf16[256,128]{1,0:T(8,128)(2,1)S(1)}, u32[]{:S(2)}, u32[]{:S(2)}) collective-permute-start(bf16[256,128]{1,0:T(8,128)(2,1)S(1)} %get-tuple-element.84), channel_id=1, source_target_pairs={{0,6},{1,7},{2,0},{3,1},{4,2},{5,3},{6,4},{7,5},{8,14},{9,15},{10,... | collective-permute-start | bytes 196616 | tf_op jit(solution)/shard_map/ppermute | solution.py:619
  44.6 6.8 %collective-permute-start.16 = (bf16[256,128]{1,0:T(8,128)(2,1)S(1)}, bf16[256,128]{1,0:T(8,128)(2,1)S(1)}, u32[]{:S(2)}, u32[]{:S(2)}) collective-permute-start(bf16[256,128]{1,0:T(8,128)(2,1)S(1)} %get-tuple-element.88), channel_id=1, source_target_pairs={{0,4},{1,5},{2,6},{3,7},{4,0},{5,1},{6,2},{7,3},{8,12},{9,13},{10,... | collective-permute-start | bytes 196616 | tf_op jit(solution)/shard_map/ppermute | solution.py:619
  44.6 11.4 %collective-permute-start.17 = (bf16[256,128]{1,0:T(8,128)(2,1)S(1)}, bf16[256,128]{1,0:T(8,128)(2,1)S(1)}, u32[]{:S(2)}, u32[]{:S(2)}) collective-permute-start(bf16[256,128]{1,0:T(8,128)(2,1)S(1)} %get-tuple-element.89), channel_id=1, source_target_pairs={{0,3},{1,4},{2,5},{3,6},{4,7},{5,0},{6,1},{7,2},{8,11},{9,12},{10,... | collective-permute-start | bytes 196616 | tf_op jit(solution)/shard_map/ppermute | solution.py:619
  47.0 11.2 %collective-permute-start.12 = (bf16[256,128]{1,0:T(8,128)(2,1)S(1)}, bf16[256,128]{1,0:T(8,128)(2,1)S(1)}, u32[]{:S(2)}, u32[]{:S(2)}) collective-permute-start(bf16[256,128]{1,0:T(8,128)(2,1)S(1)} %get-tuple-element.83), channel_id=1, source_target_pairs={{0,7},{1,0},{2,1},{3,2},{4,3},{5,4},{6,5},{7,6},{8,15},{9,8},{10,9... | collective-permute-start | bytes 196616 | tf_op jit(solution)/shard_map/ppermute | solution.py:619
  48.5 8.6 %collective-permute-start.15 = (bf16[256,128]{1,0:T(8,128)(2,1)S(1)}, bf16[256,128]{1,0:T(8,128)(2,1)S(1)}, u32[]{:S(2)}, u32[]{:S(2)}) collective-permute-start(bf16[256,128]{1,0:T(8,128)(2,1)S(1)} %get-tuple-element.87), channel_id=1, source_target_pairs={{0,5},{1,6},{2,7},{3,0},{4,1},{5,2},{6,3},{7,4},{8,13},{9,14},{10,... | collective-permute-start | bytes 196616 | tf_op jit(solution)/shard_map/ppermute | solution.py:619

commit v13 on v12

--- a/solution.py
+++ b/solution.py
@@ -166,10 +166,9 @@
     bricks, cells, width = fine.shape
     mid = w.shape[0]
     step = 8
-    blocks = bricks // step
 
     def place(i):
-        return (first + i) % blocks
+        return first - i
 
     count = len(octants)
     partials = [] if partial is None else [partial]
@@ -657,9 +656,9 @@
     octant[7], *pieces = lax.optimization_barrier((octant[7], first, middle[2], last))
     coarse = jnp.concatenate(pieces, axis=0)
     fine_out = None
-    for block_index in (3, 2, 1, 0):
-        octants = [octant[2 * block_index], octant[2 * block_index + 1]]
-        fine_out = up_call(fine, mask, w_up, octants, block_index, fine_out)
+    for block_indices in ((3,), (2, 1, 0)):
+        octants = [octant[2 * k + part] for k in block_indices for part in range(2)]
+        fine_out = up_call(fine, mask, w_up, octants, block_indices[0], fine_out)
     return fine_out, coarse.reshape(SIDE, SIDE, COLS, mid)
 
 

time: 59.9 us -> 59 us (0.985)
  Pallas kernels: 19.8 us -> 18.7 us
    pallas_call x4 -> x2, Pallas kernels: 4.52 us -> 3.4 us  [up_call(): pl.pallas_call(functools.partial(up_kernel, count), grid=(count * CAP //...]
  transfers between devices with their start and end apart: 18 -> 18, of which waited for: 3 -> 6; matrix products, arithmetic and copies ran while one was open for 2% -> 2% of each run, Pallas kernels for 17% -> 13%
where the time goes in v13:
time: 59 us; the launch traced here: 58.8 us
  starting transfers between devices  30.7 us (52%)
  Pallas kernels  18.7 us (32%)
  waiting for transfers between devices  6.12 us (10%)
  local copies, waits for them, and re-layouts  1.62 us (3%)
  other arithmetic  0.9 us (2%)
  between operations  0.83 us (1%)
    ppermute x14, starting transfers between devices, from_behind(): return lax.ppermute(value, axis, pairs)  27.2 us
    ppermute x14, waiting for transfers between devices, from_behind(): return lax.ppermute(value, axis, pairs)  6.11 us
    pallas_call x1, Pallas kernels, down_call(): pl.pallas_call(functools.partial(down_kernel, offsets), in_specs=[hbm, hb...  3.97 us
    ppermute x4, starting transfers between devices, swap_face(): return lax.ppermute(face, axis, list(enumerate(partner)))  3.49 us
    pallas_call x2, Pallas kernels, up_call(): pl.pallas_call(functools.partial(up_kernel, count), grid=(count * CAP //...  3.4 us
    pallas_call x1, Pallas kernels, middle_call(): pl.pallas_call(middle_kernel, in_specs=[smem] + [vmem] * 6, out_specs=[vm...  3.23 us
    pallas_call x1, Pallas kernels, final_call(): pl.pallas_call(functools.partial(final_kernel, count), in_specs=[smem, sm...  3.21 us
    pallas_call x1, Pallas kernels, inner_call(): pl.pallas_call(functools.partial(inner_kernel, groups), in_specs=[smem, v...  2.37 us
  transfers between devices with their start and end apart: 18, of which 6 were waited for; matrix products, arithmetic and copies ran while one was open for 2% of the time, Pallas kernels for 13%

profile of v13, /device:TPU:0, one launch (start us, length us, event | category | flops | bytes accessed | tf_op | source)
XLA Modules:
  0.0 58.8 jit_solution(1682955990587137435)
XLA Ops:
  0.7 4.0 %down.1 = (bf16[256,128]{1,0:T(8,128)(2,1)}, bf16[256,128]{1,0:T(8,128)(2,1)}, bf16[256,128]{1,0:T(8,128)(2,1)}, bf16[256,128]{1,0:T(8,128)(2,1)}, bf16[256,128]...) custom-call(bf16[32,64,512]{2,1,0:T(8,128)(2,1)} %fine_ref.4, s32[32,512]{1,0:T(8,128)} %mask_ref, ...), custom_call_target="tpu_custom_call" | custom-call | flops 234881024 | bytes 1835008 | tf_op jit(solution)/shard_map/down/pallas_call | solution.py:85
  4.7 5.0 %collective-permute-start = (bf16[256,128]{1,0:T(8,128)(2,1)}, bf16[256,128]{1,0:T(8,128)(2,1)S(1)}, u32[]{:S(2)}, u32[]{:S(2)}) collective-permute-start(bf16[256,128]{1,0:T(8,128)(2,1)} %get-tuple-element.50), channel_id=1, source_target_pairs={{0,5},{1,6},{2,7},{3,0},{4,1},{5,2},{6,3},{7,4},{8,13},{9,14},{10,... | collective-permute-start | bytes 196616 | tf_op jit(solution)/shard_map/ppermute | solution.py:618
  9.7 1.5 %collective-permute-start.1 = (bf16[256,128]{1,0:T(8,128)(2,1)}, bf16[256,128]{1,0:T(8,128)(2,1)S(1)}, u32[]{:S(2)}, u32[]{:S(2)}) collective-permute-start(bf16[256,128]{1,0:T(8,128)(2,1)} %get-tuple-element.58), channel_id=1, source_target_pairs={{0,1},{1,2},{2,3},{3,4},{4,5},{5,6},{6,7},{7,0},{8,9},{9,10},{10,1... | collective-permute-start | bytes 196616 | tf_op jit(solution)/shard_map/ppermute | solution.py:618
  11.3 1.8 %collective-permute-start.3 = (bf16[256,128]{1,0:T(8,128)(2,1)}, bf16[256,128]{1,0:T(8,128)(2,1)S(1)}, u32[]{:S(2)}, u32[]{:S(2)}) collective-permute-start(bf16[256,128]{1,0:T(8,128)(2,1)} %get-tuple-element.60), channel_id=1, source_target_pairs={{0,3},{1,4},{2,5},{3,6},{4,7},{5,0},{6,1},{7,2},{8,11},{9,12},{10,... | collective-permute-start | bytes 196616 | tf_op jit(solution)/shard_map/ppermute | solution.py:618
  13.0 3.5 %collective-permute-start.4 = (bf16[256,128]{1,0:T(8,128)(2,1)}, bf16[256,128]{1,0:T(8,128)(2,1)S(1)}, u32[]{:S(2)}, u32[]{:S(2)}) collective-permute-start(bf16[256,128]{1,0:T(8,128)(2,1)} %get-tuple-element.61), channel_id=1, source_target_pairs={{0,4},{1,5},{2,6},{3,7},{4,0},{5,1},{6,2},{7,3},{8,12},{9,13},{10,... | collective-permute-start | bytes 196616 | tf_op jit(solution)/shard_map/ppermute | solution.py:618
  16.5 1.3 %collective-permute-start.5 = (bf16[256,128]{1,0:T(8,128)(2,1)}, bf16[256,128]{1,0:T(8,128)(2,1)S(1)}, u32[]{:S(2)}, u32[]{:S(2)}) collective-permute-start(bf16[256,128]{1,0:T(8,128)(2,1)} %get-tuple-element.63), channel_id=1, source_target_pairs={{0,6},{1,7},{2,0},{3,1},{4,2},{5,3},{6,4},{7,5},{8,14},{9,15},{10,... | collective-permute-start | bytes 196616 | tf_op jit(solution)/shard_map/ppermute | solution.py:618
  17.9 1.0 %collective-permute-start.6 = (bf16[256,128]{1,0:T(8,128)(2,1)}, bf16[256,128]{1,0:T(8,128)(2,1)S(1)}, u32[]{:S(2)}, u32[]{:S(2)}) collective-permute-start(bf16[256,128]{1,0:T(8,128)(2,1)} %get-tuple-element.64), channel_id=1, source_target_pairs={{0,7},{1,0},{2,1},{3,2},{4,3},{5,4},{6,5},{7,6},{8,15},{9,8},{10,9... | collective-permute-start | bytes 196616 | tf_op jit(solution)/shard_map/ppermute | solution.py:618
  19.0 1.6 %copy-done = bf16[32,64,512]{2,1,0:T(8,128)(2,1)S(1)} copy-done((bf16[32,64,512]{2,1,0:T(8,128)(2,1)S(1)}, bf16[32,64,512]{2,1,0:T(8,128)(2,1)}, u32[]{:S(2)}) %copy-start) | copy-done | bytes 2097176
  20.6 1.1 %prepare.1 = (bf16[256,128]{1,0:T(8,128)(2,1)S(1)}, bf16[2048,512]{1,0:T(8,128)(2,1)S(1)}, bf16[1152,384]{1,0:T(8,128)(2,1)S(1)}, bf16[1152,384]{1,0:T(8,128)(2,1)S(1)}) custom-call(bf16[32,64,512]{2,1,0:T(8,128)(2,1)S(1)} %copy-done, s32[32,512]{1,0:T(8,128)S(1)} %copy-done.6, bf16[512,128]{1,0:T(8,128)(2,1)S(1)} %copy-done.5, ...), custom_call_target="tpu_custom_call" | custom-call | flops 268435456 | bytes 2097152 | tf_op jit(solution)/shard_map/prepare/pallas_call | solution.py:128
  21.7 0.8 %collective-permute-done.3.refs_3_ = bf16[256,128]{1,0:T(8,128)(2,1)S(1)} collective-permute-done((bf16[256,128]{1,0:T(8,128)(2,1)}, bf16[256,128]{1,0:T(8,128)(2,1)S(1)}, u32[]{:S(2)}, u32[]{:S(2)}) %collective-permute-start.3) | collective-permute-done | bytes 65568 | tf_op jit(solution)/shard_map/ppermute | solution.py:618
  22.5 0.3 collective-permute-done.6.refs_7_
  22.8 0.8 %place.1 = (bf16[2048,128]{1,0:T(8,128)(2,1)S(1)}, bf16[288,128]{1,0:T(8,128)(2,1)S(1)}, bf16[288,128]{1,0:T(8,128)(2,1)S(1)}) custom-call(s32[2]{0:T(128)S(1)} %pad_add_fusion.base_ref, s32[32]{0:T(128)S(1)} %copy-done.7, bf16[256,128]{1,0:T(8,128)(2,1)S(1)} %get-tuple-element.57.refs_0_, bf16[256,128]{1,0:T(8,128)(2,1)S(1)} %collective-permute-done.1.refs_1_, ...), custom_call_target="tpu_custom_call" | custom-call | tf_op jit(solution)/shard_map/place/pallas_call | solution.py:264
  23.6 2.1 %collective-permute-start.7 = (bf16[288,128]{1,0:T(8,128)(2,1)S(1)}, bf16[288,128]{1,0:T(8,128)(2,1)S(1)}, u32[]{:S(2)}, u32[]{:S(2)}) collective-permute-start(bf16[288,128]{1,0:T(8,128)(2,1)S(1)} %get-tuple-element.66), channel_id=1, source_target_pairs={{0,1},{1,0},{2,3},{3,2},{4,5},{5,4},{6,7},{7,6},{8,9},{9,8},{10,11... | collective-permute-start | bytes 221192 | tf_op jit(solution)/shard_map/ppermute | solution.py:626
  25.7 0.7 %collective-permute-start.8 = (bf16[288,128]{1,0:T(8,128)(2,1)S(1)}, bf16[288,128]{1,0:T(8,128)(2,1)S(1)}, u32[]{:S(2)}, u32[]{:S(2)}) collective-permute-start(bf16[288,128]{1,0:T(8,128)(2,1)S(1)} %get-tuple-element.67), channel_id=1, source_target_pairs={{0,0},{1,2},{2,1},{3,4},{4,3},{5,6},{6,5},{7,7},{8,8},{9,10},{10,9... | collective-permute-start | bytes 221192 | tf_op jit(solution)/shard_map/ppermute | solution.py:626
  26.3 2.4 %inner.1.refs_3_ = bf16[11,112,128]{2,1,0:T(8,128)(2,1)S(1)} custom-call(s32[32]{0:T(128)S(1)} %copy-done.7, bf16[2048,128]{1,0:T(8,128)(2,1)S(1)} %get-tuple-element.65.block_ref.refs_0_, bf16[1152,384]{1,0:T(8,128)(2,1)S(1)} %get-tuple-element.68.wide1_ref.refs_4_.refs_8_), custom_call_target="tpu_custom_call" | custom-call | flops 1089994752 | bytes 1769472 | tf_op jit(solution)/shard_map/inner/pallas_call | solution.py:423
  28.7 0.6 %edge.1 = (bf16[288,128]{1,0:T(8,128)(2,1)S(1)}, bf16[288,128]{1,0:T(8,128)(2,1)S(1)}, bf16[368,128]{1,0:T(8,128)(2,1)S(1)}, bf16[368,128]{1,0:T(8,128)(2,1)S(1)}) custom-call(s32[2]{0:T(128)S(1)} %pad_add_fusion.base_ref, s32[32]{0:T(128)S(1)} %copy-done.7, bf16[2048,128]{1,0:T(8,128)(2,1)S(1)} %get-tuple-element.65.block_ref.refs_0_, ...), custom_call_target="tpu_custom_call" | custom-call | tf_op jit(solution)/shard_map/edge/pallas_call | solution.py:314
  29.4 0.7 %collective-permute-start.10 = (bf16[368,128]{1,0:T(8,128)(2,1)S(1)}, bf16[368,128]{1,0:T(8,128)(2,1)S(1)}, u32[]{:S(2)}, u32[]{:S(2)}) collective-permute-start(bf16[368,128]{1,0:T(8,128)(2,1)S(1)} %get-tuple-element.74), channel_id=1, source_target_pairs={{0,0},{8,16},{16,8},{24,24},{1,1},{9,17},{17,9},{25,25},{2,2},{10,... | collective-permute-start | bytes 282632 | tf_op jit(solution)/shard_map/ppermute | solution.py:626
  30.1 3.2 %middle.1 = (bf16[14,144,128]{2,1,0:T(8,128)(2,1)S(1)}, bf16[14,144,128]{2,1,0:T(8,128)(2,1)S(1)}, bf16[1024,128]{1,0:T(8,128)(2,1)S(1)}) custom-call(s32[32]{0:T(128)S(1)} %copy-done.7, bf16[2048,128]{1,0:T(8,128)(2,1)S(1)} %get-tuple-element.65.block_ref.refs_0_, bf16[288,128]{1,0:T(8,128)(2,1)S(1)} %get-tuple-element.71.refs_1_, ...), custom_call_target="tpu_custom_call" | custom-call | flops 1599602688 | bytes 1769472 | tf_op jit(solution)/shard_map/middle/pallas_call | solution.py:499
  33.4 3.2 %final.1 = (bf16[512,128]{1,0:T(8,128)(2,1)S(1)}, bf16[512,128]{1,0:T(8,128)(2,1)S(1)}, bf16[256,128]{1,0:T(8,128)(2,1)S(1)}, bf16[256,128]{1,0:T(8,128)(2,1)S(1...) custom-call(s32[2]{0:T(128)S(1)} %pad_add_fusion.base_ref, ...), custom_call_target="tpu_custom_call" | custom-call | flops 1415577600 | bytes 1769472 | tf_op jit(solution)/shard_map/final/pallas_call | solution.py:594
  36.6 5.1 %collective-permute-start.14 = (bf16[256,128]{1,0:T(8,128)(2,1)S(1)}, bf16[256,128]{1,0:T(8,128)(2,1)S(1)}, u32[]{:S(2)}, u32[]{:S(2)}) collective-permute-start(bf16[256,128]{1,0:T(8,128)(2,1)S(1)} %get-tuple-element.83), channel_id=1, source_target_pairs={{0,2},{1,3},{2,4},{3,5},{4,6},{5,7},{6,0},{7,1},{8,10},{9,11},{10,... | collective-permute-start | bytes 196616 | tf_op jit(solution)/shard_map/ppermute | solution.py:618
  41.8 1.4 %collective-permute-start.11 = (bf16[256,128]{1,0:T(8,128)(2,1)S(1)}, bf16[256,128]{1,0:T(8,128)(2,1)S(1)}, u32[]{:S(2)}, u32[]{:S(2)}) collective-permute-start(bf16[256,128]{1,0:T(8,128)(2,1)S(1)} %get-tuple-element.80), channel_id=1, source_target_pairs={{0,4},{1,5},{2,6},{3,7},{4,0},{5,1},{6,2},{7,3},{8,12},{9,13},{10,... | collective-permute-start | bytes 196616 | tf_op jit(solution)/shard_map/ppermute | solution.py:618
  43.2 3.9 %collective-permute-start.12 = (bf16[256,128]{1,0:T(8,128)(2,1)S(1)}, bf16[256,128]{1,0:T(8,128)(2,1)S(1)}, u32[]{:S(2)}, u32[]{:S(2)}) collective-permute-start(bf16[256,128]{1,0:T(8,128)(2,1)S(1)} %get-tuple-element.81), channel_id=1, source_target_pairs={{0,3},{1,4},{2,5},{3,6},{4,7},{5,0},{6,1},{7,2},{8,11},{9,12},{10,... | collective-permute-start | bytes 196616 | tf_op jit(solution)/shard_map/ppermute | solution.py:618
  47.0 0.9 %collective-permute-start.13 = (bf16[256,128]{1,0:T(8,128)(2,1)S(1)}, bf16[256,128]{1,0:T(8,128)(2,1)S(1)}, u32[]{:S(2)}, u32[]{:S(2)}) collective-permute-start(bf16[256,128]{1,0:T(8,128)(2,1)S(1)} %get-tuple-element.82), channel_id=1, source_target_pairs={{0,6},{1,7},{2,0},{3,1},{4,2},{5,3},{6,4},{7,5},{8,14},{9,15},{10,... | collective-permute-start | bytes 196616 | tf_op jit(solution)/shard_map/ppermute | solution.py:618
  48.0 0.5 collective-permute-start.15
  48.5 0.5 collective-permute-done.16.refs_1_
  49.0 1.0 %collective-permute-start.17 = (bf16[256,128]{1,0:T(8,128)(2,1)S(1)}, bf16[256,128]{1,0:T(8,128)(2,1)S(1)}, u32[]{:S(2)}, u32[]{:S(2)}) collective-permute-start(bf16[256,128]{1,0:T(8,128)(2,1)S(1)} %get-tuple-element.89), channel_id=1, source_target_pairs={{0,7},{1,0},{2,1},{3,2},{4,3},{5,4},{6,5},{7,6},{8,15},{9,8},{10,9... | collective-permute-start | bytes 196616 | tf_op jit(solution)/shard_map/ppermute | solution.py:618
  50.0 0.8 %pad_maximum_fusion = bf16[2048,128]{1,0:T(8,128)(2,1)} fusion(bf16[512,128]{1,0:T(8,128)(2,1)S(1)} %get-tuple-element.97, bf16[1024,128]{1,0:T(8,128)(2,1)S(1)} %get-tuple-element.96.refs_7_, bf16[512,128]{1,0:T(8,128)(2,1)S(1)} %get-tuple-element.95), kind=kLoop, calls=%fused_computation | loop fusion | flops 1572864 | bytes 1048576 | tf_op jit(solution)/shard_map/concatenate | solution.py:657
  50.9 1.1 %up.2.refs_6_ = bf16[32,64,512]{2,1,0:T(8,128)(2,1)} custom-call(bf16[32,64,512]{2,1,0:T(8,128)(2,1)S(1)} %copy-done.1, bf16[2048,512]{1,0:T(8,128)(2,1)S(1)} %get-tuple-element.56.mask_ref, bf16[128,512]{1,0:T(8,128)(2,1)S(1)} %copy-done.4, bf16[256,128]{1,0:T(8,128)(2,1)S(1)} %collective-permute-done.14.refs_0_, ...), custom_call_target="tpu_custom_call" | custom-call | flops 134217728 | bytes 2097152 | tf_op jit(solution)/shard_map/up/pallas_call | solution.py:175
  52.0 2.6 %collective-permute-done.12.refs_1_ = bf16[256,128]{1,0:T(8,128)(2,1)S(1)} collective-permute-done((bf16[256,128]{1,0:T(8,128)(2,1)S(1)}, bf16[256,128]{1,0:T(8,128)(2,1)S(1)}, u32[]{:S(2)}, u32[]{:S(2)}) %collective-permute-start.12) | collective-permute-done | bytes 65568 | tf_op jit(solution)/shard_map/ppermute | solution.py:618
  54.6 0.9 %collective-permute-done.15.refs_3_ = bf16[256,128]{1,0:T(8,128)(2,1)S(1)} collective-permute-done((bf16[256,128]{1,0:T(8,128)(2,1)S(1)}, bf16[256,128]{1,0:T(8,128)(2,1)S(1)}, u32[]{:S(2)}, u32[]{:S(2)}) %collective-permute-start.15) | collective-permute-done | bytes 65568 | tf_op jit(solution)/shard_map/ppermute | solution.py:618
  55.4 1.1 %collective-permute-done.17.refs_5_ = bf16[256,128]{1,0:T(8,128)(2,1)S(1)} collective-permute-done((bf16[256,128]{1,0:T(8,128)(2,1)S(1)}, bf16[256,128]{1,0:T(8,128)(2,1)S(1)}, u32[]{:S(2)}, u32[]{:S(2)}) %collective-permute-start.17) | collective-permute-done | bytes 65568 | tf_op jit(solution)/shard_map/ppermute | solution.py:618
  56.5 2.3 %up.3 = bf16[32,64,512]{2,1,0:T(8,128)(2,1)} custom-call(bf16[32,64,512]{2,1,0:T(8,128)(2,1)S(1)} %copy-done.1, bf16[2048,512]{1,0:T(8,128)(2,1)S(1)} %get-tuple-element.56.mask_ref, bf16[128,512]{1,0:T(8,128)(2,1)S(1)} %copy-done.4, bf16[256,128]{1,0:T(8,128)(2,1)S(1)} %collective-permute-done.11.refs_0_, ...), custom_call_target="tpu_custom_call", output_to_operand_aliasing={{}: (9, {})} | custom-call | flops 134217728 | bytes 2097152 | tf_op jit(solution)/shard_map/up/pallas_call | solution.py:175
  (31 shorter events, 0.3 us)
Async XLA Ops:
  0.6 18.4 %copy-start.5 = (bf16[512,128]{1,0:T(8,128)(2,1)S(1)}, bf16[512,128]{1,0:T(8,128)(2,1)}, u32[]{:S(2)}) copy-start(bf16[512,128]{1,0:T(8,128)(2,1)} %w_down_ref) | copy-start | bytes 393220
  0.6 18.4 %copy-start.6 = (s32[32,512]{1,0:T(8,128)S(1)}, s32[32,512]{1,0:T(8,128)}, u32[]{:S(2)}) copy-start(s32[32,512]{1,0:T(8,128)} %mask_ref) | copy-start | bytes 196612
  0.7 18.4 %copy-start.3 = (bf16[27,128,128]{2,1,0:T(8,128)(2,1)S(1)}, bf16[27,128,128]{2,1,0:T(8,128)(2,1)}, u32[]{:S(2)}) copy-start(bf16[27,128,128]{2,1,0:T(8,128)(2,1)} %w2_ref) | copy-start | bytes 2654212
  0.7 18.4 %copy-start.2 = (bf16[27,128,128]{2,1,0:T(8,128)(2,1)S(1)}, bf16[27,128,128]{2,1,0:T(8,128)(2,1)}, u32[]{:S(2)}) copy-start(bf16[27,128,128]{2,1,0:T(8,128)(2,1)} %w1_ref) | copy-start | bytes 2654212
  4.6 18.1 %copy-start.7 = (s32[32]{0:T(128)S(1)}, s32[32]{0:T(128)}, u32[]{:S(2)}) copy-start(s32[32]{0:T(128)} %source_ref.9) | copy-start | bytes 388
  4.7 11.9 %collective-permute-start = (bf16[256,128]{1,0:T(8,128)(2,1)}, bf16[256,128]{1,0:T(8,128)(2,1)S(1)}, u32[]{:S(2)}, u32[]{:S(2)}) collective-permute-start(bf16[256,128]{1,0:T(8,128)(2,1)} %get-tuple-element.50), channel_id=1, source_target_pairs={{0,5},{1,6},{2,7},{3,0},{4,1},{5,2},{6,3},{7,4},{8,13},{9,14},{10,... | collective-permute-start | bytes 196616 | tf_op jit(solution)/shard_map/ppermute | solution.py:618
  9.7 8.2 %collective-permute-start.1 = (bf16[256,128]{1,0:T(8,128)(2,1)}, bf16[256,128]{1,0:T(8,128)(2,1)S(1)}, u32[]{:S(2)}, u32[]{:S(2)}) collective-permute-start(bf16[256,128]{1,0:T(8,128)(2,1)} %get-tuple-element.58), channel_id=1, source_target_pairs={{0,1},{1,2},{2,3},{3,4},{4,5},{5,6},{6,7},{7,0},{8,9},{9,10},{10,1... | collective-permute-start | bytes 196616 | tf_op jit(solution)/shard_map/ppermute | solution.py:618
  11.2 10.5 %collective-permute-start.2 = (bf16[256,128]{1,0:T(8,128)(2,1)}, bf16[256,128]{1,0:T(8,128)(2,1)S(1)}, u32[]{:S(2)}, u32[]{:S(2)}) collective-permute-start(bf16[256,128]{1,0:T(8,128)(2,1)} %get-tuple-element.59), channel_id=1, source_target_pairs={{0,2},{1,3},{2,4},{3,5},{4,6},{5,7},{6,0},{7,1},{8,10},{9,11},{10,... | collective-permute-start | bytes 196616 | tf_op jit(solution)/shard_map/ppermute | solution.py:618
  11.3 11.3 %collective-permute-start.3 = (bf16[256,128]{1,0:T(8,128)(2,1)}, bf16[256,128]{1,0:T(8,128)(2,1)S(1)}, u32[]{:S(2)}, u32[]{:S(2)}) collective-permute-start(bf16[256,128]{1,0:T(8,128)(2,1)} %get-tuple-element.60), channel_id=1, source_target_pairs={{0,3},{1,4},{2,5},{3,6},{4,7},{5,0},{6,1},{7,2},{8,11},{9,12},{10,... | collective-permute-start | bytes 196616 | tf_op jit(solution)/shard_map/ppermute | solution.py:618
  13.0 9.5 %collective-permute-start.4 = (bf16[256,128]{1,0:T(8,128)(2,1)}, bf16[256,128]{1,0:T(8,128)(2,1)S(1)}, u32[]{:S(2)}, u32[]{:S(2)}) collective-permute-start(bf16[256,128]{1,0:T(8,128)(2,1)} %get-tuple-element.61), channel_id=1, source_target_pairs={{0,4},{1,5},{2,6},{3,7},{4,0},{5,1},{6,2},{7,3},{8,12},{9,13},{10,... | collective-permute-start | bytes 196616 | tf_op jit(solution)/shard_map/ppermute | solution.py:618
  16.5 6.0 %collective-permute-start.5 = (bf16[256,128]{1,0:T(8,128)(2,1)}, bf16[256,128]{1,0:T(8,128)(2,1)S(1)}, u32[]{:S(2)}, u32[]{:S(2)}) collective-permute-start(bf16[256,128]{1,0:T(8,128)(2,1)} %get-tuple-element.63), channel_id=1, source_target_pairs={{0,6},{1,7},{2,0},{3,1},{4,2},{5,3},{6,4},{7,5},{8,14},{9,15},{10,... | collective-permute-start | bytes 196616 | tf_op jit(solution)/shard_map/ppermute | solution.py:618
  17.9 4.9 %collective-permute-start.6 = (bf16[256,128]{1,0:T(8,128)(2,1)}, bf16[256,128]{1,0:T(8,128)(2,1)S(1)}, u32[]{:S(2)}, u32[]{:S(2)}) collective-permute-start(bf16[256,128]{1,0:T(8,128)(2,1)} %get-tuple-element.64), channel_id=1, source_target_pairs={{0,7},{1,0},{2,1},{3,2},{4,3},{5,4},{6,5},{7,6},{8,15},{9,8},{10,9... | collective-permute-start | bytes 196616 | tf_op jit(solution)/shard_map/ppermute | solution.py:618
  19.0 1.6 %copy-start = (bf16[32,64,512]{2,1,0:T(8,128)(2,1)S(1)}, bf16[32,64,512]{2,1,0:T(8,128)(2,1)}, u32[]{:S(2)}) copy-start(bf16[32,64,512]{2,1,0:T(8,128)(2,1)} %fine_ref.4) | copy-start | bytes 6291460
  23.6 5.1 %collective-permute-start.7 = (bf16[288,128]{1,0:T(8,128)(2,1)S(1)}, bf16[288,128]{1,0:T(8,128)(2,1)S(1)}, u32[]{:S(2)}, u32[]{:S(2)}) collective-permute-start(bf16[288,128]{1,0:T(8,128)(2,1)S(1)} %get-tuple-element.66), channel_id=1, source_target_pairs={{0,1},{1,0},{2,3},{3,2},{4,5},{5,4},{6,7},{7,6},{8,9},{9,8},{10,11... | collective-permute-start | bytes 221192 | tf_op jit(solution)/shard_map/ppermute | solution.py:626
  25.7 3.0 %collective-permute-start.8 = (bf16[288,128]{1,0:T(8,128)(2,1)S(1)}, bf16[288,128]{1,0:T(8,128)(2,1)S(1)}, u32[]{:S(2)}, u32[]{:S(2)}) collective-permute-start(bf16[288,128]{1,0:T(8,128)(2,1)S(1)} %get-tuple-element.67), channel_id=1, source_target_pairs={{0,0},{1,2},{2,1},{3,4},{4,3},{5,6},{6,5},{7,7},{8,8},{9,10},{10,9... | collective-permute-start | bytes 221192 | tf_op jit(solution)/shard_map/ppermute | solution.py:626
  29.4 4.0 %collective-permute-start.9 = (bf16[368,128]{1,0:T(8,128)(2,1)S(1)}, bf16[368,128]{1,0:T(8,128)(2,1)S(1)}, u32[]{:S(2)}, u32[]{:S(2)}) collective-permute-start(bf16[368,128]{1,0:T(8,128)(2,1)S(1)} %get-tuple-element.73), channel_id=1, source_target_pairs={{0,8},{8,0},{16,24},{24,16},{1,9},{9,1},{17,25},{25,17},{2,10},{10... | collective-permute-start | bytes 282632 | tf_op jit(solution)/shard_map/ppermute | solution.py:626
  29.4 3.9 %collective-permute-start.10 = (bf16[368,128]{1,0:T(8,128)(2,1)S(1)}, bf16[368,128]{1,0:T(8,128)(2,1)S(1)}, u32[]{:S(2)}, u32[]{:S(2)}) collective-permute-start(bf16[368,128]{1,0:T(8,128)(2,1)S(1)} %get-tuple-element.74), channel_id=1, source_target_pairs={{0,0},{8,16},{16,8},{24,24},{1,1},{9,17},{17,9},{25,25},{2,2},{10,... | collective-permute-start | bytes 282632 | tf_op jit(solution)/shard_map/ppermute | solution.py:626
  33.4 17.5 %copy-start.1 = (bf16[32,64,512]{2,1,0:T(8,128)(2,1)S(1)}, bf16[32,64,512]{2,1,0:T(8,128)(2,1)}, u32[]{:S(2)}) copy-start(bf16[32,64,512]{2,1,0:T(8,128)(2,1)} %fine_ref.4) | copy-start | bytes 6291460
  33.4 17.5 %copy-start.4 = (bf16[128,512]{1,0:T(8,128)(2,1)S(1)}, bf16[128,512]{1,0:T(8,128)(2,1)}, u32[]{:S(2)}) copy-start(bf16[128,512]{1,0:T(8,128)(2,1)} %w_ref.3) | copy-start | bytes 393220
  36.6 11.3 %collective-permute-start.14 = (bf16[256,128]{1,0:T(8,128)(2,1)S(1)}, bf16[256,128]{1,0:T(8,128)(2,1)S(1)}, u32[]{:S(2)}, u32[]{:S(2)}) collective-permute-start(bf16[256,128]{1,0:T(8,128)(2,1)S(1)} %get-tuple-element.83), channel_id=1, source_target_pairs={{0,2},{1,3},{2,4},{3,5},{4,6},{5,7},{6,0},{7,1},{8,10},{9,11},{10,... | collective-permute-start | bytes 196616 | tf_op jit(solution)/shard_map/ppermute | solution.py:618
  41.7 7.2 %collective-permute-start.16 = (bf16[256,128]{1,0:T(8,128)(2,1)S(1)}, bf16[256,128]{1,0:T(8,128)(2,1)S(1)}, u32[]{:S(2)}, u32[]{:S(2)}) collective-permute-start(bf16[256,128]{1,0:T(8,128)(2,1)S(1)} %get-tuple-element.87), channel_id=1, source_target_pairs={{0,1},{1,2},{2,3},{3,4},{4,5},{5,6},{6,7},{7,0},{8,9},{9,10},{10,1... | collective-permute-start | bytes 196616 | tf_op jit(solution)/shard_map/ppermute | solution.py:618
  41.8 10.2 %collective-permute-start.11 = (bf16[256,128]{1,0:T(8,128)(2,1)S(1)}, bf16[256,128]{1,0:T(8,128)(2,1)S(1)}, u32[]{:S(2)}, u32[]{:S(2)}) collective-permute-start(bf16[256,128]{1,0:T(8,128)(2,1)S(1)} %get-tuple-element.80), channel_id=1, source_target_pairs={{0,4},{1,5},{2,6},{3,7},{4,0},{5,1},{6,2},{7,3},{8,12},{9,13},{10,... | collective-permute-start | bytes 196616 | tf_op jit(solution)/shard_map/ppermute | solution.py:618
  43.2 11.4 %collective-permute-start.12 = (bf16[256,128]{1,0:T(8,128)(2,1)S(1)}, bf16[256,128]{1,0:T(8,128)(2,1)S(1)}, u32[]{:S(2)}, u32[]{:S(2)}) collective-permute-start(bf16[256,128]{1,0:T(8,128)(2,1)S(1)} %get-tuple-element.81), channel_id=1, source_target_pairs={{0,3},{1,4},{2,5},{3,6},{4,7},{5,0},{6,1},{7,2},{8,11},{9,12},{10,... | collective-permute-start | bytes 196616 | tf_op jit(solution)/shard_map/ppermute | solution.py:618
  47.0 7.5 %collective-permute-start.13 = (bf16[256,128]{1,0:T(8,128)(2,1)S(1)}, bf16[256,128]{1,0:T(8,128)(2,1)S(1)}, u32[]{:S(2)}, u32[]{:S(2)}) collective-permute-start(bf16[256,128]{1,0:T(8,128)(2,1)S(1)} %get-tuple-element.82), channel_id=1, source_target_pairs={{0,6},{1,7},{2,0},{3,1},{4,2},{5,3},{6,4},{7,5},{8,14},{9,15},{10,... | collective-permute-start | bytes 196616 | tf_op jit(solution)/shard_map/ppermute | solution.py:618
  48.0 7.5 %collective-permute-start.15 = (bf16[256,128]{1,0:T(8,128)(2,1)S(1)}, bf16[256,128]{1,0:T(8,128)(2,1)S(1)}, u32[]{:S(2)}, u32[]{:S(2)}) collective-permute-start(bf16[256,128]{1,0:T(8,128)(2,1)S(1)} %get-tuple-element.85), channel_id=1, source_target_pairs={{0,5},{1,6},{2,7},{3,0},{4,1},{5,2},{6,3},{7,4},{8,13},{9,14},{10,... | collective-permute-start | bytes 196616 | tf_op jit(solution)/shard_map/ppermute | solution.py:618
  49.0 7.5 %collective-permute-start.17 = (bf16[256,128]{1,0:T(8,128)(2,1)S(1)}, bf16[256,128]{1,0:T(8,128)(2,1)S(1)}, u32[]{:S(2)}, u32[]{:S(2)}) collective-permute-start(bf16[256,128]{1,0:T(8,128)(2,1)S(1)} %get-tuple-element.89), channel_id=1, source_target_pairs={{0,7},{1,0},{2,1},{3,2},{4,3},{5,4},{6,5},{7,6},{8,15},{9,8},{10,9... | collective-permute-start | bytes 196616 | tf_op jit(solution)/shard_map/ppermute | solution.py:618

commit v14 on v13

--- a/solution.py
+++ b/solution.py
@@ -18,7 +18,7 @@
 LATE = ((12, 3),)
 LATE_PLANES = 3
 SENT = (4, 3, 5, 2, 6, 1, 7)
-RETURNED = (6, 7, 4, 5, 2, 3, 1)
+RETURNED = (7, 6, 4, 5, 2, 3, 1)
 DOWN_LIMIT = 62 * 1024 * 1024
 VMEM_LIMIT = 24 * 1024 * 1024
 
@@ -656,7 +656,7 @@
     octant[7], *pieces = lax.optimization_barrier((octant[7], first, middle[2], last))
     coarse = jnp.concatenate(pieces, axis=0)
     fine_out = None
-    for block_indices in ((3,), (2, 1, 0)):
+    for block_indices in ((3,), (2, 1), (0,)):
         octants = [octant[2 * k + part] for k in block_indices for part in range(2)]
         fine_out = up_call(fine, mask, w_up, octants, block_indices[0], fine_out)
     return fine_out, coarse.reshape(SIDE, SIDE, COLS, mid)

time: 59 us -> 59 us (level)
  starting transfers between devices: 30.7 us -> 29.7 us
  waiting for transfers between devices: 6.12 us -> 6.77 us
    ppermute x14, starting transfers between devices: 27.2 us -> 26.3 us  [from_behind(): return lax.ppermute(value, axis, pairs)]
    ppermute x14, waiting for transfers between devices: 6.11 us -> 6.76 us  [from_behind(): return lax.ppermute(value, axis, pairs)]
    pallas_call x2 -> x3, Pallas kernels: 3.4 us -> 3.73 us  [up_call(): pl.pallas_call(functools.partial(up_kernel, count), grid=(count * CAP //...]
  transfers between devices with their start and end apart: 18 -> 18, of which waited for: 6 -> 5; matrix products, arithmetic and copies ran while one was open for 2% -> 2% of each run, Pallas kernels for 13% -> 16%
where the time goes in v14:
time: 59 us; the launch traced here: 58.9 us
  starting transfers between devices  29.7 us (50%)
  Pallas kernels  19 us (32%)
  waiting for transfers between devices  6.77 us (11%)
  local copies, waits for them, and re-layouts  1.62 us (3%)
  other arithmetic  0.9 us (2%)
  between operations  0.83 us (1%)
    ppermute x14, starting transfers between devices, from_behind(): return lax.ppermute(value, axis, pairs)  26.3 us
    ppermute x14, waiting for transfers between devices, from_behind(): return lax.ppermute(value, axis, pairs)  6.76 us
    pallas_call x1, Pallas kernels, down_call(): pl.pallas_call(functools.partial(down_kernel, offsets), in_specs=[hbm, hb...  3.97 us
    pallas_call x3, Pallas kernels, up_call(): pl.pallas_call(functools.partial(up_kernel, count), grid=(count * CAP //...  3.73 us
    ppermute x4, starting transfers between devices, swap_face(): return lax.ppermute(face, axis, list(enumerate(partner)))  3.49 us
    pallas_call x1, Pallas kernels, middle_call(): pl.pallas_call(middle_kernel, in_specs=[smem] + [vmem] * 6, out_specs=[vm...  3.23 us
    pallas_call x1, Pallas kernels, final_call(): pl.pallas_call(functools.partial(final_kernel, count), in_specs=[smem, sm...  3.21 us
    pallas_call x1, Pallas kernels, inner_call(): pl.pallas_call(functools.partial(inner_kernel, groups), in_specs=[smem, v...  2.37 us
  transfers between devices with their start and end apart: 18, of which 5 were waited for; matrix products, arithmetic and copies ran while one was open for 2% of the time, Pallas kernels for 16%

profile of v14, /device:TPU:0, one launch (start us, length us, event | category | flops | bytes accessed | tf_op | source)
XLA Modules:
  0.0 58.9 jit_solution(9453962989564589053)
XLA Ops:
  0.7 4.0 %down.1 = (bf16[256,128]{1,0:T(8,128)(2,1)}, bf16[256,128]{1,0:T(8,128)(2,1)}, bf16[256,128]{1,0:T(8,128)(2,1)}, bf16[256,128]{1,0:T(8,128)(2,1)}, bf16[256,128]...) custom-call(bf16[32,64,512]{2,1,0:T(8,128)(2,1)} %fine_ref.6, s32[32,512]{1,0:T(8,128)} %mask_ref, ...), custom_call_target="tpu_custom_call" | custom-call | flops 234881024 | bytes 1835008 | tf_op jit(solution)/shard_map/down/pallas_call | solution.py:85
  4.7 5.0 %collective-permute-start = (bf16[256,128]{1,0:T(8,128)(2,1)}, bf16[256,128]{1,0:T(8,128)(2,1)S(1)}, u32[]{:S(2)}, u32[]{:S(2)}) collective-permute-start(bf16[256,128]{1,0:T(8,128)(2,1)} %get-tuple-element.50), channel_id=1, source_target_pairs={{0,5},{1,6},{2,7},{3,0},{4,1},{5,2},{6,3},{7,4},{8,13},{9,14},{10,... | collective-permute-start | bytes 196616 | tf_op jit(solution)/shard_map/ppermute | solution.py:618
  9.7 1.5 %collective-permute-start.1 = (bf16[256,128]{1,0:T(8,128)(2,1)}, bf16[256,128]{1,0:T(8,128)(2,1)S(1)}, u32[]{:S(2)}, u32[]{:S(2)}) collective-permute-start(bf16[256,128]{1,0:T(8,128)(2,1)} %get-tuple-element.58), channel_id=1, source_target_pairs={{0,1},{1,2},{2,3},{3,4},{4,5},{5,6},{6,7},{7,0},{8,9},{9,10},{10,1... | collective-permute-start | bytes 196616 | tf_op jit(solution)/shard_map/ppermute | solution.py:618
  11.3 1.8 %collective-permute-start.3 = (bf16[256,128]{1,0:T(8,128)(2,1)}, bf16[256,128]{1,0:T(8,128)(2,1)S(1)}, u32[]{:S(2)}, u32[]{:S(2)}) collective-permute-start(bf16[256,128]{1,0:T(8,128)(2,1)} %get-tuple-element.60), channel_id=1, source_target_pairs={{0,3},{1,4},{2,5},{3,6},{4,7},{5,0},{6,1},{7,2},{8,11},{9,12},{10,... | collective-permute-start | bytes 196616 | tf_op jit(solution)/shard_map/ppermute | solution.py:618
  13.0 3.5 %collective-permute-start.4 = (bf16[256,128]{1,0:T(8,128)(2,1)}, bf16[256,128]{1,0:T(8,128)(2,1)S(1)}, u32[]{:S(2)}, u32[]{:S(2)}) collective-permute-start(bf16[256,128]{1,0:T(8,128)(2,1)} %get-tuple-element.61), channel_id=1, source_target_pairs={{0,4},{1,5},{2,6},{3,7},{4,0},{5,1},{6,2},{7,3},{8,12},{9,13},{10,... | collective-permute-start | bytes 196616 | tf_op jit(solution)/shard_map/ppermute | solution.py:618
  16.5 1.3 %collective-permute-start.5 = (bf16[256,128]{1,0:T(8,128)(2,1)}, bf16[256,128]{1,0:T(8,128)(2,1)S(1)}, u32[]{:S(2)}, u32[]{:S(2)}) collective-permute-start(bf16[256,128]{1,0:T(8,128)(2,1)} %get-tuple-element.63), channel_id=1, source_target_pairs={{0,6},{1,7},{2,0},{3,1},{4,2},{5,3},{6,4},{7,5},{8,14},{9,15},{10,... | collective-permute-start | bytes 196616 | tf_op jit(solution)/shard_map/ppermute | solution.py:618
  17.9 1.0 %collective-permute-start.6 = (bf16[256,128]{1,0:T(8,128)(2,1)}, bf16[256,128]{1,0:T(8,128)(2,1)S(1)}, u32[]{:S(2)}, u32[]{:S(2)}) collective-permute-start(bf16[256,128]{1,0:T(8,128)(2,1)} %get-tuple-element.64), channel_id=1, source_target_pairs={{0,7},{1,0},{2,1},{3,2},{4,3},{5,4},{6,5},{7,6},{8,15},{9,8},{10,9... | collective-permute-start | bytes 196616 | tf_op jit(solution)/shard_map/ppermute | solution.py:618
  19.0 1.6 %copy-done = bf16[32,64,512]{2,1,0:T(8,128)(2,1)S(1)} copy-done((bf16[32,64,512]{2,1,0:T(8,128)(2,1)S(1)}, bf16[32,64,512]{2,1,0:T(8,128)(2,1)}, u32[]{:S(2)}) %copy-start) | copy-done | bytes 2097176
  20.6 1.1 %prepare.1 = (bf16[256,128]{1,0:T(8,128)(2,1)S(1)}, bf16[2048,512]{1,0:T(8,128)(2,1)S(1)}, bf16[1152,384]{1,0:T(8,128)(2,1)S(1)}, bf16[1152,384]{1,0:T(8,128)(2,1)S(1)}) custom-call(bf16[32,64,512]{2,1,0:T(8,128)(2,1)S(1)} %copy-done, s32[32,512]{1,0:T(8,128)S(1)} %copy-done.6, bf16[512,128]{1,0:T(8,128)(2,1)S(1)} %copy-done.5, ...), custom_call_target="tpu_custom_call" | custom-call | flops 268435456 | bytes 2097152 | tf_op jit(solution)/shard_map/prepare/pallas_call | solution.py:128
  21.7 0.8 %collective-permute-done.3.refs_3_ = bf16[256,128]{1,0:T(8,128)(2,1)S(1)} collective-permute-done((bf16[256,128]{1,0:T(8,128)(2,1)}, bf16[256,128]{1,0:T(8,128)(2,1)S(1)}, u32[]{:S(2)}, u32[]{:S(2)}) %collective-permute-start.3) | collective-permute-done | bytes 65568 | tf_op jit(solution)/shard_map/ppermute | solution.py:618
  22.5 0.3 collective-permute-done.6.refs_7_
  22.8 0.8 %place.1 = (bf16[2048,128]{1,0:T(8,128)(2,1)S(1)}, bf16[288,128]{1,0:T(8,128)(2,1)S(1)}, bf16[288,128]{1,0:T(8,128)(2,1)S(1)}) custom-call(s32[2]{0:T(128)S(1)} %pad_add_fusion.base_ref, s32[32]{0:T(128)S(1)} %copy-done.7, bf16[256,128]{1,0:T(8,128)(2,1)S(1)} %get-tuple-element.57.refs_0_, bf16[256,128]{1,0:T(8,128)(2,1)S(1)} %collective-permute-done.1.refs_1_, ...), custom_call_target="tpu_custom_call" | custom-call | tf_op jit(solution)/shard_map/place/pallas_call | solution.py:264
  23.6 2.1 %collective-permute-start.7 = (bf16[288,128]{1,0:T(8,128)(2,1)S(1)}, bf16[288,128]{1,0:T(8,128)(2,1)S(1)}, u32[]{:S(2)}, u32[]{:S(2)}) collective-permute-start(bf16[288,128]{1,0:T(8,128)(2,1)S(1)} %get-tuple-element.66), channel_id=1, source_target_pairs={{0,1},{1,0},{2,3},{3,2},{4,5},{5,4},{6,7},{7,6},{8,9},{9,8},{10,11... | collective-permute-start | bytes 221192 | tf_op jit(solution)/shard_map/ppermute | solution.py:626
  25.7 0.7 %collective-permute-start.8 = (bf16[288,128]{1,0:T(8,128)(2,1)S(1)}, bf16[288,128]{1,0:T(8,128)(2,1)S(1)}, u32[]{:S(2)}, u32[]{:S(2)}) collective-permute-start(bf16[288,128]{1,0:T(8,128)(2,1)S(1)} %get-tuple-element.67), channel_id=1, source_target_pairs={{0,0},{1,2},{2,1},{3,4},{4,3},{5,6},{6,5},{7,7},{8,8},{9,10},{10,9... | collective-permute-start | bytes 221192 | tf_op jit(solution)/shard_map/ppermute | solution.py:626
  26.3 2.4 %inner.1.refs_3_ = bf16[11,112,128]{2,1,0:T(8,128)(2,1)S(1)} custom-call(s32[32]{0:T(128)S(1)} %copy-done.7, bf16[2048,128]{1,0:T(8,128)(2,1)S(1)} %get-tuple-element.65.block_ref.refs_0_, bf16[1152,384]{1,0:T(8,128)(2,1)S(1)} %get-tuple-element.68.wide1_ref.refs_4_.refs_8_), custom_call_target="tpu_custom_call" | custom-call | flops 1089994752 | bytes 1769472 | tf_op jit(solution)/shard_map/inner/pallas_call | solution.py:423
  28.7 0.6 %edge.1 = (bf16[288,128]{1,0:T(8,128)(2,1)S(1)}, bf16[288,128]{1,0:T(8,128)(2,1)S(1)}, bf16[368,128]{1,0:T(8,128)(2,1)S(1)}, bf16[368,128]{1,0:T(8,128)(2,1)S(1)}) custom-call(s32[2]{0:T(128)S(1)} %pad_add_fusion.base_ref, s32[32]{0:T(128)S(1)} %copy-done.7, bf16[2048,128]{1,0:T(8,128)(2,1)S(1)} %get-tuple-element.65.block_ref.refs_0_, ...), custom_call_target="tpu_custom_call" | custom-call | tf_op jit(solution)/shard_map/edge/pallas_call | solution.py:314
  29.4 0.7 %collective-permute-start.10 = (bf16[368,128]{1,0:T(8,128)(2,1)S(1)}, bf16[368,128]{1,0:T(8,128)(2,1)S(1)}, u32[]{:S(2)}, u32[]{:S(2)}) collective-permute-start(bf16[368,128]{1,0:T(8,128)(2,1)S(1)} %get-tuple-element.74), channel_id=1, source_target_pairs={{0,0},{8,16},{16,8},{24,24},{1,1},{9,17},{17,9},{25,25},{2,2},{10,... | collective-permute-start | bytes 282632 | tf_op jit(solution)/shard_map/ppermute | solution.py:626
  30.1 3.2 %middle.1 = (bf16[14,144,128]{2,1,0:T(8,128)(2,1)S(1)}, bf16[14,144,128]{2,1,0:T(8,128)(2,1)S(1)}, bf16[1024,128]{1,0:T(8,128)(2,1)S(1)}) custom-call(s32[32]{0:T(128)S(1)} %copy-done.7, bf16[2048,128]{1,0:T(8,128)(2,1)S(1)} %get-tuple-element.65.block_ref.refs_0_, bf16[288,128]{1,0:T(8,128)(2,1)S(1)} %get-tuple-element.71.refs_1_, ...), custom_call_target="tpu_custom_call" | custom-call | flops 1599602688 | bytes 1769472 | tf_op jit(solution)/shard_map/middle/pallas_call | solution.py:499
  33.4 3.2 %final.1 = (bf16[512,128]{1,0:T(8,128)(2,1)S(1)}, bf16[512,128]{1,0:T(8,128)(2,1)S(1)}, bf16[256,128]{1,0:T(8,128)(2,1)S(1)}, bf16[256,128]{1,0:T(8,128)(2,1)S(1...) custom-call(s32[2]{0:T(128)S(1)} %pad_add_fusion.base_ref, ...), custom_call_target="tpu_custom_call" | custom-call | flops 1415577600 | bytes 1769472 | tf_op jit(solution)/shard_map/final/pallas_call | solution.py:594
  36.6 5.1 %collective-permute-start.11 = (bf16[256,128]{1,0:T(8,128)(2,1)S(1)}, bf16[256,128]{1,0:T(8,128)(2,1)S(1)}, u32[]{:S(2)}, u32[]{:S(2)}) collective-permute-start(bf16[256,128]{1,0:T(8,128)(2,1)S(1)} %get-tuple-element.81), channel_id=1, source_target_pairs={{0,2},{1,3},{2,4},{3,5},{4,6},{5,7},{6,0},{7,1},{8,10},{9,11},{10,... | collective-permute-start | bytes 196616 | tf_op jit(solution)/shard_map/ppermute | solution.py:618
  41.8 1.4 %collective-permute-start.13 = (bf16[256,128]{1,0:T(8,128)(2,1)S(1)}, bf16[256,128]{1,0:T(8,128)(2,1)S(1)}, u32[]{:S(2)}, u32[]{:S(2)}) collective-permute-start(bf16[256,128]{1,0:T(8,128)(2,1)S(1)} %get-tuple-element.84), channel_id=1, source_target_pairs={{0,4},{1,5},{2,6},{3,7},{4,0},{5,1},{6,2},{7,3},{8,12},{9,13},{10,... | collective-permute-start | bytes 196616 | tf_op jit(solution)/shard_map/ppermute | solution.py:618
  43.2 3.9 %collective-permute-start.14 = (bf16[256,128]{1,0:T(8,128)(2,1)S(1)}, bf16[256,128]{1,0:T(8,128)(2,1)S(1)}, u32[]{:S(2)}, u32[]{:S(2)}) collective-permute-start(bf16[256,128]{1,0:T(8,128)(2,1)S(1)} %get-tuple-element.85), channel_id=1, source_target_pairs={{0,3},{1,4},{2,5},{3,6},{4,7},{5,0},{6,1},{7,2},{8,11},{9,12},{10,... | collective-permute-start | bytes 196616 | tf_op jit(solution)/shard_map/ppermute | solution.py:618
  47.0 0.9 %collective-permute-start.15 = (bf16[256,128]{1,0:T(8,128)(2,1)S(1)}, bf16[256,128]{1,0:T(8,128)(2,1)S(1)}, u32[]{:S(2)}, u32[]{:S(2)}) collective-permute-start(bf16[256,128]{1,0:T(8,128)(2,1)S(1)} %get-tuple-element.86), channel_id=1, source_target_pairs={{0,6},{1,7},{2,0},{3,1},{4,2},{5,3},{6,4},{7,5},{8,14},{9,15},{10,... | collective-permute-start | bytes 196616 | tf_op jit(solution)/shard_map/ppermute | solution.py:618
  48.0 0.5 collective-permute-start.12
  48.5 0.5 collective-permute-done.16.refs_1_
  49.0 0.1 collective-permute-start.17
  49.1 0.8 %pad_maximum_fusion = bf16[2048,128]{1,0:T(8,128)(2,1)} fusion(bf16[512,128]{1,0:T(8,128)(2,1)S(1)} %get-tuple-element.97, bf16[1024,128]{1,0:T(8,128)(2,1)S(1)} %get-tuple-element.96.refs_7_, bf16[512,128]{1,0:T(8,128)(2,1)S(1)} %get-tuple-element.95), kind=kLoop, calls=%fused_computation | loop fusion | flops 1572864 | bytes 1048576 | tf_op jit(solution)/shard_map/concatenate | solution.py:657
  50.0 1.1 %up.3.refs_4_ = bf16[32,64,512]{2,1,0:T(8,128)(2,1)} custom-call(bf16[32,64,512]{2,1,0:T(8,128)(2,1)S(1)} %copy-done.1, bf16[2048,512]{1,0:T(8,128)(2,1)S(1)} %get-tuple-element.56.mask_ref, bf16[128,512]{1,0:T(8,128)(2,1)S(1)} %copy-done.2, bf16[256,128]{1,0:T(8,128)(2,1)S(1)} %collective-permute-done.11.refs_0_, ...), custom_call_target="tpu_custom_call" | custom-call | flops 134217728 | bytes 2097152 | tf_op jit(solution)/shard_map/up/pallas_call | solution.py:175
  51.1 3.4 %collective-permute-done.14.refs_1_ = bf16[256,128]{1,0:T(8,128)(2,1)S(1)} collective-permute-done((bf16[256,128]{1,0:T(8,128)(2,1)S(1)}, bf16[256,128]{1,0:T(8,128)(2,1)S(1)}, u32[]{:S(2)}, u32[]{:S(2)}) %collective-permute-start.14) | collective-permute-done | bytes 65568 | tf_op jit(solution)/shard_map/ppermute | solution.py:618
  54.5 1.7 %collective-permute-done.17.refs_3_ = bf16[256,128]{1,0:T(8,128)(2,1)S(1)} collective-permute-done((bf16[256,128]{1,0:T(8,128)(2,1)S(1)}, bf16[256,128]{1,0:T(8,128)(2,1)S(1)}, u32[]{:S(2)}, u32[]{:S(2)}) %collective-permute-start.17) | collective-permute-done | bytes 65568 | tf_op jit(solution)/shard_map/ppermute | solution.py:618
  56.2 1.5 %up.4.refs_2_ = bf16[32,64,512]{2,1,0:T(8,128)(2,1)} custom-call(bf16[32,64,512]{2,1,0:T(8,128)(2,1)S(1)} %copy-done.1, bf16[2048,512]{1,0:T(8,128)(2,1)S(1)} %get-tuple-element.56.mask_ref, bf16[128,512]{1,0:T(8,128)(2,1)S(1)} %copy-done.2, bf16[256,128]{1,0:T(8,128)(2,1)S(1)} %collective-permute-done.13.refs_0_, ...), custom_call_target="tpu_custom_call", output_to_operand_aliasing={{}: (7, {})} | custom-call | flops 134217728 | bytes 2097152 | tf_op jit(solution)/shard_map/up/pallas_call | solution.py:175
  57.7 1.1 %up.5 = bf16[32,64,512]{2,1,0:T(8,128)(2,1)} custom-call(bf16[32,64,512]{2,1,0:T(8,128)(2,1)S(1)} %copy-done.1, bf16[2048,512]{1,0:T(8,128)(2,1)S(1)} %get-tuple-element.56.mask_ref, bf16[128,512]{1,0:T(8,128)(2,1)S(1)} %copy-done.2, bf16[256,128]{1,0:T(8,128)(2,1)S(1)} %get-tuple-element.80.refs_0_, ...), custom_call_target="tpu_custom_call", output_to_operand_aliasing={{}: (5, {})} | custom-call | flops 134217728 | bytes 2097152 | tf_op jit(solution)/shard_map/up/pallas_call | solution.py:175
  (32 shorter events, 0.3 us)
Async XLA Ops:
  0.6 18.4 %copy-start.5 = (bf16[512,128]{1,0:T(8,128)(2,1)S(1)}, bf16[512,128]{1,0:T(8,128)(2,1)}, u32[]{:S(2)}) copy-start(bf16[512,128]{1,0:T(8,128)(2,1)} %w_down_ref) | copy-start | bytes 393220
  0.6 18.4 %copy-start.6 = (s32[32,512]{1,0:T(8,128)S(1)}, s32[32,512]{1,0:T(8,128)}, u32[]{:S(2)}) copy-start(s32[32,512]{1,0:T(8,128)} %mask_ref) | copy-start | bytes 196612
  0.7 18.4 %copy-start.4 = (bf16[27,128,128]{2,1,0:T(8,128)(2,1)S(1)}, bf16[27,128,128]{2,1,0:T(8,128)(2,1)}, u32[]{:S(2)}) copy-start(bf16[27,128,128]{2,1,0:T(8,128)(2,1)} %w2_ref) | copy-start | bytes 2654212
  0.7 18.4 %copy-start.3 = (bf16[27,128,128]{2,1,0:T(8,128)(2,1)S(1)}, bf16[27,128,128]{2,1,0:T(8,128)(2,1)}, u32[]{:S(2)}) copy-start(bf16[27,128,128]{2,1,0:T(8,128)(2,1)} %w1_ref) | copy-start | bytes 2654212
  4.6 18.1 %copy-start.7 = (s32[32]{0:T(128)S(1)}, s32[32]{0:T(128)}, u32[]{:S(2)}) copy-start(s32[32]{0:T(128)} %source_ref.9) | copy-start | bytes 388
  4.7 11.9 %collective-permute-start = (bf16[256,128]{1,0:T(8,128)(2,1)}, bf16[256,128]{1,0:T(8,128)(2,1)S(1)}, u32[]{:S(2)}, u32[]{:S(2)}) collective-permute-start(bf16[256,128]{1,0:T(8,128)(2,1)} %get-tuple-element.50), channel_id=1, source_target_pairs={{0,5},{1,6},{2,7},{3,0},{4,1},{5,2},{6,3},{7,4},{8,13},{9,14},{10,... | collective-permute-start | bytes 196616 | tf_op jit(solution)/shard_map/ppermute | solution.py:618
  9.7 8.2 %collective-permute-start.1 = (bf16[256,128]{1,0:T(8,128)(2,1)}, bf16[256,128]{1,0:T(8,128)(2,1)S(1)}, u32[]{:S(2)}, u32[]{:S(2)}) collective-permute-start(bf16[256,128]{1,0:T(8,128)(2,1)} %get-tuple-element.58), channel_id=1, source_target_pairs={{0,1},{1,2},{2,3},{3,4},{4,5},{5,6},{6,7},{7,0},{8,9},{9,10},{10,1... | collective-permute-start | bytes 196616 | tf_op jit(solution)/shard_map/ppermute | solution.py:618
  11.2 10.5 %collective-permute-start.2 = (bf16[256,128]{1,0:T(8,128)(2,1)}, bf16[256,128]{1,0:T(8,128)(2,1)S(1)}, u32[]{:S(2)}, u32[]{:S(2)}) collective-permute-start(bf16[256,128]{1,0:T(8,128)(2,1)} %get-tuple-element.59), channel_id=1, source_target_pairs={{0,2},{1,3},{2,4},{3,5},{4,6},{5,7},{6,0},{7,1},{8,10},{9,11},{10,... | collective-permute-start | bytes 196616 | tf_op jit(solution)/shard_map/ppermute | solution.py:618
  11.3 11.3 %collective-permute-start.3 = (bf16[256,128]{1,0:T(8,128)(2,1)}, bf16[256,128]{1,0:T(8,128)(2,1)S(1)}, u32[]{:S(2)}, u32[]{:S(2)}) collective-permute-start(bf16[256,128]{1,0:T(8,128)(2,1)} %get-tuple-element.60), channel_id=1, source_target_pairs={{0,3},{1,4},{2,5},{3,6},{4,7},{5,0},{6,1},{7,2},{8,11},{9,12},{10,... | collective-permute-start | bytes 196616 | tf_op jit(solution)/shard_map/ppermute | solution.py:618
  13.0 9.5 %collective-permute-start.4 = (bf16[256,128]{1,0:T(8,128)(2,1)}, bf16[256,128]{1,0:T(8,128)(2,1)S(1)}, u32[]{:S(2)}, u32[]{:S(2)}) collective-permute-start(bf16[256,128]{1,0:T(8,128)(2,1)} %get-tuple-element.61), channel_id=1, source_target_pairs={{0,4},{1,5},{2,6},{3,7},{4,0},{5,1},{6,2},{7,3},{8,12},{9,13},{10,... | collective-permute-start | bytes 196616 | tf_op jit(solution)/shard_map/ppermute | solution.py:618
  16.5 6.0 %collective-permute-start.5 = (bf16[256,128]{1,0:T(8,128)(2,1)}, bf16[256,128]{1,0:T(8,128)(2,1)S(1)}, u32[]{:S(2)}, u32[]{:S(2)}) collective-permute-start(bf16[256,128]{1,0:T(8,128)(2,1)} %get-tuple-element.63), channel_id=1, source_target_pairs={{0,6},{1,7},{2,0},{3,1},{4,2},{5,3},{6,4},{7,5},{8,14},{9,15},{10,... | collective-permute-start | bytes 196616 | tf_op jit(solution)/shard_map/ppermute | solution.py:618
  17.9 4.9 %collective-permute-start.6 = (bf16[256,128]{1,0:T(8,128)(2,1)}, bf16[256,128]{1,0:T(8,128)(2,1)S(1)}, u32[]{:S(2)}, u32[]{:S(2)}) collective-permute-start(bf16[256,128]{1,0:T(8,128)(2,1)} %get-tuple-element.64), channel_id=1, source_target_pairs={{0,7},{1,0},{2,1},{3,2},{4,3},{5,4},{6,5},{7,6},{8,15},{9,8},{10,9... | collective-permute-start | bytes 196616 | tf_op jit(solution)/shard_map/ppermute | solution.py:618
  19.0 1.6 %copy-start = (bf16[32,64,512]{2,1,0:T(8,128)(2,1)S(1)}, bf16[32,64,512]{2,1,0:T(8,128)(2,1)}, u32[]{:S(2)}) copy-start(bf16[32,64,512]{2,1,0:T(8,128)(2,1)} %fine_ref.6) | copy-start | bytes 6291460
  23.6 5.1 %collective-permute-start.7 = (bf16[288,128]{1,0:T(8,128)(2,1)S(1)}, bf16[288,128]{1,0:T(8,128)(2,1)S(1)}, u32[]{:S(2)}, u32[]{:S(2)}) collective-permute-start(bf16[288,128]{1,0:T(8,128)(2,1)S(1)} %get-tuple-element.66), channel_id=1, source_target_pairs={{0,1},{1,0},{2,3},{3,2},{4,5},{5,4},{6,7},{7,6},{8,9},{9,8},{10,11... | collective-permute-start | bytes 221192 | tf_op jit(solution)/shard_map/ppermute | solution.py:626
  25.7 3.0 %collective-permute-start.8 = (bf16[288,128]{1,0:T(8,128)(2,1)S(1)}, bf16[288,128]{1,0:T(8,128)(2,1)S(1)}, u32[]{:S(2)}, u32[]{:S(2)}) collective-permute-start(bf16[288,128]{1,0:T(8,128)(2,1)S(1)} %get-tuple-element.67), channel_id=1, source_target_pairs={{0,0},{1,2},{2,1},{3,4},{4,3},{5,6},{6,5},{7,7},{8,8},{9,10},{10,9... | collective-permute-start | bytes 221192 | tf_op jit(solution)/shard_map/ppermute | solution.py:626
  29.4 4.0 %collective-permute-start.9 = (bf16[368,128]{1,0:T(8,128)(2,1)S(1)}, bf16[368,128]{1,0:T(8,128)(2,1)S(1)}, u32[]{:S(2)}, u32[]{:S(2)}) collective-permute-start(bf16[368,128]{1,0:T(8,128)(2,1)S(1)} %get-tuple-element.73), channel_id=1, source_target_pairs={{0,8},{8,0},{16,24},{24,16},{1,9},{9,1},{17,25},{25,17},{2,10},{10... | collective-permute-start | bytes 282632 | tf_op jit(solution)/shard_map/ppermute | solution.py:626
  29.4 3.9 %collective-permute-start.10 = (bf16[368,128]{1,0:T(8,128)(2,1)S(1)}, bf16[368,128]{1,0:T(8,128)(2,1)S(1)}, u32[]{:S(2)}, u32[]{:S(2)}) collective-permute-start(bf16[368,128]{1,0:T(8,128)(2,1)S(1)} %get-tuple-element.74), channel_id=1, source_target_pairs={{0,0},{8,16},{16,8},{24,24},{1,1},{9,17},{17,9},{25,25},{2,2},{10,... | collective-permute-start | bytes 282632 | tf_op jit(solution)/shard_map/ppermute | solution.py:626
  33.4 16.6 %copy-start.1 = (bf16[32,64,512]{2,1,0:T(8,128)(2,1)S(1)}, bf16[32,64,512]{2,1,0:T(8,128)(2,1)}, u32[]{:S(2)}) copy-start(bf16[32,64,512]{2,1,0:T(8,128)(2,1)} %fine_ref.6) | copy-start | bytes 6291460
  33.4 16.6 %copy-start.2 = (bf16[128,512]{1,0:T(8,128)(2,1)S(1)}, bf16[128,512]{1,0:T(8,128)(2,1)}, u32[]{:S(2)}) copy-start(bf16[128,512]{1,0:T(8,128)(2,1)} %w_ref.5) | copy-start | bytes 393220
  36.6 11.3 %collective-permute-start.11 = (bf16[256,128]{1,0:T(8,128)(2,1)S(1)}, bf16[256,128]{1,0:T(8,128)(2,1)S(1)}, u32[]{:S(2)}, u32[]{:S(2)}) collective-permute-start(bf16[256,128]{1,0:T(8,128)(2,1)S(1)} %get-tuple-element.81), channel_id=1, source_target_pairs={{0,2},{1,3},{2,4},{3,5},{4,6},{5,7},{6,0},{7,1},{8,10},{9,11},{10,... | collective-permute-start | bytes 196616 | tf_op jit(solution)/shard_map/ppermute | solution.py:618
  41.7 7.2 %collective-permute-start.16 = (bf16[256,128]{1,0:T(8,128)(2,1)S(1)}, bf16[256,128]{1,0:T(8,128)(2,1)S(1)}, u32[]{:S(2)}, u32[]{:S(2)}) collective-permute-start(bf16[256,128]{1,0:T(8,128)(2,1)S(1)} %get-tuple-element.87), channel_id=1, source_target_pairs={{0,1},{1,2},{2,3},{3,4},{4,5},{5,6},{6,7},{7,0},{8,9},{9,10},{10,1... | collective-permute-start | bytes 196616 | tf_op jit(solution)/shard_map/ppermute | solution.py:618
  41.8 9.3 %collective-permute-start.13 = (bf16[256,128]{1,0:T(8,128)(2,1)S(1)}, bf16[256,128]{1,0:T(8,128)(2,1)S(1)}, u32[]{:S(2)}, u32[]{:S(2)}) collective-permute-start(bf16[256,128]{1,0:T(8,128)(2,1)S(1)} %get-tuple-element.84), channel_id=1, source_target_pairs={{0,4},{1,5},{2,6},{3,7},{4,0},{5,1},{6,2},{7,3},{8,12},{9,13},{10,... | collective-permute-start | bytes 196616 | tf_op jit(solution)/shard_map/ppermute | solution.py:618
  43.2 11.4 %collective-permute-start.14 = (bf16[256,128]{1,0:T(8,128)(2,1)S(1)}, bf16[256,128]{1,0:T(8,128)(2,1)S(1)}, u32[]{:S(2)}, u32[]{:S(2)}) collective-permute-start(bf16[256,128]{1,0:T(8,128)(2,1)S(1)} %get-tuple-element.85), channel_id=1, source_target_pairs={{0,3},{1,4},{2,5},{3,6},{4,7},{5,0},{6,1},{7,2},{8,11},{9,12},{10,... | collective-permute-start | bytes 196616 | tf_op jit(solution)/shard_map/ppermute | solution.py:618
  47.0 7.5 %collective-permute-start.15 = (bf16[256,128]{1,0:T(8,128)(2,1)S(1)}, bf16[256,128]{1,0:T(8,128)(2,1)S(1)}, u32[]{:S(2)}, u32[]{:S(2)}) collective-permute-start(bf16[256,128]{1,0:T(8,128)(2,1)S(1)} %get-tuple-element.86), channel_id=1, source_target_pairs={{0,6},{1,7},{2,0},{3,1},{4,2},{5,3},{6,4},{7,5},{8,14},{9,15},{10,... | collective-permute-start | bytes 196616 | tf_op jit(solution)/shard_map/ppermute | solution.py:618
  48.0 9.8 %collective-permute-start.12 = (bf16[256,128]{1,0:T(8,128)(2,1)S(1)}, bf16[256,128]{1,0:T(8,128)(2,1)S(1)}, u32[]{:S(2)}, u32[]{:S(2)}) collective-permute-start(bf16[256,128]{1,0:T(8,128)(2,1)S(1)} %get-tuple-element.83), channel_id=1, source_target_pairs={{0,7},{1,0},{2,1},{3,2},{4,3},{5,4},{6,5},{7,6},{8,15},{9,8},{10,9... | collective-permute-start | bytes 196616 | tf_op jit(solution)/shard_map/ppermute | solution.py:618
  49.0 7.3 %collective-permute-start.17 = (bf16[256,128]{1,0:T(8,128)(2,1)S(1)}, bf16[256,128]{1,0:T(8,128)(2,1)S(1)}, u32[]{:S(2)}, u32[]{:S(2)}) collective-permute-start(bf16[256,128]{1,0:T(8,128)(2,1)S(1)} %get-tuple-element.89), channel_id=1, source_target_pairs={{0,5},{1,6},{2,7},{3,0},{4,1},{5,2},{6,3},{7,4},{8,13},{9,14},{10,... | collective-permute-start | bytes 196616 | tf_op jit(solution)/shard_map/ppermute | solution.py:618

commit v15 on v13

--- a/solution.py
+++ b/solution.py
@@ -17,7 +17,7 @@
 EARLY = ((1, 3), (4, 4), (8, 4))
 LATE = ((12, 3),)
 LATE_PLANES = 3
-SENT = (4, 3, 5, 2, 6, 1, 7)
+SENT = (2, 1, 4, 3, 6, 5, 7)
 RETURNED = (6, 7, 4, 5, 2, 3, 1)
 DOWN_LIMIT = 62 * 1024 * 1024
 VMEM_LIMIT = 24 * 1024 * 1024
@@ -217,8 +217,8 @@
 
 def place_kernel(base_ref, source_ref, *refs):
     block_ref, even_ref, odd_ref, low_ref, high_ref, arrived = refs[K:]
-    for j in range(K):
-        arrived[j * CAP * CELLS : (j + 1) * CAP * CELLS] = refs[j][...]
+    for k, j in enumerate(SENT + (0,)):
+        arrived[j * CAP * CELLS : (j + 1) * CAP * CELLS] = refs[k][...]
     half = low_half((8, 8, 128))
     for depth_brick in range(4):
         for row_brick in range(4):
@@ -632,11 +632,11 @@
     counts = (lax.axis_size("gz"), lax.axis_size("xy"))
     sent = down_call(fine, fine_mask, w_down, SENT)
     arrived = {j: from_behind(sent[j], "xy", j) for j in SENT}
-    later = (arrived[SENT[2]], fine, fine_mask, w_down, w_first, w_second)
-    arrived[SENT[2]], *later = lax.optimization_barrier(later)
+    later = (arrived[SENT[0]], fine, fine_mask, w_down, w_first, w_second)
+    arrived[SENT[0]], *later = lax.optimization_barrier(later)
     prepared = lax.optimization_barrier(tuple(prepare_call(*later)))
     arrived[0], mask, wide1, wide2 = prepared
-    block, even, odd = place_call(base, slot_source, [arrived[j] for j in range(K)])
+    block, even, odd = place_call(base, slot_source, [arrived[j] for j in SENT + (0,)])
     even = swap_face(even, "xy", 0)
     odd = swap_face(odd, "xy", 1)
     early = inner_call(slot_source, block, wide1, EARLY)

time: 59 us -> 60.1 us (1.019)
  starting transfers between devices: 30.7 us -> 31.6 us
    ppermute x14, starting transfers between devices: 27.2 us -> 28.7 us  [from_behind(): return lax.ppermute(value, axis, pairs)]
    ppermute x4, starting transfers between devices: 3.49 us -> 2.87 us  [swap_face(): return lax.ppermute(face, axis, list(enumerate(partner)))]
where the time goes in v15:
time: 60.1 us; the launch traced here: 59.7 us
  starting transfers between devices  31.6 us (53%)
  Pallas kernels  18.7 us (31%)
  waiting for transfers between devices  6.09 us (10%)
  local copies, waits for them, and re-layouts  1.62 us (3%)
  other arithmetic  0.9 us (1%)
  between operations  0.83 us (1%)
    ppermute x14, starting transfers between devices, from_behind(): return lax.ppermute(value, axis, pairs)  28.7 us
    ppermute x14, waiting for transfers between devices, from_behind(): return lax.ppermute(value, axis, pairs)  6.08 us
    pallas_call x1, Pallas kernels, down_call(): pl.pallas_call(functools.partial(down_kernel, offsets), in_specs=[hbm, hb...  3.96 us
    pallas_call x2, Pallas kernels, up_call(): pl.pallas_call(functools.partial(up_kernel, count), grid=(count * CAP //...  3.4 us
    pallas_call x1, Pallas kernels, middle_call(): pl.pallas_call(middle_kernel, in_specs=[smem] + [vmem] * 6, out_specs=[vm...  3.23 us
    pallas_call x1, Pallas kernels, final_call(): pl.pallas_call(functools.partial(final_kernel, count), in_specs=[smem, sm...  3.21 us
    ppermute x4, starting transfers between devices, swap_face(): return lax.ppermute(face, axis, list(enumerate(partner)))  2.87 us
    pallas_call x1, Pallas kernels, inner_call(): pl.pallas_call(functools.partial(inner_kernel, groups), in_specs=[smem, v...  2.37 us
  transfers between devices with their start and end apart: 18, of which 6 were waited for; matrix products, arithmetic and copies ran while one was open for 2% of the time, Pallas kernels for 13%

profile of v15, /device:TPU:0, one launch (start us, length us, event | category | flops | bytes accessed | tf_op | source)
XLA Modules:
  0.0 59.7 jit_solution(69874792067010954)
XLA Ops:
  0.7 4.0 %down.1 = (bf16[256,128]{1,0:T(8,128)(2,1)}, bf16[256,128]{1,0:T(8,128)(2,1)}, bf16[256,128]{1,0:T(8,128)(2,1)}, bf16[256,128]{1,0:T(8,128)(2,1)}, bf16[256,128]...) custom-call(bf16[32,64,512]{2,1,0:T(8,128)(2,1)} %fine_ref.4, s32[32,512]{1,0:T(8,128)} %mask_ref, ...), custom_call_target="tpu_custom_call" | custom-call | flops 234881024 | bytes 1835008 | tf_op jit(solution)/shard_map/down/pallas_call | solution.py:85
  4.7 3.1 %collective-permute-start = (bf16[256,128]{1,0:T(8,128)(2,1)}, bf16[256,128]{1,0:T(8,128)(2,1)S(1)}, u32[]{:S(2)}, u32[]{:S(2)}) collective-permute-start(bf16[256,128]{1,0:T(8,128)(2,1)} %get-tuple-element.50), channel_id=1, source_target_pairs={{0,2},{1,3},{2,4},{3,5},{4,6},{5,7},{6,0},{7,1},{8,10},{9,11},{10,... | collective-permute-start | bytes 196616 | tf_op jit(solution)/shard_map/ppermute | solution.py:618
  7.7 1.5 %collective-permute-start.1 = (bf16[256,128]{1,0:T(8,128)(2,1)}, bf16[256,128]{1,0:T(8,128)(2,1)S(1)}, u32[]{:S(2)}, u32[]{:S(2)}) collective-permute-start(bf16[256,128]{1,0:T(8,128)(2,1)} %get-tuple-element.58), channel_id=1, source_target_pairs={{0,1},{1,2},{2,3},{3,4},{4,5},{5,6},{6,7},{7,0},{8,9},{9,10},{10,1... | collective-permute-start | bytes 196616 | tf_op jit(solution)/shard_map/ppermute | solution.py:618
  9.2 2.6 %collective-permute-start.2 = (bf16[256,128]{1,0:T(8,128)(2,1)}, bf16[256,128]{1,0:T(8,128)(2,1)S(1)}, u32[]{:S(2)}, u32[]{:S(2)}) collective-permute-start(bf16[256,128]{1,0:T(8,128)(2,1)} %get-tuple-element.59), channel_id=1, source_target_pairs={{0,4},{1,5},{2,6},{3,7},{4,0},{5,1},{6,2},{7,3},{8,12},{9,13},{10,... | collective-permute-start | bytes 196616 | tf_op jit(solution)/shard_map/ppermute | solution.py:618
  11.8 1.2 %collective-permute-start.3 = (bf16[256,128]{1,0:T(8,128)(2,1)}, bf16[256,128]{1,0:T(8,128)(2,1)S(1)}, u32[]{:S(2)}, u32[]{:S(2)}) collective-permute-start(bf16[256,128]{1,0:T(8,128)(2,1)} %get-tuple-element.60), channel_id=1, source_target_pairs={{0,3},{1,4},{2,5},{3,6},{4,7},{5,0},{6,1},{7,2},{8,11},{9,12},{10,... | collective-permute-start | bytes 196616 | tf_op jit(solution)/shard_map/ppermute | solution.py:618
  13.0 2.1 %collective-permute-start.4 = (bf16[256,128]{1,0:T(8,128)(2,1)}, bf16[256,128]{1,0:T(8,128)(2,1)S(1)}, u32[]{:S(2)}, u32[]{:S(2)}) collective-permute-start(bf16[256,128]{1,0:T(8,128)(2,1)} %get-tuple-element.61), channel_id=1, source_target_pairs={{0,6},{1,7},{2,0},{3,1},{4,2},{5,3},{6,4},{7,5},{8,14},{9,15},{10,... | collective-permute-start | bytes 196616 | tf_op jit(solution)/shard_map/ppermute | solution.py:618
  15.1 1.0 %collective-permute-start.5 = (bf16[256,128]{1,0:T(8,128)(2,1)}, bf16[256,128]{1,0:T(8,128)(2,1)S(1)}, u32[]{:S(2)}, u32[]{:S(2)}) collective-permute-start(bf16[256,128]{1,0:T(8,128)(2,1)} %get-tuple-element.62), channel_id=1, source_target_pairs={{0,5},{1,6},{2,7},{3,0},{4,1},{5,2},{6,3},{7,4},{8,13},{9,14},{10,... | collective-permute-start | bytes 196616 | tf_op jit(solution)/shard_map/ppermute | solution.py:618
  16.1 1.4 %collective-permute-start.6 = (bf16[256,128]{1,0:T(8,128)(2,1)}, bf16[256,128]{1,0:T(8,128)(2,1)S(1)}, u32[]{:S(2)}, u32[]{:S(2)}) collective-permute-start(bf16[256,128]{1,0:T(8,128)(2,1)} %get-tuple-element.63), channel_id=1, source_target_pairs={{0,7},{1,0},{2,1},{3,2},{4,3},{5,4},{6,5},{7,6},{8,15},{9,8},{10,9... | collective-permute-start | bytes 196616 | tf_op jit(solution)/shard_map/ppermute | solution.py:618
  17.6 1.6 %copy-done = bf16[32,64,512]{2,1,0:T(8,128)(2,1)S(1)} copy-done((bf16[32,64,512]{2,1,0:T(8,128)(2,1)S(1)}, bf16[32,64,512]{2,1,0:T(8,128)(2,1)}, u32[]{:S(2)}) %copy-start) | copy-done | bytes 2097176
  19.2 1.1 %prepare.1 = (bf16[256,128]{1,0:T(8,128)(2,1)S(1)}, bf16[2048,512]{1,0:T(8,128)(2,1)S(1)}, bf16[1152,384]{1,0:T(8,128)(2,1)S(1)}, bf16[1152,384]{1,0:T(8,128)(2,1)S(1)}) custom-call(bf16[32,64,512]{2,1,0:T(8,128)(2,1)S(1)} %copy-done, s32[32,512]{1,0:T(8,128)S(1)} %copy-done.6, bf16[512,128]{1,0:T(8,128)(2,1)S(1)} %copy-done.5, ...), custom_call_target="tpu_custom_call" | custom-call | flops 268435456 | bytes 2097152 | tf_op jit(solution)/shard_map/prepare/pallas_call | solution.py:128
  20.6 1.0 %collective-permute-done.5.refs_5_ = bf16[256,128]{1,0:T(8,128)(2,1)S(1)} collective-permute-done((bf16[256,128]{1,0:T(8,128)(2,1)}, bf16[256,128]{1,0:T(8,128)(2,1)S(1)}, u32[]{:S(2)}, u32[]{:S(2)}) %collective-permute-start.5) | collective-permute-done | bytes 65568 | tf_op jit(solution)/shard_map/ppermute | solution.py:618
  21.6 0.6 %collective-permute-done.6.refs_6_ = bf16[256,128]{1,0:T(8,128)(2,1)S(1)} collective-permute-done((bf16[256,128]{1,0:T(8,128)(2,1)}, bf16[256,128]{1,0:T(8,128)(2,1)S(1)}, u32[]{:S(2)}, u32[]{:S(2)}) %collective-permute-start.6) | collective-permute-done | bytes 65568 | tf_op jit(solution)/shard_map/ppermute | solution.py:618
  22.2 0.8 %place.1 = (bf16[2048,128]{1,0:T(8,128)(2,1)S(1)}, bf16[288,128]{1,0:T(8,128)(2,1)S(1)}, bf16[288,128]{1,0:T(8,128)(2,1)S(1)}) custom-call(s32[2]{0:T(128)S(1)} %pad_add_fusion.base_ref, s32[32]{0:T(128)S(1)} %copy-done.7, bf16[256,128]{1,0:T(8,128)(2,1)S(1)} %collective-permute-done.refs_0_, bf16[256,128]{1,0:T(8,128)(2,1)S(1)} %collective-permute-done.1.refs_1_, ...), custom_call_target="tpu_custom_call" | custom-call | tf_op jit(solution)/shard_map/place/pallas_call | solution.py:264
  23.0 1.5 %collective-permute-start.7 = (bf16[288,128]{1,0:T(8,128)(2,1)S(1)}, bf16[288,128]{1,0:T(8,128)(2,1)S(1)}, u32[]{:S(2)}, u32[]{:S(2)}) collective-permute-start(bf16[288,128]{1,0:T(8,128)(2,1)S(1)} %get-tuple-element.66), channel_id=1, source_target_pairs={{0,1},{1,0},{2,3},{3,2},{4,5},{5,4},{6,7},{7,6},{8,9},{9,8},{10,11... | collective-permute-start | bytes 221192 | tf_op jit(solution)/shard_map/ppermute | solution.py:626
  24.5 0.7 %collective-permute-start.8 = (bf16[288,128]{1,0:T(8,128)(2,1)S(1)}, bf16[288,128]{1,0:T(8,128)(2,1)S(1)}, u32[]{:S(2)}, u32[]{:S(2)}) collective-permute-start(bf16[288,128]{1,0:T(8,128)(2,1)S(1)} %get-tuple-element.67), channel_id=1, source_target_pairs={{0,0},{1,2},{2,1},{3,4},{4,3},{5,6},{6,5},{7,7},{8,8},{9,10},{10,9... | collective-permute-start | bytes 221192 | tf_op jit(solution)/shard_map/ppermute | solution.py:626
  25.1 2.4 %inner.1.refs_3_ = bf16[11,112,128]{2,1,0:T(8,128)(2,1)S(1)} custom-call(s32[32]{0:T(128)S(1)} %copy-done.7, bf16[2048,128]{1,0:T(8,128)(2,1)S(1)} %get-tuple-element.65.block_ref.refs_0_, bf16[1152,384]{1,0:T(8,128)(2,1)S(1)} %get-tuple-element.68.wide1_ref.refs_4_.refs_8_), custom_call_target="tpu_custom_call" | custom-call | flops 1089994752 | bytes 1769472 | tf_op jit(solution)/shard_map/inner/pallas_call | solution.py:423
  27.5 0.6 %edge.1 = (bf16[288,128]{1,0:T(8,128)(2,1)S(1)}, bf16[288,128]{1,0:T(8,128)(2,1)S(1)}, bf16[368,128]{1,0:T(8,128)(2,1)S(1)}, bf16[368,128]{1,0:T(8,128)(2,1)S(1)}) custom-call(s32[2]{0:T(128)S(1)} %pad_add_fusion.base_ref, s32[32]{0:T(128)S(1)} %copy-done.7, bf16[2048,128]{1,0:T(8,128)(2,1)S(1)} %get-tuple-element.65.block_ref.refs_0_, ...), custom_call_target="tpu_custom_call" | custom-call | tf_op jit(solution)/shard_map/edge/pallas_call | solution.py:314
  28.2 0.7 %collective-permute-start.10 = (bf16[368,128]{1,0:T(8,128)(2,1)S(1)}, bf16[368,128]{1,0:T(8,128)(2,1)S(1)}, u32[]{:S(2)}, u32[]{:S(2)}) collective-permute-start(bf16[368,128]{1,0:T(8,128)(2,1)S(1)} %get-tuple-element.74), channel_id=1, source_target_pairs={{0,0},{8,16},{16,8},{24,24},{1,1},{9,17},{17,9},{25,25},{2,2},{10,... | collective-permute-start | bytes 282632 | tf_op jit(solution)/shard_map/ppermute | solution.py:626
  28.9 3.2 %middle.1 = (bf16[14,144,128]{2,1,0:T(8,128)(2,1)S(1)}, bf16[14,144,128]{2,1,0:T(8,128)(2,1)S(1)}, bf16[1024,128]{1,0:T(8,128)(2,1)S(1)}) custom-call(s32[32]{0:T(128)S(1)} %copy-done.7, bf16[2048,128]{1,0:T(8,128)(2,1)S(1)} %get-tuple-element.65.block_ref.refs_0_, bf16[288,128]{1,0:T(8,128)(2,1)S(1)} %get-tuple-element.71.refs_1_, ...), custom_call_target="tpu_custom_call" | custom-call | flops 1599602688 | bytes 1769472 | tf_op jit(solution)/shard_map/middle/pallas_call | solution.py:499
  32.2 3.2 %final.1 = (bf16[512,128]{1,0:T(8,128)(2,1)S(1)}, bf16[512,128]{1,0:T(8,128)(2,1)S(1)}, bf16[256,128]{1,0:T(8,128)(2,1)S(1)}, bf16[256,128]{1,0:T(8,128)(2,1)S(1...) custom-call(s32[2]{0:T(128)S(1)} %pad_add_fusion.base_ref, ...), custom_call_target="tpu_custom_call" | custom-call | flops 1415577600 | bytes 1769472 | tf_op jit(solution)/shard_map/final/pallas_call | solution.py:594
  35.4 6.4 %collective-permute-start.14 = (bf16[256,128]{1,0:T(8,128)(2,1)S(1)}, bf16[256,128]{1,0:T(8,128)(2,1)S(1)}, u32[]{:S(2)}, u32[]{:S(2)}) collective-permute-start(bf16[256,128]{1,0:T(8,128)(2,1)S(1)} %get-tuple-element.83), channel_id=1, source_target_pairs={{0,2},{1,3},{2,4},{3,5},{4,6},{5,7},{6,0},{7,1},{8,10},{9,11},{10,... | collective-permute-start | bytes 196616 | tf_op jit(solution)/shard_map/ppermute | solution.py:618
  41.8 2.8 %collective-permute-start.11 = (bf16[256,128]{1,0:T(8,128)(2,1)S(1)}, bf16[256,128]{1,0:T(8,128)(2,1)S(1)}, u32[]{:S(2)}, u32[]{:S(2)}) collective-permute-start(bf16[256,128]{1,0:T(8,128)(2,1)S(1)} %get-tuple-element.80), channel_id=1, source_target_pairs={{0,4},{1,5},{2,6},{3,7},{4,0},{5,1},{6,2},{7,3},{8,12},{9,13},{10,... | collective-permute-start | bytes 196616 | tf_op jit(solution)/shard_map/ppermute | solution.py:618
  44.6 2.5 %collective-permute-start.12 = (bf16[256,128]{1,0:T(8,128)(2,1)S(1)}, bf16[256,128]{1,0:T(8,128)(2,1)S(1)}, u32[]{:S(2)}, u32[]{:S(2)}) collective-permute-start(bf16[256,128]{1,0:T(8,128)(2,1)S(1)} %get-tuple-element.81), channel_id=1, source_target_pairs={{0,3},{1,4},{2,5},{3,6},{4,7},{5,0},{6,1},{7,2},{8,11},{9,12},{10,... | collective-permute-start | bytes 196616 | tf_op jit(solution)/shard_map/ppermute | solution.py:618
  47.1 0.9 %collective-permute-start.13 = (bf16[256,128]{1,0:T(8,128)(2,1)S(1)}, bf16[256,128]{1,0:T(8,128)(2,1)S(1)}, u32[]{:S(2)}, u32[]{:S(2)}) collective-permute-start(bf16[256,128]{1,0:T(8,128)(2,1)S(1)} %get-tuple-element.82), channel_id=1, source_target_pairs={{0,6},{1,7},{2,0},{3,1},{4,2},{5,3},{6,4},{7,5},{8,14},{9,15},{10,... | collective-permute-start | bytes 196616 | tf_op jit(solution)/shard_map/ppermute | solution.py:618
  47.9 2.4 %collective-permute-start.15 = (bf16[256,128]{1,0:T(8,128)(2,1)S(1)}, bf16[256,128]{1,0:T(8,128)(2,1)S(1)}, u32[]{:S(2)}, u32[]{:S(2)}) collective-permute-start(bf16[256,128]{1,0:T(8,128)(2,1)S(1)} %get-tuple-element.85), channel_id=1, source_target_pairs={{0,5},{1,6},{2,7},{3,0},{4,1},{5,2},{6,3},{7,4},{8,13},{9,14},{10,... | collective-permute-start | bytes 196616 | tf_op jit(solution)/shard_map/ppermute | solution.py:618
  50.4 0.9 %collective-permute-start.17 = (bf16[256,128]{1,0:T(8,128)(2,1)S(1)}, bf16[256,128]{1,0:T(8,128)(2,1)S(1)}, u32[]{:S(2)}, u32[]{:S(2)}) collective-permute-start(bf16[256,128]{1,0:T(8,128)(2,1)S(1)} %get-tuple-element.89), channel_id=1, source_target_pairs={{0,7},{1,0},{2,1},{3,2},{4,3},{5,4},{6,5},{7,6},{8,15},{9,8},{10,9... | collective-permute-start | bytes 196616 | tf_op jit(solution)/shard_map/ppermute | solution.py:618
  51.3 0.8 %pad_maximum_fusion = bf16[2048,128]{1,0:T(8,128)(2,1)} fusion(bf16[512,128]{1,0:T(8,128)(2,1)S(1)} %get-tuple-element.97, bf16[1024,128]{1,0:T(8,128)(2,1)S(1)} %get-tuple-element.96.refs_7_, bf16[512,128]{1,0:T(8,128)(2,1)S(1)} %get-tuple-element.95), kind=kLoop, calls=%fused_computation | loop fusion | flops 1572864 | bytes 1048576 | tf_op jit(solution)/shard_map/concatenate | solution.py:657
  52.1 1.1 %up.2.refs_6_ = bf16[32,64,512]{2,1,0:T(8,128)(2,1)} custom-call(bf16[32,64,512]{2,1,0:T(8,128)(2,1)S(1)} %copy-done.1, bf16[2048,512]{1,0:T(8,128)(2,1)S(1)} %get-tuple-element.56.mask_ref, bf16[128,512]{1,0:T(8,128)(2,1)S(1)} %copy-done.4, bf16[256,128]{1,0:T(8,128)(2,1)S(1)} %collective-permute-done.14.refs_0_, ...), custom_call_target="tpu_custom_call" | custom-call | flops 134217728 | bytes 2097152 | tf_op jit(solution)/shard_map/up/pallas_call | solution.py:175
  53.2 1.8 %collective-permute-done.12.refs_1_ = bf16[256,128]{1,0:T(8,128)(2,1)S(1)} collective-permute-done((bf16[256,128]{1,0:T(8,128)(2,1)S(1)}, bf16[256,128]{1,0:T(8,128)(2,1)S(1)}, u32[]{:S(2)}, u32[]{:S(2)}) %collective-permute-start.12) | collective-permute-done | bytes 65568 | tf_op jit(solution)/shard_map/ppermute | solution.py:618
  55.0 1.0 %collective-permute-done.15.refs_3_ = bf16[256,128]{1,0:T(8,128)(2,1)S(1)} collective-permute-done((bf16[256,128]{1,0:T(8,128)(2,1)S(1)}, bf16[256,128]{1,0:T(8,128)(2,1)S(1)}, u32[]{:S(2)}, u32[]{:S(2)}) %collective-permute-start.15) | collective-permute-done | bytes 65568 | tf_op jit(solution)/shard_map/ppermute | solution.py:618
  56.0 1.4 %collective-permute-done.17.refs_5_ = bf16[256,128]{1,0:T(8,128)(2,1)S(1)} collective-permute-done((bf16[256,128]{1,0:T(8,128)(2,1)S(1)}, bf16[256,128]{1,0:T(8,128)(2,1)S(1)}, u32[]{:S(2)}, u32[]{:S(2)}) %collective-permute-start.17) | collective-permute-done | bytes 65568 | tf_op jit(solution)/shard_map/ppermute | solution.py:618
  57.4 2.3 %up.3 = bf16[32,64,512]{2,1,0:T(8,128)(2,1)} custom-call(bf16[32,64,512]{2,1,0:T(8,128)(2,1)S(1)} %copy-done.1, bf16[2048,512]{1,0:T(8,128)(2,1)S(1)} %get-tuple-element.56.mask_ref, bf16[128,512]{1,0:T(8,128)(2,1)S(1)} %copy-done.4, bf16[256,128]{1,0:T(8,128)(2,1)S(1)} %collective-permute-done.11.refs_0_, ...), custom_call_target="tpu_custom_call", output_to_operand_aliasing={{}: (9, {})} | custom-call | flops 134217728 | bytes 2097152 | tf_op jit(solution)/shard_map/up/pallas_call | solution.py:175
  (31 shorter events, 0.6 us)
Async XLA Ops:
  0.6 17.0 %copy-start.5 = (bf16[512,128]{1,0:T(8,128)(2,1)S(1)}, bf16[512,128]{1,0:T(8,128)(2,1)}, u32[]{:S(2)}) copy-start(bf16[512,128]{1,0:T(8,128)(2,1)} %w_down_ref) | copy-start | bytes 393220
  0.6 17.0 %copy-start.6 = (s32[32,512]{1,0:T(8,128)S(1)}, s32[32,512]{1,0:T(8,128)}, u32[]{:S(2)}) copy-start(s32[32,512]{1,0:T(8,128)} %mask_ref) | copy-start | bytes 196612
  0.7 17.0 %copy-start.3 = (bf16[27,128,128]{2,1,0:T(8,128)(2,1)S(1)}, bf16[27,128,128]{2,1,0:T(8,128)(2,1)}, u32[]{:S(2)}) copy-start(bf16[27,128,128]{2,1,0:T(8,128)(2,1)} %w2_ref) | copy-start | bytes 2654212
  0.7 17.0 %copy-start.2 = (bf16[27,128,128]{2,1,0:T(8,128)(2,1)S(1)}, bf16[27,128,128]{2,1,0:T(8,128)(2,1)}, u32[]{:S(2)}) copy-start(bf16[27,128,128]{2,1,0:T(8,128)(2,1)} %w1_ref) | copy-start | bytes 2654212
  4.6 17.6 %copy-start.7 = (s32[32]{0:T(128)S(1)}, s32[32]{0:T(128)}, u32[]{:S(2)}) copy-start(s32[32]{0:T(128)} %source_ref.9) | copy-start | bytes 388
  4.7 10.5 %collective-permute-start = (bf16[256,128]{1,0:T(8,128)(2,1)}, bf16[256,128]{1,0:T(8,128)(2,1)S(1)}, u32[]{:S(2)}, u32[]{:S(2)}) collective-permute-start(bf16[256,128]{1,0:T(8,128)(2,1)} %get-tuple-element.50), channel_id=1, source_target_pairs={{0,2},{1,3},{2,4},{3,5},{4,6},{5,7},{6,0},{7,1},{8,10},{9,11},{10,... | collective-permute-start | bytes 196616 | tf_op jit(solution)/shard_map/ppermute | solution.py:618
  7.7 8.4 %collective-permute-start.1 = (bf16[256,128]{1,0:T(8,128)(2,1)}, bf16[256,128]{1,0:T(8,128)(2,1)S(1)}, u32[]{:S(2)}, u32[]{:S(2)}) collective-permute-start(bf16[256,128]{1,0:T(8,128)(2,1)} %get-tuple-element.58), channel_id=1, source_target_pairs={{0,1},{1,2},{2,3},{3,4},{4,5},{5,6},{6,7},{7,0},{8,9},{9,10},{10,1... | collective-permute-start | bytes 196616 | tf_op jit(solution)/shard_map/ppermute | solution.py:618
  9.2 11.1 %collective-permute-start.2 = (bf16[256,128]{1,0:T(8,128)(2,1)}, bf16[256,128]{1,0:T(8,128)(2,1)S(1)}, u32[]{:S(2)}, u32[]{:S(2)}) collective-permute-start(bf16[256,128]{1,0:T(8,128)(2,1)} %get-tuple-element.59), channel_id=1, source_target_pairs={{0,4},{1,5},{2,6},{3,7},{4,0},{5,1},{6,2},{7,3},{8,12},{9,13},{10,... | collective-permute-start | bytes 196616 | tf_op jit(solution)/shard_map/ppermute | solution.py:618
  11.8 8.8 %collective-permute-start.3 = (bf16[256,128]{1,0:T(8,128)(2,1)}, bf16[256,128]{1,0:T(8,128)(2,1)S(1)}, u32[]{:S(2)}, u32[]{:S(2)}) collective-permute-start(bf16[256,128]{1,0:T(8,128)(2,1)} %get-tuple-element.60), channel_id=1, source_target_pairs={{0,3},{1,4},{2,5},{3,6},{4,7},{5,0},{6,1},{7,2},{8,11},{9,12},{10,... | collective-permute-start | bytes 196616 | tf_op jit(solution)/shard_map/ppermute | solution.py:618
  13.0 7.6 %collective-permute-start.4 = (bf16[256,128]{1,0:T(8,128)(2,1)}, bf16[256,128]{1,0:T(8,128)(2,1)S(1)}, u32[]{:S(2)}, u32[]{:S(2)}) collective-permute-start(bf16[256,128]{1,0:T(8,128)(2,1)} %get-tuple-element.61), channel_id=1, source_target_pairs={{0,6},{1,7},{2,0},{3,1},{4,2},{5,3},{6,4},{7,5},{8,14},{9,15},{10,... | collective-permute-start | bytes 196616 | tf_op jit(solution)/shard_map/ppermute | solution.py:618
  15.1 6.5 %collective-permute-start.5 = (bf16[256,128]{1,0:T(8,128)(2,1)}, bf16[256,128]{1,0:T(8,128)(2,1)S(1)}, u32[]{:S(2)}, u32[]{:S(2)}) collective-permute-start(bf16[256,128]{1,0:T(8,128)(2,1)} %get-tuple-element.62), channel_id=1, source_target_pairs={{0,5},{1,6},{2,7},{3,0},{4,1},{5,2},{6,3},{7,4},{8,13},{9,14},{10,... | collective-permute-start | bytes 196616 | tf_op jit(solution)/shard_map/ppermute | solution.py:618
  16.1 6.1 %collective-permute-start.6 = (bf16[256,128]{1,0:T(8,128)(2,1)}, bf16[256,128]{1,0:T(8,128)(2,1)S(1)}, u32[]{:S(2)}, u32[]{:S(2)}) collective-permute-start(bf16[256,128]{1,0:T(8,128)(2,1)} %get-tuple-element.63), channel_id=1, source_target_pairs={{0,7},{1,0},{2,1},{3,2},{4,3},{5,4},{6,5},{7,6},{8,15},{9,8},{10,9... | collective-permute-start | bytes 196616 | tf_op jit(solution)/shard_map/ppermute | solution.py:618
  17.6 1.6 %copy-start = (bf16[32,64,512]{2,1,0:T(8,128)(2,1)S(1)}, bf16[32,64,512]{2,1,0:T(8,128)(2,1)}, u32[]{:S(2)}) copy-start(bf16[32,64,512]{2,1,0:T(8,128)(2,1)} %fine_ref.4) | copy-start | bytes 6291460
  23.0 4.5 %collective-permute-start.7 = (bf16[288,128]{1,0:T(8,128)(2,1)S(1)}, bf16[288,128]{1,0:T(8,128)(2,1)S(1)}, u32[]{:S(2)}, u32[]{:S(2)}) collective-permute-start(bf16[288,128]{1,0:T(8,128)(2,1)S(1)} %get-tuple-element.66), channel_id=1, source_target_pairs={{0,1},{1,0},{2,3},{3,2},{4,5},{5,4},{6,7},{7,6},{8,9},{9,8},{10,11... | collective-permute-start | bytes 221192 | tf_op jit(solution)/shard_map/ppermute | solution.py:626
  24.5 3.0 %collective-permute-start.8 = (bf16[288,128]{1,0:T(8,128)(2,1)S(1)}, bf16[288,128]{1,0:T(8,128)(2,1)S(1)}, u32[]{:S(2)}, u32[]{:S(2)}) collective-permute-start(bf16[288,128]{1,0:T(8,128)(2,1)S(1)} %get-tuple-element.67), channel_id=1, source_target_pairs={{0,0},{1,2},{2,1},{3,4},{4,3},{5,6},{6,5},{7,7},{8,8},{9,10},{10,9... | collective-permute-start | bytes 221192 | tf_op jit(solution)/shard_map/ppermute | solution.py:626
  28.2 4.0 %collective-permute-start.9 = (bf16[368,128]{1,0:T(8,128)(2,1)S(1)}, bf16[368,128]{1,0:T(8,128)(2,1)S(1)}, u32[]{:S(2)}, u32[]{:S(2)}) collective-permute-start(bf16[368,128]{1,0:T(8,128)(2,1)S(1)} %get-tuple-element.73), channel_id=1, source_target_pairs={{0,8},{8,0},{16,24},{24,16},{1,9},{9,1},{17,25},{25,17},{2,10},{10... | collective-permute-start | bytes 282632 | tf_op jit(solution)/shard_map/ppermute | solution.py:626
  28.2 3.9 %collective-permute-start.10 = (bf16[368,128]{1,0:T(8,128)(2,1)S(1)}, bf16[368,128]{1,0:T(8,128)(2,1)S(1)}, u32[]{:S(2)}, u32[]{:S(2)}) collective-permute-start(bf16[368,128]{1,0:T(8,128)(2,1)S(1)} %get-tuple-element.74), channel_id=1, source_target_pairs={{0,0},{8,16},{16,8},{24,24},{1,1},{9,17},{17,9},{25,25},{2,2},{10,... | collective-permute-start | bytes 282632 | tf_op jit(solution)/shard_map/ppermute | solution.py:626
  32.2 19.9 %copy-start.1 = (bf16[32,64,512]{2,1,0:T(8,128)(2,1)S(1)}, bf16[32,64,512]{2,1,0:T(8,128)(2,1)}, u32[]{:S(2)}) copy-start(bf16[32,64,512]{2,1,0:T(8,128)(2,1)} %fine_ref.4) | copy-start | bytes 6291460
  32.2 19.9 %copy-start.4 = (bf16[128,512]{1,0:T(8,128)(2,1)S(1)}, bf16[128,512]{1,0:T(8,128)(2,1)}, u32[]{:S(2)}) copy-start(bf16[128,512]{1,0:T(8,128)(2,1)} %w_ref.3) | copy-start | bytes 393220
  35.4 12.5 %collective-permute-start.14 = (bf16[256,128]{1,0:T(8,128)(2,1)S(1)}, bf16[256,128]{1,0:T(8,128)(2,1)S(1)}, u32[]{:S(2)}, u32[]{:S(2)}) collective-permute-start(bf16[256,128]{1,0:T(8,128)(2,1)S(1)} %get-tuple-element.83), channel_id=1, source_target_pairs={{0,2},{1,3},{2,4},{3,5},{4,6},{5,7},{6,0},{7,1},{8,10},{9,11},{10,... | collective-permute-start | bytes 196616 | tf_op jit(solution)/shard_map/ppermute | solution.py:618
  41.8 8.6 %collective-permute-start.16 = (bf16[256,128]{1,0:T(8,128)(2,1)S(1)}, bf16[256,128]{1,0:T(8,128)(2,1)S(1)}, u32[]{:S(2)}, u32[]{:S(2)}) collective-permute-start(bf16[256,128]{1,0:T(8,128)(2,1)S(1)} %get-tuple-element.87), channel_id=1, source_target_pairs={{0,1},{1,2},{2,3},{3,4},{4,5},{5,6},{6,7},{7,0},{8,9},{9,10},{10,1... | collective-permute-start | bytes 196616 | tf_op jit(solution)/shard_map/ppermute | solution.py:618
  41.8 11.4 %collective-permute-start.11 = (bf16[256,128]{1,0:T(8,128)(2,1)S(1)}, bf16[256,128]{1,0:T(8,128)(2,1)S(1)}, u32[]{:S(2)}, u32[]{:S(2)}) collective-permute-start(bf16[256,128]{1,0:T(8,128)(2,1)S(1)} %get-tuple-element.80), channel_id=1, source_target_pairs={{0,4},{1,5},{2,6},{3,7},{4,0},{5,1},{6,2},{7,3},{8,12},{9,13},{10,... | collective-permute-start | bytes 196616 | tf_op jit(solution)/shard_map/ppermute | solution.py:618
  44.6 10.5 %collective-permute-start.12 = (bf16[256,128]{1,0:T(8,128)(2,1)S(1)}, bf16[256,128]{1,0:T(8,128)(2,1)S(1)}, u32[]{:S(2)}, u32[]{:S(2)}) collective-permute-start(bf16[256,128]{1,0:T(8,128)(2,1)S(1)} %get-tuple-element.81), channel_id=1, source_target_pairs={{0,3},{1,4},{2,5},{3,6},{4,7},{5,0},{6,1},{7,2},{8,11},{9,12},{10,... | collective-permute-start | bytes 196616 | tf_op jit(solution)/shard_map/ppermute | solution.py:618
  47.1 8.0 %collective-permute-start.13 = (bf16[256,128]{1,0:T(8,128)(2,1)S(1)}, bf16[256,128]{1,0:T(8,128)(2,1)S(1)}, u32[]{:S(2)}, u32[]{:S(2)}) collective-permute-start(bf16[256,128]{1,0:T(8,128)(2,1)S(1)} %get-tuple-element.82), channel_id=1, source_target_pairs={{0,6},{1,7},{2,0},{3,1},{4,2},{5,3},{6,4},{7,5},{8,14},{9,15},{10,... | collective-permute-start | bytes 196616 | tf_op jit(solution)/shard_map/ppermute | solution.py:618
  47.9 8.1 %collective-permute-start.15 = (bf16[256,128]{1,0:T(8,128)(2,1)S(1)}, bf16[256,128]{1,0:T(8,128)(2,1)S(1)}, u32[]{:S(2)}, u32[]{:S(2)}) collective-permute-start(bf16[256,128]{1,0:T(8,128)(2,1)S(1)} %get-tuple-element.85), channel_id=1, source_target_pairs={{0,5},{1,6},{2,7},{3,0},{4,1},{5,2},{6,3},{7,4},{8,13},{9,14},{10,... | collective-permute-start | bytes 196616 | tf_op jit(solution)/shard_map/ppermute | solution.py:618
  50.4 7.1 %collective-permute-start.17 = (bf16[256,128]{1,0:T(8,128)(2,1)S(1)}, bf16[256,128]{1,0:T(8,128)(2,1)S(1)}, u32[]{:S(2)}, u32[]{:S(2)}) collective-permute-start(bf16[256,128]{1,0:T(8,128)(2,1)S(1)} %get-tuple-element.89), channel_id=1, source_target_pairs={{0,7},{1,0},{2,1},{3,2},{4,3},{5,4},{6,5},{7,6},{8,15},{9,8},{10,9... | collective-permute-start | bytes 196616 | tf_op jit(solution)/shard_map/ppermute | solution.py:618

commit v16 on v13

--- a/solution.py
+++ b/solution.py
@@ -145,17 +145,21 @@
 
 
 def up_kernel(offsets, fine_ref, mask_ref, w_ref, *refs):
-    out_ref = refs[-1]
+    out_ref, octant_ref = refs[-2:]
     step = pl.program_id(0)
     bricks, cells, width = fine_ref.shape
     count = bricks // CAP
     steps = offsets // count
     for part in range(count):
-        octant = refs[part][...]
-        for other in range(1, steps):
-            octant = jnp.where(step == other, refs[other * count + part][...], octant)
+        for k in range(steps):
+
+            @pl.when(step == k)
+            def _():
+                octant_ref[part] = refs[k * count + part][...]
+
+    for part in range(count):
         rows = slice(part * CAP * cells, (part + 1) * CAP * cells)
-        up = jnp.dot(octant, w_ref[...], preferred_element_type=jnp.float32)
+        up = jnp.dot(octant_ref[part], w_ref[...], preferred_element_type=jnp.float32)
         fine = fine_ref[part * CAP : (part + 1) * CAP].reshape(CAP * cells, width)
         mask = mask_ref[rows].astype(jnp.float32)
         out = jnp.where(mask > 0.5, fine.astype(jnp.float32) + up, 0.0)
@@ -185,6 +189,7 @@
         out_specs=pl.BlockSpec((step, cells, width), lambda i: (place(i), 0, 0)),
         out_shape=jax.ShapeDtypeStruct(fine.shape, jnp.bfloat16),
         input_output_aliases={3 + count: 0} if partials else {},
+        scratch_shapes=[pltpu.VMEM((step // CAP, CAP * cells, mid), jnp.bfloat16)],
         compiler_params=pltpu.CompilerParams(vmem_limit_bytes=VMEM_LIMIT),
         cost_estimate=pl.CostEstimate(
             flops=bricks * cells * width * mid, bytes_accessed=bricks * cells * width * 2, transcendentals=0

time: 59 us -> 59 us (level)
  no operation moved by 1% of the time
where the time goes in v16:
time: 59 us; the launch traced here: 58.8 us
  starting transfers between devices  30.7 us (52%)
  Pallas kernels  18.7 us (32%)
  waiting for transfers between devices  6.13 us (10%)
  local copies, waits for them, and re-layouts  1.62 us (3%)
  other arithmetic  0.9 us (2%)
  between operations  0.83 us (1%)
    ppermute x14, starting transfers between devices, from_behind(): return lax.ppermute(value, axis, pairs)  27.2 us
    ppermute x14, waiting for transfers between devices, from_behind(): return lax.ppermute(value, axis, pairs)  6.11 us
    pallas_call x1, Pallas kernels, down_call(): pl.pallas_call(functools.partial(down_kernel, offsets), in_specs=[hbm, hb...  3.97 us
    ppermute x4, starting transfers between devices, swap_face(): return lax.ppermute(face, axis, list(enumerate(partner)))  3.49 us
    pallas_call x2, Pallas kernels, up_call(): pl.pallas_call(functools.partial(up_kernel, count), grid=(count * CAP //...  3.4 us
    pallas_call x1, Pallas kernels, middle_call(): pl.pallas_call(middle_kernel, in_specs=[smem] + [vmem] * 6, out_specs=[vm...  3.23 us
    pallas_call x1, Pallas kernels, final_call(): pl.pallas_call(functools.partial(final_kernel, count), in_specs=[smem, sm...  3.21 us
    pallas_call x1, Pallas kernels, inner_call(): pl.pallas_call(functools.partial(inner_kernel, groups), in_specs=[smem, v...  2.37 us
  transfers between devices with their start and end apart: 18, of which 6 were waited for; matrix products, arithmetic and copies ran while one was open for 2% of the time, Pallas kernels for 13%

profile of v16, /device:TPU:0, one launch (start us, length us, event | category | flops | bytes accessed | tf_op | source)
XLA Modules:
  0.0 58.8 jit_solution(14513826374700942431)
XLA Ops:
  0.7 4.0 %down.1 = (bf16[256,128]{1,0:T(8,128)(2,1)}, bf16[256,128]{1,0:T(8,128)(2,1)}, bf16[256,128]{1,0:T(8,128)(2,1)}, bf16[256,128]{1,0:T(8,128)(2,1)}, bf16[256,128]...) custom-call(bf16[32,64,512]{2,1,0:T(8,128)(2,1)} %fine_ref.4, s32[32,512]{1,0:T(8,128)} %mask_ref, ...), custom_call_target="tpu_custom_call" | custom-call | flops 234881024 | bytes 1835008 | tf_op jit(solution)/shard_map/down/pallas_call | solution.py:85
  4.7 5.0 %collective-permute-start = (bf16[256,128]{1,0:T(8,128)(2,1)}, bf16[256,128]{1,0:T(8,128)(2,1)S(1)}, u32[]{:S(2)}, u32[]{:S(2)}) collective-permute-start(bf16[256,128]{1,0:T(8,128)(2,1)} %get-tuple-element.50), channel_id=1, source_target_pairs={{0,5},{1,6},{2,7},{3,0},{4,1},{5,2},{6,3},{7,4},{8,13},{9,14},{10,... | collective-permute-start | bytes 196616 | tf_op jit(solution)/shard_map/ppermute | solution.py:623
  9.7 1.5 %collective-permute-start.1 = (bf16[256,128]{1,0:T(8,128)(2,1)}, bf16[256,128]{1,0:T(8,128)(2,1)S(1)}, u32[]{:S(2)}, u32[]{:S(2)}) collective-permute-start(bf16[256,128]{1,0:T(8,128)(2,1)} %get-tuple-element.58), channel_id=1, source_target_pairs={{0,1},{1,2},{2,3},{3,4},{4,5},{5,6},{6,7},{7,0},{8,9},{9,10},{10,1... | collective-permute-start | bytes 196616 | tf_op jit(solution)/shard_map/ppermute | solution.py:623
  11.3 1.8 %collective-permute-start.3 = (bf16[256,128]{1,0:T(8,128)(2,1)}, bf16[256,128]{1,0:T(8,128)(2,1)S(1)}, u32[]{:S(2)}, u32[]{:S(2)}) collective-permute-start(bf16[256,128]{1,0:T(8,128)(2,1)} %get-tuple-element.60), channel_id=1, source_target_pairs={{0,3},{1,4},{2,5},{3,6},{4,7},{5,0},{6,1},{7,2},{8,11},{9,12},{10,... | collective-permute-start | bytes 196616 | tf_op jit(solution)/shard_map/ppermute | solution.py:623
  13.0 3.5 %collective-permute-start.4 = (bf16[256,128]{1,0:T(8,128)(2,1)}, bf16[256,128]{1,0:T(8,128)(2,1)S(1)}, u32[]{:S(2)}, u32[]{:S(2)}) collective-permute-start(bf16[256,128]{1,0:T(8,128)(2,1)} %get-tuple-element.61), channel_id=1, source_target_pairs={{0,4},{1,5},{2,6},{3,7},{4,0},{5,1},{6,2},{7,3},{8,12},{9,13},{10,... | collective-permute-start | bytes 196616 | tf_op jit(solution)/shard_map/ppermute | solution.py:623
  16.5 1.3 %collective-permute-start.5 = (bf16[256,128]{1,0:T(8,128)(2,1)}, bf16[256,128]{1,0:T(8,128)(2,1)S(1)}, u32[]{:S(2)}, u32[]{:S(2)}) collective-permute-start(bf16[256,128]{1,0:T(8,128)(2,1)} %get-tuple-element.63), channel_id=1, source_target_pairs={{0,6},{1,7},{2,0},{3,1},{4,2},{5,3},{6,4},{7,5},{8,14},{9,15},{10,... | collective-permute-start | bytes 196616 | tf_op jit(solution)/shard_map/ppermute | solution.py:623
  17.9 1.0 %collective-permute-start.6 = (bf16[256,128]{1,0:T(8,128)(2,1)}, bf16[256,128]{1,0:T(8,128)(2,1)S(1)}, u32[]{:S(2)}, u32[]{:S(2)}) collective-permute-start(bf16[256,128]{1,0:T(8,128)(2,1)} %get-tuple-element.64), channel_id=1, source_target_pairs={{0,7},{1,0},{2,1},{3,2},{4,3},{5,4},{6,5},{7,6},{8,15},{9,8},{10,9... | collective-permute-start | bytes 196616 | tf_op jit(solution)/shard_map/ppermute | solution.py:623
  19.0 1.6 %copy-done = bf16[32,64,512]{2,1,0:T(8,128)(2,1)S(1)} copy-done((bf16[32,64,512]{2,1,0:T(8,128)(2,1)S(1)}, bf16[32,64,512]{2,1,0:T(8,128)(2,1)}, u32[]{:S(2)}) %copy-start) | copy-done | bytes 2097176
  20.6 1.1 %prepare.1 = (bf16[256,128]{1,0:T(8,128)(2,1)S(1)}, bf16[2048,512]{1,0:T(8,128)(2,1)S(1)}, bf16[1152,384]{1,0:T(8,128)(2,1)S(1)}, bf16[1152,384]{1,0:T(8,128)(2,1)S(1)}) custom-call(bf16[32,64,512]{2,1,0:T(8,128)(2,1)S(1)} %copy-done, s32[32,512]{1,0:T(8,128)S(1)} %copy-done.6, bf16[512,128]{1,0:T(8,128)(2,1)S(1)} %copy-done.5, ...), custom_call_target="tpu_custom_call" | custom-call | flops 268435456 | bytes 2097152 | tf_op jit(solution)/shard_map/prepare/pallas_call | solution.py:128
  21.7 0.8 %collective-permute-done.3.refs_3_ = bf16[256,128]{1,0:T(8,128)(2,1)S(1)} collective-permute-done((bf16[256,128]{1,0:T(8,128)(2,1)}, bf16[256,128]{1,0:T(8,128)(2,1)S(1)}, u32[]{:S(2)}, u32[]{:S(2)}) %collective-permute-start.3) | collective-permute-done | bytes 65568 | tf_op jit(solution)/shard_map/ppermute | solution.py:623
  22.5 0.3 collective-permute-done.6.refs_7_
  22.8 0.8 %place.1 = (bf16[2048,128]{1,0:T(8,128)(2,1)S(1)}, bf16[288,128]{1,0:T(8,128)(2,1)S(1)}, bf16[288,128]{1,0:T(8,128)(2,1)S(1)}) custom-call(s32[2]{0:T(128)S(1)} %pad_add_fusion.base_ref, s32[32]{0:T(128)S(1)} %copy-done.7, bf16[256,128]{1,0:T(8,128)(2,1)S(1)} %get-tuple-element.57.refs_0_, bf16[256,128]{1,0:T(8,128)(2,1)S(1)} %collective-permute-done.1.refs_1_, ...), custom_call_target="tpu_custom_call" | custom-call | tf_op jit(solution)/shard_map/place/pallas_call | solution.py:269
  23.6 2.1 %collective-permute-start.7 = (bf16[288,128]{1,0:T(8,128)(2,1)S(1)}, bf16[288,128]{1,0:T(8,128)(2,1)S(1)}, u32[]{:S(2)}, u32[]{:S(2)}) collective-permute-start(bf16[288,128]{1,0:T(8,128)(2,1)S(1)} %get-tuple-element.66), channel_id=1, source_target_pairs={{0,1},{1,0},{2,3},{3,2},{4,5},{5,4},{6,7},{7,6},{8,9},{9,8},{10,11... | collective-permute-start | bytes 221192 | tf_op jit(solution)/shard_map/ppermute | solution.py:631
  25.7 0.7 %collective-permute-start.8 = (bf16[288,128]{1,0:T(8,128)(2,1)S(1)}, bf16[288,128]{1,0:T(8,128)(2,1)S(1)}, u32[]{:S(2)}, u32[]{:S(2)}) collective-permute-start(bf16[288,128]{1,0:T(8,128)(2,1)S(1)} %get-tuple-element.67), channel_id=1, source_target_pairs={{0,0},{1,2},{2,1},{3,4},{4,3},{5,6},{6,5},{7,7},{8,8},{9,10},{10,9... | collective-permute-start | bytes 221192 | tf_op jit(solution)/shard_map/ppermute | solution.py:631
  26.3 2.4 %inner.1.refs_3_ = bf16[11,112,128]{2,1,0:T(8,128)(2,1)S(1)} custom-call(s32[32]{0:T(128)S(1)} %copy-done.7, bf16[2048,128]{1,0:T(8,128)(2,1)S(1)} %get-tuple-element.65.block_ref.refs_0_, bf16[1152,384]{1,0:T(8,128)(2,1)S(1)} %get-tuple-element.68.wide1_ref.refs_4_.refs_8_), custom_call_target="tpu_custom_call" | custom-call | flops 1089994752 | bytes 1769472 | tf_op jit(solution)/shard_map/inner/pallas_call | solution.py:428
  28.7 0.6 %edge.1 = (bf16[288,128]{1,0:T(8,128)(2,1)S(1)}, bf16[288,128]{1,0:T(8,128)(2,1)S(1)}, bf16[368,128]{1,0:T(8,128)(2,1)S(1)}, bf16[368,128]{1,0:T(8,128)(2,1)S(1)}) custom-call(s32[2]{0:T(128)S(1)} %pad_add_fusion.base_ref, s32[32]{0:T(128)S(1)} %copy-done.7, bf16[2048,128]{1,0:T(8,128)(2,1)S(1)} %get-tuple-element.65.block_ref.refs_0_, ...), custom_call_target="tpu_custom_call" | custom-call | tf_op jit(solution)/shard_map/edge/pallas_call | solution.py:319
  29.4 0.7 %collective-permute-start.10 = (bf16[368,128]{1,0:T(8,128)(2,1)S(1)}, bf16[368,128]{1,0:T(8,128)(2,1)S(1)}, u32[]{:S(2)}, u32[]{:S(2)}) collective-permute-start(bf16[368,128]{1,0:T(8,128)(2,1)S(1)} %get-tuple-element.74), channel_id=1, source_target_pairs={{0,0},{8,16},{16,8},{24,24},{1,1},{9,17},{17,9},{25,25},{2,2},{10,... | collective-permute-start | bytes 282632 | tf_op jit(solution)/shard_map/ppermute | solution.py:631
  30.1 3.2 %middle.1 = (bf16[14,144,128]{2,1,0:T(8,128)(2,1)S(1)}, bf16[14,144,128]{2,1,0:T(8,128)(2,1)S(1)}, bf16[1024,128]{1,0:T(8,128)(2,1)S(1)}) custom-call(s32[32]{0:T(128)S(1)} %copy-done.7, bf16[2048,128]{1,0:T(8,128)(2,1)S(1)} %get-tuple-element.65.block_ref.refs_0_, bf16[288,128]{1,0:T(8,128)(2,1)S(1)} %get-tuple-element.71.refs_1_, ...), custom_call_target="tpu_custom_call" | custom-call | flops 1599602688 | bytes 1769472 | tf_op jit(solution)/shard_map/middle/pallas_call | solution.py:504
  33.4 3.2 %final.1 = (bf16[512,128]{1,0:T(8,128)(2,1)S(1)}, bf16[512,128]{1,0:T(8,128)(2,1)S(1)}, bf16[256,128]{1,0:T(8,128)(2,1)S(1)}, bf16[256,128]{1,0:T(8,128)(2,1)S(1...) custom-call(s32[2]{0:T(128)S(1)} %pad_add_fusion.base_ref, ...), custom_call_target="tpu_custom_call" | custom-call | flops 1415577600 | bytes 1769472 | tf_op jit(solution)/shard_map/final/pallas_call | solution.py:599
  36.6 5.1 %collective-permute-start.14 = (bf16[256,128]{1,0:T(8,128)(2,1)S(1)}, bf16[256,128]{1,0:T(8,128)(2,1)S(1)}, u32[]{:S(2)}, u32[]{:S(2)}) collective-permute-start(bf16[256,128]{1,0:T(8,128)(2,1)S(1)} %get-tuple-element.83), channel_id=1, source_target_pairs={{0,2},{1,3},{2,4},{3,5},{4,6},{5,7},{6,0},{7,1},{8,10},{9,11},{10,... | collective-permute-start | bytes 196616 | tf_op jit(solution)/shard_map/ppermute | solution.py:623
  41.8 1.4 %collective-permute-start.11 = (bf16[256,128]{1,0:T(8,128)(2,1)S(1)}, bf16[256,128]{1,0:T(8,128)(2,1)S(1)}, u32[]{:S(2)}, u32[]{:S(2)}) collective-permute-start(bf16[256,128]{1,0:T(8,128)(2,1)S(1)} %get-tuple-element.80), channel_id=1, source_target_pairs={{0,4},{1,5},{2,6},{3,7},{4,0},{5,1},{6,2},{7,3},{8,12},{9,13},{10,... | collective-permute-start | bytes 196616 | tf_op jit(solution)/shard_map/ppermute | solution.py:623
  43.2 3.9 %collective-permute-start.12 = (bf16[256,128]{1,0:T(8,128)(2,1)S(1)}, bf16[256,128]{1,0:T(8,128)(2,1)S(1)}, u32[]{:S(2)}, u32[]{:S(2)}) collective-permute-start(bf16[256,128]{1,0:T(8,128)(2,1)S(1)} %get-tuple-element.81), channel_id=1, source_target_pairs={{0,3},{1,4},{2,5},{3,6},{4,7},{5,0},{6,1},{7,2},{8,11},{9,12},{10,... | collective-permute-start | bytes 196616 | tf_op jit(solution)/shard_map/ppermute | solution.py:623
  47.0 0.9 %collective-permute-start.13 = (bf16[256,128]{1,0:T(8,128)(2,1)S(1)}, bf16[256,128]{1,0:T(8,128)(2,1)S(1)}, u32[]{:S(2)}, u32[]{:S(2)}) collective-permute-start(bf16[256,128]{1,0:T(8,128)(2,1)S(1)} %get-tuple-element.82), channel_id=1, source_target_pairs={{0,6},{1,7},{2,0},{3,1},{4,2},{5,3},{6,4},{7,5},{8,14},{9,15},{10,... | collective-permute-start | bytes 196616 | tf_op jit(solution)/shard_map/ppermute | solution.py:623
  48.0 0.5 collective-permute-start.15
  48.5 0.5 collective-permute-done.16.refs_1_
  49.0 1.0 %collective-permute-start.17 = (bf16[256,128]{1,0:T(8,128)(2,1)S(1)}, bf16[256,128]{1,0:T(8,128)(2,1)S(1)}, u32[]{:S(2)}, u32[]{:S(2)}) collective-permute-start(bf16[256,128]{1,0:T(8,128)(2,1)S(1)} %get-tuple-element.89), channel_id=1, source_target_pairs={{0,7},{1,0},{2,1},{3,2},{4,3},{5,4},{6,5},{7,6},{8,15},{9,8},{10,9... | collective-permute-start | bytes 196616 | tf_op jit(solution)/shard_map/ppermute | solution.py:623
  50.0 0.8 %pad_maximum_fusion = bf16[2048,128]{1,0:T(8,128)(2,1)} fusion(bf16[512,128]{1,0:T(8,128)(2,1)S(1)} %get-tuple-element.97, bf16[1024,128]{1,0:T(8,128)(2,1)S(1)} %get-tuple-element.96.refs_7_, bf16[512,128]{1,0:T(8,128)(2,1)S(1)} %get-tuple-element.95), kind=kLoop, calls=%fused_computation | loop fusion | flops 1572864 | bytes 1048576 | tf_op jit(solution)/shard_map/concatenate | solution.py:662
  50.9 1.1 %up.2.refs_6_ = bf16[32,64,512]{2,1,0:T(8,128)(2,1)} custom-call(bf16[32,64,512]{2,1,0:T(8,128)(2,1)S(1)} %copy-done.1, bf16[2048,512]{1,0:T(8,128)(2,1)S(1)} %get-tuple-element.56.mask_ref, bf16[128,512]{1,0:T(8,128)(2,1)S(1)} %copy-done.4, bf16[256,128]{1,0:T(8,128)(2,1)S(1)} %collective-permute-done.14.refs_0_, ...), custom_call_target="tpu_custom_call" | custom-call | flops 134217728 | bytes 2097152 | tf_op jit(solution)/shard_map/up/pallas_call | solution.py:179
  52.0 2.6 %collective-permute-done.12.refs_1_ = bf16[256,128]{1,0:T(8,128)(2,1)S(1)} collective-permute-done((bf16[256,128]{1,0:T(8,128)(2,1)S(1)}, bf16[256,128]{1,0:T(8,128)(2,1)S(1)}, u32[]{:S(2)}, u32[]{:S(2)}) %collective-permute-start.12) | collective-permute-done | bytes 65568 | tf_op jit(solution)/shard_map/ppermute | solution.py:623
  54.6 0.9 %collective-permute-done.15.refs_3_ = bf16[256,128]{1,0:T(8,128)(2,1)S(1)} collective-permute-done((bf16[256,128]{1,0:T(8,128)(2,1)S(1)}, bf16[256,128]{1,0:T(8,128)(2,1)S(1)}, u32[]{:S(2)}, u32[]{:S(2)}) %collective-permute-start.15) | collective-permute-done | bytes 65568 | tf_op jit(solution)/shard_map/ppermute | solution.py:623
  55.4 1.1 %collective-permute-done.17.refs_5_ = bf16[256,128]{1,0:T(8,128)(2,1)S(1)} collective-permute-done((bf16[256,128]{1,0:T(8,128)(2,1)S(1)}, bf16[256,128]{1,0:T(8,128)(2,1)S(1)}, u32[]{:S(2)}, u32[]{:S(2)}) %collective-permute-start.17) | collective-permute-done | bytes 65568 | tf_op jit(solution)/shard_map/ppermute | solution.py:623
  56.5 2.3 %up.3 = bf16[32,64,512]{2,1,0:T(8,128)(2,1)} custom-call(bf16[32,64,512]{2,1,0:T(8,128)(2,1)S(1)} %copy-done.1, bf16[2048,512]{1,0:T(8,128)(2,1)S(1)} %get-tuple-element.56.mask_ref, bf16[128,512]{1,0:T(8,128)(2,1)S(1)} %copy-done.4, bf16[256,128]{1,0:T(8,128)(2,1)S(1)} %collective-permute-done.11.refs_0_, ...), custom_call_target="tpu_custom_call", output_to_operand_aliasing={{}: (9, {})} | custom-call | flops 134217728 | bytes 2097152 | tf_op jit(solution)/shard_map/up/pallas_call | solution.py:179
  (31 shorter events, 0.3 us)
Async XLA Ops:
  0.6 18.4 %copy-start.5 = (bf16[512,128]{1,0:T(8,128)(2,1)S(1)}, bf16[512,128]{1,0:T(8,128)(2,1)}, u32[]{:S(2)}) copy-start(bf16[512,128]{1,0:T(8,128)(2,1)} %w_down_ref) | copy-start | bytes 393220
  0.6 18.4 %copy-start.6 = (s32[32,512]{1,0:T(8,128)S(1)}, s32[32,512]{1,0:T(8,128)}, u32[]{:S(2)}) copy-start(s32[32,512]{1,0:T(8,128)} %mask_ref) | copy-start | bytes 196612
  0.7 18.4 %copy-start.3 = (bf16[27,128,128]{2,1,0:T(8,128)(2,1)S(1)}, bf16[27,128,128]{2,1,0:T(8,128)(2,1)}, u32[]{:S(2)}) copy-start(bf16[27,128,128]{2,1,0:T(8,128)(2,1)} %w2_ref) | copy-start | bytes 2654212
  0.7 18.4 %copy-start.2 = (bf16[27,128,128]{2,1,0:T(8,128)(2,1)S(1)}, bf16[27,128,128]{2,1,0:T(8,128)(2,1)}, u32[]{:S(2)}) copy-start(bf16[27,128,128]{2,1,0:T(8,128)(2,1)} %w1_ref) | copy-start | bytes 2654212
  4.6 18.1 %copy-start.7 = (s32[32]{0:T(128)S(1)}, s32[32]{0:T(128)}, u32[]{:S(2)}) copy-start(s32[32]{0:T(128)} %source_ref.9) | copy-start | bytes 388
  4.7 11.9 %collective-permute-start = (bf16[256,128]{1,0:T(8,128)(2,1)}, bf16[256,128]{1,0:T(8,128)(2,1)S(1)}, u32[]{:S(2)}, u32[]{:S(2)}) collective-permute-start(bf16[256,128]{1,0:T(8,128)(2,1)} %get-tuple-element.50), channel_id=1, source_target_pairs={{0,5},{1,6},{2,7},{3,0},{4,1},{5,2},{6,3},{7,4},{8,13},{9,14},{10,... | collective-permute-start | bytes 196616 | tf_op jit(solution)/shard_map/ppermute | solution.py:623
  9.7 8.2 %collective-permute-start.1 = (bf16[256,128]{1,0:T(8,128)(2,1)}, bf16[256,128]{1,0:T(8,128)(2,1)S(1)}, u32[]{:S(2)}, u32[]{:S(2)}) collective-permute-start(bf16[256,128]{1,0:T(8,128)(2,1)} %get-tuple-element.58), channel_id=1, source_target_pairs={{0,1},{1,2},{2,3},{3,4},{4,5},{5,6},{6,7},{7,0},{8,9},{9,10},{10,1... | collective-permute-start | bytes 196616 | tf_op jit(solution)/shard_map/ppermute | solution.py:623
  11.2 10.5 %collective-permute-start.2 = (bf16[256,128]{1,0:T(8,128)(2,1)}, bf16[256,128]{1,0:T(8,128)(2,1)S(1)}, u32[]{:S(2)}, u32[]{:S(2)}) collective-permute-start(bf16[256,128]{1,0:T(8,128)(2,1)} %get-tuple-element.59), channel_id=1, source_target_pairs={{0,2},{1,3},{2,4},{3,5},{4,6},{5,7},{6,0},{7,1},{8,10},{9,11},{10,... | collective-permute-start | bytes 196616 | tf_op jit(solution)/shard_map/ppermute | solution.py:623
  11.3 11.3 %collective-permute-start.3 = (bf16[256,128]{1,0:T(8,128)(2,1)}, bf16[256,128]{1,0:T(8,128)(2,1)S(1)}, u32[]{:S(2)}, u32[]{:S(2)}) collective-permute-start(bf16[256,128]{1,0:T(8,128)(2,1)} %get-tuple-element.60), channel_id=1, source_target_pairs={{0,3},{1,4},{2,5},{3,6},{4,7},{5,0},{6,1},{7,2},{8,11},{9,12},{10,... | collective-permute-start | bytes 196616 | tf_op jit(solution)/shard_map/ppermute | solution.py:623
  13.0 9.5 %collective-permute-start.4 = (bf16[256,128]{1,0:T(8,128)(2,1)}, bf16[256,128]{1,0:T(8,128)(2,1)S(1)}, u32[]{:S(2)}, u32[]{:S(2)}) collective-permute-start(bf16[256,128]{1,0:T(8,128)(2,1)} %get-tuple-element.61), channel_id=1, source_target_pairs={{0,4},{1,5},{2,6},{3,7},{4,0},{5,1},{6,2},{7,3},{8,12},{9,13},{10,... | collective-permute-start | bytes 196616 | tf_op jit(solution)/shard_map/ppermute | solution.py:623
  16.5 6.0 %collective-permute-start.5 = (bf16[256,128]{1,0:T(8,128)(2,1)}, bf16[256,128]{1,0:T(8,128)(2,1)S(1)}, u32[]{:S(2)}, u32[]{:S(2)}) collective-permute-start(bf16[256,128]{1,0:T(8,128)(2,1)} %get-tuple-element.63), channel_id=1, source_target_pairs={{0,6},{1,7},{2,0},{3,1},{4,2},{5,3},{6,4},{7,5},{8,14},{9,15},{10,... | collective-permute-start | bytes 196616 | tf_op jit(solution)/shard_map/ppermute | solution.py:623
  17.9 4.9 %collective-permute-start.6 = (bf16[256,128]{1,0:T(8,128)(2,1)}, bf16[256,128]{1,0:T(8,128)(2,1)S(1)}, u32[]{:S(2)}, u32[]{:S(2)}) collective-permute-start(bf16[256,128]{1,0:T(8,128)(2,1)} %get-tuple-element.64), channel_id=1, source_target_pairs={{0,7},{1,0},{2,1},{3,2},{4,3},{5,4},{6,5},{7,6},{8,15},{9,8},{10,9... | collective-permute-start | bytes 196616 | tf_op jit(solution)/shard_map/ppermute | solution.py:623
  19.0 1.6 %copy-start = (bf16[32,64,512]{2,1,0:T(8,128)(2,1)S(1)}, bf16[32,64,512]{2,1,0:T(8,128)(2,1)}, u32[]{:S(2)}) copy-start(bf16[32,64,512]{2,1,0:T(8,128)(2,1)} %fine_ref.4) | copy-start | bytes 6291460
  23.6 5.1 %collective-permute-start.7 = (bf16[288,128]{1,0:T(8,128)(2,1)S(1)}, bf16[288,128]{1,0:T(8,128)(2,1)S(1)}, u32[]{:S(2)}, u32[]{:S(2)}) collective-permute-start(bf16[288,128]{1,0:T(8,128)(2,1)S(1)} %get-tuple-element.66), channel_id=1, source_target_pairs={{0,1},{1,0},{2,3},{3,2},{4,5},{5,4},{6,7},{7,6},{8,9},{9,8},{10,11... | collective-permute-start | bytes 221192 | tf_op jit(solution)/shard_map/ppermute | solution.py:631
  25.7 3.0 %collective-permute-start.8 = (bf16[288,128]{1,0:T(8,128)(2,1)S(1)}, bf16[288,128]{1,0:T(8,128)(2,1)S(1)}, u32[]{:S(2)}, u32[]{:S(2)}) collective-permute-start(bf16[288,128]{1,0:T(8,128)(2,1)S(1)} %get-tuple-element.67), channel_id=1, source_target_pairs={{0,0},{1,2},{2,1},{3,4},{4,3},{5,6},{6,5},{7,7},{8,8},{9,10},{10,9... | collective-permute-start | bytes 221192 | tf_op jit(solution)/shard_map/ppermute | solution.py:631
  29.4 4.0 %collective-permute-start.9 = (bf16[368,128]{1,0:T(8,128)(2,1)S(1)}, bf16[368,128]{1,0:T(8,128)(2,1)S(1)}, u32[]{:S(2)}, u32[]{:S(2)}) collective-permute-start(bf16[368,128]{1,0:T(8,128)(2,1)S(1)} %get-tuple-element.73), channel_id=1, source_target_pairs={{0,8},{8,0},{16,24},{24,16},{1,9},{9,1},{17,25},{25,17},{2,10},{10... | collective-permute-start | bytes 282632 | tf_op jit(solution)/shard_map/ppermute | solution.py:631
  29.4 3.9 %collective-permute-start.10 = (bf16[368,128]{1,0:T(8,128)(2,1)S(1)}, bf16[368,128]{1,0:T(8,128)(2,1)S(1)}, u32[]{:S(2)}, u32[]{:S(2)}) collective-permute-start(bf16[368,128]{1,0:T(8,128)(2,1)S(1)} %get-tuple-element.74), channel_id=1, source_target_pairs={{0,0},{8,16},{16,8},{24,24},{1,1},{9,17},{17,9},{25,25},{2,2},{10,... | collective-permute-start | bytes 282632 | tf_op jit(solution)/shard_map/ppermute | solution.py:631
  33.4 17.5 %copy-start.1 = (bf16[32,64,512]{2,1,0:T(8,128)(2,1)S(1)}, bf16[32,64,512]{2,1,0:T(8,128)(2,1)}, u32[]{:S(2)}) copy-start(bf16[32,64,512]{2,1,0:T(8,128)(2,1)} %fine_ref.4) | copy-start | bytes 6291460
  33.4 17.5 %copy-start.4 = (bf16[128,512]{1,0:T(8,128)(2,1)S(1)}, bf16[128,512]{1,0:T(8,128)(2,1)}, u32[]{:S(2)}) copy-start(bf16[128,512]{1,0:T(8,128)(2,1)} %w_ref.3) | copy-start | bytes 393220
  36.6 11.3 %collective-permute-start.14 = (bf16[256,128]{1,0:T(8,128)(2,1)S(1)}, bf16[256,128]{1,0:T(8,128)(2,1)S(1)}, u32[]{:S(2)}, u32[]{:S(2)}) collective-permute-start(bf16[256,128]{1,0:T(8,128)(2,1)S(1)} %get-tuple-element.83), channel_id=1, source_target_pairs={{0,2},{1,3},{2,4},{3,5},{4,6},{5,7},{6,0},{7,1},{8,10},{9,11},{10,... | collective-permute-start | bytes 196616 | tf_op jit(solution)/shard_map/ppermute | solution.py:623
  41.7 7.2 %collective-permute-start.16 = (bf16[256,128]{1,0:T(8,128)(2,1)S(1)}, bf16[256,128]{1,0:T(8,128)(2,1)S(1)}, u32[]{:S(2)}, u32[]{:S(2)}) collective-permute-start(bf16[256,128]{1,0:T(8,128)(2,1)S(1)} %get-tuple-element.87), channel_id=1, source_target_pairs={{0,1},{1,2},{2,3},{3,4},{4,5},{5,6},{6,7},{7,0},{8,9},{9,10},{10,1... | collective-permute-start | bytes 196616 | tf_op jit(solution)/shard_map/ppermute | solution.py:623
  41.8 10.2 %collective-permute-start.11 = (bf16[256,128]{1,0:T(8,128)(2,1)S(1)}, bf16[256,128]{1,0:T(8,128)(2,1)S(1)}, u32[]{:S(2)}, u32[]{:S(2)}) collective-permute-start(bf16[256,128]{1,0:T(8,128)(2,1)S(1)} %get-tuple-element.80), channel_id=1, source_target_pairs={{0,4},{1,5},{2,6},{3,7},{4,0},{5,1},{6,2},{7,3},{8,12},{9,13},{10,... | collective-permute-start | bytes 196616 | tf_op jit(solution)/shard_map/ppermute | solution.py:623
  43.2 11.4 %collective-permute-start.12 = (bf16[256,128]{1,0:T(8,128)(2,1)S(1)}, bf16[256,128]{1,0:T(8,128)(2,1)S(1)}, u32[]{:S(2)}, u32[]{:S(2)}) collective-permute-start(bf16[256,128]{1,0:T(8,128)(2,1)S(1)} %get-tuple-element.81), channel_id=1, source_target_pairs={{0,3},{1,4},{2,5},{3,6},{4,7},{5,0},{6,1},{7,2},{8,11},{9,12},{10,... | collective-permute-start | bytes 196616 | tf_op jit(solution)/shard_map/ppermute | solution.py:623
  47.0 7.5 %collective-permute-start.13 = (bf16[256,128]{1,0:T(8,128)(2,1)S(1)}, bf16[256,128]{1,0:T(8,128)(2,1)S(1)}, u32[]{:S(2)}, u32[]{:S(2)}) collective-permute-start(bf16[256,128]{1,0:T(8,128)(2,1)S(1)} %get-tuple-element.82), channel_id=1, source_target_pairs={{0,6},{1,7},{2,0},{3,1},{4,2},{5,3},{6,4},{7,5},{8,14},{9,15},{10,... | collective-permute-start | bytes 196616 | tf_op jit(solution)/shard_map/ppermute | solution.py:623
  48.0 7.5 %collective-permute-start.15 = (bf16[256,128]{1,0:T(8,128)(2,1)S(1)}, bf16[256,128]{1,0:T(8,128)(2,1)S(1)}, u32[]{:S(2)}, u32[]{:S(2)}) collective-permute-start(bf16[256,128]{1,0:T(8,128)(2,1)S(1)} %get-tuple-element.85), channel_id=1, source_target_pairs={{0,5},{1,6},{2,7},{3,0},{4,1},{5,2},{6,3},{7,4},{8,13},{9,14},{10,... | collective-permute-start | bytes 196616 | tf_op jit(solution)/shard_map/ppermute | solution.py:623
  49.0 7.5 %collective-permute-start.17 = (bf16[256,128]{1,0:T(8,128)(2,1)S(1)}, bf16[256,128]{1,0:T(8,128)(2,1)S(1)}, u32[]{:S(2)}, u32[]{:S(2)}) collective-permute-start(bf16[256,128]{1,0:T(8,128)(2,1)S(1)} %get-tuple-element.89), channel_id=1, source_target_pairs={{0,7},{1,0},{2,1},{3,2},{4,3},{5,4},{6,5},{7,6},{8,15},{9,8},{10,9... | collective-permute-start | bytes 196616 | tf_op jit(solution)/shard_map/ppermute | solution.py:623

commit v17 on v16

--- a/solution.py
+++ b/solution.py
@@ -19,7 +19,7 @@
 LATE_PLANES = 3
 SENT = (4, 3, 5, 2, 6, 1, 7)
 RETURNED = (6, 7, 4, 5, 2, 3, 1)
-DOWN_LIMIT = 62 * 1024 * 1024
+DOWN_LIMIT = 66000000
 VMEM_LIMIT = 24 * 1024 * 1024
 
 

time: 59 us -> 59 us (level)
  local copies, waits for them, and re-layouts: 1.62 us -> 3.62 us
  waiting for transfers between devices: 6.13 us -> 4.45 us
    unnamed x16, local copies, waits for them, and re-layouts: 1.62 us -> 3.62 us
    ppermute x14, waiting for transfers between devices: 6.11 us -> 4.18 us  [from_behind(): return lax.ppermute(value, axis, pairs)]
    ppermute x4, starting transfers between devices: 3.49 us -> 2.51 us  [swap_face(): return lax.ppermute(face, axis, list(enumerate(partner)))]
    ppermute x14, starting transfers between devices: 27.2 us -> 27.8 us  [from_behind(): return lax.ppermute(value, axis, pairs)]
  transfers between devices with their start and end apart: 18 -> 18, of which waited for: 6 -> 5; matrix products, arithmetic and copies ran while one was open for 2% -> 2% of each run, Pallas kernels for 13% -> 13%
where the time goes in v17:
time: 59 us; the launch traced here: 58.8 us
  starting transfers between devices  30.3 us (51%)
  Pallas kernels  18.7 us (32%)
  waiting for transfers between devices  4.45 us (8%)
  local copies, waits for them, and re-layouts  3.62 us (6%)
  other arithmetic  0.9 us (2%)
  between operations  0.82 us (1%)
    ppermute x14, starting transfers between devices, from_behind(): return lax.ppermute(value, axis, pairs)  27.8 us
    ppermute x14, waiting for transfers between devices, from_behind(): return lax.ppermute(value, axis, pairs)  4.18 us
    pallas_call x1, Pallas kernels, down_call(): pl.pallas_call(functools.partial(down_kernel, offsets), in_specs=[hbm, hb...  3.91 us
    unnamed x16, local copies, waits for them, and re-layouts  3.62 us
    pallas_call x2, Pallas kernels, up_call(): pl.pallas_call(functools.partial(up_kernel, count), grid=(count * CAP //...  3.42 us
    pallas_call x1, Pallas kernels, middle_call(): pl.pallas_call(middle_kernel, in_specs=[smem] + [vmem] * 6, out_specs=[vm...  3.23 us
    pallas_call x1, Pallas kernels, final_call(): pl.pallas_call(functools.partial(final_kernel, count), in_specs=[smem, sm...  3.23 us
    ppermute x4, starting transfers between devices, swap_face(): return lax.ppermute(face, axis, list(enumerate(partner)))  2.51 us
  transfers between devices with their start and end apart: 18, of which 5 were waited for; matrix products, arithmetic and copies ran while one was open for 2% of the time, Pallas kernels for 13%

profile of v17, /device:TPU:0, one launch (start us, length us, event | category | flops | bytes accessed | tf_op | source)
XLA Modules:
  0.0 58.8 jit_solution(8201453469357506718)
XLA Ops:
  0.6 3.9 %down.1 = (bf16[256,128]{1,0:T(8,128)(2,1)}, bf16[256,128]{1,0:T(8,128)(2,1)}, bf16[256,128]{1,0:T(8,128)(2,1)}, bf16[256,128]{1,0:T(8,128)(2,1)}, bf16[256,128]...) custom-call(bf16[32,64,512]{2,1,0:T(8,128)(2,1)} %fine_ref.4, s32[32,512]{1,0:T(8,128)} %mask_ref, ...), custom_call_target="tpu_custom_call" | custom-call | flops 234881024 | bytes 1835008 | tf_op jit(solution)/shard_map/down/pallas_call | solution.py:85
  4.6 5.0 %collective-permute-start = (bf16[256,128]{1,0:T(8,128)(2,1)}, bf16[256,128]{1,0:T(8,128)(2,1)S(1)}, u32[]{:S(2)}, u32[]{:S(2)}) collective-permute-start(bf16[256,128]{1,0:T(8,128)(2,1)} %get-tuple-element.50), channel_id=1, source_target_pairs={{0,5},{1,6},{2,7},{3,0},{4,1},{5,2},{6,3},{7,4},{8,13},{9,14},{10,... | collective-permute-start | bytes 196616 | tf_op jit(solution)/shard_map/ppermute | solution.py:623
  9.6 1.5 %collective-permute-start.1 = (bf16[256,128]{1,0:T(8,128)(2,1)}, bf16[256,128]{1,0:T(8,128)(2,1)S(1)}, u32[]{:S(2)}, u32[]{:S(2)}) collective-permute-start(bf16[256,128]{1,0:T(8,128)(2,1)} %get-tuple-element.58), channel_id=1, source_target_pairs={{0,1},{1,2},{2,3},{3,4},{4,5},{5,6},{6,7},{7,0},{8,9},{9,10},{10,1... | collective-permute-start | bytes 196616 | tf_op jit(solution)/shard_map/ppermute | solution.py:623
  11.2 1.8 %collective-permute-start.3 = (bf16[256,128]{1,0:T(8,128)(2,1)}, bf16[256,128]{1,0:T(8,128)(2,1)S(1)}, u32[]{:S(2)}, u32[]{:S(2)}) collective-permute-start(bf16[256,128]{1,0:T(8,128)(2,1)} %get-tuple-element.60), channel_id=1, source_target_pairs={{0,3},{1,4},{2,5},{3,6},{4,7},{5,0},{6,1},{7,2},{8,11},{9,12},{10,... | collective-permute-start | bytes 196616 | tf_op jit(solution)/shard_map/ppermute | solution.py:623
  13.0 3.5 %collective-permute-start.4 = (bf16[256,128]{1,0:T(8,128)(2,1)}, bf16[256,128]{1,0:T(8,128)(2,1)S(1)}, u32[]{:S(2)}, u32[]{:S(2)}) collective-permute-start(bf16[256,128]{1,0:T(8,128)(2,1)} %get-tuple-element.61), channel_id=1, source_target_pairs={{0,4},{1,5},{2,6},{3,7},{4,0},{5,1},{6,2},{7,3},{8,12},{9,13},{10,... | collective-permute-start | bytes 196616 | tf_op jit(solution)/shard_map/ppermute | solution.py:623
  16.5 1.3 %collective-permute-start.5 = (bf16[256,128]{1,0:T(8,128)(2,1)}, bf16[256,128]{1,0:T(8,128)(2,1)S(1)}, u32[]{:S(2)}, u32[]{:S(2)}) collective-permute-start(bf16[256,128]{1,0:T(8,128)(2,1)} %get-tuple-element.63), channel_id=1, source_target_pairs={{0,6},{1,7},{2,0},{3,1},{4,2},{5,3},{6,4},{7,5},{8,14},{9,15},{10,... | collective-permute-start | bytes 196616 | tf_op jit(solution)/shard_map/ppermute | solution.py:623
  17.8 1.0 %collective-permute-start.6 = (bf16[256,128]{1,0:T(8,128)(2,1)}, bf16[256,128]{1,0:T(8,128)(2,1)S(1)}, u32[]{:S(2)}, u32[]{:S(2)}) collective-permute-start(bf16[256,128]{1,0:T(8,128)(2,1)} %get-tuple-element.64), channel_id=1, source_target_pairs={{0,7},{1,0},{2,1},{3,2},{4,3},{5,4},{6,5},{7,6},{8,15},{9,8},{10,9... | collective-permute-start | bytes 196616 | tf_op jit(solution)/shard_map/ppermute | solution.py:623
  18.9 1.6 %copy-done = bf16[32,64,512]{2,1,0:T(8,128)(2,1)S(1)} copy-done((bf16[32,64,512]{2,1,0:T(8,128)(2,1)S(1)}, bf16[32,64,512]{2,1,0:T(8,128)(2,1)}, u32[]{:S(2)}) %copy-start) | copy-done | bytes 2097176
  20.5 1.2 %copy-done.3 = bf16[27,128,128]{2,1,0:T(8,128)(2,1)S(1)} copy-done((bf16[27,128,128]{2,1,0:T(8,128)(2,1)S(1)}, bf16[27,128,128]{2,1,0:T(8,128)(2,1)}, u32[]{:S(2)}) %copy-start.3) | copy-done | bytes 884760
  21.7 0.8 %copy-done.6 = s32[32,512]{1,0:T(8,128)S(1)} copy-done((s32[32,512]{1,0:T(8,128)S(1)}, s32[32,512]{1,0:T(8,128)}, u32[]{:S(2)}) %copy-start.6) | copy-done | bytes 65560
  22.5 1.1 %prepare.1 = (bf16[256,128]{1,0:T(8,128)(2,1)S(1)}, bf16[2048,512]{1,0:T(8,128)(2,1)S(1)}, bf16[1152,384]{1,0:T(8,128)(2,1)S(1)}, bf16[1152,384]{1,0:T(8,128)(2,1)S(1)}) custom-call(bf16[32,64,512]{2,1,0:T(8,128)(2,1)S(1)} %copy-done, s32[32,512]{1,0:T(8,128)S(1)} %copy-done.6, bf16[512,128]{1,0:T(8,128)(2,1)S(1)} %copy-done.5, ...), custom_call_target="tpu_custom_call" | custom-call | flops 268435456 | bytes 2097152 | tf_op jit(solution)/shard_map/prepare/pallas_call | solution.py:128
  23.7 0.8 %place.1 = (bf16[2048,128]{1,0:T(8,128)(2,1)S(1)}, bf16[288,128]{1,0:T(8,128)(2,1)S(1)}, bf16[288,128]{1,0:T(8,128)(2,1)S(1)}) custom-call(s32[2]{0:T(128)S(1)} %pad_add_fusion.base_ref, s32[32]{0:T(128)S(1)} %copy-done.7, bf16[256,128]{1,0:T(8,128)(2,1)S(1)} %get-tuple-element.57.refs_0_, bf16[256,128]{1,0:T(8,128)(2,1)S(1)} %collective-permute-done.1.refs_1_, ...), custom_call_target="tpu_custom_call" | custom-call | tf_op jit(solution)/shard_map/place/pallas_call | solution.py:269
  24.5 1.1 %collective-permute-start.7 = (bf16[288,128]{1,0:T(8,128)(2,1)S(1)}, bf16[288,128]{1,0:T(8,128)(2,1)S(1)}, u32[]{:S(2)}, u32[]{:S(2)}) collective-permute-start(bf16[288,128]{1,0:T(8,128)(2,1)S(1)} %get-tuple-element.66), channel_id=1, source_target_pairs={{0,1},{1,0},{2,3},{3,2},{4,5},{5,4},{6,7},{7,6},{8,9},{9,8},{10,11... | collective-permute-start | bytes 221192 | tf_op jit(solution)/shard_map/ppermute | solution.py:631
  25.6 0.7 %collective-permute-start.8 = (bf16[288,128]{1,0:T(8,128)(2,1)S(1)}, bf16[288,128]{1,0:T(8,128)(2,1)S(1)}, u32[]{:S(2)}, u32[]{:S(2)}) collective-permute-start(bf16[288,128]{1,0:T(8,128)(2,1)S(1)} %get-tuple-element.67), channel_id=1, source_target_pairs={{0,0},{1,2},{2,1},{3,4},{4,3},{5,6},{6,5},{7,7},{8,8},{9,10},{10,9... | collective-permute-start | bytes 221192 | tf_op jit(solution)/shard_map/ppermute | solution.py:631
  26.3 2.4 %inner.1.refs_3_ = bf16[11,112,128]{2,1,0:T(8,128)(2,1)S(1)} custom-call(s32[32]{0:T(128)S(1)} %copy-done.7, bf16[2048,128]{1,0:T(8,128)(2,1)S(1)} %get-tuple-element.65.block_ref.refs_0_, bf16[1152,384]{1,0:T(8,128)(2,1)S(1)} %get-tuple-element.68.wide1_ref.refs_4_.refs_8_), custom_call_target="tpu_custom_call" | custom-call | flops 1089994752 | bytes 1769472 | tf_op jit(solution)/shard_map/inner/pallas_call | solution.py:428
  28.6 0.3 collective-permute-done.7.even_ref
  28.9 0.6 %edge.1 = (bf16[288,128]{1,0:T(8,128)(2,1)S(1)}, bf16[288,128]{1,0:T(8,128)(2,1)S(1)}, bf16[368,128]{1,0:T(8,128)(2,1)S(1)}, bf16[368,128]{1,0:T(8,128)(2,1)S(1)}) custom-call(s32[2]{0:T(128)S(1)} %pad_add_fusion.base_ref, s32[32]{0:T(128)S(1)} %copy-done.7, bf16[2048,128]{1,0:T(8,128)(2,1)S(1)} %get-tuple-element.65.block_ref.refs_0_, ...), custom_call_target="tpu_custom_call" | custom-call | tf_op jit(solution)/shard_map/edge/pallas_call | solution.py:319
  29.6 0.7 %collective-permute-start.10 = (bf16[368,128]{1,0:T(8,128)(2,1)S(1)}, bf16[368,128]{1,0:T(8,128)(2,1)S(1)}, u32[]{:S(2)}, u32[]{:S(2)}) collective-permute-start(bf16[368,128]{1,0:T(8,128)(2,1)S(1)} %get-tuple-element.74), channel_id=1, source_target_pairs={{0,0},{8,16},{16,8},{24,24},{1,1},{9,17},{17,9},{25,25},{2,2},{10,... | collective-permute-start | bytes 282632 | tf_op jit(solution)/shard_map/ppermute | solution.py:631
  30.3 3.2 %middle.1 = (bf16[14,144,128]{2,1,0:T(8,128)(2,1)S(1)}, bf16[14,144,128]{2,1,0:T(8,128)(2,1)S(1)}, bf16[1024,128]{1,0:T(8,128)(2,1)S(1)}) custom-call(s32[32]{0:T(128)S(1)} %copy-done.7, bf16[2048,128]{1,0:T(8,128)(2,1)S(1)} %get-tuple-element.65.block_ref.refs_0_, bf16[288,128]{1,0:T(8,128)(2,1)S(1)} %get-tuple-element.71.refs_1_, ...), custom_call_target="tpu_custom_call" | custom-call | flops 1599602688 | bytes 1769472 | tf_op jit(solution)/shard_map/middle/pallas_call | solution.py:504
  33.6 3.2 %final.1 = (bf16[512,128]{1,0:T(8,128)(2,1)S(1)}, bf16[512,128]{1,0:T(8,128)(2,1)S(1)}, bf16[256,128]{1,0:T(8,128)(2,1)S(1)}, bf16[256,128]{1,0:T(8,128)(2,1)S(1...) custom-call(s32[2]{0:T(128)S(1)} %pad_add_fusion.base_ref, ...), custom_call_target="tpu_custom_call" | custom-call | flops 1415577600 | bytes 1769472 | tf_op jit(solution)/shard_map/final/pallas_call | solution.py:599
  36.8 4.9 %collective-permute-start.14 = (bf16[256,128]{1,0:T(8,128)(2,1)S(1)}, bf16[256,128]{1,0:T(8,128)(2,1)S(1)}, u32[]{:S(2)}, u32[]{:S(2)}) collective-permute-start(bf16[256,128]{1,0:T(8,128)(2,1)S(1)} %get-tuple-element.83), channel_id=1, source_target_pairs={{0,2},{1,3},{2,4},{3,5},{4,6},{5,7},{6,0},{7,1},{8,10},{9,11},{10,... | collective-permute-start | bytes 196616 | tf_op jit(solution)/shard_map/ppermute | solution.py:623
  41.7 1.9 %collective-permute-start.16 = (bf16[256,128]{1,0:T(8,128)(2,1)S(1)}, bf16[256,128]{1,0:T(8,128)(2,1)S(1)}, u32[]{:S(2)}, u32[]{:S(2)}) collective-permute-start(bf16[256,128]{1,0:T(8,128)(2,1)S(1)} %get-tuple-element.87), channel_id=1, source_target_pairs={{0,1},{1,2},{2,3},{3,4},{4,5},{5,6},{6,7},{7,0},{8,9},{9,10},{10,1... | collective-permute-start | bytes 196616 | tf_op jit(solution)/shard_map/ppermute | solution.py:623
  43.6 3.3 %collective-permute-start.12 = (bf16[256,128]{1,0:T(8,128)(2,1)S(1)}, bf16[256,128]{1,0:T(8,128)(2,1)S(1)}, u32[]{:S(2)}, u32[]{:S(2)}) collective-permute-start(bf16[256,128]{1,0:T(8,128)(2,1)S(1)} %get-tuple-element.81), channel_id=1, source_target_pairs={{0,3},{1,4},{2,5},{3,6},{4,7},{5,0},{6,1},{7,2},{8,11},{9,12},{10,... | collective-permute-start | bytes 196616 | tf_op jit(solution)/shard_map/ppermute | solution.py:623
  47.0 0.9 %collective-permute-start.13 = (bf16[256,128]{1,0:T(8,128)(2,1)S(1)}, bf16[256,128]{1,0:T(8,128)(2,1)S(1)}, u32[]{:S(2)}, u32[]{:S(2)}) collective-permute-start(bf16[256,128]{1,0:T(8,128)(2,1)S(1)} %get-tuple-element.82), channel_id=1, source_target_pairs={{0,6},{1,7},{2,0},{3,1},{4,2},{5,3},{6,4},{7,5},{8,14},{9,15},{10,... | collective-permute-start | bytes 196616 | tf_op jit(solution)/shard_map/ppermute | solution.py:623
  47.9 1.1 %collective-permute-start.15 = (bf16[256,128]{1,0:T(8,128)(2,1)S(1)}, bf16[256,128]{1,0:T(8,128)(2,1)S(1)}, u32[]{:S(2)}, u32[]{:S(2)}) collective-permute-start(bf16[256,128]{1,0:T(8,128)(2,1)S(1)} %get-tuple-element.85), channel_id=1, source_target_pairs={{0,5},{1,6},{2,7},{3,0},{4,1},{5,2},{6,3},{7,4},{8,13},{9,14},{10,... | collective-permute-start | bytes 196616 | tf_op jit(solution)/shard_map/ppermute | solution.py:623
  49.1 1.4 %collective-permute-start.17 = (bf16[256,128]{1,0:T(8,128)(2,1)S(1)}, bf16[256,128]{1,0:T(8,128)(2,1)S(1)}, u32[]{:S(2)}, u32[]{:S(2)}) collective-permute-start(bf16[256,128]{1,0:T(8,128)(2,1)S(1)} %get-tuple-element.89), channel_id=1, source_target_pairs={{0,7},{1,0},{2,1},{3,2},{4,3},{5,4},{6,5},{7,6},{8,15},{9,8},{10,9... | collective-permute-start | bytes 196616 | tf_op jit(solution)/shard_map/ppermute | solution.py:623
  50.5 0.8 %pad_maximum_fusion = bf16[2048,128]{1,0:T(8,128)(2,1)} fusion(bf16[512,128]{1,0:T(8,128)(2,1)S(1)} %get-tuple-element.97, bf16[1024,128]{1,0:T(8,128)(2,1)S(1)} %get-tuple-element.96.refs_7_, bf16[512,128]{1,0:T(8,128)(2,1)S(1)} %get-tuple-element.95), kind=kLoop, calls=%fused_computation | loop fusion | flops 1572864 | bytes 1048576 | tf_op jit(solution)/shard_map/concatenate | solution.py:662
  51.3 1.1 %up.2.refs_6_ = bf16[32,64,512]{2,1,0:T(8,128)(2,1)} custom-call(bf16[32,64,512]{2,1,0:T(8,128)(2,1)S(1)} %copy-done.1, bf16[2048,512]{1,0:T(8,128)(2,1)S(1)} %get-tuple-element.56.mask_ref, bf16[128,512]{1,0:T(8,128)(2,1)S(1)} %copy-done.4, bf16[256,128]{1,0:T(8,128)(2,1)S(1)} %collective-permute-done.14.refs_0_, ...), custom_call_target="tpu_custom_call" | custom-call | flops 134217728 | bytes 2097152 | tf_op jit(solution)/shard_map/up/pallas_call | solution.py:179
  52.5 2.6 %collective-permute-done.12.refs_1_ = bf16[256,128]{1,0:T(8,128)(2,1)S(1)} collective-permute-done((bf16[256,128]{1,0:T(8,128)(2,1)S(1)}, bf16[256,128]{1,0:T(8,128)(2,1)S(1)}, u32[]{:S(2)}, u32[]{:S(2)}) %collective-permute-start.12) | collective-permute-done | bytes 65568 | tf_op jit(solution)/shard_map/ppermute | solution.py:623
  55.0 1.0 %collective-permute-done.15.refs_3_ = bf16[256,128]{1,0:T(8,128)(2,1)S(1)} collective-permute-done((bf16[256,128]{1,0:T(8,128)(2,1)S(1)}, bf16[256,128]{1,0:T(8,128)(2,1)S(1)}, u32[]{:S(2)}, u32[]{:S(2)}) %collective-permute-start.15) | collective-permute-done | bytes 65568 | tf_op jit(solution)/shard_map/ppermute | solution.py:623
  56.1 0.4 collective-permute-done.17.refs_5_
  56.5 2.3 %up.3 = bf16[32,64,512]{2,1,0:T(8,128)(2,1)} custom-call(bf16[32,64,512]{2,1,0:T(8,128)(2,1)S(1)} %copy-done.1, bf16[2048,512]{1,0:T(8,128)(2,1)S(1)} %get-tuple-element.56.mask_ref, bf16[128,512]{1,0:T(8,128)(2,1)S(1)} %copy-done.4, bf16[256,128]{1,0:T(8,128)(2,1)S(1)} %collective-permute-done.11.refs_0_, ...), custom_call_target="tpu_custom_call", output_to_operand_aliasing={{}: (9, {})} | custom-call | flops 134217728 | bytes 2097152 | tf_op jit(solution)/shard_map/up/pallas_call | solution.py:179
  (31 shorter events, 0.4 us)
Async XLA Ops:
  0.6 18.3 %copy-start.5 = (bf16[512,128]{1,0:T(8,128)(2,1)S(1)}, bf16[512,128]{1,0:T(8,128)(2,1)}, u32[]{:S(2)}) copy-start(bf16[512,128]{1,0:T(8,128)(2,1)} %w_down_ref) | copy-start | bytes 393220
  0.6 18.3 %copy-start.2 = (bf16[27,128,128]{2,1,0:T(8,128)(2,1)S(1)}, bf16[27,128,128]{2,1,0:T(8,128)(2,1)}, u32[]{:S(2)}) copy-start(bf16[27,128,128]{2,1,0:T(8,128)(2,1)} %w1_ref) | copy-start | bytes 2654212
  4.6 19.1 %copy-start.7 = (s32[32]{0:T(128)S(1)}, s32[32]{0:T(128)}, u32[]{:S(2)}) copy-start(s32[32]{0:T(128)} %source_ref.9) | copy-start | bytes 388
  4.6 11.9 %collective-permute-start = (bf16[256,128]{1,0:T(8,128)(2,1)}, bf16[256,128]{1,0:T(8,128)(2,1)S(1)}, u32[]{:S(2)}, u32[]{:S(2)}) collective-permute-start(bf16[256,128]{1,0:T(8,128)(2,1)} %get-tuple-element.50), channel_id=1, source_target_pairs={{0,5},{1,6},{2,7},{3,0},{4,1},{5,2},{6,3},{7,4},{8,13},{9,14},{10,... | collective-permute-start | bytes 196616 | tf_op jit(solution)/shard_map/ppermute | solution.py:623
  9.6 8.2 %collective-permute-start.1 = (bf16[256,128]{1,0:T(8,128)(2,1)}, bf16[256,128]{1,0:T(8,128)(2,1)S(1)}, u32[]{:S(2)}, u32[]{:S(2)}) collective-permute-start(bf16[256,128]{1,0:T(8,128)(2,1)} %get-tuple-element.58), channel_id=1, source_target_pairs={{0,1},{1,2},{2,3},{3,4},{4,5},{5,6},{6,7},{7,0},{8,9},{9,10},{10,1... | collective-permute-start | bytes 196616 | tf_op jit(solution)/shard_map/ppermute | solution.py:623
  11.1 12.5 %collective-permute-start.2 = (bf16[256,128]{1,0:T(8,128)(2,1)}, bf16[256,128]{1,0:T(8,128)(2,1)S(1)}, u32[]{:S(2)}, u32[]{:S(2)}) collective-permute-start(bf16[256,128]{1,0:T(8,128)(2,1)} %get-tuple-element.59), channel_id=1, source_target_pairs={{0,2},{1,3},{2,4},{3,5},{4,6},{5,7},{6,0},{7,1},{8,10},{9,11},{10,... | collective-permute-start | bytes 196616 | tf_op jit(solution)/shard_map/ppermute | solution.py:623
  11.2 12.5 %collective-permute-start.3 = (bf16[256,128]{1,0:T(8,128)(2,1)}, bf16[256,128]{1,0:T(8,128)(2,1)S(1)}, u32[]{:S(2)}, u32[]{:S(2)}) collective-permute-start(bf16[256,128]{1,0:T(8,128)(2,1)} %get-tuple-element.60), channel_id=1, source_target_pairs={{0,3},{1,4},{2,5},{3,6},{4,7},{5,0},{6,1},{7,2},{8,11},{9,12},{10,... | collective-permute-start | bytes 196616 | tf_op jit(solution)/shard_map/ppermute | solution.py:623
  13.0 10.7 %collective-permute-start.4 = (bf16[256,128]{1,0:T(8,128)(2,1)}, bf16[256,128]{1,0:T(8,128)(2,1)S(1)}, u32[]{:S(2)}, u32[]{:S(2)}) collective-permute-start(bf16[256,128]{1,0:T(8,128)(2,1)} %get-tuple-element.61), channel_id=1, source_target_pairs={{0,4},{1,5},{2,6},{3,7},{4,0},{5,1},{6,2},{7,3},{8,12},{9,13},{10,... | collective-permute-start | bytes 196616 | tf_op jit(solution)/shard_map/ppermute | solution.py:623
  16.5 7.2 %collective-permute-start.5 = (bf16[256,128]{1,0:T(8,128)(2,1)}, bf16[256,128]{1,0:T(8,128)(2,1)S(1)}, u32[]{:S(2)}, u32[]{:S(2)}) collective-permute-start(bf16[256,128]{1,0:T(8,128)(2,1)} %get-tuple-element.63), channel_id=1, source_target_pairs={{0,6},{1,7},{2,0},{3,1},{4,2},{5,3},{6,4},{7,5},{8,14},{9,15},{10,... | collective-permute-start | bytes 196616 | tf_op jit(solution)/shard_map/ppermute | solution.py:623
  17.8 5.9 %collective-permute-start.6 = (bf16[256,128]{1,0:T(8,128)(2,1)}, bf16[256,128]{1,0:T(8,128)(2,1)S(1)}, u32[]{:S(2)}, u32[]{:S(2)}) collective-permute-start(bf16[256,128]{1,0:T(8,128)(2,1)} %get-tuple-element.64), channel_id=1, source_target_pairs={{0,7},{1,0},{2,1},{3,2},{4,3},{5,4},{6,5},{7,6},{8,15},{9,8},{10,9... | collective-permute-start | bytes 196616 | tf_op jit(solution)/shard_map/ppermute | solution.py:623
  18.9 1.6 %copy-start = (bf16[32,64,512]{2,1,0:T(8,128)(2,1)S(1)}, bf16[32,64,512]{2,1,0:T(8,128)(2,1)}, u32[]{:S(2)}) copy-start(bf16[32,64,512]{2,1,0:T(8,128)(2,1)} %fine_ref.4) | copy-start | bytes 6291460
  20.5 1.2 %copy-start.3 = (bf16[27,128,128]{2,1,0:T(8,128)(2,1)S(1)}, bf16[27,128,128]{2,1,0:T(8,128)(2,1)}, u32[]{:S(2)}) copy-start(bf16[27,128,128]{2,1,0:T(8,128)(2,1)} %w2_ref) | copy-start | bytes 2654212
  21.7 0.8 %copy-start.6 = (s32[32,512]{1,0:T(8,128)S(1)}, s32[32,512]{1,0:T(8,128)}, u32[]{:S(2)}) copy-start(s32[32,512]{1,0:T(8,128)} %mask_ref) | copy-start | bytes 196612
  24.5 4.4 %collective-permute-start.7 = (bf16[288,128]{1,0:T(8,128)(2,1)S(1)}, bf16[288,128]{1,0:T(8,128)(2,1)S(1)}, u32[]{:S(2)}, u32[]{:S(2)}) collective-permute-start(bf16[288,128]{1,0:T(8,128)(2,1)S(1)} %get-tuple-element.66), channel_id=1, source_target_pairs={{0,1},{1,0},{2,3},{3,2},{4,5},{5,4},{6,7},{7,6},{8,9},{9,8},{10,11... | collective-permute-start | bytes 221192 | tf_op jit(solution)/shard_map/ppermute | solution.py:631
  25.6 3.3 %collective-permute-start.8 = (bf16[288,128]{1,0:T(8,128)(2,1)S(1)}, bf16[288,128]{1,0:T(8,128)(2,1)S(1)}, u32[]{:S(2)}, u32[]{:S(2)}) collective-permute-start(bf16[288,128]{1,0:T(8,128)(2,1)S(1)} %get-tuple-element.67), channel_id=1, source_target_pairs={{0,0},{1,2},{2,1},{3,4},{4,3},{5,6},{6,5},{7,7},{8,8},{9,10},{10,9... | collective-permute-start | bytes 221192 | tf_op jit(solution)/shard_map/ppermute | solution.py:631
  29.5 4.0 %collective-permute-start.9 = (bf16[368,128]{1,0:T(8,128)(2,1)S(1)}, bf16[368,128]{1,0:T(8,128)(2,1)S(1)}, u32[]{:S(2)}, u32[]{:S(2)}) collective-permute-start(bf16[368,128]{1,0:T(8,128)(2,1)S(1)} %get-tuple-element.73), channel_id=1, source_target_pairs={{0,8},{8,0},{16,24},{24,16},{1,9},{9,1},{17,25},{25,17},{2,10},{10... | collective-permute-start | bytes 282632 | tf_op jit(solution)/shard_map/ppermute | solution.py:631
  29.6 3.9 %collective-permute-start.10 = (bf16[368,128]{1,0:T(8,128)(2,1)S(1)}, bf16[368,128]{1,0:T(8,128)(2,1)S(1)}, u32[]{:S(2)}, u32[]{:S(2)}) collective-permute-start(bf16[368,128]{1,0:T(8,128)(2,1)S(1)} %get-tuple-element.74), channel_id=1, source_target_pairs={{0,0},{8,16},{16,8},{24,24},{1,1},{9,17},{17,9},{25,25},{2,2},{10,... | collective-permute-start | bytes 282632 | tf_op jit(solution)/shard_map/ppermute | solution.py:631
  33.6 17.8 %copy-start.1 = (bf16[32,64,512]{2,1,0:T(8,128)(2,1)S(1)}, bf16[32,64,512]{2,1,0:T(8,128)(2,1)}, u32[]{:S(2)}) copy-start(bf16[32,64,512]{2,1,0:T(8,128)(2,1)} %fine_ref.4) | copy-start | bytes 6291460
  33.6 17.8 %copy-start.4 = (bf16[128,512]{1,0:T(8,128)(2,1)S(1)}, bf16[128,512]{1,0:T(8,128)(2,1)}, u32[]{:S(2)}) copy-start(bf16[128,512]{1,0:T(8,128)(2,1)} %w_ref.3) | copy-start | bytes 393220
  36.8 11.1 %collective-permute-start.14 = (bf16[256,128]{1,0:T(8,128)(2,1)S(1)}, bf16[256,128]{1,0:T(8,128)(2,1)S(1)}, u32[]{:S(2)}, u32[]{:S(2)}) collective-permute-start(bf16[256,128]{1,0:T(8,128)(2,1)S(1)} %get-tuple-element.83), channel_id=1, source_target_pairs={{0,2},{1,3},{2,4},{3,5},{4,6},{5,7},{6,0},{7,1},{8,10},{9,11},{10,... | collective-permute-start | bytes 196616 | tf_op jit(solution)/shard_map/ppermute | solution.py:623
  41.7 7.4 %collective-permute-start.16 = (bf16[256,128]{1,0:T(8,128)(2,1)S(1)}, bf16[256,128]{1,0:T(8,128)(2,1)S(1)}, u32[]{:S(2)}, u32[]{:S(2)}) collective-permute-start(bf16[256,128]{1,0:T(8,128)(2,1)S(1)} %get-tuple-element.87), channel_id=1, source_target_pairs={{0,1},{1,2},{2,3},{3,4},{4,5},{5,6},{6,7},{7,0},{8,9},{9,10},{10,1... | collective-permute-start | bytes 196616 | tf_op jit(solution)/shard_map/ppermute | solution.py:623
  43.6 8.8 %collective-permute-start.11 = (bf16[256,128]{1,0:T(8,128)(2,1)S(1)}, bf16[256,128]{1,0:T(8,128)(2,1)S(1)}, u32[]{:S(2)}, u32[]{:S(2)}) collective-permute-start(bf16[256,128]{1,0:T(8,128)(2,1)S(1)} %get-tuple-element.80), channel_id=1, source_target_pairs={{0,4},{1,5},{2,6},{3,7},{4,0},{5,1},{6,2},{7,3},{8,12},{9,13},{10,... | collective-permute-start | bytes 196616 | tf_op jit(solution)/shard_map/ppermute | solution.py:623
  43.6 11.4 %collective-permute-start.12 = (bf16[256,128]{1,0:T(8,128)(2,1)S(1)}, bf16[256,128]{1,0:T(8,128)(2,1)S(1)}, u32[]{:S(2)}, u32[]{:S(2)}) collective-permute-start(bf16[256,128]{1,0:T(8,128)(2,1)S(1)} %get-tuple-element.81), channel_id=1, source_target_pairs={{0,3},{1,4},{2,5},{3,6},{4,7},{5,0},{6,1},{7,2},{8,11},{9,12},{10,... | collective-permute-start | bytes 196616 | tf_op jit(solution)/shard_map/ppermute | solution.py:623
  47.0 8.0 %collective-permute-start.13 = (bf16[256,128]{1,0:T(8,128)(2,1)S(1)}, bf16[256,128]{1,0:T(8,128)(2,1)S(1)}, u32[]{:S(2)}, u32[]{:S(2)}) collective-permute-start(bf16[256,128]{1,0:T(8,128)(2,1)S(1)} %get-tuple-element.82), channel_id=1, source_target_pairs={{0,6},{1,7},{2,0},{3,1},{4,2},{5,3},{6,4},{7,5},{8,14},{9,15},{10,... | collective-permute-start | bytes 196616 | tf_op jit(solution)/shard_map/ppermute | solution.py:623
  47.9 8.1 %collective-permute-start.15 = (bf16[256,128]{1,0:T(8,128)(2,1)S(1)}, bf16[256,128]{1,0:T(8,128)(2,1)S(1)}, u32[]{:S(2)}, u32[]{:S(2)}) collective-permute-start(bf16[256,128]{1,0:T(8,128)(2,1)S(1)} %get-tuple-element.85), channel_id=1, source_target_pairs={{0,5},{1,6},{2,7},{3,0},{4,1},{5,2},{6,3},{7,4},{8,13},{9,14},{10,... | collective-permute-start | bytes 196616 | tf_op jit(solution)/shard_map/ppermute | solution.py:623
  49.1 7.4 %collective-permute-start.17 = (bf16[256,128]{1,0:T(8,128)(2,1)S(1)}, bf16[256,128]{1,0:T(8,128)(2,1)S(1)}, u32[]{:S(2)}, u32[]{:S(2)}) collective-permute-start(bf16[256,128]{1,0:T(8,128)(2,1)S(1)} %get-tuple-element.89), channel_id=1, source_target_pairs={{0,7},{1,0},{2,1},{3,2},{4,3},{5,4},{6,5},{7,6},{8,15},{9,8},{10,9... | collective-permute-start | bytes 196616 | tf_op jit(solution)/shard_map/ppermute | solution.py:623
